TPU v7x, 32 devices: a whole 2x2x4 slice. The times are simulated.
32 devices in a mesh: parts: 2 (over x), leaf: 16 (over z, y, core).
Axes of the slice: x: 2, y: 2, z: 4, core: 2. Of those that a mesh axis runs over, the one named last changes fastest.
Arguments:
- samples: bfloat16 [64, 8, 8192], P(None, None, ('parts', 'leaf')), parts along dimension 2, may hold values from -6 to 6
- interp_in: bfloat16 [32, 64, 8192], P(None, None, ('parts', 'leaf')), parts along dimension 2, may hold values from -0.75 to 0.75
- top_blocks: bfloat16 [4, 32, 64, 8192], P(None, None, None, ('parts', 'leaf')), parts along dimension 3, may hold values from -0.875 to 0.875
- top_pattern: int32 [4, 2, 8192], P(None, None, ('parts', 'leaf')), parts along dimension 2, may hold values 0 or 1
- bottom_blocks: bfloat16 [4, 32, 64, 8192], P(None, None, None, ('parts', 'leaf')), parts along dimension 3, may hold values from -0.875 to 0.875
- bottom_pattern: int32 [4, 2, 8192], P(None, None, ('parts', 'leaf')), parts along dimension 2, may hold values 0 or 1
- interp_out: bfloat16 [64, 32, 8192], P(None, None, ('parts', 'leaf')), parts along dimension 2, may hold values from -1 to 1
Outputs:
- image: bfloat16 [64, 8, 8192], P(None, None, ('parts', 'leaf')), parts along dimension 2
There are 2 independent parts, one for each index of `parts`. A program takes and returns all parts, laid end to end along the dimension named above; each array names one. Nothing has to cross between parts.
All inputs are finite; a program needn't handle non-finite values. No bound on the sum of `top_pattern` or of `bottom_pattern` on one device may be relied on, other than what follows from the above.
Results may differ from a plain program's by a relative error of at most 0.0094.
Values may be sent and summed in bfloat16 or wider, within the bound.
No kernel may reach another device: no remote copies, remote signals or barrier semaphores. Data moves between devices by JAX's collectives and lax.ppermute only.
A program may use at most 64 MiB of HBM per device.

v0:
```python
import jax
import jax.numpy as jnp
from jax import lax
from jax.sharding import PartitionSpec as P


def swapped(value, axis, apart):
    mask = 2**apart
    pairs = [(source, source ^ mask) for source in range(lax.axis_size(axis))]
    return lax.ppermute(value, axis, pairs)


def contract(weights, state):
    product = weights[:, :, None].astype(jnp.float32) * state[None].astype(jnp.float32)
    return jnp.sum(product, axis=1)


def apply_pattern(blocks, pattern):
    rank_size = blocks.shape[0]
    present = jnp.repeat(pattern, rank_size, axis=0).astype(jnp.bfloat16)
    return blocks * present[None]


def partner_level(current, partner, weights, is_lower):
    lower_state = jnp.where(is_lower, current, partner)
    upper_state = jnp.where(is_lower, partner, current)
    both_states = jnp.concatenate([lower_state, upper_state], axis=0)
    return contract(weights, both_states).astype(jnp.bfloat16)


def transpose_boxes(values):
    return lax.all_to_all(values, "leaf", split_axis=1, concat_axis=1, tiled=True)


def local(samples, interp_in, top_blocks, top_pattern, bottom_blocks, bottom_pattern, interp_out):
    level_count = top_blocks.shape[0]
    rank_size = interp_in.shape[0]
    rhs_count = samples.shape[1]
    box_count = samples.shape[2]
    leaf_count = lax.axis_size("leaf")
    bit_count = leaf_count.bit_length() - 1
    leaf_place = lax.axis_index("leaf")
    current = contract(interp_in, samples).astype(jnp.bfloat16)
    for level in range(level_count):
        bit_high = bit_count - 1 - level
        partner = swapped(current, "leaf", bit_high)
        weights = apply_pattern(top_blocks[level], top_pattern[level])
        is_lower = leaf_place // 2**bit_high % 2 == 0
        current = partner_level(current, partner, weights, is_lower)
    flat_rows = current.reshape(rank_size * rhs_count, box_count)
    current = transpose_boxes(flat_rows).reshape(rank_size, rhs_count, box_count)
    for level in range(level_count):
        partner = swapped(current, "leaf", level)
        weights = apply_pattern(bottom_blocks[level], bottom_pattern[level])
        is_lower = leaf_place // 2**level % 2 == 0
        current = partner_level(current, partner, weights, is_lower)
    result = contract(interp_out, current)
    return result.astype(jnp.bfloat16)


def solution(mesh):
    return jax.shard_map(
        local,
        mesh=mesh,
        in_specs=(
            P(None, None, ("parts", "leaf")),
            P(None, None, ("parts", "leaf")),
            P(None, None, None, ("parts", "leaf")),
            P(None, None, ("parts", "leaf")),
            P(None, None, None, ("parts", "leaf")),
            P(None, None, ("parts", "leaf")),
            P(None, None, ("parts", "leaf")),
        ),
        out_specs=P(None, None, ("parts", "leaf")),
        check_vma=False,
    )
```

profile of v0, /device:TPU:0, one launch (start us, length us, event | category | flops | bytes accessed | tf_op | source)
XLA Modules:
  0.0 87.3 jit_solution(2819829314520045976)
XLA Ops:
  0.0 0.0 copy-start.2
  0.0 0.0 copy-start
  0.0 1.6 %convert_element_type.308 = f32[32,64,256]{2,1,0:T(8,128)S(1)} convert(bf16[32,64,256]{2,1,0:T(8,128)(2,1)} %param.8) | non-fusion elementwise | flops 524288 | bytes 3145728 | tf_op jit(solution)/shard_map/convert_element_type | solution.py:14
  1.6 1.0 %convert_element_type.309 = f32[64,8,256]{2,1,0:T(8,128)S(1)} convert(bf16[64,8,256]{2,1,0:T(8,128)(2,1)} %param.7) | non-fusion elementwise | flops 131072 | bytes 786432 | tf_op jit(solution)/shard_map/convert_element_type | solution.py:14
  2.6 1.6 %multiply_reduce_fusion.9 = bf16[32,8,256]{2,1,0:T(8,128)(2,1)S(1)} fusion(f32[64,8,256]{2,1,0:T(8,128)S(1)} %convert_element_type.309, f32[32,64,256]{2,1,0:T(8,128)S(1)} %convert_element_type.308), kind=kLoop, calls=%fused_computation.9 | loop fusion | flops 8323072 | bytes 2752512 | tf_op jit(solution)/shard_map/reduce_sum | solution.py:15
  4.2 4.1 %collective-permute-start = (bf16[32,8,256]{2,1,0:T(8,128)(2,1)S(1)}, bf16[32,8,256]{2,1,0:T(8,128)(2,1)S(1)}, u32[]{:S(2)}, u32[]{:S(2)}) collective-permute-start(bf16[32,8,256]{2,1,0:T(8,128)(2,1)S(1)} %multiply_reduce_fusion.9), channel_id=1, source_target_pairs={{0,8},{1,9},{2,10},{3,11},{4,12},{5,13},{6,14},{7,15},{8,0},{9,1},... | collective-permute-start | bytes 393224 | tf_op jit(solution)/shard_map/ppermute | solution.py:10
  8.3 0.0 copy-done.2
  8.4 0.0 copy-done
  8.4 2.7 %fusion.3 = (f32[32,64,256]{2,1,0:T(8,128)S(1)}, f32[32,64,256]{2,1,0:T(8,128)}, f32[32,64,256]{2,1,0:T(8,128)}, f32[32,64,256]{2,1,0:T(8,128)}) fusion(bf16[4,32,64,256]{3,2,1,0:T(8,128)(2,1)S(1)} %copy-done, bf16[64,256]{1,0:T(8,128)(2,1)S(1)} %bitcast.56, bf16[64,256]{1,0:T(8,128)(2,1)S(1)} %bitcast.58, bf16[64,256]{1,0:T(8,128)(2,1)S(1)} %bitcast.62, ...), kind=kLoop, calls=%fused_computation.17 | loop fusion | flops 4194304 | bytes 12713984 | tf_op jit(solution)/shard_map/convert_element_type | solution.py:14
  11.1 3.5 %collective-permute-done = bf16[32,8,256]{2,1,0:T(8,128)(2,1)S(1)} collective-permute-done((bf16[32,8,256]{2,1,0:T(8,128)(2,1)S(1)}, bf16[32,8,256]{2,1,0:T(8,128)(2,1)S(1)}, u32[]{:S(2)}, u32[]{:S(2)}) %collective-permute-start) | collective-permute-done | bytes 131104 | tf_op jit(solution)/shard_map/ppermute | solution.py:10
  14.7 3.1 %multiply_reduce_fusion.8 = bf16[32,8,256]{2,1,0:T(8,128)(2,1)S(1)} fusion(f32[64,8,256]{2,1,0:T(8,128)S(1)} %maximum_convert_fusion, f32[32,64,256]{2,1,0:T(8,128)} %get-tuple-element.11), kind=kLoop, calls=%fused_computation.8 | loop fusion | flops 8323072 | bytes 2752512 | tf_op jit(solution)/shard_map/reduce_sum | solution.py:15
  17.8 0.8 collective-permute-start.1
  18.6 4.2 %collective-permute-done.1 = bf16[32,8,256]{2,1,0:T(8,128)(2,1)S(1)} collective-permute-done((bf16[32,8,256]{2,1,0:T(8,128)(2,1)S(1)}, bf16[32,8,256]{2,1,0:T(8,128)(2,1)S(1)}, u32[]{:S(2)}, u32[]{:S(2)}) %collective-permute-start.1) | collective-permute-done | bytes 131104 | tf_op jit(solution)/shard_map/ppermute | solution.py:10
  22.9 3.1 %multiply_reduce_fusion.7 = bf16[32,8,256]{2,1,0:T(8,128)(2,1)S(1)} fusion(f32[64,8,256]{2,1,0:T(8,128)S(1)} %maximum_convert_fusion.1, f32[32,64,256]{2,1,0:T(8,128)} %get-tuple-element.12), kind=kLoop, calls=%fused_computation.7 | loop fusion | flops 8323072 | bytes 2752512 | tf_op jit(solution)/shard_map/reduce_sum | solution.py:15
  26.0 1.6 %collective-permute-start.2 = (bf16[32,8,256]{2,1,0:T(8,128)(2,1)S(1)}, bf16[32,8,256]{2,1,0:T(8,128)(2,1)S(1)}, u32[]{:S(2)}, u32[]{:S(2)}) collective-permute-start(bf16[32,8,256]{2,1,0:T(8,128)(2,1)S(1)} %multiply_reduce_fusion.7), channel_id=1, source_target_pairs={{0,2},{1,3},{2,0},{3,1},{4,6},{5,7},{6,4},{7,5},{8,10},{9,11},{10,... | collective-permute-start | bytes 393224 | tf_op jit(solution)/shard_map/ppermute | solution.py:10
  27.6 3.4 %collective-permute-done.2 = bf16[32,8,256]{2,1,0:T(8,128)(2,1)S(1)} collective-permute-done((bf16[32,8,256]{2,1,0:T(8,128)(2,1)S(1)}, bf16[32,8,256]{2,1,0:T(8,128)(2,1)S(1)}, u32[]{:S(2)}, u32[]{:S(2)}) %collective-permute-start.2) | collective-permute-done | bytes 131104 | tf_op jit(solution)/shard_map/ppermute | solution.py:10
  31.1 0.0 copy-start.3
  31.1 3.1 %multiply_reduce_fusion.6 = bf16[32,8,256]{2,1,0:T(8,128)(2,1)S(1)} fusion(f32[64,8,256]{2,1,0:T(8,128)S(1)} %maximum_convert_fusion.2, f32[32,64,256]{2,1,0:T(8,128)} %get-tuple-element.10), kind=kLoop, calls=%fused_computation.6 | loop fusion | flops 8323072 | bytes 2752512 | tf_op jit(solution)/shard_map/reduce_sum | solution.py:15
  34.2 0.1 collective-permute-start.3
  34.3 1.3 %collective-permute-done.3 = bf16[32,8,256]{2,1,0:T(8,128)(2,1)S(1)} collective-permute-done((bf16[32,8,256]{2,1,0:T(8,128)(2,1)S(1)}, bf16[32,8,256]{2,1,0:T(8,128)(2,1)S(1)}, u32[]{:S(2)}, u32[]{:S(2)}) %collective-permute-start.3) | collective-permute-done | bytes 131104 | tf_op jit(solution)/shard_map/ppermute | solution.py:10
  35.7 1.6 %multiply_reduce_fusion.5 = bf16[32,8,256]{2,1,0:T(8,128)(2,1)S(1)} fusion(f32[64,8,256]{2,1,0:T(8,128)S(1)} %maximum_convert_fusion.3, f32[32,64,256]{2,1,0:T(8,128)S(1)} %get-tuple-element.9), kind=kLoop, calls=%fused_computation.5 | loop fusion | flops 8323072 | bytes 2752512 | tf_op jit(solution)/shard_map/reduce_sum | solution.py:15
  37.3 0.7 convert_element_type.319
  38.0 1.5 %copy.10 = bf16[256,16,16]{0,2,1:T(8,128)(2,1)} copy(bf16[256,16,16]{2,1,0:T(8,128)(2,1)S(1)} %convert_element_type.319) | data formatting | bytes 262144 | tf_op jit(solution)/shard_map/convert_element_type | solution.py:28
  39.5 6.5 %all-to-all-start = ((bf16[256,16,16]{0,2,1:T(8,128)(2,1)}), bf16[256,16,16]{0,2,1:T(8,128)(2,1)S(1)}, u32[]{:S(2)}, u32[]{:S(2)}) async-start(bf16[256,16,16]{0,2,1:T(8,128)(2,1)} %copy.10), calls=%async_computation | async-start | bytes 262144 | tf_op jit(solution)/shard_map/all_to_all | solution.py:32
  46.0 0.0 copy-done.3
  46.0 7.7 %all-to-all-done = bf16[256,16,16]{0,2,1:T(8,128)(2,1)S(1)} async-done(((bf16[256,16,16]{0,2,1:T(8,128)(2,1)}), bf16[256,16,16]{0,2,1:T(8,128)(2,1)S(1)}, u32[]{:S(2)}, u32[]{:S(2)}) %all-to-all-start) | async-done | bytes 131104 | tf_op jit(solution)/shard_map/all_to_all | solution.py:32
  53.7 0.9 %copy.11 = bf16[256,16,16]{2,1,0:T(8,128)(2,1)S(1)} copy(bf16[256,16,16]{0,2,1:T(8,128)(2,1)S(1)} %all-to-all-done) | data formatting | bytes 262144 | tf_op jit(solution)/shard_map/all_to_all | solution.py:32
  54.7 1.0 %reshape.269 = bf16[32,8,256]{2,1,0:T(8,128)(2,1)S(1)} reshape(bf16[256,16,16]{2,1,0:T(8,128)(2,1)S(1)} %copy.11) | data formatting | bytes 262144 | tf_op jit(solution)/shard_map/reshape | solution.py:51
  55.7 0.1 collective-permute-start.4
  55.8 2.7 %fusion.7 = (f32[32,64,256]{2,1,0:T(8,128)S(1)}, f32[32,64,256]{2,1,0:T(8,128)S(1)}, f32[32,64,256]{2,1,0:T(8,128)S(1)}, f32[32,64,256]{2,1,0:T(8,128)S(1)}) fusion(bf16[4,32,64,256]{3,2,1,0:T(8,128)(2,1)} %param.11, bf16[64,256]{1,0:T(8,128)(2,1)S(1)} %bitcast.59, bf16[64,256]{1,0:T(8,128)(2,1)S(1)} %bitcast.61, bf16[64,256]{1,0:T(8,128)(2,1)S(1)} %bitcast.57, ...), kind=kLoop, calls=%fused_computation.25 | loop fusion | flops 4194304 | bytes 12713984 | tf_op jit(solution)/shard_map/convert_element_type | solution.py:14
  58.6 0.0 collective-permute-done.4
  58.7 1.6 %multiply_reduce_fusion.4 = bf16[32,8,256]{2,1,0:T(8,128)(2,1)S(1)} fusion(f32[64,8,256]{2,1,0:T(8,128)S(1)} %maximum_convert_fusion.4, f32[32,64,256]{2,1,0:T(8,128)S(1)} %get-tuple-element.7), kind=kLoop, calls=%fused_computation.4 | loop fusion | flops 8323072 | bytes 2752512 | tf_op jit(solution)/shard_map/reduce_sum | solution.py:15
  60.2 0.0 copy-start.1
  60.2 0.1 collective-permute-start.5
  60.3 5.9 %collective-permute-done.5 = bf16[32,8,256]{2,1,0:T(8,128)(2,1)S(1)} collective-permute-done((bf16[32,8,256]{2,1,0:T(8,128)(2,1)S(1)}, bf16[32,8,256]{2,1,0:T(8,128)(2,1)S(1)}, u32[]{:S(2)}, u32[]{:S(2)}) %collective-permute-start.5) | collective-permute-done | bytes 131104 | tf_op jit(solution)/shard_map/ppermute | solution.py:10
  66.3 1.6 %multiply_reduce_fusion.3 = bf16[32,8,256]{2,1,0:T(8,128)(2,1)S(1)} fusion(f32[64,8,256]{2,1,0:T(8,128)S(1)} %maximum_convert_fusion.5, f32[32,64,256]{2,1,0:T(8,128)S(1)} %get-tuple-element.8), kind=kLoop, calls=%fused_computation.3 | loop fusion | flops 8323072 | bytes 2752512 | tf_op jit(solution)/shard_map/reduce_sum | solution.py:15
  67.8 0.1 collective-permute-start.6
  67.9 5.1 %collective-permute-done.6 = bf16[32,8,256]{2,1,0:T(8,128)(2,1)S(1)} collective-permute-done((bf16[32,8,256]{2,1,0:T(8,128)(2,1)S(1)}, bf16[32,8,256]{2,1,0:T(8,128)(2,1)S(1)}, u32[]{:S(2)}, u32[]{:S(2)}) %collective-permute-start.6) | collective-permute-done | bytes 131104 | tf_op jit(solution)/shard_map/ppermute | solution.py:10
  73.1 1.6 %multiply_reduce_fusion.2 = bf16[32,8,256]{2,1,0:T(8,128)(2,1)S(1)} fusion(f32[64,8,256]{2,1,0:T(8,128)S(1)} %maximum_convert_fusion.6, f32[32,64,256]{2,1,0:T(8,128)S(1)} %get-tuple-element.6), kind=kLoop, calls=%fused_computation.2 | loop fusion | flops 8323072 | bytes 2752512 | tf_op jit(solution)/shard_map/reduce_sum | solution.py:15
  74.7 0.5 collective-permute-start.7
  75.1 0.0 copy-done.1
  75.1 0.2 convert_element_type.283
  75.4 7.3 %collective-permute-done.7 = bf16[32,8,256]{2,1,0:T(8,128)(2,1)S(1)} collective-permute-done((bf16[32,8,256]{2,1,0:T(8,128)(2,1)S(1)}, bf16[32,8,256]{2,1,0:T(8,128)(2,1)S(1)}, u32[]{:S(2)}, u32[]{:S(2)}) %collective-permute-start.7) | collective-permute-done | bytes 131104 | tf_op jit(solution)/shard_map/ppermute | solution.py:10
  82.7 1.6 %multiply_reduce_fusion.1 = bf16[32,8,256]{2,1,0:T(8,128)(2,1)S(1)} fusion(f32[64,8,256]{2,1,0:T(8,128)S(1)} %maximum_convert_fusion.7, f32[32,64,256]{2,1,0:T(8,128)S(1)} %get-tuple-element.5), kind=kLoop, calls=%fused_computation.1 | loop fusion | flops 8323072 | bytes 2752512 | tf_op jit(solution)/shard_map/reduce_sum | solution.py:15
  84.3 3.0 %multiply_reduce_fusion = bf16[64,8,256]{2,1,0:T(8,128)(2,1)} fusion(f32[32,8,256]{2,1,0:T(8,128)S(1)} %convert_element_type.348, f32[64,32,256]{2,1,0:T(8,128)S(1)} %convert_element_type.283), kind=kLoop, calls=%fused_computation | loop fusion | flops 8257536 | bytes 2621440 | tf_op jit(solution)/shard_map/reduce_sum | solution.py:15
  (29 shorter events, 0.6 us)
Async XLA Ops:
  0.0 8.3 %copy-start.2 = (s32[4,2,256]{2,1,0:T(2,128)S(1)}, s32[4,2,256]{2,1,0:T(2,128)}, u32[]{:S(2)}) copy-start(s32[4,2,256]{2,1,0:T(2,128)} %param.10) | copy-start | bytes 24580
  0.0 8.4 %copy-start = (bf16[4,32,64,256]{3,2,1,0:T(8,128)(2,1)S(1)}, bf16[4,32,64,256]{3,2,1,0:T(8,128)(2,1)}, u32[]{:S(2)}) copy-start(bf16[4,32,64,256]{3,2,1,0:T(8,128)(2,1)} %param.9) | copy-start | bytes 12582916
  4.2 10.4 %collective-permute-start = (bf16[32,8,256]{2,1,0:T(8,128)(2,1)S(1)}, bf16[32,8,256]{2,1,0:T(8,128)(2,1)S(1)}, u32[]{:S(2)}, u32[]{:S(2)}) collective-permute-start(bf16[32,8,256]{2,1,0:T(8,128)(2,1)S(1)} %multiply_reduce_fusion.9), channel_id=1, source_target_pairs={{0,8},{1,9},{2,10},{3,11},{4,12},{5,13},{6,14},{7,15},{8,0},{9,1},... | collective-permute-start | bytes 393224 | tf_op jit(solution)/shard_map/ppermute | solution.py:10
  17.8 5.0 %collective-permute-start.1 = (bf16[32,8,256]{2,1,0:T(8,128)(2,1)S(1)}, bf16[32,8,256]{2,1,0:T(8,128)(2,1)S(1)}, u32[]{:S(2)}, u32[]{:S(2)}) collective-permute-start(bf16[32,8,256]{2,1,0:T(8,128)(2,1)S(1)} %multiply_reduce_fusion.8), channel_id=1, source_target_pairs={{0,4},{1,5},{2,6},{3,7},{4,0},{5,1},{6,2},{7,3},{8,12},{9,13},{10,... | collective-permute-start | bytes 393224 | tf_op jit(solution)/shard_map/ppermute | solution.py:10
  26.0 5.0 %collective-permute-start.2 = (bf16[32,8,256]{2,1,0:T(8,128)(2,1)S(1)}, bf16[32,8,256]{2,1,0:T(8,128)(2,1)S(1)}, u32[]{:S(2)}, u32[]{:S(2)}) collective-permute-start(bf16[32,8,256]{2,1,0:T(8,128)(2,1)S(1)} %multiply_reduce_fusion.7), channel_id=1, source_target_pairs={{0,2},{1,3},{2,0},{3,1},{4,6},{5,7},{6,4},{7,5},{8,10},{9,11},{10,... | collective-permute-start | bytes 393224 | tf_op jit(solution)/shard_map/ppermute | solution.py:10
  31.1 14.9 %copy-start.3 = (s32[4,2,256]{2,1,0:T(2,128)S(1)}, s32[4,2,256]{2,1,0:T(2,128)}, u32[]{:S(2)}) copy-start(s32[4,2,256]{2,1,0:T(2,128)} %param.12) | copy-start | bytes 24580
  34.2 1.4 %collective-permute-start.3 = (bf16[32,8,256]{2,1,0:T(8,128)(2,1)S(1)}, bf16[32,8,256]{2,1,0:T(8,128)(2,1)S(1)}, u32[]{:S(2)}, u32[]{:S(2)}) collective-permute-start(bf16[32,8,256]{2,1,0:T(8,128)(2,1)S(1)} %multiply_reduce_fusion.6), channel_id=1, source_target_pairs={{0,1},{1,0},{2,3},{3,2},{4,5},{5,4},{6,7},{7,6},{8,9},{9,8},{10,11... | collective-permute-start | bytes 393224 | tf_op jit(solution)/shard_map/ppermute | solution.py:10
  39.5 14.3 %all-to-all-start = ((bf16[256,16,16]{0,2,1:T(8,128)(2,1)}), bf16[256,16,16]{0,2,1:T(8,128)(2,1)S(1)}, u32[]{:S(2)}, u32[]{:S(2)}) async-start(bf16[256,16,16]{0,2,1:T(8,128)(2,1)} %copy.10), calls=%async_computation | async-start | bytes 262144 | tf_op jit(solution)/shard_map/all_to_all | solution.py:32
  55.7 2.9 %collective-permute-start.4 = (bf16[32,8,256]{2,1,0:T(8,128)(2,1)S(1)}, bf16[32,8,256]{2,1,0:T(8,128)(2,1)S(1)}, u32[]{:S(2)}, u32[]{:S(2)}) collective-permute-start(bf16[32,8,256]{2,1,0:T(8,128)(2,1)S(1)} %reshape.269), channel_id=1, source_target_pairs={{0,1},{1,0},{2,3},{3,2},{4,5},{5,4},{6,7},{7,6},{8,9},{9,8},{10,11... | collective-permute-start | bytes 393224 | tf_op jit(solution)/shard_map/ppermute | solution.py:10
  60.2 14.9 %copy-start.1 = (bf16[64,32,256]{2,1,0:T(8,128)(2,1)S(1)}, bf16[64,32,256]{2,1,0:T(8,128)(2,1)}, u32[]{:S(2)}) copy-start(bf16[64,32,256]{2,1,0:T(8,128)(2,1)} %param.13) | copy-start | bytes 3145732
  60.2 6.0 %collective-permute-start.5 = (bf16[32,8,256]{2,1,0:T(8,128)(2,1)S(1)}, bf16[32,8,256]{2,1,0:T(8,128)(2,1)S(1)}, u32[]{:S(2)}, u32[]{:S(2)}) collective-permute-start(bf16[32,8,256]{2,1,0:T(8,128)(2,1)S(1)} %multiply_reduce_fusion.4), channel_id=1, source_target_pairs={{0,2},{1,3},{2,0},{3,1},{4,6},{5,7},{6,4},{7,5},{8,10},{9,11},{10,... | collective-permute-start | bytes 393224 | tf_op jit(solution)/shard_map/ppermute | solution.py:10
  67.8 5.2 %collective-permute-start.6 = (bf16[32,8,256]{2,1,0:T(8,128)(2,1)S(1)}, bf16[32,8,256]{2,1,0:T(8,128)(2,1)S(1)}, u32[]{:S(2)}, u32[]{:S(2)}) collective-permute-start(bf16[32,8,256]{2,1,0:T(8,128)(2,1)S(1)} %multiply_reduce_fusion.3), channel_id=1, source_target_pairs={{0,4},{1,5},{2,6},{3,7},{4,0},{5,1},{6,2},{7,3},{8,12},{9,13},{10,... | collective-permute-start | bytes 393224 | tf_op jit(solution)/shard_map/ppermute | solution.py:10
  74.7 8.0 %collective-permute-start.7 = (bf16[32,8,256]{2,1,0:T(8,128)(2,1)S(1)}, bf16[32,8,256]{2,1,0:T(8,128)(2,1)S(1)}, u32[]{:S(2)}, u32[]{:S(2)}) collective-permute-start(bf16[32,8,256]{2,1,0:T(8,128)(2,1)S(1)} %multiply_reduce_fusion.2), channel_id=1, source_target_pairs={{0,8},{1,9},{2,10},{3,11},{4,12},{5,13},{6,14},{7,15},{8,0},{9,1},... | collective-permute-start | bytes 393224 | tf_op jit(solution)/shard_map/ppermute | solution.py:10
where the time goes:
time: 87.6 us; the launch traced here: 87.3 us
  waiting for transfers between devices  38.4 us (44%)
  other arithmetic  30.5 us (35%)
  starting transfers between devices  13.8 us (16%)
  local copies, waits for them, and re-layouts  4.22 us (5%)
    ppermute x8, waiting for transfers between devices, swapped(): return lax.ppermute(value, axis, pairs)  30.7 us
    reduce_sum x10, other arithmetic, contract(): return jnp.sum(product, axis=1)  21.7 us
    all_to_all x1, waiting for transfers between devices, transpose_boxes(): lax.all_to_all(values, 'leaf', split_axis=1, concat_axis=1, tiled=True)  7.72 us
    convert_element_type x4, other arithmetic, contract(): weights[:, :, None].astype(jnp.float32) * state[None].astype(jnp.float32)  7.34 us
    ppermute x8, starting transfers between devices, swapped(): return lax.ppermute(value, axis, pairs)  7.26 us
    all_to_all x1, starting transfers between devices, transpose_boxes(): lax.all_to_all(values, 'leaf', split_axis=1, concat_axis=1, tiled=True)  6.51 us
    convert_element_type x2, local copies, waits for them, and re-layouts, partner_level(): return contract(weights, both_states).astype(jnp.bfloat16)  2.2 us
  transfers between devices with their start and end apart: 9, of which 8 were waited for; matrix products, arithmetic and copies ran while one was open for 7% of the time, Pallas kernels for 0%

commit v1 on v0

v1 whole, which is shorter than its diff:
```python
import functools

import jax
import jax.numpy as jnp
from jax import lax
from jax.experimental import pallas as pl
from jax.experimental.pallas import tpu as pltpu
from jax.sharding import PartitionSpec as P

CHUNKS = 2


def swapped(value, axis, apart):
    mask = 2**apart
    pairs = [(source, source ^ mask) for source in range(lax.axis_size(axis))]
    return lax.ppermute(value, axis, pairs)


def contract(weights, state):
    product = weights[:, :, None].astype(jnp.float32) * state[None].astype(jnp.float32)
    return jnp.sum(product, axis=1)


def half_of(blocks, pattern, half, box_slice):
    rank_size = blocks.shape[0]
    part = lax.dynamic_slice_in_dim(blocks, half * rank_size, rank_size, axis=1)
    present = lax.dynamic_index_in_dim(pattern, half, axis=0, keepdims=False)
    return part[:, :, box_slice], present[box_slice].astype(jnp.float32)


def level_step(states, blocks, pattern, bit, leaf_place):
    own = leaf_place // 2**bit % 2
    chunk = states[0].shape[2]
    partners = [swapped(state, "leaf", bit) for state in states]
    out = []
    for place, (state, partner) in enumerate(zip(states, partners)):
        boxes = slice(place * chunk, (place + 1) * chunk)
        own_blocks, own_present = half_of(blocks, pattern, own, boxes)
        far_blocks, far_present = half_of(blocks, pattern, 1 - own, boxes)
        near = contract(own_blocks, state) * own_present
        far = contract(far_blocks, partner) * far_present
        out.append((near + far).astype(jnp.bfloat16))
    return out


def exchange_groups(tile, slot, fold):
    lane_group = lax.broadcasted_iota(jnp.int32, tile.shape[1:], 2) // slot
    pieces = [tile[index] for index in range(fold)]
    width = tile.shape[-1]
    step = 1
    while step < fold:
        low = (lane_group // step) % 2 == 0
        fresh = list(pieces)
        for index in range(fold):
            if index & step:
                continue
            first, second = pieces[index], pieces[index + step]
            fresh[index] = jnp.where(low, first, pltpu.roll(second, step * slot, 2))
            fresh[index + step] = jnp.where(low, pltpu.roll(first, width - step * slot, 2), second)
        pieces = fresh
        step *= 2
    return pieces


def pack_kernel(slot, fold, *refs):
    count = len(refs) // 2
    for source, target in zip(refs[:count], refs[count:]):
        rank_size, rhs_count, width = source.shape
        tile = source[...].astype(jnp.float32).reshape(fold, rank_size // fold, rhs_count, width)
        for index, piece in enumerate(exchange_groups(tile, slot, fold)):
            target[index] = piece.astype(jnp.bfloat16)


def unpack_kernel(slot, fold, *refs):
    count = len(refs) // 2
    for source, target in zip(refs[:count], refs[count:]):
        rank_size, rhs_count, width = target.shape
        tile = source[...].astype(jnp.float32)
        rows = rank_size // fold
        for index, piece in enumerate(exchange_groups(tile, slot, fold)):
            target[index * rows:(index + 1) * rows] = piece.astype(jnp.bfloat16)


def switch_boxes(states, leaf_count):
    rank_size, rhs_count, chunk = states[0].shape
    slot = len(states) * chunk // leaf_count
    fold = chunk // slot
    rows = rank_size // fold
    whole = pl.BlockSpec(memory_space=pltpu.VMEM)
    packed = pl.pallas_call(
        functools.partial(pack_kernel, slot, fold),
        out_shape=[jax.ShapeDtypeStruct((fold, rows, rhs_count, chunk), jnp.bfloat16)] * len(states),
        in_specs=[whole] * len(states),
        out_specs=[whole] * len(states),
    )(*states)
    joined = jnp.concatenate(packed, axis=0)
    moved = lax.all_to_all(joined, "leaf", split_axis=0, concat_axis=0, tiled=True)
    parts = jnp.split(moved, len(states), axis=0)
    return pl.pallas_call(
        functools.partial(unpack_kernel, slot, fold),
        out_shape=[jax.ShapeDtypeStruct((rank_size, rhs_count, chunk), jnp.bfloat16)] * len(states),
        in_specs=[whole] * len(states),
        out_specs=[whole] * len(states),
    )(*parts)


def plain_switch(states):
    joined = jnp.concatenate(states, axis=2)
    rank_size, rhs_count, box_count = joined.shape
    flat = joined.reshape(rank_size * rhs_count, box_count)
    moved = lax.all_to_all(flat, "leaf", split_axis=1, concat_axis=1, tiled=True)
    moved = moved.reshape(rank_size, rhs_count, box_count)
    return jnp.split(moved, len(states), axis=2)


def local(samples, interp_in, top_blocks, top_pattern, bottom_blocks, bottom_pattern, interp_out):
    level_count = top_blocks.shape[0]
    rank_size = interp_in.shape[0]
    box_count = samples.shape[2]
    leaf_count = lax.axis_size("leaf")
    bit_count = leaf_count.bit_length() - 1
    leaf_place = lax.axis_index("leaf")
    chunk = box_count // CHUNKS
    parts = [slice(place * chunk, (place + 1) * chunk) for place in range(CHUNKS)]
    states = [contract(interp_in[:, :, part], samples[:, :, part]).astype(jnp.bfloat16) for part in parts]
    for level in range(level_count):
        bit = bit_count - 1 - level
        states = level_step(states, top_blocks[level], top_pattern[level], bit, leaf_place)
    slot = box_count // leaf_count
    fold = chunk // slot
    if chunk == 128 and fold <= rank_size:
        states = switch_boxes(states, leaf_count)
    else:
        states = plain_switch(states)
    for level in range(level_count):
        states = level_step(states, bottom_blocks[level], bottom_pattern[level], level, leaf_place)
    images = [contract(interp_out[:, :, part], state) for part, state in zip(parts, states)]
    return jnp.concatenate(images, axis=2).astype(jnp.bfloat16)


def solution(mesh):
    boxes = ("parts", "leaf")
    return jax.shard_map(
        local,
        mesh=mesh,
        in_specs=(
            P(None, None, boxes),
            P(None, None, boxes),
            P(None, None, None, boxes),
            P(None, None, boxes),
            P(None, None, None, boxes),
            P(None, None, boxes),
            P(None, None, boxes),
        ),
        out_specs=P(None, None, boxes),
        check_vma=False,
    )
```

time: 87.6 us -> 112 us (1.28)
  other arithmetic: 30.5 us -> 63.8 us
  waiting for transfers between devices: 38.4 us -> 12.7 us
  starting transfers between devices: 13.8 us -> 21 us
  local copies, waits for them, and re-layouts: 4.22 us -> 8.9 us
  Pallas kernels: 0 us -> 3.53 us
    ppermute x8 -> x16, waiting for transfers between devices: 30.7 us -> 6.96 us  [swapped(): return lax.ppermute(value, axis, pairs)]
    convert_element_type x4 -> x18, other arithmetic: 7.34 us -> 24 us  [contract(): weights[:, :, None].astype(jnp.float32) * state[None].astype(jnp.float32)]
    ppermute x8 -> x16, starting transfers between devices: 7.26 us -> 15.9 us  [swapped(): return lax.ppermute(value, axis, pairs)]
    convert_element_type x10 -> x35, other arithmetic: 1.32 us -> 7.45 us  [contract(): state[None].astype(jnp.float32)]
    dynamic_slice x0 -> x4, local copies, waits for them, and re-layouts: none -> 4.06 us  [half_of(): part = lax.dynamic_slice_in_dim(blocks, half * rank_size, rank_size, axis=1)]
    slice x0 -> x4, local copies, waits for them, and re-layouts: none -> 4.01 us  [the longest x1 3.56 us: local(): top_blocks[level]]
    mul x0 -> x8, other arithmetic: none -> 3.91 us  [level_step(): near = contract(own_blocks, state) * own_present]
    pallas_call x0 -> x2, Pallas kernels: none -> 3.53 us  [the longest x1 1.77 us: switch_boxes(): pl.pallas_call(functools.partial(pack_kernel, slot, fold), out_shape=[jax...]
  transfers between devices with their start and end apart: 9 -> 17, of which waited for: 8 -> 8; matrix products, arithmetic and copies ran while one was open for 7% -> 56% of each run, Pallas kernels for 0% -> 0%
where the time goes in v1:
time: 112 us; the launch traced here: 111 us
  other arithmetic  63.8 us (57%)
  starting transfers between devices  21 us (19%)
  waiting for transfers between devices  12.7 us (11%)
  local copies, waits for them, and re-layouts  8.9 us (8%)
  Pallas kernels  3.53 us (3%)
  between operations  1.18 us (1%)
    reduce_sum x36, other arithmetic, contract(): return jnp.sum(product, axis=1)  24.9 us
    convert_element_type x18, other arithmetic, contract(): weights[:, :, None].astype(jnp.float32) * state[None].astype(jnp.float32)  24 us
    ppermute x16, starting transfers between devices, swapped(): return lax.ppermute(value, axis, pairs)  15.9 us
    convert_element_type x35, other arithmetic, contract(): state[None].astype(jnp.float32)  7.45 us
    ppermute x16, waiting for transfers between devices, swapped(): return lax.ppermute(value, axis, pairs)  6.96 us
    all_to_all x1, waiting for transfers between devices, switch_boxes(): lax.all_to_all(joined, 'leaf', split_axis=0, concat_axis=0, tiled=True)  5.78 us
    all_to_all x1, starting transfers between devices, switch_boxes(): lax.all_to_all(joined, 'leaf', split_axis=0, concat_axis=0, tiled=True)  5.16 us
    dynamic_slice x4, local copies, waits for them, and re-layouts, half_of(): part = lax.dynamic_slice_in_dim(blocks, half * rank_size, rank_size, axis=1)  4.06 us
  transfers between devices with their start and end apart: 17, of which 8 were waited for; matrix products, arithmetic and copies ran while one was open for 56% of the time, Pallas kernels for 0%

profile of v1, /device:TPU:0, one launch (start us, length us, event | category | flops | bytes accessed | tf_op | source)
XLA Modules:
  0.0 111.2 jit_solution(14151129020802436886)
XLA Ops:
  0.0 1.4 %slice_convert_fusion.1 = (f32[32,64,128]{2,1,0:T(8,128)S(1)}, f32[32,64,128]{2,1,0:T(8,128)S(1)}) fusion(bf16[32,64,256]{2,1,0:T(8,128)(2,1)} %param.8), kind=kLoop, calls=%fused_computation.41 | loop fusion | flops 524288 | bytes 3145728 | tf_op jit(solution)/shard_map/convert_element_type | solution.py:20
  1.5 1.0 slice_convert_fusion.36
  2.5 1.3 %multiply_reduce_fusion.2 = bf16[32,8,128]{2,1,0:T(8,128)(2,1)} fusion(f32[64,8,128]{2,1,0:T(8,128)S(1)} %get-tuple-element.97, f32[32,64,128]{2,1,0:T(8,128)S(1)} %get-tuple-element.55), kind=kLoop, calls=%fused_computation.2 | loop fusion | flops 4161536 | bytes 1376256 | tf_op jit(solution)/shard_map/reduce_sum | solution.py:21
  3.7 4.0 %collective-permute-start.4 = (bf16[32,8,128]{2,1,0:T(8,128)(2,1)}, bf16[32,8,128]{2,1,0:T(8,128)(2,1)}, u32[]{:S(2)}, u32[]{:S(2)}) collective-permute-start(bf16[32,8,128]{2,1,0:T(8,128)(2,1)} %multiply_reduce_fusion.2), channel_id=1, source_target_pairs={{0,8},{1,9},{2,10},{3,11},{4,12},{5,13},{6,14},{7,15},{8,0},{9,1},... | collective-permute-start | bytes 196616 | tf_op jit(solution)/shard_map/ppermute | solution.py:16
  7.8 1.3 %multiply_reduce_fusion.3 = bf16[32,8,128]{2,1,0:T(8,128)(2,1)} fusion(f32[64,8,128]{2,1,0:T(8,128)S(1)} %get-tuple-element.98, f32[32,64,128]{2,1,0:T(8,128)S(1)} %get-tuple-element.56), kind=kLoop, calls=%fused_computation.3 | loop fusion | flops 4161536 | bytes 1376256 | tf_op jit(solution)/shard_map/reduce_sum | solution.py:21
  9.0 0.8 convert_element_type.642
  10.0 0.9 convert_element_type.611
  10.8 3.6 %fusion.79 = (bf16[1,32,64,256]{3,2,1,0:T(8,128)(2,1)S(1)}, bf16[1,32,64,256]{3,2,1,0:T(8,128)(2,1)S(1)}, bf16[1,32,64,256]{3,2,1,0:T(8,128)(2,1)S(1)}, bf16[1,32,64,256]{3,2,1,0:T(8,128)(2,1)}) fusion(bf16[4,32,64,256]{3,2,1,0:T(8,128)(2,1)} %param.9), kind=kLoop, calls=%fused_computation.219 | loop fusion | bytes 8388608 | tf_op jit(solution)/shard_map/slice | solution.py:128
  14.4 2.4 %dynamic-slice_bitcast_fusion.8 = (bf16[32,32,256]{2,1,0:T(8,128)(2,1)S(1)}, bf16[32,32,256]{2,1,0:T(8,128)(2,1)S(1)}, bf16[32,32,256]{2,1,0:T(8,128)(2,1)}, bf16[32,32,256]{2,1,0:T(8,128)(2,1)}) fusion(bf16[1,32,64,256]{3,2,1,0:T(8,128)(2,1)S(1)} %get-tuple-element.43, s32[]{:T(128)S(6)} %select_n.141, s32[]{:T(128)S(6)} %select_n.151, ...), kind=kLoop, calls=%fused_computation.47 | loop fusion | bytes 4194320 | tf_op jit(solution)/shard_map/dynamic_slice | solution.py:26
  16.8 1.2 %slice_convert_fusion.19 = (f32[32,32,128]{2,1,0:T(8,128)}, f32[32,32,128]{2,1,0:T(8,128)}) fusion(bf16[32,32,256]{2,1,0:T(8,128)(2,1)S(1)} %get-tuple-element.64), kind=kLoop, calls=%fused_computation.71 | loop fusion | flops 262144 | bytes 1572864 | tf_op jit(solution)/shard_map/convert_element_type | solution.py:20
  18.0 1.2 %slice_convert_fusion.20 = (f32[32,32,128]{2,1,0:T(8,128)}, f32[32,32,128]{2,1,0:T(8,128)}) fusion(bf16[32,32,256]{2,1,0:T(8,128)(2,1)S(1)} %get-tuple-element.63), kind=kLoop, calls=%fused_computation.72 | loop fusion | flops 262144 | bytes 1572864 | tf_op jit(solution)/shard_map/convert_element_type | solution.py:20
  19.2 2.2 %slice_convert_fusion.21 = (f32[32,32,128]{2,1,0:T(8,128)}, f32[32,32,128]{2,1,0:T(8,128)}) fusion(bf16[32,32,256]{2,1,0:T(8,128)(2,1)} %get-tuple-element.142), kind=kLoop, calls=%fused_computation.73 | loop fusion | flops 262144 | bytes 1572864 | tf_op jit(solution)/shard_map/convert_element_type | solution.py:20
  21.3 1.1 slice_convert_fusion.18
  22.7 1.2 %slice_convert_fusion.22 = (f32[32,32,128]{2,1,0:T(8,128)}, f32[32,32,128]{2,1,0:T(8,128)}) fusion(bf16[32,32,256]{2,1,0:T(8,128)(2,1)S(1)} %get-tuple-element.59), kind=kLoop, calls=%fused_computation.74 | loop fusion | flops 262144 | bytes 1572864 | tf_op jit(solution)/shard_map/convert_element_type | solution.py:20
  23.8 1.2 %slice_convert_fusion.17 = (f32[32,32,128]{2,1,0:T(8,128)}, f32[32,32,128]{2,1,0:T(8,128)}) fusion(bf16[32,32,256]{2,1,0:T(8,128)(2,1)S(1)} %get-tuple-element.60), kind=kLoop, calls=%fused_computation.69 | loop fusion | flops 262144 | bytes 1572864 | tf_op jit(solution)/shard_map/convert_element_type | solution.py:20
  25.0 1.2 %slice_convert_fusion.23 = (f32[32,32,128]{2,1,0:T(8,128)}, f32[32,32,128]{2,1,0:T(8,128)}) fusion(bf16[32,32,256]{2,1,0:T(8,128)(2,1)S(1)} %get-tuple-element.144), kind=kLoop, calls=%fused_computation.75 | loop fusion | flops 262144 | bytes 1572864 | tf_op jit(solution)/shard_map/convert_element_type | solution.py:20
  26.2 1.2 %slice_convert_fusion.16 = (f32[32,32,128]{2,1,0:T(8,128)}, f32[32,32,128]{2,1,0:T(8,128)}) fusion(bf16[32,32,256]{2,1,0:T(8,128)(2,1)S(1)} %get-tuple-element.143), kind=kLoop, calls=%fused_computation.68 | loop fusion | flops 262144 | bytes 1572864 | tf_op jit(solution)/shard_map/convert_element_type | solution.py:20
  28.1 1.1 %slice_convert_fusion.15 = (f32[32,32,128]{2,1,0:T(8,128)}, f32[32,32,128]{2,1,0:T(8,128)}) fusion(bf16[32,32,256]{2,1,0:T(8,128)(2,1)S(1)} %get-tuple-element.54), kind=kLoop, calls=%fused_computation.67 | loop fusion | flops 262144 | bytes 1572864 | tf_op jit(solution)/shard_map/convert_element_type | solution.py:20
  29.2 1.1 %slice_convert_fusion.32 = (f32[32,32,128]{2,1,0:T(8,128)}, f32[32,32,128]{2,1,0:T(8,128)}) fusion(bf16[32,32,256]{2,1,0:T(8,128)(2,1)S(1)} %get-tuple-element.53), kind=kLoop, calls=%fused_computation.84 | loop fusion | flops 262144 | bytes 1572864 | tf_op jit(solution)/shard_map/convert_element_type | solution.py:20
  30.9 0.7 fusion.65
  31.6 1.1 slice_convert_fusion.33
  32.7 1.1 %slice_convert_fusion.14 = (f32[32,32,128]{2,1,0:T(8,128)}, f32[32,32,128]{2,1,0:T(8,128)}) fusion(bf16[32,32,256]{2,1,0:T(8,128)(2,1)S(1)} %get-tuple-element.145), kind=kLoop, calls=%fused_computation.66 | loop fusion | flops 262144 | bytes 1572864 | tf_op jit(solution)/shard_map/convert_element_type | solution.py:20
  34.4 0.7 fusion.53
  35.1 1.2 %dynamic-slice_bitcast_fusion.14 = (bf16[32,32,256]{2,1,0:T(8,128)(2,1)S(1)}, bf16[32,32,256]{2,1,0:T(8,128)(2,1)S(1)}, bf16[32,32,256]{2,1,0:T(8,128)(2,1)}, bf16[32,32,256]{2,1,0:T(8,128)(2,1)}) fusion(bf16[1,32,64,256]{3,2,1,0:T(8,128)(2,1)S(1)} %get-tuple-element.38, s32[]{:T(128)S(6)} %select_n.144, s32[]{:T(128)S(6)} %select_n.154, ...), kind=kLoop, calls=%fused_computation.53 | loop fusion | bytes 4194320 | tf_op jit(solution)/shard_map/dynamic_slice | solution.py:26
  36.3 1.2 %slice_convert_fusion.34 = (f32[32,32,128]{2,1,0:T(8,128)}, f32[32,32,128]{2,1,0:T(8,128)}) fusion(bf16[32,32,256]{2,1,0:T(8,128)(2,1)S(1)} %get-tuple-element.49), kind=kLoop, calls=%fused_computation.86 | loop fusion | flops 262144 | bytes 1572864 | tf_op jit(solution)/shard_map/convert_element_type | solution.py:20
  37.5 0.9 slice_convert_fusion.13
  39.7 1.9 %slice_convert_fusion.35 = (f32[32,32,128]{2,1,0:T(8,128)}, f32[32,32,128]{2,1,0:T(8,128)S(1)}) fusion(bf16[32,32,256]{2,1,0:T(8,128)(2,1)} %get-tuple-element.148), kind=kLoop, calls=%fused_computation.87 | loop fusion | flops 262144 | bytes 1572864 | tf_op jit(solution)/shard_map/convert_element_type | solution.py:20
  41.6 1.5 %slice_convert_fusion.3 = (f32[64,32,128]{2,1,0:T(8,128)S(1)}, f32[64,32,128]{2,1,0:T(8,128)S(1)}) fusion(bf16[64,32,256]{2,1,0:T(8,128)(2,1)} %param.13), kind=kLoop, calls=%fused_computation.55 | loop fusion | flops 524288 | bytes 3145728 | tf_op jit(solution)/shard_map/convert_element_type | solution.py:20
  43.1 1.4 %multiply_reduce_fusion.27 = f32[32,8,128]{2,1,0:T(8,128)S(1)} fusion(f32[32,8,128]{2,1,0:T(8,128)S(1)} %convert_element_type.642, f32[32,32,128]{2,1,0:T(8,128)} %get-tuple-element.93), kind=kLoop, calls=%fused_computation.27 | loop fusion | flops 2064384 | bytes 786432 | tf_op jit(solution)/shard_map/reduce_sum | solution.py:21
  44.6 1.5 %multiply_reduce_fusion.35 = f32[32,8,128]{2,1,0:T(8,128)S(1)} fusion(f32[32,8,128]{2,1,0:T(8,128)S(1)} %convert_element_type.611, f32[32,32,128]{2,1,0:T(8,128)} %get-tuple-element.94), kind=kLoop, calls=%fused_computation.35 | loop fusion | flops 2064384 | bytes 786432 | tf_op jit(solution)/shard_map/reduce_sum | solution.py:21
  46.3 0.9 convert_element_type.645
  47.1 1.4 %multiply_reduce_fusion.26 = f32[32,8,128]{2,1,0:T(8,128)S(1)} fusion(f32[32,8,128]{2,1,0:T(8,128)S(1)} %convert_element_type.645, f32[32,32,128]{2,1,0:T(8,128)} %get-tuple-element.95), kind=kLoop, calls=%fused_computation.26 | loop fusion | flops 2064384 | bytes 786432 | tf_op jit(solution)/shard_map/reduce_sum | solution.py:21
  48.5 2.0 %collective-permute-start.5 = (bf16[32,8,128]{2,1,0:T(8,128)(2,1)S(1)}, bf16[32,8,128]{2,1,0:T(8,128)(2,1)S(1)}, u32[]{:S(2)}, u32[]{:S(2)}) collective-permute-start(bf16[32,8,128]{2,1,0:T(8,128)(2,1)S(1)} %get-tuple-element.30), channel_id=1, source_target_pairs={{0,4},{1,5},{2,6},{3,7},{4,0},{5,1},{6,2},{7,3},{8,12},{9,13},{10,... | collective-permute-start | bytes 196616 | tf_op jit(solution)/shard_map/ppermute | solution.py:16
  50.5 0.8 convert_element_type.614
  51.4 1.4 %multiply_reduce_fusion.34 = f32[32,8,128]{2,1,0:T(8,128)S(1)} fusion(f32[32,8,128]{2,1,0:T(8,128)S(1)} %convert_element_type.614, f32[32,32,128]{2,1,0:T(8,128)} %get-tuple-element.96), kind=kLoop, calls=%fused_computation.34 | loop fusion | flops 2064384 | bytes 786432 | tf_op jit(solution)/shard_map/reduce_sum | solution.py:21
  53.0 1.4 %multiply_reduce_fusion.25 = f32[32,8,128]{2,1,0:T(8,128)S(1)} fusion(f32[32,8,128]{2,1,0:T(8,128)S(1)} %get-tuple-element.29, f32[32,32,128]{2,1,0:T(8,128)} %get-tuple-element.89), kind=kLoop, calls=%fused_computation.25 | loop fusion | flops 2064384 | bytes 786432 | tf_op jit(solution)/shard_map/reduce_sum | solution.py:21
  55.1 0.7 fusion.73
  55.9 1.9 %collective-permute-start.6 = (bf16[32,8,128]{2,1,0:T(8,128)(2,1)S(1)}, bf16[32,8,128]{2,1,0:T(8,128)(2,1)S(1)}, u32[]{:S(2)}, u32[]{:S(2)}) collective-permute-start(bf16[32,8,128]{2,1,0:T(8,128)(2,1)S(1)} %get-tuple-element.28), channel_id=1, source_target_pairs={{0,2},{1,3},{2,0},{3,1},{4,6},{5,7},{6,4},{7,5},{8,10},{9,11},{10,... | collective-permute-start | bytes 196616 | tf_op jit(solution)/shard_map/ppermute | solution.py:16
  58.2 1.0 collective-permute-start.2
  59.9 0.9 collective-permute-done.6
  61.2 1.3 %collective-permute-done.2 = bf16[32,8,128]{2,1,0:T(8,128)(2,1)S(1)} collective-permute-done((bf16[32,8,128]{2,1,0:T(8,128)(2,1)S(1)}, bf16[32,8,128]{2,1,0:T(8,128)(2,1)S(1)}, u32[]{:S(2)}, u32[]{:S(2)}) %collective-permute-start.2) | collective-permute-done | bytes 65568 | tf_op jit(solution)/shard_map/ppermute | solution.py:16
  65.4 0.7 add_convert_fusion.12.refs_0_
  66.0 1.8 %shard_map.73 = (bf16[8,4,8,128]{3,2,1,0:T(8,128)(2,1)}, bf16[8,4,8,128]{3,2,1,0:T(8,128)(2,1)}) custom-call(bf16[32,8,128]{2,1,0:T(8,128)(2,1)} %add_convert_fusion.12.refs_0_, bf16[32,8,128]{2,1,0:T(8,128)(2,1)} %add_convert_fusion.8.refs_1_), custom_call_target="tpu_custom_call" | custom-call | tf_op jit(solution)/shard_map/pallas_call | solution.py:90
  67.8 1.5 %pad_maximum_fusion.1 = bf16[16,4,8,128]{3,2,1,0:T(8,128)(2,1)} fusion(bf16[8,4,8,128]{3,2,1,0:T(8,128)(2,1)} %get-tuple-element.10, bf16[8,4,8,128]{3,2,1,0:T(8,128)(2,1)} %get-tuple-element.9), kind=kLoop, calls=%fused_computation.89 | loop fusion | flops 65536 | bytes 262144 | tf_op jit(solution)/shard_map/concatenate | solution.py:96
  69.3 5.2 %all-to-all-start = ((bf16[16,4,8,128]{3,2,1,0:T(8,128)(2,1)}), bf16[16,4,8,128]{3,2,1,0:T(8,128)(2,1)S(1)}, u32[]{:S(2)}, u32[]{:S(2)}) async-start(bf16[16,4,8,128]{3,2,1,0:T(8,128)(2,1)} %pad_maximum_fusion.1), calls=%async_computation | async-start | bytes 262144 | tf_op jit(solution)/shard_map/all_to_all | solution.py:97
  74.5 2.2 %slice_convert_fusion.12 = (f32[32,32,128]{2,1,0:T(8,128)}, f32[32,32,128]{2,1,0:T(8,128)}) fusion(bf16[32,32,256]{2,1,0:T(8,128)(2,1)} %get-tuple-element.147), kind=kLoop, calls=%fused_computation.64 | loop fusion | flops 262144 | bytes 1572864 | tf_op jit(solution)/shard_map/convert_element_type | solution.py:20
  76.7 5.8 %all-to-all-done = bf16[16,4,8,128]{3,2,1,0:T(8,128)(2,1)S(1)} async-done(((bf16[16,4,8,128]{3,2,1,0:T(8,128)(2,1)}), bf16[16,4,8,128]{3,2,1,0:T(8,128)(2,1)S(1)}, u32[]{:S(2)}, u32[]{:S(2)}) %all-to-all-start) | async-done | bytes 131104 | tf_op jit(solution)/shard_map/all_to_all | solution.py:97
  83.1 1.8 %shard_map.74 = (bf16[32,8,128]{2,1,0:T(8,128)(2,1)}, bf16[32,8,128]{2,1,0:T(8,128)(2,1)}) custom-call(bf16[8,4,8,128]{3,2,1,0:T(8,128)(2,1)} %get-tuple-element.100.refs_0_, bf16[8,4,8,128]{3,2,1,0:T(8,128)(2,1)} %get-tuple-element.99.refs_1_), custom_call_target="tpu_custom_call" | custom-call | tf_op jit(solution)/shard_map/pallas_call | solution.py:99
  84.9 1.0 convert_element_type.666
  85.9 0.9 convert_element_type.696
  87.2 1.4 %multiply_reduce_fusion.19 = f32[32,8,128]{2,1,0:T(8,128)S(1)} fusion(f32[32,8,128]{2,1,0:T(8,128)S(1)} %convert_element_type.666, f32[32,32,128]{2,1,0:T(8,128)} %get-tuple-element.77), kind=kLoop, calls=%fused_computation.19 | loop fusion | flops 2064384 | bytes 786432 | tf_op jit(solution)/shard_map/reduce_sum | solution.py:21
  88.6 1.4 %multiply_reduce_fusion.11 = f32[32,8,128]{2,1,0:T(8,128)S(1)} fusion(f32[32,8,128]{2,1,0:T(8,128)S(1)} %convert_element_type.696, f32[32,32,128]{2,1,0:T(8,128)} %get-tuple-element.78), kind=kLoop, calls=%fused_computation.11 | loop fusion | flops 2064384 | bytes 786432 | tf_op jit(solution)/shard_map/reduce_sum | solution.py:21
  90.1 1.4 %multiply_reduce_fusion.18 = f32[32,8,128]{2,1,0:T(8,128)S(1)} fusion(f32[32,8,128]{2,1,0:T(8,128)S(1)} %convert_element_type.669, f32[32,32,128]{2,1,0:T(8,128)} %get-tuple-element.79), kind=kLoop, calls=%fused_computation.18 | loop fusion | flops 2064384 | bytes 786432 | tf_op jit(solution)/shard_map/reduce_sum | solution.py:21
  91.7 1.4 %multiply_reduce_fusion.10 = f32[32,8,128]{2,1,0:T(8,128)S(1)} fusion(f32[32,8,128]{2,1,0:T(8,128)S(1)} %convert_element_type.699, f32[32,32,128]{2,1,0:T(8,128)} %get-tuple-element.80), kind=kLoop, calls=%fused_computation.10 | loop fusion | flops 2064384 | bytes 786432 | tf_op jit(solution)/shard_map/reduce_sum | solution.py:21
  93.2 2.1 %collective-permute-start.13 = (bf16[32,8,128]{2,1,0:T(8,128)(2,1)S(1)}, bf16[32,8,128]{2,1,0:T(8,128)(2,1)S(1)}, u32[]{:S(2)}, u32[]{:S(2)}) collective-permute-start(bf16[32,8,128]{2,1,0:T(8,128)(2,1)S(1)} %get-tuple-element.24), channel_id=1, source_target_pairs={{0,2},{1,3},{2,0},{3,1},{4,6},{5,7},{6,4},{7,5},{8,10},{9,11},{10,... | collective-permute-start | bytes 196616 | tf_op jit(solution)/shard_map/ppermute | solution.py:16
  96.4 1.1 collective-permute-done.13
  97.9 1.0 collective-permute-start.14
  99.6 1.4 %collective-permute-done.10 = bf16[32,8,128]{2,1,0:T(8,128)(2,1)S(1)} collective-permute-done((bf16[32,8,128]{2,1,0:T(8,128)(2,1)S(1)}, bf16[32,8,128]{2,1,0:T(8,128)(2,1)S(1)}, u32[]{:S(2)}, u32[]{:S(2)}) %collective-permute-start.10) | collective-permute-done | bytes 65568 | tf_op jit(solution)/shard_map/ppermute | solution.py:16
  101.4 0.8 collective-permute-start.11
  102.6 2.2 %collective-permute-start.15 = (bf16[32,8,128]{2,1,0:T(8,128)(2,1)S(1)}, bf16[32,8,128]{2,1,0:T(8,128)(2,1)S(1)}, u32[]{:S(2)}, u32[]{:S(2)}) collective-permute-start(bf16[32,8,128]{2,1,0:T(8,128)(2,1)S(1)} %get-tuple-element.20), channel_id=1, source_target_pairs={{0,8},{1,9},{2,10},{3,11},{4,12},{5,13},{6,14},{7,15},{8,0},{9,1},... | collective-permute-start | bytes 196616 | tf_op jit(solution)/shard_map/ppermute | solution.py:16
  105.5 2.0 %collective-permute-done.11 = bf16[32,8,128]{2,1,0:T(8,128)(2,1)S(1)} collective-permute-done((bf16[32,8,128]{2,1,0:T(8,128)(2,1)S(1)}, bf16[32,8,128]{2,1,0:T(8,128)(2,1)S(1)}, u32[]{:S(2)}, u32[]{:S(2)}) %collective-permute-start.11) | collective-permute-done | bytes 65568 | tf_op jit(solution)/shard_map/ppermute | solution.py:16
  107.9 1.1 multiply_reduce_fusion.1
  109.4 1.1 multiply_reduce_fusion
  110.5 0.7 pad_maximum_fusion
  (172 shorter events, 14.2 us)
Async XLA Ops:
  3.7 42.5 %collective-permute-start.4 = (bf16[32,8,128]{2,1,0:T(8,128)(2,1)}, bf16[32,8,128]{2,1,0:T(8,128)(2,1)}, u32[]{:S(2)}, u32[]{:S(2)}) collective-permute-start(bf16[32,8,128]{2,1,0:T(8,128)(2,1)} %multiply_reduce_fusion.2), channel_id=1, source_target_pairs={{0,8},{1,9},{2,10},{3,11},{4,12},{5,13},{6,14},{7,15},{8,0},{9,1},... | collective-permute-start | bytes 196616 | tf_op jit(solution)/shard_map/ppermute | solution.py:16
  9.0 41.5 %collective-permute-start = (bf16[32,8,128]{2,1,0:T(8,128)(2,1)}, bf16[32,8,128]{2,1,0:T(8,128)(2,1)}, u32[]{:S(2)}, u32[]{:S(2)}) collective-permute-start(bf16[32,8,128]{2,1,0:T(8,128)(2,1)} %multiply_reduce_fusion.3), channel_id=1, source_target_pairs={{0,8},{1,9},{2,10},{3,11},{4,12},{5,13},{6,14},{7,15},{8,0},{9,1},... | collective-permute-start | bytes 196616 | tf_op jit(solution)/shard_map/ppermute | solution.py:16
  14.4 4.8 %copy-start.23 = (s32[4,2,256]{2,1,0:T(2,128)S(1)}, s32[4,2,256]{2,1,0:T(2,128)}, u32[]{:S(2)}) copy-start(s32[4,2,256]{2,1,0:T(2,128)} %param.10) | copy-start | bytes 24580
  16.8 4.5 %copy-start.22 = (bf16[32,32,256]{2,1,0:T(8,128)(2,1)S(1)}, bf16[32,32,256]{2,1,0:T(8,128)(2,1)}, u32[]{:S(2)}) copy-start(bf16[32,32,256]{2,1,0:T(8,128)(2,1)} %get-tuple-element.141) | copy-start | bytes 1572868
  22.7 4.7 %copy-start = (bf16[4,32,64,256]{3,2,1,0:T(8,128)(2,1)S(1)}, bf16[4,32,64,256]{3,2,1,0:T(8,128)(2,1)}, u32[]{:S(2)}) copy-start(bf16[4,32,64,256]{3,2,1,0:T(8,128)(2,1)} %param.11) | copy-start | bytes 12582916
  27.8 2.5 %copy-start.24 = (s32[4,2,256]{2,1,0:T(2,128)S(1)}, s32[4,2,256]{2,1,0:T(2,128)}, u32[]{:S(2)}) copy-start(s32[4,2,256]{2,1,0:T(2,128)} %param.12) | copy-start | bytes 24580
  44.5 13.7 %copy-start.43 = (f32[128]{0:T(128)S(1)}, f32[128]{0:T(128)}, u32[]{:S(2)}) copy-start(f32[128]{0:T(128)} %get-tuple-element.134) | copy-start | bytes 1540
  44.5 13.7 %copy-start.44 = (f32[128]{0:T(128)S(1)}, f32[128]{0:T(128)}, u32[]{:S(2)}) copy-start(f32[128]{0:T(128)} %get-tuple-element.135) | copy-start | bytes 1540
  44.5 9.9 %copy-start.19 = (f32[32,32,128]{2,1,0:T(8,128)S(1)}, f32[32,32,128]{2,1,0:T(8,128)}, u32[]{:S(2)}) copy-start(f32[32,32,128]{2,1,0:T(8,128)} %get-tuple-element.90) | copy-start | bytes 1572868
  44.5 10.3 %copy-start.18 = (f32[32,32,128]{2,1,0:T(8,128)S(1)}, f32[32,32,128]{2,1,0:T(8,128)}, u32[]{:S(2)}) copy-start(f32[32,32,128]{2,1,0:T(8,128)} %get-tuple-element.91) | copy-start | bytes 1572868
  44.5 13.3 %copy-start.14 = (f32[32,32,128]{2,1,0:T(8,128)S(1)}, f32[32,32,128]{2,1,0:T(8,128)}, u32[]{:S(2)}) copy-start(f32[32,32,128]{2,1,0:T(8,128)} %get-tuple-element.92) | copy-start | bytes 1572868
  44.5 14.7 %copy-start.17 = (f32[32,32,128]{2,1,0:T(8,128)S(1)}, f32[32,32,128]{2,1,0:T(8,128)}, u32[]{:S(2)}) copy-start(f32[32,32,128]{2,1,0:T(8,128)} %get-tuple-element.85) | copy-start | bytes 1572868
  46.1 13.4 %copy-start.16 = (f32[32,32,128]{2,1,0:T(8,128)S(1)}, f32[32,32,128]{2,1,0:T(8,128)}, u32[]{:S(2)}) copy-start(f32[32,32,128]{2,1,0:T(8,128)} %get-tuple-element.86) | copy-start | bytes 1572868
  48.5 12.3 %copy-start.15 = (f32[32,32,128]{2,1,0:T(8,128)S(1)}, f32[32,32,128]{2,1,0:T(8,128)}, u32[]{:S(2)}) copy-start(f32[32,32,128]{2,1,0:T(8,128)} %get-tuple-element.87) | copy-start | bytes 1572868
  48.5 6.2 %collective-permute-start.5 = (bf16[32,8,128]{2,1,0:T(8,128)(2,1)S(1)}, bf16[32,8,128]{2,1,0:T(8,128)(2,1)S(1)}, u32[]{:S(2)}, u32[]{:S(2)}) collective-permute-start(bf16[32,8,128]{2,1,0:T(8,128)(2,1)S(1)} %get-tuple-element.30), channel_id=1, source_target_pairs={{0,4},{1,5},{2,6},{3,7},{4,0},{5,1},{6,2},{7,3},{8,12},{9,13},{10,... | collective-permute-start | bytes 196616 | tf_op jit(solution)/shard_map/ppermute | solution.py:16
  51.4 9.7 %copy-start.41 = (f32[128]{0:T(128)S(1)}, f32[128]{0:T(128)}, u32[]{:S(2)}) copy-start(f32[128]{0:T(128)} %get-tuple-element.129) | copy-start | bytes 1540
  51.4 9.7 %copy-start.42 = (f32[128]{0:T(128)S(1)}, f32[128]{0:T(128)}, u32[]{:S(2)}) copy-start(f32[128]{0:T(128)} %get-tuple-element.132) | copy-start | bytes 1540
  52.8 9.8 %copy-start.13 = (f32[32,32,128]{2,1,0:T(8,128)S(1)}, f32[32,32,128]{2,1,0:T(8,128)}, u32[]{:S(2)}) copy-start(f32[32,32,128]{2,1,0:T(8,128)} %get-tuple-element.88) | copy-start | bytes 1572868
  52.8 5.0 %collective-permute-start.1 = (bf16[32,8,128]{2,1,0:T(8,128)(2,1)S(1)}, bf16[32,8,128]{2,1,0:T(8,128)(2,1)S(1)}, u32[]{:S(2)}, u32[]{:S(2)}) collective-permute-start(bf16[32,8,128]{2,1,0:T(8,128)(2,1)S(1)} %get-tuple-element.36), channel_id=1, source_target_pairs={{0,4},{1,5},{2,6},{3,7},{4,0},{5,1},{6,2},{7,3},{8,12},{9,13},{10,... | collective-permute-start | bytes 196616 | tf_op jit(solution)/shard_map/ppermute | solution.py:16
  53.0 9.9 %copy-start.39 = (f32[128]{0:T(128)S(1)}, f32[128]{0:T(128)}, u32[]{:S(2)}) copy-start(f32[128]{0:T(128)} %get-tuple-element.130) | copy-start | bytes 1540
  53.0 9.9 %copy-start.40 = (f32[128]{0:T(128)S(1)}, f32[128]{0:T(128)}, u32[]{:S(2)}) copy-start(f32[128]{0:T(128)} %get-tuple-element.131) | copy-start | bytes 1540
  54.4 8.7 %copy-start.12 = (f32[32,32,128]{2,1,0:T(8,128)S(1)}, f32[32,32,128]{2,1,0:T(8,128)}, u32[]{:S(2)}) copy-start(f32[32,32,128]{2,1,0:T(8,128)} %get-tuple-element.81) | copy-start | bytes 1572868
  54.8 8.7 %copy-start.11 = (f32[32,32,128]{2,1,0:T(8,128)S(1)}, f32[32,32,128]{2,1,0:T(8,128)}, u32[]{:S(2)}) copy-start(f32[32,32,128]{2,1,0:T(8,128)} %get-tuple-element.82) | copy-start | bytes 1572868
  55.1 8.7 %copy-start.10 = (f32[32,32,128]{2,1,0:T(8,128)S(1)}, f32[32,32,128]{2,1,0:T(8,128)}, u32[]{:S(2)}) copy-start(f32[32,32,128]{2,1,0:T(8,128)} %get-tuple-element.83) | copy-start | bytes 1572868
  55.9 4.9 %collective-permute-start.6 = (bf16[32,8,128]{2,1,0:T(8,128)(2,1)S(1)}, bf16[32,8,128]{2,1,0:T(8,128)(2,1)S(1)}, u32[]{:S(2)}, u32[]{:S(2)}) collective-permute-start(bf16[32,8,128]{2,1,0:T(8,128)(2,1)S(1)} %get-tuple-element.28), channel_id=1, source_target_pairs={{0,2},{1,3},{2,0},{3,1},{4,6},{5,7},{6,4},{7,5},{8,10},{9,11},{10,... | collective-permute-start | bytes 196616 | tf_op jit(solution)/shard_map/ppermute | solution.py:16
  57.8 6.5 %copy-start.9 = (f32[32,32,128]{2,1,0:T(8,128)S(1)}, f32[32,32,128]{2,1,0:T(8,128)}, u32[]{:S(2)}) copy-start(f32[32,32,128]{2,1,0:T(8,128)} %get-tuple-element.84) | copy-start | bytes 1572868
  58.2 6.5 %copy-start.37 = (f32[128]{0:T(128)S(1)}, f32[128]{0:T(128)}, u32[]{:S(2)}) copy-start(f32[128]{0:T(128)} %get-tuple-element.125) | copy-start | bytes 1540
  58.2 6.5 %copy-start.38 = (f32[128]{0:T(128)S(1)}, f32[128]{0:T(128)}, u32[]{:S(2)}) copy-start(f32[128]{0:T(128)} %get-tuple-element.128) | copy-start | bytes 1540
  58.2 7.1 %copy-start.35 = (f32[128]{0:T(128)S(1)}, f32[128]{0:T(128)}, u32[]{:S(2)}) copy-start(f32[128]{0:T(128)} %get-tuple-element.126) | copy-start | bytes 1540
  58.2 7.1 %copy-start.36 = (f32[128]{0:T(128)S(1)}, f32[128]{0:T(128)}, u32[]{:S(2)}) copy-start(f32[128]{0:T(128)} %get-tuple-element.127) | copy-start | bytes 1540
  58.2 4.3 %collective-permute-start.2 = (bf16[32,8,128]{2,1,0:T(8,128)(2,1)S(1)}, bf16[32,8,128]{2,1,0:T(8,128)(2,1)S(1)}, u32[]{:S(2)}, u32[]{:S(2)}) collective-permute-start(bf16[32,8,128]{2,1,0:T(8,128)(2,1)S(1)} %get-tuple-element.34), channel_id=1, source_target_pairs={{0,2},{1,3},{2,0},{3,1},{4,6},{5,7},{6,4},{7,5},{8,10},{9,11},{10,... | collective-permute-start | bytes 196616 | tf_op jit(solution)/shard_map/ppermute | solution.py:16
  61.2 2.6 %collective-permute-start.7 = (bf16[32,8,128]{2,1,0:T(8,128)(2,1)S(1)}, bf16[32,8,128]{2,1,0:T(8,128)(2,1)S(1)}, u32[]{:S(2)}, u32[]{:S(2)}) collective-permute-start(bf16[32,8,128]{2,1,0:T(8,128)(2,1)S(1)} %get-tuple-element.26), channel_id=1, source_target_pairs={{0,1},{1,0},{2,3},{3,2},{4,5},{5,4},{6,7},{7,6},{8,9},{9,8},{10,11... | collective-permute-start | bytes 196616 | tf_op jit(solution)/shard_map/ppermute | solution.py:16
  63.0 1.3 %collective-permute-start.3 = (bf16[32,8,128]{2,1,0:T(8,128)(2,1)S(1)}, bf16[32,8,128]{2,1,0:T(8,128)(2,1)S(1)}, u32[]{:S(2)}, u32[]{:S(2)}) collective-permute-start(bf16[32,8,128]{2,1,0:T(8,128)(2,1)S(1)} %get-tuple-element.32), channel_id=1, source_target_pairs={{0,1},{1,0},{2,3},{3,2},{4,5},{5,4},{6,7},{7,6},{8,9},{9,8},{10,11... | collective-permute-start | bytes 196616 | tf_op jit(solution)/shard_map/ppermute | solution.py:16
  63.8 27.8 %copy-start.33 = (f32[128]{0:T(128)S(1)}, f32[128]{0:T(128)}, u32[]{:S(2)}) copy-start(f32[128]{0:T(128)} %get-tuple-element.121) | copy-start | bytes 1540
  63.8 27.8 %copy-start.34 = (f32[128]{0:T(128)S(1)}, f32[128]{0:T(128)}, u32[]{:S(2)}) copy-start(f32[128]{0:T(128)} %get-tuple-element.122) | copy-start | bytes 1540
  64.3 28.8 %copy-start.31 = (f32[128]{0:T(128)S(1)}, f32[128]{0:T(128)}, u32[]{:S(2)}) copy-start(f32[128]{0:T(128)} %get-tuple-element.123) | copy-start | bytes 1540
  64.3 28.8 %copy-start.32 = (f32[128]{0:T(128)S(1)}, f32[128]{0:T(128)}, u32[]{:S(2)}) copy-start(f32[128]{0:T(128)} %get-tuple-element.124) | copy-start | bytes 1540
  69.3 13.1 %all-to-all-start = ((bf16[16,4,8,128]{3,2,1,0:T(8,128)(2,1)}), bf16[16,4,8,128]{3,2,1,0:T(8,128)(2,1)S(1)}, u32[]{:S(2)}, u32[]{:S(2)}) async-start(bf16[16,4,8,128]{3,2,1,0:T(8,128)(2,1)} %pad_maximum_fusion.1), calls=%async_computation | async-start | bytes 262144 | tf_op jit(solution)/shard_map/all_to_all | solution.py:97
  76.6 19.6 %copy-start.29 = (f32[128]{0:T(128)S(1)}, f32[128]{0:T(128)}, u32[]{:S(2)}) copy-start(f32[128]{0:T(128)} %get-tuple-element.117) | copy-start | bytes 1540
  76.7 19.6 %copy-start.30 = (f32[128]{0:T(128)S(1)}, f32[128]{0:T(128)}, u32[]{:S(2)}) copy-start(f32[128]{0:T(128)} %get-tuple-element.118) | copy-start | bytes 1540
  84.8 10.4 %copy-start.8 = (f32[32,32,128]{2,1,0:T(8,128)S(1)}, f32[32,32,128]{2,1,0:T(8,128)}, u32[]{:S(2)}) copy-start(f32[32,32,128]{2,1,0:T(8,128)} %get-tuple-element.73) | copy-start | bytes 1572868
  84.8 10.7 %copy-start.7 = (f32[32,32,128]{2,1,0:T(8,128)S(1)}, f32[32,32,128]{2,1,0:T(8,128)}, u32[]{:S(2)}) copy-start(f32[32,32,128]{2,1,0:T(8,128)} %get-tuple-element.74) | copy-start | bytes 1572868
  84.8 11.1 %copy-start.5 = (f32[32,32,128]{2,1,0:T(8,128)S(1)}, f32[32,32,128]{2,1,0:T(8,128)}, u32[]{:S(2)}) copy-start(f32[32,32,128]{2,1,0:T(8,128)} %get-tuple-element.75) | copy-start | bytes 1572868
  84.8 12.7 %copy-start.2 = (f32[32,32,128]{2,1,0:T(8,128)S(1)}, f32[32,32,128]{2,1,0:T(8,128)}, u32[]{:S(2)}) copy-start(f32[32,32,128]{2,1,0:T(8,128)} %get-tuple-element.76) | copy-start | bytes 1572868
  84.8 5.2 %collective-permute-start.8 = (bf16[32,8,128]{2,1,0:T(8,128)(2,1)}, bf16[32,8,128]{2,1,0:T(8,128)(2,1)S(1)}, u32[]{:S(2)}, u32[]{:S(2)}) collective-permute-start(bf16[32,8,128]{2,1,0:T(8,128)(2,1)} %get-tuple-element.11), channel_id=1, source_target_pairs={{0,1},{1,0},{2,3},{3,2},{4,5},{5,4},{6,7},{7,6},{8,9},{9,8},{10,11... | collective-permute-start | bytes 196616 | tf_op jit(solution)/shard_map/ppermute | solution.py:16
  86.8 4.9 %collective-permute-start.12 = (bf16[32,8,128]{2,1,0:T(8,128)(2,1)}, bf16[32,8,128]{2,1,0:T(8,128)(2,1)S(1)}, u32[]{:S(2)}, u32[]{:S(2)}) collective-permute-start(bf16[32,8,128]{2,1,0:T(8,128)(2,1)} %get-tuple-element.12), channel_id=1, source_target_pairs={{0,1},{1,0},{2,3},{3,2},{4,5},{5,4},{6,7},{7,6},{8,9},{9,8},{10,11... | collective-permute-start | bytes 196616 | tf_op jit(solution)/shard_map/ppermute | solution.py:16
  87.2 10.6 %copy-start.25 = (f32[128]{0:T(128)S(1)}, f32[128]{0:T(128)}, u32[]{:S(2)}) copy-start(f32[128]{0:T(128)} %get-tuple-element.119) | copy-start | bytes 1540
  87.2 10.7 %copy-start.26 = (f32[128]{0:T(128)S(1)}, f32[128]{0:T(128)}, u32[]{:S(2)}) copy-start(f32[128]{0:T(128)} %get-tuple-element.120) | copy-start | bytes 1540
  88.6 10.3 %copy-start.6 = (f32[32,32,128]{2,1,0:T(8,128)S(1)}, f32[32,32,128]{2,1,0:T(8,128)}, u32[]{:S(2)}) copy-start(f32[32,32,128]{2,1,0:T(8,128)} %get-tuple-element.69) | copy-start | bytes 1572868
  90.0 9.2 %copy-start.4 = (f32[32,32,128]{2,1,0:T(8,128)S(1)}, f32[32,32,128]{2,1,0:T(8,128)}, u32[]{:S(2)}) copy-start(f32[32,32,128]{2,1,0:T(8,128)} %get-tuple-element.70) | copy-start | bytes 1572868
  91.5 9.5 %copy-start.3 = (f32[32,32,128]{2,1,0:T(8,128)S(1)}, f32[32,32,128]{2,1,0:T(8,128)}, u32[]{:S(2)}) copy-start(f32[32,32,128]{2,1,0:T(8,128)} %get-tuple-element.71) | copy-start | bytes 1572868
  91.6 4.3 %collective-permute-start.9 = (bf16[32,8,128]{2,1,0:T(8,128)(2,1)S(1)}, bf16[32,8,128]{2,1,0:T(8,128)(2,1)S(1)}, u32[]{:S(2)}, u32[]{:S(2)}) collective-permute-start(bf16[32,8,128]{2,1,0:T(8,128)(2,1)S(1)} %get-tuple-element.18), channel_id=1, source_target_pairs={{0,2},{1,3},{2,0},{3,1},{4,6},{5,7},{6,4},{7,5},{8,10},{9,11},{10,... | collective-permute-start | bytes 196616 | tf_op jit(solution)/shard_map/ppermute | solution.py:16
  91.7 9.6 %copy-start.27 = (f32[128]{0:T(128)S(1)}, f32[128]{0:T(128)}, u32[]{:S(2)}) copy-start(f32[128]{0:T(128)} %get-tuple-element.113) | copy-start | bytes 1540
  91.7 9.6 %copy-start.28 = (f32[128]{0:T(128)S(1)}, f32[128]{0:T(128)}, u32[]{:S(2)}) copy-start(f32[128]{0:T(128)} %get-tuple-element.114) | copy-start | bytes 1540
  93.2 4.3 %collective-permute-start.13 = (bf16[32,8,128]{2,1,0:T(8,128)(2,1)S(1)}, bf16[32,8,128]{2,1,0:T(8,128)(2,1)S(1)}, u32[]{:S(2)}, u32[]{:S(2)}) collective-permute-start(bf16[32,8,128]{2,1,0:T(8,128)(2,1)S(1)} %get-tuple-element.24), channel_id=1, source_target_pairs={{0,2},{1,3},{2,0},{3,1},{4,6},{5,7},{6,4},{7,5},{8,10},{9,11},{10,... | collective-permute-start | bytes 196616 | tf_op jit(solution)/shard_map/ppermute | solution.py:16
  95.5 9.3 %copy-start.1 = (f32[32,32,128]{2,1,0:T(8,128)S(1)}, f32[32,32,128]{2,1,0:T(8,128)}, u32[]{:S(2)}) copy-start(f32[32,32,128]{2,1,0:T(8,128)} %get-tuple-element.65) | copy-start | bytes 1572868
  96.3 11.2 %copy-start.21 = (f32[32,32,128]{2,1,0:T(8,128)S(1)}, f32[32,32,128]{2,1,0:T(8,128)}, u32[]{:S(2)}) copy-start(f32[32,32,128]{2,1,0:T(8,128)} %get-tuple-element.67) | copy-start | bytes 1572868
  96.3 4.6 %collective-permute-start.10 = (bf16[32,8,128]{2,1,0:T(8,128)(2,1)S(1)}, bf16[32,8,128]{2,1,0:T(8,128)(2,1)S(1)}, u32[]{:S(2)}, u32[]{:S(2)}) collective-permute-start(bf16[32,8,128]{2,1,0:T(8,128)(2,1)S(1)} %get-tuple-element.16), channel_id=1, source_target_pairs={{0,4},{1,5},{2,6},{3,7},{4,0},{5,1},{6,2},{7,3},{8,12},{9,13},{10,... | collective-permute-start | bytes 196616 | tf_op jit(solution)/shard_map/ppermute | solution.py:16
  97.9 4.3 %collective-permute-start.14 = (bf16[32,8,128]{2,1,0:T(8,128)(2,1)S(1)}, bf16[32,8,128]{2,1,0:T(8,128)(2,1)S(1)}, u32[]{:S(2)}, u32[]{:S(2)}) collective-permute-start(bf16[32,8,128]{2,1,0:T(8,128)(2,1)S(1)} %get-tuple-element.22), channel_id=1, source_target_pairs={{0,4},{1,5},{2,6},{3,7},{4,0},{5,1},{6,2},{7,3},{8,12},{9,13},{10,... | collective-permute-start | bytes 196616 | tf_op jit(solution)/shard_map/ppermute | solution.py:16
  99.2 9.8 %copy-start.20 = (f32[32,32,128]{2,1,0:T(8,128)S(1)}, f32[32,32,128]{2,1,0:T(8,128)}, u32[]{:S(2)}) copy-start(f32[32,32,128]{2,1,0:T(8,128)} %get-tuple-element.68) | copy-start | bytes 1572868
  101.4 6.1 %collective-permute-start.11 = (bf16[32,8,128]{2,1,0:T(8,128)(2,1)S(1)}, bf16[32,8,128]{2,1,0:T(8,128)(2,1)S(1)}, u32[]{:S(2)}, u32[]{:S(2)}) collective-permute-start(bf16[32,8,128]{2,1,0:T(8,128)(2,1)S(1)} %get-tuple-element.14), channel_id=1, source_target_pairs={{0,8},{1,9},{2,10},{3,11},{4,12},{5,13},{6,14},{7,15},{8,0},{9,1},... | collective-permute-start | bytes 196616 | tf_op jit(solution)/shard_map/ppermute | solution.py:16
  102.6 6.4 %collective-permute-start.15 = (bf16[32,8,128]{2,1,0:T(8,128)(2,1)S(1)}, bf16[32,8,128]{2,1,0:T(8,128)(2,1)S(1)}, u32[]{:S(2)}, u32[]{:S(2)}) collective-permute-start(bf16[32,8,128]{2,1,0:T(8,128)(2,1)S(1)} %get-tuple-element.20), channel_id=1, source_target_pairs={{0,8},{1,9},{2,10},{3,11},{4,12},{5,13},{6,14},{7,15},{8,0},{9,1},... | collective-permute-start | bytes 196616 | tf_op jit(solution)/shard_map/ppermute | solution.py:16

commit v2 on v0

v2 whole, which is shorter than its diff:
```python
import functools

import jax
import jax.numpy as jnp
from jax import lax
from jax.experimental import pallas as pl
from jax.experimental.pallas import tpu as pltpu
from jax.sharding import PartitionSpec as P

LANES = 128
GROUP = 4


def digits():
    place = lax.axis_index("leaf")
    return lax.rem(place // 8, 2), lax.rem(place // 4, 2), lax.rem(place // 2, 2), lax.rem(place, 2)


def lanes_of(chunk):
    return pl.ds(pl.multiple_of(chunk * LANES, LANES), LANES)


def rows_of(half, rank):
    return pl.ds(pl.multiple_of(half * rank, rank), rank)


def spread(wide, load, row_count, rank):
    def body(step, carry):
        rows = load(step * GROUP).astype(jnp.float32)
        wide[pl.ds(step * GROUP * rank, GROUP * rank), :] = rows.reshape(GROUP * rank, LANES)
        return carry

    lax.fori_loop(0, row_count // GROUP, body, 0)


def multiply(wide, state, row_count, emit):
    rank = len(state)

    def body(step, carry):
        for inner in range(GROUP):
            sums = [None, None]
            for index in range(rank):
                weight = wide[pl.ds(step * GROUP * rank + inner * rank + index, 8, stride=0), :]
                term = weight * state[index]
                old = sums[index % 2]
                sums[index % 2] = term if old is None else old + term
            emit(step * GROUP + inner, sums[0] + sums[1])
        return carry

    lax.fori_loop(0, row_count // GROUP, body, 0)


def state_rows(ref, present=None):
    rows = [ref[index].astype(jnp.float32) for index in range(ref.shape[0])]
    return rows if present is None else [row * present for row in rows]


def level_load(blocks, level, half, chunk):
    rank = blocks.shape[1]
    return lambda row: blocks[level, pl.ds(row, GROUP), rows_of(half, rank), lanes_of(chunk)]


def present_of(pattern, level, half, chunk):
    pair = [pattern[level, place:place + 1, lanes_of(chunk)].astype(jnp.float32) for place in range(2)]
    return jnp.where(half == 0, pair[0], pair[1])


def coeff_kernel(flip, interp, samples, out, wide, total):
    rank, depth = interp.shape[0], interp.shape[1] // 2
    chunk = digits()[3] ^ flip
    for half in range(2):
        spread(wide, lambda row: interp[pl.ds(row, GROUP), pl.ds(half * depth, depth), lanes_of(chunk)], rank, depth)
        state = [samples[half * depth + index, :, lanes_of(chunk)].astype(jnp.float32) for index in range(depth)]

        def emit(row, value):
            if half == 0:
                total[row] = value
            else:
                out[row] = (total[row] + value).astype(jnp.bfloat16)

        multiply(wide, state, rank, emit)


def near_kernel(level, bit, flip, blocks, pattern, state, out, wide):
    places = digits()
    chunk, own = places[3] ^ flip, places[3 - bit]
    spread(wide, level_load(blocks, level, own, chunk), blocks.shape[1], blocks.shape[1])

    def emit(row, value):
        out[row] = value

    multiply(wide, state_rows(state, present_of(pattern, level, own, chunk)), blocks.shape[1], emit)


def far_kernel(level, bit, flip, blocks, pattern, partner, near, out, wide):
    places = digits()
    chunk, other = places[3] ^ flip, 1 - places[3 - bit]
    spread(wide, level_load(blocks, level, other, chunk), blocks.shape[1], blocks.shape[1])

    def emit(row, value):
        out[row] = (near[row] + value).astype(jnp.bfloat16)

    multiply(wide, state_rows(partner, present_of(pattern, level, other, chunk)), blocks.shape[1], emit)


def share_kernel(top_level, top_blocks, top_pattern, bottom_blocks, bottom_pattern, after, out):
    rank = top_blocks.shape[1]
    chunk = 1 - digits()[3]
    for place, (blocks, pattern, level) in enumerate(((top_blocks, top_pattern, top_level), (bottom_blocks, bottom_pattern, 0))):
        for half in range(2):
            present = present_of(pattern, level, half, chunk)[None]

            def body(row, carry):
                rows = blocks[level, pl.ds(row, 1), half * rank:(half + 1) * rank, lanes_of(chunk)]
                out[place, pl.ds(row, 1), half * rank:(half + 1) * rank, :] = (rows.astype(jnp.float32) * present).astype(jnp.bfloat16)
                return carry

            lax.fori_loop(0, rank, body, 0)


def swap_groups(tile, slot):
    lane_group = lax.broadcasted_iota(jnp.int32, tile[0].shape, 2) // slot
    step = 1
    while step < len(tile):
        low = (lane_group // step) % 2 == 0
        fresh = list(tile)
        for place in range(len(tile)):
            if place & step == 0:
                first, second = tile[place], tile[place + step]
                fresh[place] = jnp.where(low, first, pltpu.roll(second, step * slot, 2))
                fresh[place + step] = jnp.where(low, pltpu.roll(first, LANES - step * slot, 2), second)
        tile = fresh
        step *= 2
    return tile


def pair_near_kernel(level, blocks, pattern, shared, state, out, wide):
    rank = blocks.shape[1]
    core = digits()[3]
    rows = state_rows(state)
    present = present_of(pattern, level, core, core)
    for box in range(2):
        load = (
            level_load(blocks, level, core, core)
            if box == 0
            else lambda row: shared[0, pl.ds(row, GROUP), rows_of(core, rank), :]
        )
        spread(wide, load, rank, rank)

        def emit(row, value):
            out[box, row] = value

        multiply(wide, [row * present for row in rows] if box == 0 else rows, rank, emit)


def pair_far_kernel(level, slot, blocks, pattern, shared, partner, near, *rest):
    outs, (wide, total, packed) = rest[:4], rest[4:]
    rank = blocks.shape[1]
    _, mid, low, core = digits()
    rows = state_rows(partner)
    present = present_of(pattern, level, 1 - core, core)
    fold = LANES // slot
    for box in range(2):
        load = (
            level_load(blocks, level, 1 - core, core)
            if box == 0
            else lambda row: shared[0, pl.ds(row, GROUP), rows_of(1 - core, rank), :]
        )
        spread(wide, load, rank, rank)

        def emit(row, value):
            total[row] = near[box, row] + value

        multiply(wide, [row * present for row in rows] if box == 0 else rows, rank, emit)
        depth = rank // fold
        pieces = swap_groups([total[place * depth:(place + 1) * depth] for place in range(fold)], slot)
        for place, piece in enumerate(pieces):
            packed[core ^ box, place] = piece.astype(jnp.bfloat16)
    for turn, out in enumerate(outs):
        first = ((mid ^ (turn // 2)) * 2 + (low ^ (turn % 2))) * 2
        for box in range(2):
            for last in range(2):
                out[box, last] = packed[box, first + last]


def pair_box(level, wide, total, states, loads, presents, rank, out):
    for half in range(2):
        spread(wide, loads[half], rank, rank)
        present = presents[half]
        rows = [states[half, index].astype(jnp.float32) for index in range(rank)]
        if present is not None:
            rows = [row * present for row in rows]

        def emit(row, value):
            if half == 0:
                total[row] = value
            else:
                out[row] = (total[row] + value).astype(jnp.bfloat16)

        multiply(wide, rows, rank, emit)


def open_kernel(slot, blocks, pattern, *rest):
    pieces, (out, states, wide, total, packed) = rest[:4], rest[4:]
    rank = blocks.shape[1]
    _, mid, low, core = digits()
    fold = LANES // slot
    depth = rank // fold
    for turn, piece in enumerate(pieces):
        first = ((mid ^ (turn // 2)) * 2 + (low ^ (turn % 2))) * 2
        for box in range(2):
            for last in range(2):
                packed[last, first + box] = piece[box, last]
    for last in range(2):
        tile = swap_groups([packed[last, place].astype(jnp.float32) for place in range(fold)], slot)
        for place, rows in enumerate(tile):
            states[last, place * depth:(place + 1) * depth] = rows.astype(jnp.bfloat16)
    loads = [level_load(blocks, 0, half, core) for half in range(2)]
    presents = [present_of(pattern, 0, half, core) for half in range(2)]
    pair_box(0, wide, total, states, loads, presents, rank, out)


def other_kernel(shared, states, out, wide, total):
    rank = out.shape[0]
    loads = [
        functools.partial(lambda half, row: shared[1, pl.ds(row, GROUP), half * rank:(half + 1) * rank, :], half)
        for half in range(2)
    ]
    pair_box(0, wide, total, states, loads, (None, None), rank, out)


def last_kernel(level, bit, flip, joins, blocks, pattern, interp, partner, near, *rest):
    places = digits()
    chunk, other = places[3] ^ flip, 1 - places[3 - bit]
    rank = blocks.shape[1]
    if joins:
        ready, out, wide, total = rest
        for index in range(out.shape[0]):
            out[index, :, lanes_of(1 - chunk)] = ready[index]
    else:
        out, wide, total = rest
    spread(wide, level_load(blocks, level, other, chunk), rank, rank)

    def emit_state(row, value):
        total[row] = (near[row] + value).astype(jnp.bfloat16).astype(jnp.float32)

    multiply(wide, state_rows(partner, present_of(pattern, level, other, chunk)), rank, emit_state)
    spread(wide, lambda row: interp[pl.ds(row, GROUP), :, lanes_of(chunk)], out.shape[0], rank)

    def emit(row, value):
        if joins:
            out[row, :, lanes_of(chunk)] = value.astype(jnp.bfloat16)
        else:
            out[row] = value.astype(jnp.bfloat16)

    multiply(wide, [total[index] for index in range(rank)], out.shape[0], emit)


def run(kernel, outs, operands, scratch=(), products=1):
    whole = pl.BlockSpec(memory_space=pltpu.VMEM)
    single = not isinstance(outs, list)
    shapes = [outs] if single else outs
    result = pl.pallas_call(
        kernel,
        out_shape=shapes,
        in_specs=[whole] * len(operands),
        out_specs=[whole] * len(shapes),
        scratch_shapes=list(scratch),
        compiler_params=pltpu.CompilerParams(vmem_limit_bytes=16 * 2**20),
        cost_estimate=pl.CostEstimate(flops=products * 2**21, bytes_accessed=products * 2**19, transcendentals=0),
    )(*operands)
    return result[0] if single else result


def permuted(value, target_of):
    pairs = [(source, target_of(source)) for source in range(lax.axis_size("leaf"))]
    return lax.ppermute(value, "leaf", pairs)


def swapped(value, bit):
    return permuted(value, lambda source: source ^ 2**bit)


def crossed(source, turn):
    high, mid, low, core = source // 8 % 2, source // 4 % 2, source // 2 % 2, source % 2
    return ((core * 2 + (mid ^ (turn // 2))) * 2 + (low ^ (turn % 2))) * 2 + high


def fast_local(samples, interp_in, top_blocks, top_pattern, bottom_blocks, bottom_pattern, interp_out):
    rank, depth = interp_in.shape[:2]
    rhs_count, box_count = samples.shape[1:]
    out_depth = interp_out.shape[0]
    slot = box_count // lax.axis_size("leaf")
    fold = LANES // slot
    state = jax.ShapeDtypeStruct((rank, rhs_count, LANES), jnp.bfloat16)
    partial = jax.ShapeDtypeStruct((rank, rhs_count, LANES), jnp.float32)
    total = pltpu.VMEM((rank, rhs_count, LANES), jnp.float32)
    wide = pltpu.VMEM((rank * rank, LANES), jnp.float32)
    packed = pltpu.VMEM((2, fold, rank // fold, rhs_count, LANES), jnp.bfloat16)

    current = {}
    for flip in (1, 0):
        current[flip] = run(
            functools.partial(coeff_kernel, flip), state, (interp_in, samples),
            (pltpu.VMEM((rank * depth // 2, LANES), jnp.float32), total), 2,
        )
    after = current[0]
    for level in range(3):
        bit = 3 - level
        partner = {flip: swapped(current[flip], bit) for flip in (1, 0)}
        near = {
            flip: run(functools.partial(near_kernel, level, bit, flip), partial, (top_blocks, top_pattern, current[flip]), (wide,))
            for flip in (1, 0)
        }
        for flip in (1, 0):
            current[flip] = run(
                functools.partial(far_kernel, level, bit, flip), state,
                (top_blocks, top_pattern, partner[flip], near[flip]), (wide,),
            )
    shared = run(
        functools.partial(share_kernel, 3), jax.ShapeDtypeStruct((2, rank, 2 * rank, LANES), jnp.bfloat16),
        (top_blocks, top_pattern, bottom_blocks, bottom_pattern, after),
    )
    shared = swapped(shared, 0)

    far = swapped(current[1], 0)
    near = run(
        functools.partial(pair_near_kernel, 3), jax.ShapeDtypeStruct((2, rank, rhs_count, LANES), jnp.float32),
        (top_blocks, top_pattern, shared, current[0]), (wide,), 2,
    )
    piece = jax.ShapeDtypeStruct((2, 2, rank // fold, rhs_count, LANES), jnp.bfloat16)
    pieces = run(
        functools.partial(pair_far_kernel, 3, slot), [piece] * 4,
        (top_blocks, top_pattern, shared, far, near), (wide, total, packed), 2,
    )
    pieces = [permuted(value, functools.partial(crossed, turn=turn)) for turn, value in enumerate(pieces)]
    first, states = run(
        functools.partial(open_kernel, slot), [state, jax.ShapeDtypeStruct((2, rank, rhs_count, LANES), jnp.bfloat16)],
        (bottom_blocks, bottom_pattern, *pieces), (wide, total, packed), 2,
    )
    second = run(other_kernel, state, (shared, states), (wide, total), 2)
    current = {0: first, 1: swapped(second, 0)}

    for level in (1, 2, 3):
        partner = {flip: swapped(current[flip], level) for flip in (0, 1)}
        near = {
            flip: run(functools.partial(near_kernel, level, level, flip), partial, (bottom_blocks, bottom_pattern, current[flip]), (wide,))
            for flip in (0, 1)
        }
        if level < 3:
            for flip in (0, 1):
                current[flip] = run(
                    functools.partial(far_kernel, level, level, flip), state,
                    (bottom_blocks, bottom_pattern, partner[flip], near[flip]), (wide,),
                )
    broad = pltpu.VMEM((out_depth * rank, LANES), jnp.float32)
    ready = run(
        functools.partial(last_kernel, 3, 3, 0, False), jax.ShapeDtypeStruct((out_depth, rhs_count, LANES), jnp.bfloat16),
        (bottom_blocks, bottom_pattern, interp_out, partner[0], near[0]), (broad, total), 3,
    )
    return run(
        functools.partial(last_kernel, 3, 3, 1, True), jax.ShapeDtypeStruct((out_depth, rhs_count, box_count), jnp.bfloat16),
        (bottom_blocks, bottom_pattern, interp_out, partner[1], near[1], ready), (broad, total), 3,
    )


def contract(weights, state):
    product = weights[:, :, None].astype(jnp.float32) * state[None].astype(jnp.float32)
    return jnp.sum(product, axis=1)


def plain_level(current, blocks, pattern, bit):
    rank = blocks.shape[0]
    partner = swapped(current, bit)
    is_lower = lax.axis_index("leaf") // 2**bit % 2 == 0
    lower = jnp.where(is_lower, current, partner)
    upper = jnp.where(is_lower, partner, current)
    weights = blocks * jnp.repeat(pattern, rank, axis=0).astype(jnp.bfloat16)[None]
    return contract(weights, jnp.concatenate([lower, upper], axis=0)).astype(jnp.bfloat16)


def plain_local(samples, interp_in, top_blocks, top_pattern, bottom_blocks, bottom_pattern, interp_out):
    bit_count = lax.axis_size("leaf").bit_length() - 1
    current = contract(interp_in, samples).astype(jnp.bfloat16)
    for level in range(top_blocks.shape[0]):
        current = plain_level(current, top_blocks[level], top_pattern[level], bit_count - 1 - level)
    flat = current.reshape(-1, current.shape[2])
    current = lax.all_to_all(flat, "leaf", split_axis=1, concat_axis=1, tiled=True).reshape(current.shape)
    for level in range(bottom_blocks.shape[0]):
        current = plain_level(current, bottom_blocks[level], bottom_pattern[level], level)
    return contract(interp_out, current).astype(jnp.bfloat16)


def local(samples, interp_in, top_blocks, *rest):
    four_digits = lax.axis_size("leaf") == 16 and top_blocks.shape[0] == 4
    chosen = fast_local if four_digits and samples.shape[1:] == (8, 2 * LANES) else plain_local
    return chosen(samples, interp_in, top_blocks, *rest)


def solution(mesh):
    boxes = ("parts", "leaf")
    return jax.shard_map(
        local,
        mesh=mesh,
        in_specs=(
            P(None, None, boxes),
            P(None, None, boxes),
            P(None, None, None, boxes),
            P(None, None, boxes),
            P(None, None, None, boxes),
            P(None, None, boxes),
            P(None, None, boxes),
        ),
        out_specs=P(None, None, boxes),
        check_vma=False,
    )
```

time: 87.6 us -> 72.4 us (0.83)
  other arithmetic: 30.5 us -> 0 us
  waiting for transfers between devices: 38.4 us -> 17.1 us
  Pallas kernels: 0 us -> 20.2 us
  starting transfers between devices: 13.8 us -> 26.6 us
  local copies, waits for them, and re-layouts: 4.22 us -> 7.96 us
    reduce_sum x10 -> x0, other arithmetic: 21.7 us -> none  [contract(): return jnp.sum(product, axis=1)]
    pallas_call x0 -> x31, Pallas kernels: none -> 20.2 us  [run(): pl.pallas_call(kernel, out_shape=shapes, in_specs=[whole] * len(operands)...]
    ppermute x8 -> x19, starting transfers between devices: 7.26 us -> 26.6 us  [permuted(): return lax.ppermute(value, 'leaf', pairs)]
    ppermute x8 -> x19, waiting for transfers between devices: 30.7 us -> 17.1 us  [permuted(): return lax.ppermute(value, 'leaf', pairs)]
    convert_element_type x14 -> x0, other arithmetic: 8.65 us -> none  [the longest x4 7.34 us: contract(): weights[:, :, None].astype(jnp.float32) * state[None].astype(jnp.float32)]
    unnamed x8 -> x24, local copies, waits for them, and re-layouts: 0.02 us -> 7.96 us
    all_to_all x1 -> x0, waiting for transfers between devices: 7.72 us -> none  [transpose_boxes(): lax.all_to_all(values, 'leaf', split_axis=1, concat_axis=1, tiled=True)]
    all_to_all x1 -> x0, starting transfers between devices: 6.51 us -> none  [transpose_boxes(): lax.all_to_all(values, 'leaf', split_axis=1, concat_axis=1, tiled=True)]
  transfers between devices with their start and end apart: 9 -> 19, of which waited for: 8 -> 12; matrix products, arithmetic and copies ran while one was open for 7% -> 0% of each run, Pallas kernels for 0% -> 18%
where the time goes in v2:
time: 72.4 us; the launch traced here: 72.1 us
  starting transfers between devices  26.6 us (37%)
  Pallas kernels  20.2 us (28%)
  waiting for transfers between devices  17.1 us (24%)
  local copies, waits for them, and re-layouts  7.96 us (11%)
    ppermute x19, starting transfers between devices, permuted(): return lax.ppermute(value, 'leaf', pairs)  26.6 us
    pallas_call x31, Pallas kernels, run(): pl.pallas_call(kernel, out_shape=shapes, in_specs=[whole] * len(operands)...  20.2 us
    ppermute x19, waiting for transfers between devices, permuted(): return lax.ppermute(value, 'leaf', pairs)  17.1 us
    unnamed x24, local copies, waits for them, and re-layouts  7.96 us
  transfers between devices with their start and end apart: 19, of which 12 were waited for; matrix products, arithmetic and copies ran while one was open for 0% of the time, Pallas kernels for 18%

profile of v2, /device:TPU:0, one launch (start us, length us, event | category | flops | bytes accessed | tf_op | source)
XLA Modules:
  0.0 72.1 jit_solution(14322382388045087081)
XLA Ops:
  0.0 1.2 %copy-done.4 = bf16[32,64,256]{2,1,0:T(8,128)(2,1)S(1)} copy-done((bf16[32,64,256]{2,1,0:T(8,128)(2,1)S(1)}, bf16[32,64,256]{2,1,0:T(8,128)(2,1)}, u32[]{:S(2)}) %copy-start.4) | copy-done | bytes 1048600
  1.2 0.9 %copy-done.10 = bf16[64,8,256]{2,1,0:T(8,128)(2,1)S(1)} copy-done((bf16[64,8,256]{2,1,0:T(8,128)(2,1)S(1)}, bf16[64,8,256]{2,1,0:T(8,128)(2,1)}, u32[]{:S(2)}) %copy-start.10) | copy-done | bytes 262168
  2.2 0.9 %shard_map.73.after.state = bf16[32,8,128]{2,1,0:T(8,128)(2,1)S(1)} custom-call(bf16[32,64,256]{2,1,0:T(8,128)(2,1)S(1)} %copy-done.4, bf16[64,8,256]{2,1,0:T(8,128)(2,1)S(1)} %copy-done.10), custom_call_target="tpu_custom_call" | custom-call | flops 4194304 | bytes 1048576 | tf_op jit(solution)/shard_map/pallas_call | solution.py:263
  3.1 2.2 %copy-done = bf16[4,32,64,256]{3,2,1,0:T(8,128)(2,1)S(1)} copy-done((bf16[4,32,64,256]{3,2,1,0:T(8,128)(2,1)S(1)}, bf16[4,32,64,256]{3,2,1,0:T(8,128)(2,1)}, u32[]{:S(2)}) %copy-start) | copy-done | bytes 4194328
  5.2 2.2 %copy-done.2 = bf16[4,32,64,256]{3,2,1,0:T(8,128)(2,1)S(1)} copy-done((bf16[4,32,64,256]{3,2,1,0:T(8,128)(2,1)S(1)}, bf16[4,32,64,256]{3,2,1,0:T(8,128)(2,1)}, u32[]{:S(2)}) %copy-start.2) | copy-done | bytes 4194328
  7.4 0.7 copy-done.7
  8.1 0.7 copy-done.9
  8.8 0.9 %shard_map.74 = bf16[2,32,64,128]{3,2,1,0:T(8,128)(2,1)S(1)} custom-call(bf16[4,32,64,256]{3,2,1,0:T(8,128)(2,1)S(1)} %copy-done, s32[4,2,256]{2,1,0:T(2,128)S(1)} %copy-done.7, bf16[4,32,64,256]{3,2,1,0:T(8,128)(2,1)S(1)} %copy-done.2, s32[4,2,256]{2,1,0:T(2,128)S(1)} %copy-done.9, bf16[32,8,128]{2,1,0:T(8,128)(2,1)S(1)} %shard_map.73.after.state), custom_call_target="tpu_custom_call" | custom-call | flops 2097152 | bytes 524288 | tf_op jit(solution)/shard_map/pallas_call | solution.py:263
  9.7 0.5 collective-permute-start
  10.2 0.9 %shard_map.75.state = bf16[32,8,128]{2,1,0:T(8,128)(2,1)S(1)} custom-call(bf16[32,64,256]{2,1,0:T(8,128)(2,1)S(1)} %copy-done.5, bf16[64,8,256]{2,1,0:T(8,128)(2,1)S(1)} %copy-done.11), custom_call_target="tpu_custom_call" | custom-call | flops 4194304 | bytes 1048576 | tf_op jit(solution)/shard_map/pallas_call | solution.py:263
  11.1 4.0 %collective-permute-start.1 = (bf16[32,8,128]{2,1,0:T(8,128)(2,1)S(1)}, bf16[32,8,128]{2,1,0:T(8,128)(2,1)S(1)}, u32[]{:S(2)}, u32[]{:S(2)}) collective-permute-start(bf16[32,8,128]{2,1,0:T(8,128)(2,1)S(1)} %shard_map.75.state), channel_id=1, source_target_pairs={{0,8},{1,9},{2,10},{3,11},{4,12},{5,13},{6,14},{7,15},{8,0},{9,1},... | collective-permute-start | bytes 196616 | tf_op jit(solution)/shard_map/ppermute | solution.py:277
  15.1 0.4 shard_map.76.near
  15.6 3.5 %collective-permute-done.1.partner = bf16[32,8,128]{2,1,0:T(8,128)(2,1)S(1)} collective-permute-done((bf16[32,8,128]{2,1,0:T(8,128)(2,1)S(1)}, bf16[32,8,128]{2,1,0:T(8,128)(2,1)S(1)}, u32[]{:S(2)}, u32[]{:S(2)}) %collective-permute-start.1) | collective-permute-done | bytes 65568 | tf_op jit(solution)/shard_map/ppermute | solution.py:277
  19.1 0.5 shard_map.77.state
  19.5 2.1 %collective-permute-start.2 = (bf16[32,8,128]{2,1,0:T(8,128)(2,1)S(1)}, bf16[32,8,128]{2,1,0:T(8,128)(2,1)S(1)}, u32[]{:S(2)}, u32[]{:S(2)}) collective-permute-start(bf16[32,8,128]{2,1,0:T(8,128)(2,1)S(1)} %shard_map.77.state), channel_id=1, source_target_pairs={{0,4},{1,5},{2,6},{3,7},{4,0},{5,1},{6,2},{7,3},{8,12},{9,13},{10,... | collective-permute-start | bytes 196616 | tf_op jit(solution)/shard_map/ppermute | solution.py:277
  21.6 0.4 shard_map.82.near
  22.1 0.5 shard_map.83.state
  22.6 0.4 collective-permute-start.6
  23.0 0.4 shard_map.78.near
  23.4 0.5 collective-permute-done.2.partner
  23.9 0.5 shard_map.79.state
  24.3 1.9 %collective-permute-start.3 = (bf16[32,8,128]{2,1,0:T(8,128)(2,1)S(1)}, bf16[32,8,128]{2,1,0:T(8,128)(2,1)S(1)}, u32[]{:S(2)}, u32[]{:S(2)}) collective-permute-start(bf16[32,8,128]{2,1,0:T(8,128)(2,1)S(1)} %shard_map.79.state), channel_id=1, source_target_pairs={{0,2},{1,3},{2,0},{3,1},{4,6},{5,7},{6,4},{7,5},{8,10},{9,11},{10,... | collective-permute-start | bytes 196616 | tf_op jit(solution)/shard_map/ppermute | solution.py:277
  26.2 0.4 shard_map.84.near
  26.9 0.5 shard_map.85.state
  27.3 1.6 %collective-permute-start.7 = (bf16[32,8,128]{2,1,0:T(8,128)(2,1)S(1)}, bf16[32,8,128]{2,1,0:T(8,128)(2,1)S(1)}, u32[]{:S(2)}, u32[]{:S(2)}) collective-permute-start(bf16[32,8,128]{2,1,0:T(8,128)(2,1)S(1)} %shard_map.85.state), channel_id=1, source_target_pairs={{0,2},{1,3},{2,0},{3,1},{4,6},{5,7},{6,4},{7,5},{8,10},{9,11},{10,... | collective-permute-start | bytes 196616 | tf_op jit(solution)/shard_map/ppermute | solution.py:277
  28.9 0.4 shard_map.80.near
  29.4 0.5 shard_map.81
  29.9 0.5 shard_map.86.near
  30.4 1.3 %collective-permute-done.7.partner = bf16[32,8,128]{2,1,0:T(8,128)(2,1)S(1)} collective-permute-done((bf16[32,8,128]{2,1,0:T(8,128)(2,1)S(1)}, bf16[32,8,128]{2,1,0:T(8,128)(2,1)S(1)}, u32[]{:S(2)}, u32[]{:S(2)}) %collective-permute-start.7) | collective-permute-done | bytes 65568 | tf_op jit(solution)/shard_map/ppermute | solution.py:277
  31.7 0.5 shard_map.87.state
  32.2 0.9 %shard_map.88.near = f32[2,32,8,128]{3,2,1,0:T(8,128)S(1)} custom-call(bf16[4,32,64,256]{3,2,1,0:T(8,128)(2,1)S(1)} %copy-done.1, s32[4,2,256]{2,1,0:T(2,128)S(1)} %copy-done.8, bf16[2,32,64,128]{3,2,1,0:T(8,128)(2,1)S(1)} %collective-permute-done.shared, bf16[32,8,128]{2,1,0:T(8,128)(2,1)S(1)} %shard_map.87.state), custom_call_target="tpu_custom_call" | custom-call | flops 4194304 | bytes 1048576 | tf_op jit(solution)/shard_map/pallas_call | solution.py:263
  33.1 1.4 %shard_map.89 = (bf16[2,2,4,8,128]{4,3,2,1,0:T(8,128)(2,1)S(1)}, bf16[2,2,4,8,128]{4,3,2,1,0:T(8,128)(2,1)S(1)}, bf16[2,2,4,8,128]{4,3,2,1,0:T(8,128)(2,1)S(1)}, bf16[2,2,4,8,128]{4,3,2,1,0:T(8,128)(2,1)S(1)}) custom-call(bf16[4,32,64,256]{3,2,1,0:T(8,128)(2,1)S(1)} %copy-done.1, s32[4,2,256]{2,1,0:T(2,128)S(1)} %copy-done.8, ...), custom_call_target="tpu_custom_call" | custom-call | flops 4194304 | bytes 1048576 | tf_op jit(solution)/shard_map/pallas_call | solution.py:263
  34.5 2.0 %collective-permute-start.10 = (bf16[2,2,4,8,128]{4,3,2,1,0:T(8,128)(2,1)S(1)}, bf16[2,2,4,8,128]{4,3,2,1,0:T(8,128)(2,1)S(1)}, u32[]{:S(2)}, u32[]{:S(2)}) collective-permute-start(bf16[2,2,4,8,128]{4,3,2,1,0:T(8,128)(2,1)S(1)} %get-tuple-element.13), channel_id=1, source_target_pairs={{0,4},{1,12},{2,6},{3,14},{4,0},{5,8},{6,2},{7,10},{8,5},{9,13},{1... | collective-permute-start | bytes 98312 | tf_op jit(solution)/shard_map/ppermute | solution.py:277
  36.5 1.1 %collective-permute-start.11 = (bf16[2,2,4,8,128]{4,3,2,1,0:T(8,128)(2,1)S(1)}, bf16[2,2,4,8,128]{4,3,2,1,0:T(8,128)(2,1)S(1)}, u32[]{:S(2)}, u32[]{:S(2)}) collective-permute-start(bf16[2,2,4,8,128]{4,3,2,1,0:T(8,128)(2,1)S(1)} %get-tuple-element.14), channel_id=1, source_target_pairs={{0,6},{1,14},{2,4},{3,12},{4,2},{5,10},{6,0},{7,8},{8,7},{9,15},{1... | collective-permute-start | bytes 98312 | tf_op jit(solution)/shard_map/ppermute | solution.py:277
  37.5 0.7 collective-permute-start.8
  38.2 0.6 collective-permute-start.9
  38.8 2.7 %collective-permute-done.11.rest_3_ = bf16[2,2,4,8,128]{4,3,2,1,0:T(8,128)(2,1)S(1)} collective-permute-done((bf16[2,2,4,8,128]{4,3,2,1,0:T(8,128)(2,1)S(1)}, bf16[2,2,4,8,128]{4,3,2,1,0:T(8,128)(2,1)S(1)}, u32[]{:S(2)}, u32[]{:S(2)}) %collective-permute-start.11) | collective-permute-done | bytes 32800 | tf_op jit(solution)/shard_map/ppermute | solution.py:277
  41.5 0.7 collective-permute-done.9.rest_1_
  42.2 1.2 %shard_map.90 = (bf16[32,8,128]{2,1,0:T(8,128)(2,1)S(1)}, bf16[2,32,8,128]{3,2,1,0:T(8,128)(2,1)S(1)}) custom-call(bf16[4,32,64,256]{3,2,1,0:T(8,128)(2,1)S(1)} %copy-done.3, s32[4,2,256]{2,1,0:T(2,128)S(1)} %copy-done.9, bf16[2,2,4,8,128]{4,3,2,1,0:T(8,128)(2,1)S(1)} %collective-permute-done.8.rest_0_, ...), custom_call_target="tpu_custom_call" | custom-call | flops 4194304 | bytes 1048576 | tf_op jit(solution)/shard_map/pallas_call | solution.py:263
  43.4 0.9 %shard_map.91 = bf16[32,8,128]{2,1,0:T(8,128)(2,1)S(1)} custom-call(bf16[2,32,64,128]{3,2,1,0:T(8,128)(2,1)S(1)} %collective-permute-done.shared, bf16[2,32,8,128]{3,2,1,0:T(8,128)(2,1)S(1)} %get-tuple-element.15.states), custom_call_target="tpu_custom_call" | custom-call | flops 4194304 | bytes 1048576 | tf_op jit(solution)/shard_map/pallas_call | solution.py:263
  44.2 5.7 %collective-permute-start.12 = (bf16[32,8,128]{2,1,0:T(8,128)(2,1)S(1)}, bf16[32,8,128]{2,1,0:T(8,128)(2,1)S(1)}, u32[]{:S(2)}, u32[]{:S(2)}) collective-permute-start(bf16[32,8,128]{2,1,0:T(8,128)(2,1)S(1)} %shard_map.91), channel_id=1, source_target_pairs={{0,1},{1,0},{2,3},{3,2},{4,5},{5,4},{6,7},{7,6},{8,9},{9,8},{10,11... | collective-permute-start | bytes 196616 | tf_op jit(solution)/shard_map/ppermute | solution.py:277
  50.0 0.5 collective-permute-start.16
  50.5 0.4 collective-permute-done.12.state
  50.9 1.1 %collective-permute-start.13 = (bf16[32,8,128]{2,1,0:T(8,128)(2,1)S(1)}, bf16[32,8,128]{2,1,0:T(8,128)(2,1)S(1)}, u32[]{:S(2)}, u32[]{:S(2)}) collective-permute-start(bf16[32,8,128]{2,1,0:T(8,128)(2,1)S(1)} %collective-permute-done.12.state), channel_id=1, source_target_pairs={{0,2},{1,3},{2,0},{3,1},{4,6},{5,7},{6,4},{7,5},{8,10},{9,11},{10,... | collective-permute-start | bytes 196616 | tf_op jit(solution)/shard_map/ppermute | solution.py:277
  52.0 0.4 shard_map.97.near
  52.4 2.2 %collective-permute-done.16.partner = bf16[32,8,128]{2,1,0:T(8,128)(2,1)S(1)} collective-permute-done((bf16[32,8,128]{2,1,0:T(8,128)(2,1)S(1)}, bf16[32,8,128]{2,1,0:T(8,128)(2,1)S(1)}, u32[]{:S(2)}, u32[]{:S(2)}) %collective-permute-start.16) | collective-permute-done | bytes 65568 | tf_op jit(solution)/shard_map/ppermute | solution.py:277
  54.6 0.5 shard_map.98.state
  55.1 2.8 %collective-permute-start.17 = (bf16[32,8,128]{2,1,0:T(8,128)(2,1)S(1)}, bf16[32,8,128]{2,1,0:T(8,128)(2,1)S(1)}, u32[]{:S(2)}, u32[]{:S(2)}) collective-permute-start(bf16[32,8,128]{2,1,0:T(8,128)(2,1)S(1)} %shard_map.98.state), channel_id=1, source_target_pairs={{0,4},{1,5},{2,6},{3,7},{4,0},{5,1},{6,2},{7,3},{8,12},{9,13},{10,... | collective-permute-start | bytes 196616 | tf_op jit(solution)/shard_map/ppermute | solution.py:277
  57.9 0.4 shard_map.92.near
  58.3 0.5 shard_map.93.state
  59.0 0.4 shard_map.99.near
  59.4 1.2 %collective-permute-done.17.partner = bf16[32,8,128]{2,1,0:T(8,128)(2,1)S(1)} collective-permute-done((bf16[32,8,128]{2,1,0:T(8,128)(2,1)S(1)}, bf16[32,8,128]{2,1,0:T(8,128)(2,1)S(1)}, u32[]{:S(2)}, u32[]{:S(2)}) %collective-permute-start.17) | collective-permute-done | bytes 65568 | tf_op jit(solution)/shard_map/ppermute | solution.py:277
  60.6 0.5 shard_map.100.state
  61.0 0.5 collective-permute-start.18
  61.5 0.4 shard_map.94.near
  61.9 1.7 %collective-permute-done.14.partner = bf16[32,8,128]{2,1,0:T(8,128)(2,1)S(1)} collective-permute-done((bf16[32,8,128]{2,1,0:T(8,128)(2,1)S(1)}, bf16[32,8,128]{2,1,0:T(8,128)(2,1)S(1)}, u32[]{:S(2)}, u32[]{:S(2)}) %collective-permute-start.14) | collective-permute-done | bytes 65568 | tf_op jit(solution)/shard_map/ppermute | solution.py:277
  63.6 0.5 shard_map.95.state
  64.1 0.9 %collective-permute-start.15 = (bf16[32,8,128]{2,1,0:T(8,128)(2,1)S(1)}, bf16[32,8,128]{2,1,0:T(8,128)(2,1)S(1)}, u32[]{:S(2)}, u32[]{:S(2)}) collective-permute-start(bf16[32,8,128]{2,1,0:T(8,128)(2,1)S(1)} %shard_map.95.state), channel_id=1, source_target_pairs={{0,8},{1,9},{2,10},{3,11},{4,12},{5,13},{6,14},{7,15},{8,0},{9,1},... | collective-permute-start | bytes 196616 | tf_op jit(solution)/shard_map/ppermute | solution.py:277
  65.0 0.4 shard_map.101.near
  65.5 0.5 shard_map.96.near
  65.9 1.6 %collective-permute-done.18.partner = bf16[32,8,128]{2,1,0:T(8,128)(2,1)S(1)} collective-permute-done((bf16[32,8,128]{2,1,0:T(8,128)(2,1)S(1)}, bf16[32,8,128]{2,1,0:T(8,128)(2,1)S(1)}, u32[]{:S(2)}, u32[]{:S(2)}) %collective-permute-start.18) | collective-permute-done | bytes 65568 | tf_op jit(solution)/shard_map/ppermute | solution.py:277
  67.5 1.3 %shard_map.102.rest_0_ = bf16[64,8,128]{2,1,0:T(8,128)(2,1)S(1)} custom-call(bf16[4,32,64,256]{3,2,1,0:T(8,128)(2,1)S(1)} %copy-done.3, s32[4,2,256]{2,1,0:T(2,128)S(1)} %copy-done.9, bf16[64,32,256]{2,1,0:T(8,128)(2,1)S(1)} %copy-done.6, bf16[32,8,128]{2,1,0:T(8,128)(2,1)S(1)} %collective-permute-done.18.partner, f32[32,8,128]{2,1,0:T(8,128)S(1)} %shard_map.101.near), custom_call_target="tpu_custom_call" | custom-call | flops 6291456 | bytes 1572864 | tf_op jit(solution)/shard_map/pallas_call | solution.py:263
  68.9 1.2 %collective-permute-done.15.partner = bf16[32,8,128]{2,1,0:T(8,128)(2,1)S(1)} collective-permute-done((bf16[32,8,128]{2,1,0:T(8,128)(2,1)S(1)}, bf16[32,8,128]{2,1,0:T(8,128)(2,1)S(1)}, u32[]{:S(2)}, u32[]{:S(2)}) %collective-permute-start.15) | collective-permute-done | bytes 65568 | tf_op jit(solution)/shard_map/ppermute | solution.py:277
  70.0 2.1 %shard_map.103 = bf16[64,8,256]{2,1,0:T(8,128)(2,1)} custom-call(bf16[4,32,64,256]{3,2,1,0:T(8,128)(2,1)S(1)} %copy-done.3, s32[4,2,256]{2,1,0:T(2,128)S(1)} %copy-done.9, bf16[64,32,256]{2,1,0:T(8,128)(2,1)S(1)} %copy-done.6, bf16[32,8,128]{2,1,0:T(8,128)(2,1)S(1)} %collective-permute-done.15.partner, f32[32,8,128]{2,1,0:T(8,128)S(1)} %shard_map.96.near, ...), custom_call_target="tpu_custom_call" | custom-call | flops 6291456 | bytes 1572864 | tf_op jit(solution)/shard_map/pallas_call | solution.py:263
  (29 shorter events, 0.6 us)
Async XLA Ops:
  0.0 1.2 %copy-start.4 = (bf16[32,64,256]{2,1,0:T(8,128)(2,1)S(1)}, bf16[32,64,256]{2,1,0:T(8,128)(2,1)}, u32[]{:S(2)}) copy-start(bf16[32,64,256]{2,1,0:T(8,128)(2,1)} %interp.5) | copy-start | bytes 3145732
  1.2 0.9 %copy-start.10 = (bf16[64,8,256]{2,1,0:T(8,128)(2,1)S(1)}, bf16[64,8,256]{2,1,0:T(8,128)(2,1)}, u32[]{:S(2)}) copy-start(bf16[64,8,256]{2,1,0:T(8,128)(2,1)} %samples.3) | copy-start | bytes 786436
  3.0 2.2 %copy-start = (bf16[4,32,64,256]{3,2,1,0:T(8,128)(2,1)S(1)}, bf16[4,32,64,256]{3,2,1,0:T(8,128)(2,1)}, u32[]{:S(2)}) copy-start(bf16[4,32,64,256]{3,2,1,0:T(8,128)(2,1)} %blocks.40) | copy-start | bytes 12582916
  5.2 2.2 %copy-start.2 = (bf16[4,32,64,256]{3,2,1,0:T(8,128)(2,1)S(1)}, bf16[4,32,64,256]{3,2,1,0:T(8,128)(2,1)}, u32[]{:S(2)}) copy-start(bf16[4,32,64,256]{3,2,1,0:T(8,128)(2,1)} %blocks.53) | copy-start | bytes 12582916
  7.4 0.7 copy-start.7
  8.1 0.7 copy-start.9
  8.8 1.4 %copy-start.5 = (bf16[32,64,256]{2,1,0:T(8,128)(2,1)S(1)}, bf16[32,64,256]{2,1,0:T(8,128)(2,1)}, u32[]{:S(2)}) copy-start(bf16[32,64,256]{2,1,0:T(8,128)(2,1)} %interp.5) | copy-start | bytes 3145732
  8.8 1.4 %copy-start.11 = (bf16[64,8,256]{2,1,0:T(8,128)(2,1)S(1)}, bf16[64,8,256]{2,1,0:T(8,128)(2,1)}, u32[]{:S(2)}) copy-start(bf16[64,8,256]{2,1,0:T(8,128)(2,1)} %samples.3) | copy-start | bytes 786436
  8.8 6.3 %copy-start.1 = (bf16[4,32,64,256]{3,2,1,0:T(8,128)(2,1)S(1)}, bf16[4,32,64,256]{3,2,1,0:T(8,128)(2,1)}, u32[]{:S(2)}) copy-start(bf16[4,32,64,256]{3,2,1,0:T(8,128)(2,1)} %blocks.40) | copy-start | bytes 12582916
  8.8 6.3 %copy-start.8 = (s32[4,2,256]{2,1,0:T(2,128)S(1)}, s32[4,2,256]{2,1,0:T(2,128)}, u32[]{:S(2)}) copy-start(s32[4,2,256]{2,1,0:T(2,128)} %pattern.40) | copy-start | bytes 24580
  9.7 22.5 %collective-permute-start = (bf16[2,32,64,128]{3,2,1,0:T(8,128)(2,1)S(1)}, bf16[2,32,64,128]{3,2,1,0:T(8,128)(2,1)S(1)}, u32[]{:S(2)}, u32[]{:S(2)}) collective-permute-start(bf16[2,32,64,128]{3,2,1,0:T(8,128)(2,1)S(1)} %shard_map.74), channel_id=1, source_target_pairs={{0,1},{1,0},{2,3},{3,2},{4,5},{5,4},{6,7},{7,6},{8,9},{9,8},{10,11... | collective-permute-start | bytes 3145736 | tf_op jit(solution)/shard_map/ppermute | solution.py:277
  11.1 8.0 %collective-permute-start.1 = (bf16[32,8,128]{2,1,0:T(8,128)(2,1)S(1)}, bf16[32,8,128]{2,1,0:T(8,128)(2,1)S(1)}, u32[]{:S(2)}, u32[]{:S(2)}) collective-permute-start(bf16[32,8,128]{2,1,0:T(8,128)(2,1)S(1)} %shard_map.75.state), channel_id=1, source_target_pairs={{0,8},{1,9},{2,10},{3,11},{4,12},{5,13},{6,14},{7,15},{8,0},{9,1},... | collective-permute-start | bytes 196616 | tf_op jit(solution)/shard_map/ppermute | solution.py:277
  15.1 7.0 %collective-permute-start.5 = (bf16[32,8,128]{2,1,0:T(8,128)(2,1)S(1)}, bf16[32,8,128]{2,1,0:T(8,128)(2,1)S(1)}, u32[]{:S(2)}, u32[]{:S(2)}) collective-permute-start(bf16[32,8,128]{2,1,0:T(8,128)(2,1)S(1)} %shard_map.73.after.state), channel_id=1, source_target_pairs={{0,8},{1,9},{2,10},{3,11},{4,12},{5,13},{6,14},{7,15},{8,0},{9,1},... | collective-permute-start | bytes 196616 | tf_op jit(solution)/shard_map/ppermute | solution.py:277
  19.5 4.3 %collective-permute-start.2 = (bf16[32,8,128]{2,1,0:T(8,128)(2,1)S(1)}, bf16[32,8,128]{2,1,0:T(8,128)(2,1)S(1)}, u32[]{:S(2)}, u32[]{:S(2)}) collective-permute-start(bf16[32,8,128]{2,1,0:T(8,128)(2,1)S(1)} %shard_map.77.state), channel_id=1, source_target_pairs={{0,4},{1,5},{2,6},{3,7},{4,0},{5,1},{6,2},{7,3},{8,12},{9,13},{10,... | collective-permute-start | bytes 196616 | tf_op jit(solution)/shard_map/ppermute | solution.py:277
  22.6 4.3 %collective-permute-start.6 = (bf16[32,8,128]{2,1,0:T(8,128)(2,1)S(1)}, bf16[32,8,128]{2,1,0:T(8,128)(2,1)S(1)}, u32[]{:S(2)}, u32[]{:S(2)}) collective-permute-start(bf16[32,8,128]{2,1,0:T(8,128)(2,1)S(1)} %shard_map.83.state), channel_id=1, source_target_pairs={{0,4},{1,5},{2,6},{3,7},{4,0},{5,1},{6,2},{7,3},{8,12},{9,13},{10,... | collective-permute-start | bytes 196616 | tf_op jit(solution)/shard_map/ppermute | solution.py:277
  24.3 5.0 %collective-permute-start.3 = (bf16[32,8,128]{2,1,0:T(8,128)(2,1)S(1)}, bf16[32,8,128]{2,1,0:T(8,128)(2,1)S(1)}, u32[]{:S(2)}, u32[]{:S(2)}) collective-permute-start(bf16[32,8,128]{2,1,0:T(8,128)(2,1)S(1)} %shard_map.79.state), channel_id=1, source_target_pairs={{0,2},{1,3},{2,0},{3,1},{4,6},{5,7},{6,4},{7,5},{8,10},{9,11},{10,... | collective-permute-start | bytes 196616 | tf_op jit(solution)/shard_map/ppermute | solution.py:277
  27.3 4.3 %collective-permute-start.7 = (bf16[32,8,128]{2,1,0:T(8,128)(2,1)S(1)}, bf16[32,8,128]{2,1,0:T(8,128)(2,1)S(1)}, u32[]{:S(2)}, u32[]{:S(2)}) collective-permute-start(bf16[32,8,128]{2,1,0:T(8,128)(2,1)S(1)} %shard_map.85.state), channel_id=1, source_target_pairs={{0,2},{1,3},{2,0},{3,1},{4,6},{5,7},{6,4},{7,5},{8,10},{9,11},{10,... | collective-permute-start | bytes 196616 | tf_op jit(solution)/shard_map/ppermute | solution.py:277
  29.9 3.2 %collective-permute-start.4 = (bf16[32,8,128]{2,1,0:T(8,128)(2,1)S(1)}, bf16[32,8,128]{2,1,0:T(8,128)(2,1)S(1)}, u32[]{:S(2)}, u32[]{:S(2)}) collective-permute-start(bf16[32,8,128]{2,1,0:T(8,128)(2,1)S(1)} %shard_map.81), channel_id=1, source_target_pairs={{0,1},{1,0},{2,3},{3,2},{4,5},{5,4},{6,7},{7,6},{8,9},{9,8},{10,11... | collective-permute-start | bytes 196616 | tf_op jit(solution)/shard_map/ppermute | solution.py:277
  32.1 10.1 %copy-start.3 = (bf16[4,32,64,256]{3,2,1,0:T(8,128)(2,1)S(1)}, bf16[4,32,64,256]{3,2,1,0:T(8,128)(2,1)}, u32[]{:S(2)}) copy-start(bf16[4,32,64,256]{3,2,1,0:T(8,128)(2,1)} %blocks.53) | copy-start | bytes 12582916
  34.5 4.3 %collective-permute-start.10 = (bf16[2,2,4,8,128]{4,3,2,1,0:T(8,128)(2,1)S(1)}, bf16[2,2,4,8,128]{4,3,2,1,0:T(8,128)(2,1)S(1)}, u32[]{:S(2)}, u32[]{:S(2)}) collective-permute-start(bf16[2,2,4,8,128]{4,3,2,1,0:T(8,128)(2,1)S(1)} %get-tuple-element.13), channel_id=1, source_target_pairs={{0,4},{1,12},{2,6},{3,14},{4,0},{5,8},{6,2},{7,10},{8,5},{9,13},{1... | collective-permute-start | bytes 98312 | tf_op jit(solution)/shard_map/ppermute | solution.py:277
  36.5 5.0 %collective-permute-start.11 = (bf16[2,2,4,8,128]{4,3,2,1,0:T(8,128)(2,1)S(1)}, bf16[2,2,4,8,128]{4,3,2,1,0:T(8,128)(2,1)S(1)}, u32[]{:S(2)}, u32[]{:S(2)}) collective-permute-start(bf16[2,2,4,8,128]{4,3,2,1,0:T(8,128)(2,1)S(1)} %get-tuple-element.14), channel_id=1, source_target_pairs={{0,6},{1,14},{2,4},{3,12},{4,2},{5,10},{6,0},{7,8},{8,7},{9,15},{1... | collective-permute-start | bytes 98312 | tf_op jit(solution)/shard_map/ppermute | solution.py:277
  37.5 4.0 %collective-permute-start.8 = (bf16[2,2,4,8,128]{4,3,2,1,0:T(8,128)(2,1)S(1)}, bf16[2,2,4,8,128]{4,3,2,1,0:T(8,128)(2,1)S(1)}, u32[]{:S(2)}, u32[]{:S(2)}) collective-permute-start(bf16[2,2,4,8,128]{4,3,2,1,0:T(8,128)(2,1)S(1)} %get-tuple-element.11), channel_id=1, source_target_pairs={{0,0},{1,8},{2,2},{3,10},{4,4},{5,12},{6,6},{7,14},{8,1},{9,9},{10... | collective-permute-start | bytes 98312 | tf_op jit(solution)/shard_map/ppermute | solution.py:277
  38.2 4.0 %collective-permute-start.9 = (bf16[2,2,4,8,128]{4,3,2,1,0:T(8,128)(2,1)S(1)}, bf16[2,2,4,8,128]{4,3,2,1,0:T(8,128)(2,1)S(1)}, u32[]{:S(2)}, u32[]{:S(2)}) collective-permute-start(bf16[2,2,4,8,128]{4,3,2,1,0:T(8,128)(2,1)S(1)} %get-tuple-element.12), channel_id=1, source_target_pairs={{0,2},{1,10},{2,0},{3,8},{4,6},{5,14},{6,4},{7,12},{8,3},{9,11},{1... | collective-permute-start | bytes 98312 | tf_op jit(solution)/shard_map/ppermute | solution.py:277
  44.2 6.7 %collective-permute-start.12 = (bf16[32,8,128]{2,1,0:T(8,128)(2,1)S(1)}, bf16[32,8,128]{2,1,0:T(8,128)(2,1)S(1)}, u32[]{:S(2)}, u32[]{:S(2)}) collective-permute-start(bf16[32,8,128]{2,1,0:T(8,128)(2,1)S(1)} %shard_map.91), channel_id=1, source_target_pairs={{0,1},{1,0},{2,3},{3,2},{4,5},{5,4},{6,7},{7,6},{8,9},{9,8},{10,11... | collective-permute-start | bytes 196616 | tf_op jit(solution)/shard_map/ppermute | solution.py:277
  50.0 4.7 %collective-permute-start.16 = (bf16[32,8,128]{2,1,0:T(8,128)(2,1)S(1)}, bf16[32,8,128]{2,1,0:T(8,128)(2,1)S(1)}, u32[]{:S(2)}, u32[]{:S(2)}) collective-permute-start(bf16[32,8,128]{2,1,0:T(8,128)(2,1)S(1)} %get-tuple-element.16.state), channel_id=1, source_target_pairs={{0,2},{1,3},{2,0},{3,1},{4,6},{5,7},{6,4},{7,5},{8,10},{9,11},{10,... | collective-permute-start | bytes 196616 | tf_op jit(solution)/shard_map/ppermute | solution.py:277
  50.9 7.5 %collective-permute-start.13 = (bf16[32,8,128]{2,1,0:T(8,128)(2,1)S(1)}, bf16[32,8,128]{2,1,0:T(8,128)(2,1)S(1)}, u32[]{:S(2)}, u32[]{:S(2)}) collective-permute-start(bf16[32,8,128]{2,1,0:T(8,128)(2,1)S(1)} %collective-permute-done.12.state), channel_id=1, source_target_pairs={{0,2},{1,3},{2,0},{3,1},{4,6},{5,7},{6,4},{7,5},{8,10},{9,11},{10,... | collective-permute-start | bytes 196616 | tf_op jit(solution)/shard_map/ppermute | solution.py:277
  55.1 5.5 %collective-permute-start.17 = (bf16[32,8,128]{2,1,0:T(8,128)(2,1)S(1)}, bf16[32,8,128]{2,1,0:T(8,128)(2,1)S(1)}, u32[]{:S(2)}, u32[]{:S(2)}) collective-permute-start(bf16[32,8,128]{2,1,0:T(8,128)(2,1)S(1)} %shard_map.98.state), channel_id=1, source_target_pairs={{0,4},{1,5},{2,6},{3,7},{4,0},{5,1},{6,2},{7,3},{8,12},{9,13},{10,... | collective-permute-start | bytes 196616 | tf_op jit(solution)/shard_map/ppermute | solution.py:277
  58.8 4.8 %collective-permute-start.14 = (bf16[32,8,128]{2,1,0:T(8,128)(2,1)S(1)}, bf16[32,8,128]{2,1,0:T(8,128)(2,1)S(1)}, u32[]{:S(2)}, u32[]{:S(2)}) collective-permute-start(bf16[32,8,128]{2,1,0:T(8,128)(2,1)S(1)} %shard_map.93.state), channel_id=1, source_target_pairs={{0,4},{1,5},{2,6},{3,7},{4,0},{5,1},{6,2},{7,3},{8,12},{9,13},{10,... | collective-permute-start | bytes 196616 | tf_op jit(solution)/shard_map/ppermute | solution.py:277
  61.0 6.5 %collective-permute-start.18 = (bf16[32,8,128]{2,1,0:T(8,128)(2,1)S(1)}, bf16[32,8,128]{2,1,0:T(8,128)(2,1)S(1)}, u32[]{:S(2)}, u32[]{:S(2)}) collective-permute-start(bf16[32,8,128]{2,1,0:T(8,128)(2,1)S(1)} %shard_map.100.state), channel_id=1, source_target_pairs={{0,8},{1,9},{2,10},{3,11},{4,12},{5,13},{6,14},{7,15},{8,0},{9,1},... | collective-permute-start | bytes 196616 | tf_op jit(solution)/shard_map/ppermute | solution.py:277
  64.1 3.4 %copy-start.6 = (bf16[64,32,256]{2,1,0:T(8,128)(2,1)S(1)}, bf16[64,32,256]{2,1,0:T(8,128)(2,1)}, u32[]{:S(2)}) copy-start(bf16[64,32,256]{2,1,0:T(8,128)(2,1)} %interp.7) | copy-start | bytes 3145732
  64.1 5.9 %collective-permute-start.15 = (bf16[32,8,128]{2,1,0:T(8,128)(2,1)S(1)}, bf16[32,8,128]{2,1,0:T(8,128)(2,1)S(1)}, u32[]{:S(2)}, u32[]{:S(2)}) collective-permute-start(bf16[32,8,128]{2,1,0:T(8,128)(2,1)S(1)} %shard_map.95.state), channel_id=1, source_target_pairs={{0,8},{1,9},{2,10},{3,11},{4,12},{5,13},{6,14},{7,15},{8,0},{9,1},... | collective-permute-start | bytes 196616 | tf_op jit(solution)/shard_map/ppermute | solution.py:277

commit v3 on v2

--- a/solution.py
+++ b/solution.py
@@ -100,7 +100,7 @@
     def emit(row, value):
         out[row] = (near[row] + value).astype(jnp.bfloat16)
 
-    multiply(wide, state_rows(partner, present_of(pattern, level, other, chunk)), blocks.shape[1], emit)
+    multiply(wide, state_rows(partner.at[other], present_of(pattern, level, other, chunk)), blocks.shape[1], emit)
 
 
 def share_kernel(top_level, top_blocks, top_pattern, bottom_blocks, bottom_pattern, after, out):
@@ -244,7 +244,7 @@
     def emit_state(row, value):
         total[row] = (near[row] + value).astype(jnp.bfloat16).astype(jnp.float32)
 
-    multiply(wide, state_rows(partner, present_of(pattern, level, other, chunk)), rank, emit_state)
+    multiply(wide, state_rows(partner.at[other], present_of(pattern, level, other, chunk)), rank, emit_state)
     spread(wide, lambda row: interp[pl.ds(row, GROUP), :, lanes_of(chunk)], out.shape[0], rank)
 
     def emit(row, value):
@@ -281,6 +281,12 @@
     return permuted(value, lambda source: source ^ 2**bit)
 
 
+def gathered(value, bit):
+    count = lax.axis_size("leaf")
+    pairs = [[place, place + 2**bit] for place in range(count) if place // 2**bit % 2 == 0]
+    return lax.all_gather(value, "leaf", axis_index_groups=pairs)
+
+
 def crossed(source, turn):
     high, mid, low, core = source // 8 % 2, source // 4 % 2, source // 2 % 2, source % 2
     return ((core * 2 + (mid ^ (turn // 2))) * 2 + (low ^ (turn % 2))) * 2 + high
@@ -304,14 +310,15 @@
             functools.partial(coeff_kernel, flip), state, (interp_in, samples),
             (pltpu.VMEM((rank * depth // 2, LANES), jnp.float32), total), 2,
         )
-    after = current[0]
     for level in range(3):
         bit = 3 - level
-        partner = {flip: swapped(current[flip], bit) for flip in (1, 0)}
+        partner = {flip: gathered(current[flip], bit) for flip in (1, 0)}
         near = {
             flip: run(functools.partial(near_kernel, level, bit, flip), partial, (top_blocks, top_pattern, current[flip]), (wide,))
             for flip in (1, 0)
         }
+        if level == 0:
+            after = near[0]
         for flip in (1, 0):
             current[flip] = run(
                 functools.partial(far_kernel, level, bit, flip), state,
@@ -342,7 +349,7 @@
     current = {0: first, 1: swapped(second, 0)}
 
     for level in (1, 2, 3):
-        partner = {flip: swapped(current[flip], level) for flip in (0, 1)}
+        partner = {flip: gathered(current[flip], level) for flip in (0, 1)}
         near = {
             flip: run(functools.partial(near_kernel, level, level, flip), partial, (bottom_blocks, bottom_pattern, current[flip]), (wide,))
             for flip in (0, 1)

time: 72.4 us -> 112 us (1.55)
  blocking collectives: 0 us -> 67.4 us
  starting transfers between devices: 26.6 us -> 11.2 us
  waiting for transfers between devices: 17.1 us -> 3.06 us
    all_gather x0 -> x12, blocking collectives: none -> 67.4 us  [gathered(): return lax.all_gather(value, 'leaf', axis_index_groups=pairs)]
    ppermute x19 -> x7, starting transfers between devices: 26.6 us -> 11.2 us  [permuted(): return lax.ppermute(value, 'leaf', pairs)]
    ppermute x19 -> x7, waiting for transfers between devices: 17.1 us -> 3.06 us  [permuted(): return lax.ppermute(value, 'leaf', pairs)]
  transfers between devices with their start and end apart: 19 -> 7, of which waited for: 12 -> 3; matrix products, arithmetic and copies ran while one was open for 0% -> 0% of each run, Pallas kernels for 18% -> 8%
where the time goes in v3:
time: 112 us; the launch traced here: 111 us
  blocking collectives  67.4 us (60%)
  Pallas kernels  20.4 us (18%)
  starting transfers between devices  11.2 us (10%)
  local copies, waits for them, and re-layouts  8.99 us (8%)
  waiting for transfers between devices  3.06 us (3%)
    all_gather x12, blocking collectives, gathered(): return lax.all_gather(value, 'leaf', axis_index_groups=pairs)  67.4 us
    pallas_call x31, Pallas kernels, run(): pl.pallas_call(kernel, out_shape=shapes, in_specs=[whole] * len(operands)...  20.4 us
    ppermute x7, starting transfers between devices, permuted(): return lax.ppermute(value, 'leaf', pairs)  11.2 us
    unnamed x24, local copies, waits for them, and re-layouts  8.99 us
    ppermute x7, waiting for transfers between devices, permuted(): return lax.ppermute(value, 'leaf', pairs)  3.06 us
  transfers between devices with their start and end apart: 7, of which 3 were waited for; matrix products, arithmetic and copies ran while one was open for 0% of the time, Pallas kernels for 8%

profile of v3, /device:TPU:0, one launch (start us, length us, event | category | flops | bytes accessed | tf_op | source)
XLA Modules:
  0.0 111.2 jit_solution(14369248881564373936)
XLA Ops:
  0.0 1.2 %copy-done.4 = bf16[32,64,256]{2,1,0:T(8,128)(2,1)S(1)} copy-done((bf16[32,64,256]{2,1,0:T(8,128)(2,1)S(1)}, bf16[32,64,256]{2,1,0:T(8,128)(2,1)}, u32[]{:S(2)}) %copy-start.4) | copy-done | bytes 1048600
  1.2 0.9 copy-done.10
  2.2 0.9 shard_map.73.state
  3.0 0.0 copy-start
  3.1 2.2 %copy-done = bf16[4,32,64,256]{3,2,1,0:T(8,128)(2,1)S(1)} copy-done((bf16[4,32,64,256]{3,2,1,0:T(8,128)(2,1)S(1)}, bf16[4,32,64,256]{3,2,1,0:T(8,128)(2,1)}, u32[]{:S(2)}) %copy-start) | copy-done | bytes 4194328
  5.2 0.7 copy-done.7
  5.9 0.4 shard_map.74.after.near
  6.4 1.7 %copy-done.1 = bf16[4,32,64,256]{3,2,1,0:T(8,128)(2,1)S(1)} copy-done((bf16[4,32,64,256]{3,2,1,0:T(8,128)(2,1)S(1)}, bf16[4,32,64,256]{3,2,1,0:T(8,128)(2,1)}, u32[]{:S(2)}) %copy-start.1) | copy-done | bytes 4194328
  8.1 2.2 %copy-done.2 = bf16[4,32,64,256]{3,2,1,0:T(8,128)(2,1)S(1)} copy-done((bf16[4,32,64,256]{3,2,1,0:T(8,128)(2,1)S(1)}, bf16[4,32,64,256]{3,2,1,0:T(8,128)(2,1)}, u32[]{:S(2)}) %copy-start.2) | copy-done | bytes 4194328
  10.3 0.8 shard_map.75
  11.2 0.5 collective-permute-start
  11.7 0.9 shard_map.76.state
  12.6 0.5 shard_map.77.near
  13.0 8.4 %all-gather = bf16[64,8,128]{2,1,0:T(8,128)(2,1)S(1)} all-gather(bf16[32,8,128]{2,1,0:T(8,128)(2,1)S(1)} %shard_map.76.state), channel_id=2, replica_groups={{0,8},{1,9},{2,10},{3,11},{4,12},{5,13},{6,14},{7,15},{16,24},{17,25},{..., dimensions={0}, use_global_device_ids=true | all-gather | bytes 196608 | tf_op jit(solution)/shard_map/all_gather | solution.py:287
  21.4 0.5 shard_map.78.state
  21.9 0.5 shard_map.79.near
  22.4 4.9 %all-gather.1 = bf16[64,8,128]{2,1,0:T(8,128)(2,1)S(1)} all-gather(bf16[32,8,128]{2,1,0:T(8,128)(2,1)S(1)} %shard_map.78.state), channel_id=3, replica_groups={{0,4},{1,5},{2,6},{3,7},{8,12},{9,13},{10,14},{11,15},{16,20},{17,21},{..., dimensions={0}, use_global_device_ids=true | all-gather | bytes 196608 | tf_op jit(solution)/shard_map/all_gather | solution.py:287
  27.3 0.5 shard_map.80.state
  27.8 0.5 shard_map.81.near
  28.2 4.9 %all-gather.2 = bf16[64,8,128]{2,1,0:T(8,128)(2,1)S(1)} all-gather(bf16[32,8,128]{2,1,0:T(8,128)(2,1)S(1)} %shard_map.80.state), channel_id=4, replica_groups={{0,2},{1,3},{4,6},{5,7},{8,10},{9,11},{12,14},{13,15},{16,18},{17,19},{..., dimensions={0}, use_global_device_ids=true | all-gather | bytes 196608 | tf_op jit(solution)/shard_map/all_gather | solution.py:287
  33.2 0.5 shard_map.82
  33.6 0.1 collective-permute-start.1
  33.7 7.5 %all-gather.3 = bf16[64,8,128]{2,1,0:T(8,128)(2,1)S(1)} all-gather(bf16[32,8,128]{2,1,0:T(8,128)(2,1)S(1)} %shard_map.73.state), channel_id=5, replica_groups={{0,8},{1,9},{2,10},{3,11},{4,12},{5,13},{6,14},{7,15},{16,24},{17,25},{..., dimensions={0}, use_global_device_ids=true | all-gather | bytes 196608 | tf_op jit(solution)/shard_map/all_gather | solution.py:287
  41.2 0.5 shard_map.83.state
  41.6 0.5 shard_map.84.near
  42.1 4.9 %all-gather.4 = bf16[64,8,128]{2,1,0:T(8,128)(2,1)S(1)} all-gather(bf16[32,8,128]{2,1,0:T(8,128)(2,1)S(1)} %shard_map.83.state), channel_id=6, replica_groups={{0,4},{1,5},{2,6},{3,7},{8,12},{9,13},{10,14},{11,15},{16,20},{17,21},{..., dimensions={0}, use_global_device_ids=true | all-gather | bytes 196608 | tf_op jit(solution)/shard_map/all_gather | solution.py:287
  47.0 0.5 shard_map.85.state
  47.5 0.5 shard_map.86.near
  48.0 4.9 %all-gather.5 = bf16[64,8,128]{2,1,0:T(8,128)(2,1)S(1)} all-gather(bf16[32,8,128]{2,1,0:T(8,128)(2,1)S(1)} %shard_map.85.state), channel_id=7, replica_groups={{0,2},{1,3},{4,6},{5,7},{8,10},{9,11},{12,14},{13,15},{16,18},{17,19},{..., dimensions={0}, use_global_device_ids=true | all-gather | bytes 196608 | tf_op jit(solution)/shard_map/all_gather | solution.py:287
  52.9 0.5 shard_map.87.state
  53.4 0.0 copy-start.3
  53.4 0.0 collective-permute-done.shared
  53.4 0.9 shard_map.88.near
  54.3 0.0 collective-permute-done.1.partner
  54.3 1.4 %shard_map.89 = (bf16[2,2,4,8,128]{4,3,2,1,0:T(8,128)(2,1)S(1)}, bf16[2,2,4,8,128]{4,3,2,1,0:T(8,128)(2,1)S(1)}, bf16[2,2,4,8,128]{4,3,2,1,0:T(8,128)(2,1)S(1)}, bf16[2,2,4,8,128]{4,3,2,1,0:T(8,128)(2,1)S(1)}) custom-call(bf16[4,32,64,256]{3,2,1,0:T(8,128)(2,1)S(1)} %copy-done.1, s32[4,2,256]{2,1,0:T(2,128)S(1)} %copy-done.8, ...), custom_call_target="tpu_custom_call" | custom-call | flops 4194304 | bytes 1048576 | tf_op jit(solution)/shard_map/pallas_call | solution.py:263
  55.7 0.7 collective-permute-start.2
  56.4 1.8 %collective-permute-start.3 = (bf16[2,2,4,8,128]{4,3,2,1,0:T(8,128)(2,1)S(1)}, bf16[2,2,4,8,128]{4,3,2,1,0:T(8,128)(2,1)S(1)}, u32[]{:S(2)}, u32[]{:S(2)}) collective-permute-start(bf16[2,2,4,8,128]{4,3,2,1,0:T(8,128)(2,1)S(1)} %get-tuple-element.12), channel_id=1, source_target_pairs={{0,2},{1,10},{2,0},{3,8},{4,6},{5,14},{6,4},{7,12},{8,3},{9,11},{1... | collective-permute-start | bytes 98312 | tf_op jit(solution)/shard_map/ppermute | solution.py:277
  58.2 0.0 collective-permute-start.4
  58.2 1.8 %collective-permute-start.5 = (bf16[2,2,4,8,128]{4,3,2,1,0:T(8,128)(2,1)S(1)}, bf16[2,2,4,8,128]{4,3,2,1,0:T(8,128)(2,1)S(1)}, u32[]{:S(2)}, u32[]{:S(2)}) collective-permute-start(bf16[2,2,4,8,128]{4,3,2,1,0:T(8,128)(2,1)S(1)} %get-tuple-element.14), channel_id=1, source_target_pairs={{0,6},{1,14},{2,4},{3,12},{4,2},{5,10},{6,0},{7,8},{8,7},{9,15},{1... | collective-permute-start | bytes 98312 | tf_op jit(solution)/shard_map/ppermute | solution.py:277
  60.0 0.4 collective-permute-done.3.rest_1_
  60.4 1.7 %collective-permute-done.4.rest_2_ = bf16[2,2,4,8,128]{4,3,2,1,0:T(8,128)(2,1)S(1)} collective-permute-done((bf16[2,2,4,8,128]{4,3,2,1,0:T(8,128)(2,1)S(1)}, bf16[2,2,4,8,128]{4,3,2,1,0:T(8,128)(2,1)S(1)}, u32[]{:S(2)}, u32[]{:S(2)}) %collective-permute-start.4) | collective-permute-done | bytes 32800 | tf_op jit(solution)/shard_map/ppermute | solution.py:277
  62.1 0.9 collective-permute-done.5.rest_3_
  63.0 1.2 %shard_map.90 = (bf16[32,8,128]{2,1,0:T(8,128)(2,1)S(1)}, bf16[2,32,8,128]{3,2,1,0:T(8,128)(2,1)S(1)}) custom-call(bf16[4,32,64,256]{3,2,1,0:T(8,128)(2,1)S(1)} %copy-done.3, s32[4,2,256]{2,1,0:T(2,128)S(1)} %copy-done.9, bf16[2,2,4,8,128]{4,3,2,1,0:T(8,128)(2,1)S(1)} %collective-permute-done.2.rest_0_, ...), custom_call_target="tpu_custom_call" | custom-call | flops 4194304 | bytes 1048576 | tf_op jit(solution)/shard_map/pallas_call | solution.py:263
  64.2 4.9 %all-gather.9 = bf16[64,8,128]{2,1,0:T(8,128)(2,1)S(1)} all-gather(bf16[32,8,128]{2,1,0:T(8,128)(2,1)S(1)} %get-tuple-element.16.state), channel_id=11, replica_groups={{0,2},{1,3},{4,6},{5,7},{8,10},{9,11},{12,14},{13,15},{16,18},{17,19},{..., dimensions={0}, use_global_device_ids=true | all-gather | bytes 196608 | tf_op jit(solution)/shard_map/all_gather | solution.py:287
  69.1 0.4 shard_map.97.near
  69.6 0.5 shard_map.98.state
  70.0 0.5 shard_map.99.near
  70.5 0.9 shard_map.91
  71.4 6.4 %collective-permute-start.6 = (bf16[32,8,128]{2,1,0:T(8,128)(2,1)S(1)}, bf16[32,8,128]{2,1,0:T(8,128)(2,1)S(1)}, u32[]{:S(2)}, u32[]{:S(2)}) collective-permute-start(bf16[32,8,128]{2,1,0:T(8,128)(2,1)S(1)} %shard_map.91), channel_id=1, source_target_pairs={{0,1},{1,0},{2,3},{3,2},{4,5},{5,4},{6,7},{7,6},{8,9},{9,8},{10,11... | collective-permute-start | bytes 196616 | tf_op jit(solution)/shard_map/ppermute | solution.py:277
  77.7 4.9 %all-gather.10 = bf16[64,8,128]{2,1,0:T(8,128)(2,1)S(1)} all-gather(bf16[32,8,128]{2,1,0:T(8,128)(2,1)S(1)} %shard_map.98.state), channel_id=12, replica_groups={{0,4},{1,5},{2,6},{3,7},{8,12},{9,13},{10,14},{11,15},{16,20},{17,21},{..., dimensions={0}, use_global_device_ids=true | all-gather | bytes 196608 | tf_op jit(solution)/shard_map/all_gather | solution.py:287
  82.7 0.5 shard_map.100.state
  83.1 0.5 shard_map.101.near
  83.6 6.0 %all-gather.11 = bf16[64,8,128]{2,1,0:T(8,128)(2,1)S(1)} all-gather(bf16[32,8,128]{2,1,0:T(8,128)(2,1)S(1)} %shard_map.100.state), channel_id=13, replica_groups={{0,8},{1,9},{2,10},{3,11},{4,12},{5,13},{6,14},{7,15},{16,24},{17,25},{..., dimensions={0}, use_global_device_ids=true | all-gather | bytes 196608 | tf_op jit(solution)/shard_map/all_gather | solution.py:287
  89.6 1.3 %shard_map.102.rest_0_ = bf16[64,8,128]{2,1,0:T(8,128)(2,1)S(1)} custom-call(bf16[4,32,64,256]{3,2,1,0:T(8,128)(2,1)S(1)} %copy-done.3, s32[4,2,256]{2,1,0:T(2,128)S(1)} %copy-done.9, bf16[64,32,256]{2,1,0:T(8,128)(2,1)S(1)} %copy-done.6, bf16[2,32,8,128]{3,2,1,0:T(8,128)(2,1)S(1)} %bitcast.21, f32[32,8,128]{2,1,0:T(8,128)S(1)} %shard_map.101.near), custom_call_target="tpu_custom_call" | custom-call | flops 6291456 | bytes 1572864 | tf_op jit(solution)/shard_map/pallas_call | solution.py:263
  90.9 0.0 collective-permute-done.6.state
  90.9 4.9 %all-gather.6 = bf16[64,8,128]{2,1,0:T(8,128)(2,1)S(1)} all-gather(bf16[32,8,128]{2,1,0:T(8,128)(2,1)S(1)} %collective-permute-done.6.state), channel_id=8, replica_groups={{0,2},{1,3},{4,6},{5,7},{8,10},{9,11},{12,14},{13,15},{16,18},{17,19},{..., dimensions={0}, use_global_device_ids=true | all-gather | bytes 196608 | tf_op jit(solution)/shard_map/all_gather | solution.py:287
  95.9 0.4 shard_map.92.near
  96.3 0.5 shard_map.93.state
  96.8 4.9 %all-gather.7 = bf16[64,8,128]{2,1,0:T(8,128)(2,1)S(1)} all-gather(bf16[32,8,128]{2,1,0:T(8,128)(2,1)S(1)} %shard_map.93.state), channel_id=9, replica_groups={{0,4},{1,5},{2,6},{3,7},{8,12},{9,13},{10,14},{11,15},{16,20},{17,21},{..., dimensions={0}, use_global_device_ids=true | all-gather | bytes 196608 | tf_op jit(solution)/shard_map/all_gather | solution.py:287
  101.8 0.4 shard_map.94.near
  102.2 0.5 shard_map.95.state
  102.7 6.0 %all-gather.8 = bf16[64,8,128]{2,1,0:T(8,128)(2,1)S(1)} all-gather(bf16[32,8,128]{2,1,0:T(8,128)(2,1)S(1)} %shard_map.95.state), channel_id=10, replica_groups={{0,8},{1,9},{2,10},{3,11},{4,12},{5,13},{6,14},{7,15},{16,24},{17,25},{..., dimensions={0}, use_global_device_ids=true | all-gather | bytes 196608 | tf_op jit(solution)/shard_map/all_gather | solution.py:287
  108.6 0.4 shard_map.96.near
  109.1 2.1 %shard_map.103 = bf16[64,8,256]{2,1,0:T(8,128)(2,1)} custom-call(bf16[4,32,64,256]{3,2,1,0:T(8,128)(2,1)S(1)} %copy-done.3, s32[4,2,256]{2,1,0:T(2,128)S(1)} %copy-done.9, bf16[64,32,256]{2,1,0:T(8,128)(2,1)S(1)} %copy-done.6, bf16[2,32,8,128]{3,2,1,0:T(8,128)(2,1)S(1)} %bitcast.12, f32[32,8,128]{2,1,0:T(8,128)S(1)} %shard_map.96.near, ...), custom_call_target="tpu_custom_call" | custom-call | flops 6291456 | bytes 1572864 | tf_op jit(solution)/shard_map/pallas_call | solution.py:263
  (17 shorter events, 0.0 us)
Async XLA Ops:
  0.0 1.2 %copy-start.4 = (bf16[32,64,256]{2,1,0:T(8,128)(2,1)S(1)}, bf16[32,64,256]{2,1,0:T(8,128)(2,1)}, u32[]{:S(2)}) copy-start(bf16[32,64,256]{2,1,0:T(8,128)(2,1)} %interp.5) | copy-start | bytes 3145732
  1.2 0.9 copy-start.10
  2.2 4.2 %copy-start.8 = (s32[4,2,256]{2,1,0:T(2,128)S(1)}, s32[4,2,256]{2,1,0:T(2,128)}, u32[]{:S(2)}) copy-start(s32[4,2,256]{2,1,0:T(2,128)} %pattern.40) | copy-start | bytes 24580
  2.2 4.2 %copy-start.9 = (s32[4,2,256]{2,1,0:T(2,128)S(1)}, s32[4,2,256]{2,1,0:T(2,128)}, u32[]{:S(2)}) copy-start(s32[4,2,256]{2,1,0:T(2,128)} %pattern.53) | copy-start | bytes 24580
  3.0 2.2 %copy-start = (bf16[4,32,64,256]{3,2,1,0:T(8,128)(2,1)S(1)}, bf16[4,32,64,256]{3,2,1,0:T(8,128)(2,1)}, u32[]{:S(2)}) copy-start(bf16[4,32,64,256]{3,2,1,0:T(8,128)(2,1)} %blocks.40) | copy-start | bytes 12582916
  5.2 0.7 copy-start.7
  5.9 2.2 %copy-start.1 = (bf16[4,32,64,256]{3,2,1,0:T(8,128)(2,1)S(1)}, bf16[4,32,64,256]{3,2,1,0:T(8,128)(2,1)}, u32[]{:S(2)}) copy-start(bf16[4,32,64,256]{3,2,1,0:T(8,128)(2,1)} %blocks.40) | copy-start | bytes 12582916
  8.1 2.2 %copy-start.2 = (bf16[4,32,64,256]{3,2,1,0:T(8,128)(2,1)S(1)}, bf16[4,32,64,256]{3,2,1,0:T(8,128)(2,1)}, u32[]{:S(2)}) copy-start(bf16[4,32,64,256]{3,2,1,0:T(8,128)(2,1)} %blocks.53) | copy-start | bytes 12582916
  10.3 1.4 %copy-start.5 = (bf16[32,64,256]{2,1,0:T(8,128)(2,1)S(1)}, bf16[32,64,256]{2,1,0:T(8,128)(2,1)}, u32[]{:S(2)}) copy-start(bf16[32,64,256]{2,1,0:T(8,128)(2,1)} %interp.5) | copy-start | bytes 3145732
  10.3 1.4 %copy-start.11 = (bf16[64,8,256]{2,1,0:T(8,128)(2,1)S(1)}, bf16[64,8,256]{2,1,0:T(8,128)(2,1)}, u32[]{:S(2)}) copy-start(bf16[64,8,256]{2,1,0:T(8,128)(2,1)} %samples.3) | copy-start | bytes 786436
  11.2 42.2 %collective-permute-start = (bf16[2,32,64,128]{3,2,1,0:T(8,128)(2,1)S(1)}, bf16[2,32,64,128]{3,2,1,0:T(8,128)(2,1)S(1)}, u32[]{:S(2)}, u32[]{:S(2)}) collective-permute-start(bf16[2,32,64,128]{3,2,1,0:T(8,128)(2,1)S(1)} %shard_map.75), channel_id=1, source_target_pairs={{0,1},{1,0},{2,3},{3,2},{4,5},{5,4},{6,7},{7,6},{8,9},{9,8},{10,11... | collective-permute-start | bytes 3145736 | tf_op jit(solution)/shard_map/ppermute | solution.py:277
  33.6 20.7 %collective-permute-start.1 = (bf16[32,8,128]{2,1,0:T(8,128)(2,1)S(1)}, bf16[32,8,128]{2,1,0:T(8,128)(2,1)S(1)}, u32[]{:S(2)}, u32[]{:S(2)}) collective-permute-start(bf16[32,8,128]{2,1,0:T(8,128)(2,1)S(1)} %shard_map.82), channel_id=1, source_target_pairs={{0,1},{1,0},{2,3},{3,2},{4,5},{5,4},{6,7},{7,6},{8,9},{9,8},{10,11... | collective-permute-start | bytes 196616 | tf_op jit(solution)/shard_map/ppermute | solution.py:277
  53.4 9.7 %copy-start.3 = (bf16[4,32,64,256]{3,2,1,0:T(8,128)(2,1)S(1)}, bf16[4,32,64,256]{3,2,1,0:T(8,128)(2,1)}, u32[]{:S(2)}) copy-start(bf16[4,32,64,256]{3,2,1,0:T(8,128)(2,1)} %blocks.53) | copy-start | bytes 12582916
  55.7 4.2 %collective-permute-start.2 = (bf16[2,2,4,8,128]{4,3,2,1,0:T(8,128)(2,1)S(1)}, bf16[2,2,4,8,128]{4,3,2,1,0:T(8,128)(2,1)S(1)}, u32[]{:S(2)}, u32[]{:S(2)}) collective-permute-start(bf16[2,2,4,8,128]{4,3,2,1,0:T(8,128)(2,1)S(1)} %get-tuple-element.11), channel_id=1, source_target_pairs={{0,0},{1,8},{2,2},{3,10},{4,4},{5,12},{6,6},{7,14},{8,1},{9,9},{10... | collective-permute-start | bytes 98312 | tf_op jit(solution)/shard_map/ppermute | solution.py:277
  56.4 4.0 %collective-permute-start.3 = (bf16[2,2,4,8,128]{4,3,2,1,0:T(8,128)(2,1)S(1)}, bf16[2,2,4,8,128]{4,3,2,1,0:T(8,128)(2,1)S(1)}, u32[]{:S(2)}, u32[]{:S(2)}) collective-permute-start(bf16[2,2,4,8,128]{4,3,2,1,0:T(8,128)(2,1)S(1)} %get-tuple-element.12), channel_id=1, source_target_pairs={{0,2},{1,10},{2,0},{3,8},{4,6},{5,14},{6,4},{7,12},{8,3},{9,11},{1... | collective-permute-start | bytes 98312 | tf_op jit(solution)/shard_map/ppermute | solution.py:277
  58.2 3.9 %collective-permute-start.4 = (bf16[2,2,4,8,128]{4,3,2,1,0:T(8,128)(2,1)S(1)}, bf16[2,2,4,8,128]{4,3,2,1,0:T(8,128)(2,1)S(1)}, u32[]{:S(2)}, u32[]{:S(2)}) collective-permute-start(bf16[2,2,4,8,128]{4,3,2,1,0:T(8,128)(2,1)S(1)} %get-tuple-element.13), channel_id=1, source_target_pairs={{0,4},{1,12},{2,6},{3,14},{4,0},{5,8},{6,2},{7,10},{8,5},{9,13},{1... | collective-permute-start | bytes 98312 | tf_op jit(solution)/shard_map/ppermute | solution.py:277
  58.2 4.8 %collective-permute-start.5 = (bf16[2,2,4,8,128]{4,3,2,1,0:T(8,128)(2,1)S(1)}, bf16[2,2,4,8,128]{4,3,2,1,0:T(8,128)(2,1)S(1)}, u32[]{:S(2)}, u32[]{:S(2)}) collective-permute-start(bf16[2,2,4,8,128]{4,3,2,1,0:T(8,128)(2,1)S(1)} %get-tuple-element.14), channel_id=1, source_target_pairs={{0,6},{1,14},{2,4},{3,12},{4,2},{5,10},{6,0},{7,8},{8,7},{9,15},{1... | collective-permute-start | bytes 98312 | tf_op jit(solution)/shard_map/ppermute | solution.py:277
  71.4 19.6 %collective-permute-start.6 = (bf16[32,8,128]{2,1,0:T(8,128)(2,1)S(1)}, bf16[32,8,128]{2,1,0:T(8,128)(2,1)S(1)}, u32[]{:S(2)}, u32[]{:S(2)}) collective-permute-start(bf16[32,8,128]{2,1,0:T(8,128)(2,1)S(1)} %shard_map.91), channel_id=1, source_target_pairs={{0,1},{1,0},{2,3},{3,2},{4,5},{5,4},{6,7},{7,6},{8,9},{9,8},{10,11... | collective-permute-start | bytes 196616 | tf_op jit(solution)/shard_map/ppermute | solution.py:277
  82.7 6.9 %copy-start.6 = (bf16[64,32,256]{2,1,0:T(8,128)(2,1)S(1)}, bf16[64,32,256]{2,1,0:T(8,128)(2,1)}, u32[]{:S(2)}) copy-start(bf16[64,32,256]{2,1,0:T(8,128)(2,1)} %interp.7) | copy-start | bytes 3145732

commit v4 on v2

v4 whole, which is shorter than its diff:
```python
import functools

import jax
import jax.numpy as jnp
from jax import lax
from jax.experimental import pallas as pl
from jax.experimental.pallas import tpu as pltpu
from jax.sharding import PartitionSpec as P

LANES = 128
GROUP = 4
START_LIMIT = 62_700_000


def digits():
    place = lax.axis_index("leaf")
    return lax.rem(place // 8, 2), lax.rem(place // 4, 2), lax.rem(place // 2, 2), lax.rem(place, 2)


def lanes_of(chunk):
    return pl.ds(pl.multiple_of(chunk * LANES, LANES), LANES)


def rows_of(half, rank):
    return pl.ds(pl.multiple_of(half * rank, rank), rank)


def spread(wide, load, row_count, rank):
    def body(step, carry):
        rows = load(step * GROUP).astype(jnp.float32)
        wide[pl.ds(step * GROUP * rank, GROUP * rank), :] = rows.reshape(GROUP * rank, LANES)
        return carry

    lax.fori_loop(0, row_count // GROUP, body, 0)


def multiply(wide, state, row_count, emit):
    rank = len(state)

    def body(step, carry):
        for inner in range(GROUP):
            sums = [None, None]
            for index in range(rank):
                weight = wide[pl.ds(step * GROUP * rank + inner * rank + index, 8, stride=0), :]
                term = weight * state[index]
                old = sums[index % 2]
                sums[index % 2] = term if old is None else old + term
            emit(step * GROUP + inner, sums[0] + sums[1])
        return carry

    lax.fori_loop(0, row_count // GROUP, body, 0)


def state_rows(ref, present=None):
    rows = [ref[index].astype(jnp.float32) for index in range(ref.shape[0])]
    return rows if present is None else [row * present for row in rows]


def level_load(blocks, level, half, chunk):
    rank = blocks.shape[1]
    return lambda row: blocks[level, pl.ds(row, GROUP), rows_of(half, rank), lanes_of(chunk)]


def present_of(pattern, level, half, chunk):
    pair = [pattern[level, place:place + 1, lanes_of(chunk)].astype(jnp.float32) for place in range(2)]
    return jnp.where(half == 0, pair[0], pair[1])


def coeff_kernel(interp, samples, first, second, held_interp, held_samples, wide, total, sems):
    rank, depth = first.shape[0], held_samples.shape[1]
    core = digits()[3]
    pairs = []
    for turn, chunk in enumerate((1 - core, core)):
        for half in range(2):
            place, part = turn * 2 + half, pl.ds(half * depth, depth)
            pairs.append((
                pltpu.make_async_copy(samples.at[part, :, lanes_of(chunk)], held_samples.at[place], sems.at[2 * place]),
                pltpu.make_async_copy(interp.at[:, part, lanes_of(chunk)], held_interp.at[place], sems.at[2 * place + 1]),
            ))
    for pair in pairs:
        for copy in pair:
            copy.start()
    for place, pair in enumerate(pairs):
        for copy in pair:
            copy.wait()
        spread(wide, lambda row: held_interp[place, pl.ds(row, GROUP)], rank, depth)
        state = [held_samples[place, index].astype(jnp.float32) for index in range(depth)]
        out = (first, second)[place // 2]

        def emit(row, value):
            if place % 2 == 0:
                total[row] = value
            else:
                out[row] = (total[row] + value).astype(jnp.bfloat16)

        multiply(wide, state, rank, emit)


def near_kernel(level, bit, flip, blocks, pattern, state, *rest):
    out, far_wide, wide = rest[-3:]
    places = digits()
    chunk, own = places[3] ^ flip, places[3 - bit]
    spread(wide, level_load(blocks, level, own, chunk), blocks.shape[1], blocks.shape[1])
    spread(far_wide, level_load(blocks, level, 1 - own, chunk), blocks.shape[1], blocks.shape[1])

    def emit(row, value):
        out[row] = value

    multiply(wide, state_rows(state, present_of(pattern, level, own, chunk)), blocks.shape[1], emit)


def far_kernel(level, bit, flip, pattern, partner, near, wide, out):
    places = digits()
    chunk, other = places[3] ^ flip, 1 - places[3 - bit]

    def emit(row, value):
        out[row] = (near[row] + value).astype(jnp.bfloat16)

    multiply(wide, state_rows(partner, present_of(pattern, level, other, chunk)), out.shape[0], emit)


def share_kernel(top_level, top_blocks, top_pattern, bottom_blocks, bottom_pattern, out):
    rank = top_blocks.shape[1]
    chunk = 1 - digits()[3]
    for place, (blocks, pattern, level) in enumerate(((top_blocks, top_pattern, top_level), (bottom_blocks, bottom_pattern, 0))):
        for half in range(2):
            present = present_of(pattern, level, half, chunk)[None]

            def body(row, carry):
                rows = blocks[level, pl.ds(row, 1), half * rank:(half + 1) * rank, lanes_of(chunk)]
                out[place * rank + row, half * rank:(half + 1) * rank, :] = (rows.astype(jnp.float32) * present)[0].astype(jnp.bfloat16)
                return carry

            lax.fori_loop(0, rank, body, 0)


def shared_load(shared, place, half):
    rank = shared.shape[1] // 2
    return lambda row: shared[pl.ds(place * rank + row, GROUP), rows_of(half, rank), :]


def send_kernel(level, bit, flip, pattern, partner, near, wide, shared, out):
    rank, per = partner.shape[0], shared.shape[1] // partner.shape[1]
    places = digits()
    chunk, other = places[3] ^ flip, 1 - places[3 - bit]

    def emit(row, value):
        place = pl.ds(pl.multiple_of(lax.rem(row, per) * 8, 8), 8)
        out[2 * rank + row // per, place, :] = (near[row] + value).astype(jnp.bfloat16)

    multiply(wide, state_rows(partner, present_of(pattern, level, other, chunk)), rank, emit)


def sent_rows(shared):
    rank = shared.shape[1] // 2
    per = shared.shape[1] // 8
    return [
        shared[2 * rank + row // per, row % per * 8:(row % per + 1) * 8, :].astype(jnp.float32) for row in range(rank)
    ]


def swap_groups(tile, slot):
    lane_group = lax.broadcasted_iota(jnp.int32, tile[0].shape, 2) // slot
    step = 1
    while step < len(tile):
        low = (lane_group // step) % 2 == 0
        fresh = list(tile)
        for place in range(len(tile)):
            if place & step == 0:
                first, second = tile[place], tile[place + step]
                fresh[place] = jnp.where(low, first, pltpu.roll(second, step * slot, 2))
                fresh[place + step] = jnp.where(low, pltpu.roll(first, LANES - step * slot, 2), second)
        tile = fresh
        step *= 2
    return tile


def pair_near_kernel(level, blocks, pattern, shared, state, out, far_wide, wide):
    rank = blocks.shape[1]
    core = digits()[3]
    rows = state_rows(state)
    present = present_of(pattern, level, core, core)
    for box in range(2):
        for target, half in ((wide, core), (far_wide.at[box], 1 - core)):
            load = (
                level_load(blocks, level, half, core)
                if box == 0
                else shared_load(shared, 0, half)
            )
            spread(target, load, rank, rank)

        def emit(row, value):
            out[box, row] = value

        multiply(wide, [row * present for row in rows] if box == 0 else rows, rank, emit)


def pair_far_kernel(level, slot, pattern, wide, shared, near, *rest):
    outs, (total, packed) = rest[:4], rest[4:]
    rank = near.shape[1]
    _, mid, low, core = digits()
    rows = sent_rows(shared)
    present = present_of(pattern, level, 1 - core, core)
    fold = LANES // slot
    for box in range(2):
        def emit(row, value):
            total[row] = near[box, row] + value

        multiply(wide.at[box], [row * present for row in rows] if box == 0 else rows, rank, emit)
        depth = rank // fold
        pieces = swap_groups([total[place * depth:(place + 1) * depth] for place in range(fold)], slot)
        for place, piece in enumerate(pieces):
            packed[core ^ box, place] = piece.astype(jnp.bfloat16)
    for turn, out in enumerate(outs):
        first = ((mid ^ (turn // 2)) * 2 + (low ^ (turn % 2))) * 2
        for box in range(2):
            for last in range(2):
                out[box, last] = packed[box, first + last]


def wide_kernel(blocks, shared, own_wide, other_wide):
    rank = blocks.shape[1]
    core = digits()[3]
    for half in range(2):
        spread(own_wide.at[half], level_load(blocks, 0, half, core), rank, rank)
        spread(other_wide.at[half], shared_load(shared, 1, half), rank, rank)


def pair_box(wide, total, states, presents, out):
    for half in range(2):
        present = presents[half]
        rows = [states[half, index].astype(jnp.float32) for index in range(out.shape[0])]
        if present is not None:
            rows = [row * present for row in rows]

        def emit(row, value):
            if half == 0:
                total[row] = value
            else:
                out[row] = (total[row] + value).astype(jnp.bfloat16)

        multiply(wide.at[half], rows, out.shape[0], emit)


def open_kernel(slot, pattern, wide, *rest):
    pieces, (out, states, total, packed) = rest[:4], rest[4:]
    _, mid, low, core = digits()
    fold = LANES // slot
    depth = out.shape[0] // fold
    for turn, piece in enumerate(pieces):
        first = ((mid ^ (turn // 2)) * 2 + (low ^ (turn % 2))) * 2
        for box in range(2):
            for last in range(2):
                packed[last, first + box] = piece[box, last]
    for last in range(2):
        tile = swap_groups([packed[last, place].astype(jnp.float32) for place in range(fold)], slot)
        for place, rows in enumerate(tile):
            states[last, place * depth:(place + 1) * depth] = rows.astype(jnp.bfloat16)
    pair_box(wide, total, states, [present_of(pattern, 0, half, core) for half in range(2)], out)


def other_kernel(wide, states, after, out, total):
    pair_box(wide, total, states, (None, None), out)


def interp_kernel(interp, after, first_wide, second_wide):
    core = digits()[3]
    for wide, chunk in ((first_wide, core), (second_wide, 1 - core)):
        spread(wide, lambda row: interp[pl.ds(row, GROUP), :, lanes_of(chunk)], interp.shape[0], interp.shape[1])


def last_kernel(level, bit, flip, pattern, wide, image_wide, partner, near, *rest):
    image, held, total, sems = rest[-4:]
    places = digits()
    chunk, other = places[3] ^ flip, 1 - places[3 - bit]
    rank, depth = total.shape[0], held.shape[0]

    def emit_state(row, value):
        total[row] = (near[row] + value).astype(jnp.bfloat16).astype(jnp.float32)

    multiply(wide, state_rows(partner, present_of(pattern, level, other, chunk)), rank, emit_state)
    rows = [total[index] for index in range(rank)]
    parts = 4
    size = depth // parts
    copies = []
    for part in range(parts):

        def emit(row, value):
            held[part * size + row] = value.astype(jnp.bfloat16)

        multiply(image_wide.at[pl.ds(part * size * rank, size * rank), :], rows, size, emit)
        span = pl.ds(part * size, size)
        copies.append(pltpu.make_async_copy(held.at[span], image.at[span, :, lanes_of(chunk)], sems.at[part]))
        copies[-1].start()
    for copy in copies:
        copy.wait()


def run(kernel, outs, operands, scratch=(), products=1, in_specs=None, out_specs=None, aliases=None, limit=16 * 2**20):
    whole = pl.BlockSpec(memory_space=pltpu.VMEM)
    single = not isinstance(outs, list)
    shapes = [outs] if single else outs
    result = pl.pallas_call(
        kernel,
        out_shape=shapes,
        in_specs=in_specs or [whole] * len(operands),
        out_specs=out_specs or [whole] * len(shapes),
        scratch_shapes=list(scratch),
        input_output_aliases=aliases or {},
        compiler_params=pltpu.CompilerParams(vmem_limit_bytes=limit),
        cost_estimate=pl.CostEstimate(flops=products * 2**21, bytes_accessed=products * 2**19, transcendentals=0),
    )(*operands)
    return result[0] if single else result


def permuted(value, target_of):
    pairs = [(source, target_of(source)) for source in range(lax.axis_size("leaf"))]
    return lax.ppermute(value, "leaf", pairs)


def swapped(value, bit):
    return permuted(value, lambda source: source ^ 2**bit)


def crossed(source, turn):
    high, mid, low, core = source // 8 % 2, source // 4 % 2, source // 2 % 2, source % 2
    return ((core * 2 + (mid ^ (turn // 2))) * 2 + (low ^ (turn % 2))) * 2 + high


def fast_local(samples, interp_in, top_blocks, top_pattern, bottom_blocks, bottom_pattern, interp_out):
    rank, depth = interp_in.shape[:2]
    rhs_count, box_count = samples.shape[1:]
    out_depth = interp_out.shape[0]
    slot = box_count // lax.axis_size("leaf")
    fold = LANES // slot
    state = jax.ShapeDtypeStruct((rank, rhs_count, LANES), jnp.bfloat16)
    partial = jax.ShapeDtypeStruct((rank, rhs_count, LANES), jnp.float32)
    spread_out = jax.ShapeDtypeStruct((rank * rank, LANES), jnp.float32)
    pair_spread = jax.ShapeDtypeStruct((2, rank * rank, LANES), jnp.float32)
    total = pltpu.VMEM((rank, rhs_count, LANES), jnp.float32)
    wide = pltpu.VMEM((rank * rank, LANES), jnp.float32)
    packed = pltpu.VMEM((2, fold, rank // fold, rhs_count, LANES), jnp.bfloat16)
    whole, anywhere = pl.BlockSpec(memory_space=pltpu.VMEM), pl.BlockSpec(memory_space=pl.ANY)

    def level_nears(blocks, pattern, level, bit, order):
        return {
            flip: run(
                functools.partial(near_kernel, level, bit, flip), [partial, spread_out],
                (blocks, pattern, current[flip]) + ((current[1 - flip],) if place < len(order) - 1 else ()), (wide,),
            )
            for place, flip in enumerate(order)
        }

    def level_fars(pattern, level, bit, order):
        return {
            flip: run(
                functools.partial(far_kernel, level, bit, flip), state, (pattern, partner[flip], *near[flip]),
            )
            for flip in order
        }

    current = {}
    current[1], current[0] = run(
        coeff_kernel, [state, state], (interp_in, samples),
        (
            pltpu.VMEM((4, rank, depth // 2, LANES), jnp.bfloat16),
            pltpu.VMEM((4, depth // 2, rhs_count, LANES), jnp.bfloat16),
            pltpu.VMEM((rank * depth // 2, LANES), jnp.float32), total, pltpu.SemaphoreType.DMA((8,)),
        ),
        4, [anywhere] * 2, limit=START_LIMIT,
    )
    for level in range(3):
        bit = 3 - level
        partner = {flip: swapped(current[flip], bit) for flip in (1, 0)}
        near = level_nears(top_blocks, top_pattern, level, bit, (1, 0))
        if level < 2:
            current = level_fars(top_pattern, level, bit, (1, 0))

    share_rows = 2 * rank + rank * rhs_count // (2 * rank)
    shared_shape = jax.ShapeDtypeStruct((share_rows, 2 * rank, LANES), jnp.bfloat16)
    shared = run(functools.partial(share_kernel, 3), shared_shape, (top_blocks, top_pattern, bottom_blocks, bottom_pattern))
    shared = run(
        functools.partial(send_kernel, 2, 1, 1), shared_shape, (top_pattern, partner[1], *near[1], shared), aliases={4: 0},
    )
    shared = swapped(shared, 0)
    current = level_fars(top_pattern, 2, 1, (0,))

    pair_near = run(
        functools.partial(pair_near_kernel, 3),
        [jax.ShapeDtypeStruct((2, rank, rhs_count, LANES), jnp.float32), pair_spread],
        (top_blocks, top_pattern, shared, current[0]), (wide,), 2,
    )
    piece = jax.ShapeDtypeStruct((2, 2, rank // fold, rhs_count, LANES), jnp.bfloat16)
    pieces = run(
        functools.partial(pair_far_kernel, 3, slot), [piece] * 4,
        (top_pattern, pair_near[1], shared, pair_near[0]), (total, packed), 2,
    )
    pieces = [permuted(value, functools.partial(crossed, turn=turn)) for turn, value in enumerate(pieces)]
    own_wide, other_wide = run(wide_kernel, [pair_spread] * 2, (bottom_blocks, shared))
    first, states = run(
        functools.partial(open_kernel, slot), [state, jax.ShapeDtypeStruct((2, rank, rhs_count, LANES), jnp.bfloat16)],
        (bottom_pattern, own_wide, *pieces), (total, packed), 2,
    )
    current = {0: first}
    partner = {0: swapped(first, 1)}
    near = level_nears(bottom_blocks, bottom_pattern, 1, 1, (0,))
    current[1] = swapped(run(other_kernel, state, (other_wide, states, near[0][0]), (total,), 2), 0)
    partner[1] = swapped(current[1], 1)
    near.update(level_nears(bottom_blocks, bottom_pattern, 1, 1, (1,)))
    current = level_fars(bottom_pattern, 1, 1, (0, 1))
    for level in (2, 3):
        partner = {flip: swapped(current[flip], level) for flip in (0, 1)}
        near = level_nears(bottom_blocks, bottom_pattern, level, level, (0, 1))
        if level == 2:
            current = level_fars(bottom_pattern, level, level, (0, 1))

    image_spread = jax.ShapeDtypeStruct((out_depth * rank, LANES), jnp.float32)
    image_wide = run(interp_kernel, [image_spread] * 2, (interp_out, near[0][0]))
    image = jax.ShapeDtypeStruct((out_depth, rhs_count, box_count), jnp.bfloat16)
    out = ()
    for flip in (0, 1):
        operands = (bottom_pattern, near[flip][1], image_wide[flip], partner[flip], near[flip][0])
        out = (run(
            functools.partial(last_kernel, 3, 3, flip), image, operands + out,
            (pltpu.VMEM((out_depth, rhs_count, LANES), jnp.bfloat16), total, pltpu.SemaphoreType.DMA((4,))), 3,
            [whole] * 5 + [anywhere] * flip, [anywhere], {5: 0} if flip else None,
        ),)
    return out[0]


def contract(weights, state):
    product = weights[:, :, None].astype(jnp.float32) * state[None].astype(jnp.float32)
    return jnp.sum(product, axis=1)


def plain_level(current, blocks, pattern, bit):
    rank = blocks.shape[0]
    partner = swapped(current, bit)
    is_lower = lax.axis_index("leaf") // 2**bit % 2 == 0
    lower = jnp.where(is_lower, current, partner)
    upper = jnp.where(is_lower, partner, current)
    weights = blocks * jnp.repeat(pattern, rank, axis=0).astype(jnp.bfloat16)[None]
    return contract(weights, jnp.concatenate([lower, upper], axis=0)).astype(jnp.bfloat16)


def plain_local(samples, interp_in, top_blocks, top_pattern, bottom_blocks, bottom_pattern, interp_out):
    bit_count = lax.axis_size("leaf").bit_length() - 1
    current = contract(interp_in, samples).astype(jnp.bfloat16)
    for level in range(top_blocks.shape[0]):
        current = plain_level(current, top_blocks[level], top_pattern[level], bit_count - 1 - level)
    flat = current.reshape(-1, current.shape[2])
    current = lax.all_to_all(flat, "leaf", split_axis=1, concat_axis=1, tiled=True).reshape(current.shape)
    for level in range(bottom_blocks.shape[0]):
        current = plain_level(current, bottom_blocks[level], bottom_pattern[level], level)
    return contract(interp_out, current).astype(jnp.bfloat16)


def local(samples, interp_in, top_blocks, *rest):
    four_digits = lax.axis_size("leaf") == 16 and top_blocks.shape[0] == 4
    chosen = fast_local if four_digits and samples.shape[1:] == (8, 2 * LANES) else plain_local
    return chosen(samples, interp_in, top_blocks, *rest)


def solution(mesh):
    boxes = ("parts", "leaf")
    return jax.shard_map(
        local,
        mesh=mesh,
        in_specs=(
            P(None, None, boxes),
            P(None, None, boxes),
            P(None, None, None, boxes),
            P(None, None, boxes),
            P(None, None, None, boxes),
            P(None, None, boxes),
            P(None, None, boxes),
        ),
        out_specs=P(None, None, boxes),
        check_vma=False,
    )
```

time: 72.4 us -> 67.1 us (0.927)
  waiting for transfers between devices: 17.1 us -> 9.22 us
  local copies, waits for them, and re-layouts: 7.96 us -> 4.56 us
  starting transfers between devices: 26.6 us -> 29.7 us
  Pallas kernels: 20.2 us -> 23.1 us
    ppermute x19 -> x18, waiting for transfers between devices: 17.1 us -> 9.22 us  [permuted(): return lax.ppermute(value, 'leaf', pairs)]
    unnamed x24 -> x18, local copies, waits for them, and re-layouts: 7.96 us -> 4.56 us
    ppermute x19 -> x18, starting transfers between devices: 26.6 us -> 29.7 us  [permuted(): return lax.ppermute(value, 'leaf', pairs)]
    pallas_call x31 -> x32, Pallas kernels: 20.2 us -> 23.1 us  [run(): pl.pallas_call(kernel, out_shape=shapes, in_specs=in_specs or [whole] * l...]
  transfers between devices with their start and end apart: 19 -> 18, of which waited for: 12 -> 7; matrix products, arithmetic and copies ran while one was open for 0% -> 0% of each run, Pallas kernels for 18% -> 19%
where the time goes in v4:
time: 67.1 us; the launch traced here: 66.8 us
  starting transfers between devices  29.7 us (44%)
  Pallas kernels  23.1 us (34%)
  waiting for transfers between devices  9.22 us (14%)
  local copies, waits for them, and re-layouts  4.56 us (7%)
    ppermute x18, starting transfers between devices, permuted(): return lax.ppermute(value, 'leaf', pairs)  29.7 us
    pallas_call x32, Pallas kernels, run(): pl.pallas_call(kernel, out_shape=shapes, in_specs=in_specs or [whole] * l...  23.1 us
    ppermute x18, waiting for transfers between devices, permuted(): return lax.ppermute(value, 'leaf', pairs)  9.22 us
    unnamed x18, local copies, waits for them, and re-layouts  4.56 us
  transfers between devices with their start and end apart: 18, of which 7 were waited for; matrix products, arithmetic and copies ran while one was open for 0% of the time, Pallas kernels for 19%

profile of v4, /device:TPU:0, one launch (start us, length us, event | category | flops | bytes accessed | tf_op | source)
XLA Modules:
  0.0 66.8 jit_solution(1995498032075595455)
XLA Ops:
  0.0 3.4 %shard_map.73 = (bf16[32,8,128]{2,1,0:T(8,128)(2,1)}, bf16[32,8,128]{2,1,0:T(8,128)(2,1)}) custom-call(bf16[32,64,256]{2,1,0:T(8,128)(2,1)} %interp.2, bf16[64,8,256]{2,1,0:T(8,128)(2,1)} %samples.1), custom_call_target="tpu_custom_call" | custom-call | flops 8388608 | bytes 2097152 | tf_op jit(solution)/shard_map/pallas_call | solution.py:303
  3.4 4.1 %collective-permute-start = (bf16[32,8,128]{2,1,0:T(8,128)(2,1)}, bf16[32,8,128]{2,1,0:T(8,128)(2,1)S(1)}, u32[]{:S(2)}, u32[]{:S(2)}) collective-permute-start(bf16[32,8,128]{2,1,0:T(8,128)(2,1)} %get-tuple-element.43.state), channel_id=1, source_target_pairs={{0,8},{1,9},{2,10},{3,11},{4,12},{5,13},{6,14},{7,15},{8,0},{9,1},... | collective-permute-start | bytes 196616 | tf_op jit(solution)/shard_map/ppermute | solution.py:318
  7.5 0.1 collective-permute-start.2
  7.6 2.2 %copy-done = bf16[4,32,64,256]{3,2,1,0:T(8,128)(2,1)S(1)} copy-done((bf16[4,32,64,256]{3,2,1,0:T(8,128)(2,1)S(1)}, bf16[4,32,64,256]{3,2,1,0:T(8,128)(2,1)}, u32[]{:S(2)}) %copy-start) | copy-done | bytes 4194328
  9.8 0.8 %copy-done.6 = bf16[32,8,128]{2,1,0:T(8,128)(2,1)S(1)} copy-done((bf16[32,8,128]{2,1,0:T(8,128)(2,1)S(1)}, bf16[32,8,128]{2,1,0:T(8,128)(2,1)}, u32[]{:S(2)}) %copy-start.6) | copy-done | bytes 65560
  10.6 0.8 %copy-done.8 = bf16[32,8,128]{2,1,0:T(8,128)(2,1)S(1)} copy-done((bf16[32,8,128]{2,1,0:T(8,128)(2,1)S(1)}, bf16[32,8,128]{2,1,0:T(8,128)(2,1)}, u32[]{:S(2)}) %copy-start.8) | copy-done | bytes 65560
  11.5 0.5 shard_map.74
  12.0 0.4 shard_map.75.state
  12.4 1.9 %collective-permute-start.1 = (bf16[32,8,128]{2,1,0:T(8,128)(2,1)S(1)}, bf16[32,8,128]{2,1,0:T(8,128)(2,1)S(1)}, u32[]{:S(2)}, u32[]{:S(2)}) collective-permute-start(bf16[32,8,128]{2,1,0:T(8,128)(2,1)S(1)} %shard_map.75.state), channel_id=1, source_target_pairs={{0,4},{1,5},{2,6},{3,7},{4,0},{5,1},{6,2},{7,3},{8,12},{9,13},{10,... | collective-permute-start | bytes 196616 | tf_op jit(solution)/shard_map/ppermute | solution.py:318
  14.3 0.5 shard_map.76
  14.9 0.4 shard_map.77.rest_0_.state
  15.3 0.0 copy-start.4
  15.3 1.2 %collective-permute-start.4 = (bf16[32,8,128]{2,1,0:T(8,128)(2,1)S(1)}, bf16[32,8,128]{2,1,0:T(8,128)(2,1)S(1)}, u32[]{:S(2)}, u32[]{:S(2)}) collective-permute-start(bf16[32,8,128]{2,1,0:T(8,128)(2,1)S(1)} %shard_map.77.rest_0_.state), channel_id=1, source_target_pairs={{0,4},{1,5},{2,6},{3,7},{4,0},{5,1},{6,2},{7,3},{8,12},{9,13},{10,... | collective-permute-start | bytes 196616 | tf_op jit(solution)/shard_map/ppermute | solution.py:318
  16.5 0.5 shard_map.78
  17.1 0.4 shard_map.79.state
  17.5 1.6 %collective-permute-start.3 = (bf16[32,8,128]{2,1,0:T(8,128)(2,1)S(1)}, bf16[32,8,128]{2,1,0:T(8,128)(2,1)S(1)}, u32[]{:S(2)}, u32[]{:S(2)}) collective-permute-start(bf16[32,8,128]{2,1,0:T(8,128)(2,1)S(1)} %shard_map.79.state), channel_id=1, source_target_pairs={{0,2},{1,3},{2,0},{3,1},{4,6},{5,7},{6,4},{7,5},{8,10},{9,11},{10,... | collective-permute-start | bytes 196616 | tf_op jit(solution)/shard_map/ppermute | solution.py:318
  19.1 0.8 %shard_map.83.shared = bf16[68,64,128]{2,1,0:T(8,128)(2,1)S(1)} custom-call(bf16[4,32,64,256]{3,2,1,0:T(8,128)(2,1)S(1)} %copy-done.1, s32[4,2,256]{2,1,0:T(2,128)S(1)} %copy-done.3, bf16[4,32,64,256]{3,2,1,0:T(8,128)(2,1)S(1)} %copy-done.2, s32[4,2,256]{2,1,0:T(2,128)S(1)} %copy-done.4), custom_call_target="tpu_custom_call" | custom-call | flops 2097152 | bytes 524288 | tf_op jit(solution)/shard_map/pallas_call | solution.py:303
  19.9 0.5 shard_map.80
  20.5 0.4 shard_map.81.rest_0_.state
  20.9 0.5 shard_map.82
  21.5 0.4 collective-permute-done.3.partner
  21.8 0.4 shard_map.84
  22.2 0.1 collective-permute-start.5
  22.3 1.6 %collective-permute-start.6 = (bf16[32,8,128]{2,1,0:T(8,128)(2,1)S(1)}, bf16[32,8,128]{2,1,0:T(8,128)(2,1)S(1)}, u32[]{:S(2)}, u32[]{:S(2)}) collective-permute-start(bf16[32,8,128]{2,1,0:T(8,128)(2,1)S(1)} %shard_map.81.rest_0_.state), channel_id=1, source_target_pairs={{0,2},{1,3},{2,0},{3,1},{4,6},{5,7},{6,4},{7,5},{8,10},{9,11},{10,... | collective-permute-start | bytes 196616 | tf_op jit(solution)/shard_map/ppermute | solution.py:318
  23.9 0.5 shard_map.86
  24.4 2.4 %collective-permute-done.6.partner = bf16[32,8,128]{2,1,0:T(8,128)(2,1)S(1)} collective-permute-done((bf16[32,8,128]{2,1,0:T(8,128)(2,1)S(1)}, bf16[32,8,128]{2,1,0:T(8,128)(2,1)S(1)}, u32[]{:S(2)}, u32[]{:S(2)}) %collective-permute-start.6) | collective-permute-done | bytes 65568 | tf_op jit(solution)/shard_map/ppermute | solution.py:318
  26.8 0.4 shard_map.87.state
  27.2 1.1 %shard_map.88 = (f32[2,32,8,128]{3,2,1,0:T(8,128)S(1)}, f32[2,1024,128]{2,1,0:T(8,128)S(1)}) custom-call(bf16[4,32,64,256]{3,2,1,0:T(8,128)(2,1)S(1)} %copy-done.1, s32[4,2,256]{2,1,0:T(2,128)S(1)} %copy-done.3, bf16[68,64,128]{2,1,0:T(8,128)(2,1)S(1)} %collective-permute-done.5.shared, bf16[32,8,128]{2,1,0:T(8,128)(2,1)S(1)} %shard_map.87.state), custom_call_target="tpu_custom_call" | custom-call | flops 4194304 | bytes 1048576 | tf_op jit(solution)/shard_map/pallas_call | solution.py:303
  28.3 1.3 %shard_map.89 = (bf16[2,2,4,8,128]{4,3,2,1,0:T(8,128)(2,1)S(1)}, bf16[2,2,4,8,128]{4,3,2,1,0:T(8,128)(2,1)S(1)}, bf16[2,2,4,8,128]{4,3,2,1,0:T(8,128)(2,1)S(1)}, bf16[2,2,4,8,128]{4,3,2,1,0:T(8,128)(2,1)S(1)}) custom-call(s32[4,2,256]{2,1,0:T(2,128)S(1)} %copy-done.3, f32[2,1024,128]{2,1,0:T(8,128)S(1)} %get-tuple-element.59.wide, ...), custom_call_target="tpu_custom_call" | custom-call | flops 4194304 | bytes 1048576 | tf_op jit(solution)/shard_map/pallas_call | solution.py:303
  29.6 2.8 %collective-permute-start.10 = (bf16[2,2,4,8,128]{4,3,2,1,0:T(8,128)(2,1)S(1)}, bf16[2,2,4,8,128]{4,3,2,1,0:T(8,128)(2,1)S(1)}, u32[]{:S(2)}, u32[]{:S(2)}) collective-permute-start(bf16[2,2,4,8,128]{4,3,2,1,0:T(8,128)(2,1)S(1)} %get-tuple-element.64), channel_id=1, source_target_pairs={{0,6},{1,14},{2,4},{3,12},{4,2},{5,10},{6,0},{7,8},{8,7},{9,15},{1... | collective-permute-start | bytes 98312 | tf_op jit(solution)/shard_map/ppermute | solution.py:318
  32.4 0.7 collective-permute-start.7
  33.1 0.6 collective-permute-start.8
  33.6 0.3 collective-permute-start.9
  33.9 0.2 shard_map.85
  34.1 0.3 collective-permute-done.10.rest_3_
  34.5 2.7 %collective-permute-done.8.rest_1_ = bf16[2,2,4,8,128]{4,3,2,1,0:T(8,128)(2,1)S(1)} collective-permute-done((bf16[2,2,4,8,128]{4,3,2,1,0:T(8,128)(2,1)S(1)}, bf16[2,2,4,8,128]{4,3,2,1,0:T(8,128)(2,1)S(1)}, u32[]{:S(2)}, u32[]{:S(2)}) %collective-permute-start.8) | collective-permute-done | bytes 32800 | tf_op jit(solution)/shard_map/ppermute | solution.py:318
  37.2 0.3 collective-permute-done.9.rest_2_
  37.5 1.0 %shard_map.90 = (bf16[32,8,128]{2,1,0:T(8,128)(2,1)S(1)}, bf16[2,32,8,128]{3,2,1,0:T(8,128)(2,1)S(1)}) custom-call(s32[4,2,256]{2,1,0:T(2,128)S(1)} %copy-done.4, f32[2,1024,128]{2,1,0:T(8,128)S(1)} %get-tuple-element.56.wide, bf16[2,2,4,8,128]{4,3,2,1,0:T(8,128)(2,1)S(1)} %collective-permute-done.7.rest_0_, ...), custom_call_target="tpu_custom_call" | custom-call | flops 4194304 | bytes 1048576 | tf_op jit(solution)/shard_map/pallas_call | solution.py:303
  38.6 0.5 shard_map.91
  39.1 0.8 %shard_map.92 = bf16[32,8,128]{2,1,0:T(8,128)(2,1)S(1)} custom-call(f32[2,1024,128]{2,1,0:T(8,128)S(1)} %get-tuple-element.55.wide, bf16[2,32,8,128]{3,2,1,0:T(8,128)(2,1)S(1)} %get-tuple-element.65.states, f32[32,8,128]{2,1,0:T(8,128)S(1)} %get-tuple-element.67.after.near), custom_call_target="tpu_custom_call" | custom-call | flops 4194304 | bytes 1048576 | tf_op jit(solution)/shard_map/pallas_call | solution.py:303
  39.9 7.3 %collective-permute-start.11 = (bf16[32,8,128]{2,1,0:T(8,128)(2,1)S(1)}, bf16[32,8,128]{2,1,0:T(8,128)(2,1)S(1)}, u32[]{:S(2)}, u32[]{:S(2)}) collective-permute-start(bf16[32,8,128]{2,1,0:T(8,128)(2,1)S(1)} %shard_map.92), channel_id=1, source_target_pairs={{0,1},{1,0},{2,3},{3,2},{4,5},{5,4},{6,7},{7,6},{8,9},{9,8},{10,11... | collective-permute-start | bytes 196616 | tf_op jit(solution)/shard_map/ppermute | solution.py:318
  47.2 1.5 %collective-permute-start.14 = (bf16[32,8,128]{2,1,0:T(8,128)(2,1)S(1)}, bf16[32,8,128]{2,1,0:T(8,128)(2,1)S(1)}, u32[]{:S(2)}, u32[]{:S(2)}) collective-permute-start(bf16[32,8,128]{2,1,0:T(8,128)(2,1)S(1)} %get-tuple-element.66.state), channel_id=1, source_target_pairs={{0,2},{1,3},{2,0},{3,1},{4,6},{5,7},{6,4},{7,5},{8,10},{9,11},{10,... | collective-permute-start | bytes 196616 | tf_op jit(solution)/shard_map/ppermute | solution.py:318
  48.7 0.9 %collective-permute-start.12 = (bf16[32,8,128]{2,1,0:T(8,128)(2,1)S(1)}, bf16[32,8,128]{2,1,0:T(8,128)(2,1)S(1)}, u32[]{:S(2)}, u32[]{:S(2)}) collective-permute-start(bf16[32,8,128]{2,1,0:T(8,128)(2,1)S(1)} %collective-permute-done.11.state), channel_id=1, source_target_pairs={{0,2},{1,3},{2,0},{3,1},{4,6},{5,7},{6,4},{7,5},{8,10},{9,11},{10,... | collective-permute-start | bytes 196616 | tf_op jit(solution)/shard_map/ppermute | solution.py:318
  49.6 2.3 %collective-permute-done.14.partner = bf16[32,8,128]{2,1,0:T(8,128)(2,1)S(1)} collective-permute-done((bf16[32,8,128]{2,1,0:T(8,128)(2,1)S(1)}, bf16[32,8,128]{2,1,0:T(8,128)(2,1)S(1)}, u32[]{:S(2)}, u32[]{:S(2)}) %collective-permute-start.14) | collective-permute-done | bytes 65568 | tf_op jit(solution)/shard_map/ppermute | solution.py:318
  51.9 0.4 shard_map.98.state
  52.3 0.1 collective-permute-start.15
  52.4 0.5 shard_map.93
  53.0 0.0 collective-permute-done.12.partner
  53.0 0.4 shard_map.94.state.rest_0_
  53.4 2.0 %collective-permute-start.13 = (bf16[32,8,128]{2,1,0:T(8,128)(2,1)S(1)}, bf16[32,8,128]{2,1,0:T(8,128)(2,1)S(1)}, u32[]{:S(2)}, u32[]{:S(2)}) collective-permute-start(bf16[32,8,128]{2,1,0:T(8,128)(2,1)S(1)} %shard_map.94.state.rest_0_), channel_id=1, source_target_pairs={{0,4},{1,5},{2,6},{3,7},{4,0},{5,1},{6,2},{7,3},{8,12},{9,13},{10,... | collective-permute-start | bytes 196616 | tf_op jit(solution)/shard_map/ppermute | solution.py:318
  55.5 0.5 shard_map.99
  56.0 0.7 %collective-permute-done.15.partner = bf16[32,8,128]{2,1,0:T(8,128)(2,1)S(1)} collective-permute-done((bf16[32,8,128]{2,1,0:T(8,128)(2,1)S(1)}, bf16[32,8,128]{2,1,0:T(8,128)(2,1)S(1)}, u32[]{:S(2)}, u32[]{:S(2)}) %collective-permute-start.15) | collective-permute-done | bytes 65568 | tf_op jit(solution)/shard_map/ppermute | solution.py:318
  56.7 0.4 shard_map.100.state
  57.1 0.8 %collective-permute-start.17 = (bf16[32,8,128]{2,1,0:T(8,128)(2,1)S(1)}, bf16[32,8,128]{2,1,0:T(8,128)(2,1)S(1)}, u32[]{:S(2)}, u32[]{:S(2)}) collective-permute-start(bf16[32,8,128]{2,1,0:T(8,128)(2,1)S(1)} %shard_map.100.state), channel_id=1, source_target_pairs={{0,8},{1,9},{2,10},{3,11},{4,12},{5,13},{6,14},{7,15},{8,0},{9,1},... | collective-permute-start | bytes 196616 | tf_op jit(solution)/shard_map/ppermute | solution.py:318
  57.9 0.5 shard_map.95
  58.4 0.4 shard_map.96.state.rest_0_
  58.9 2.2 %collective-permute-start.16 = (bf16[32,8,128]{2,1,0:T(8,128)(2,1)S(1)}, bf16[32,8,128]{2,1,0:T(8,128)(2,1)S(1)}, u32[]{:S(2)}, u32[]{:S(2)}) collective-permute-start(bf16[32,8,128]{2,1,0:T(8,128)(2,1)S(1)} %shard_map.96.state.rest_0_), channel_id=1, source_target_pairs={{0,8},{1,9},{2,10},{3,11},{4,12},{5,13},{6,14},{7,15},{8,0},{9,1},... | collective-permute-start | bytes 196616 | tf_op jit(solution)/shard_map/ppermute | solution.py:318
  61.1 0.5 shard_map.101
  61.6 0.0 copy-start.5
  61.6 0.5 shard_map.97
  62.2 0.7 %copy-done.5 = bf16[64,32,256]{2,1,0:T(8,128)(2,1)S(1)} copy-done((bf16[64,32,256]{2,1,0:T(8,128)(2,1)S(1)}, bf16[64,32,256]{2,1,0:T(8,128)(2,1)}, u32[]{:S(2)}) %copy-start.5) | copy-done | bytes 1048600
  62.9 0.3 shard_map.102
  63.1 1.8 %shard_map.103.rest_0_ = bf16[64,8,256]{2,1,0:T(8,128)(2,1)} custom-call(s32[4,2,256]{2,1,0:T(2,128)S(1)} %copy-done.4, f32[1024,128]{1,0:T(8,128)S(1)} %get-tuple-element.79.wide, f32[2048,128]{1,0:T(8,128)S(1)} %get-tuple-element.80.image_wide, bf16[32,8,128]{2,1,0:T(8,128)(2,1)S(1)} %collective-permute-done.17.partner, ...), custom_call_target="tpu_custom_call" | custom-call | flops 6291456 | bytes 1572864 | tf_op jit(solution)/shard_map/pallas_call | solution.py:303
  65.0 1.8 %shard_map.104 = bf16[64,8,256]{2,1,0:T(8,128)(2,1)} custom-call(s32[4,2,256]{2,1,0:T(2,128)S(1)} %copy-done.4, f32[1024,128]{1,0:T(8,128)S(1)} %get-tuple-element.72.wide, f32[2048,128]{1,0:T(8,128)S(1)} %get-tuple-element.77.image_wide, bf16[32,8,128]{2,1,0:T(8,128)(2,1)S(1)} %collective-permute-done.16.partner, ...), custom_call_target="tpu_custom_call", output_to_operand_aliasing={{}: (5, {})} | custom-call | flops 6291456 | bytes 1572864 | tf_op jit(solution)/shard_map/pallas_call | solution.py:303
  (22 shorter events, 0.0 us)
Async XLA Ops:
  0.0 7.6 %copy-start.3 = (s32[4,2,256]{2,1,0:T(2,128)S(1)}, s32[4,2,256]{2,1,0:T(2,128)}, u32[]{:S(2)}) copy-start(s32[4,2,256]{2,1,0:T(2,128)} %pattern.40) | copy-start | bytes 24580
  3.4 8.6 %collective-permute-start = (bf16[32,8,128]{2,1,0:T(8,128)(2,1)}, bf16[32,8,128]{2,1,0:T(8,128)(2,1)S(1)}, u32[]{:S(2)}, u32[]{:S(2)}) collective-permute-start(bf16[32,8,128]{2,1,0:T(8,128)(2,1)} %get-tuple-element.43.state), channel_id=1, source_target_pairs={{0,8},{1,9},{2,10},{3,11},{4,12},{5,13},{6,14},{7,15},{8,0},{9,1},... | collective-permute-start | bytes 196616 | tf_op jit(solution)/shard_map/ppermute | solution.py:318
  7.5 7.3 %collective-permute-start.2 = (bf16[32,8,128]{2,1,0:T(8,128)(2,1)}, bf16[32,8,128]{2,1,0:T(8,128)(2,1)S(1)}, u32[]{:S(2)}, u32[]{:S(2)}) collective-permute-start(bf16[32,8,128]{2,1,0:T(8,128)(2,1)} %get-tuple-element.44.rest_0_.state), channel_id=1, source_target_pairs={{0,8},{1,9},{2,10},{3,11},{4,12},{5,13},{6,14},{7,15},{8,0},{9,1},... | collective-permute-start | bytes 196616 | tf_op jit(solution)/shard_map/ppermute | solution.py:318
  7.6 2.2 %copy-start = (bf16[4,32,64,256]{3,2,1,0:T(8,128)(2,1)S(1)}, bf16[4,32,64,256]{3,2,1,0:T(8,128)(2,1)}, u32[]{:S(2)}) copy-start(bf16[4,32,64,256]{3,2,1,0:T(8,128)(2,1)} %blocks.21) | copy-start | bytes 12582916
  9.8 0.8 %copy-start.6 = (bf16[32,8,128]{2,1,0:T(8,128)(2,1)S(1)}, bf16[32,8,128]{2,1,0:T(8,128)(2,1)}, u32[]{:S(2)}) copy-start(bf16[32,8,128]{2,1,0:T(8,128)(2,1)} %get-tuple-element.44.rest_0_.state) | copy-start | bytes 196612
  10.6 0.8 %copy-start.8 = (bf16[32,8,128]{2,1,0:T(8,128)(2,1)S(1)}, bf16[32,8,128]{2,1,0:T(8,128)(2,1)}, u32[]{:S(2)}) copy-start(bf16[32,8,128]{2,1,0:T(8,128)(2,1)} %get-tuple-element.43.state) | copy-start | bytes 196612
  11.5 2.9 %copy-start.1 = (bf16[4,32,64,256]{3,2,1,0:T(8,128)(2,1)S(1)}, bf16[4,32,64,256]{3,2,1,0:T(8,128)(2,1)}, u32[]{:S(2)}) copy-start(bf16[4,32,64,256]{3,2,1,0:T(8,128)(2,1)} %blocks.21) | copy-start | bytes 12582916
  11.5 2.9 %copy-start.7 = (bf16[32,8,128]{2,1,0:T(8,128)(2,1)S(1)}, bf16[32,8,128]{2,1,0:T(8,128)(2,1)}, u32[]{:S(2)}) copy-start(bf16[32,8,128]{2,1,0:T(8,128)(2,1)} %get-tuple-element.44.rest_0_.state) | copy-start | bytes 196612
  12.4 4.6 %collective-permute-start.1 = (bf16[32,8,128]{2,1,0:T(8,128)(2,1)S(1)}, bf16[32,8,128]{2,1,0:T(8,128)(2,1)S(1)}, u32[]{:S(2)}, u32[]{:S(2)}) collective-permute-start(bf16[32,8,128]{2,1,0:T(8,128)(2,1)S(1)} %shard_map.75.state), channel_id=1, source_target_pairs={{0,4},{1,5},{2,6},{3,7},{4,0},{5,1},{6,2},{7,3},{8,12},{9,13},{10,... | collective-permute-start | bytes 196616 | tf_op jit(solution)/shard_map/ppermute | solution.py:318
  15.3 3.8 %copy-start.4 = (s32[4,2,256]{2,1,0:T(2,128)S(1)}, s32[4,2,256]{2,1,0:T(2,128)}, u32[]{:S(2)}) copy-start(s32[4,2,256]{2,1,0:T(2,128)} %pattern.53) | copy-start | bytes 24580
  15.3 5.2 %collective-permute-start.4 = (bf16[32,8,128]{2,1,0:T(8,128)(2,1)S(1)}, bf16[32,8,128]{2,1,0:T(8,128)(2,1)S(1)}, u32[]{:S(2)}, u32[]{:S(2)}) collective-permute-start(bf16[32,8,128]{2,1,0:T(8,128)(2,1)S(1)} %shard_map.77.rest_0_.state), channel_id=1, source_target_pairs={{0,4},{1,5},{2,6},{3,7},{4,0},{5,1},{6,2},{7,3},{8,12},{9,13},{10,... | collective-permute-start | bytes 196616 | tf_op jit(solution)/shard_map/ppermute | solution.py:318
  16.5 2.6 %copy-start.2 = (bf16[4,32,64,256]{3,2,1,0:T(8,128)(2,1)S(1)}, bf16[4,32,64,256]{3,2,1,0:T(8,128)(2,1)}, u32[]{:S(2)}) copy-start(bf16[4,32,64,256]{3,2,1,0:T(8,128)(2,1)} %blocks.27) | copy-start | bytes 12582916
  17.5 4.3 %collective-permute-start.3 = (bf16[32,8,128]{2,1,0:T(8,128)(2,1)S(1)}, bf16[32,8,128]{2,1,0:T(8,128)(2,1)S(1)}, u32[]{:S(2)}, u32[]{:S(2)}) collective-permute-start(bf16[32,8,128]{2,1,0:T(8,128)(2,1)S(1)} %shard_map.79.state), channel_id=1, source_target_pairs={{0,2},{1,3},{2,0},{3,1},{4,6},{5,7},{6,4},{7,5},{8,10},{9,11},{10,... | collective-permute-start | bytes 196616 | tf_op jit(solution)/shard_map/ppermute | solution.py:318
  22.2 5.0 %collective-permute-start.5 = (bf16[68,64,128]{2,1,0:T(8,128)(2,1)S(1)}, bf16[68,64,128]{2,1,0:T(8,128)(2,1)S(1)}, u32[]{:S(2)}, u32[]{:S(2)}) collective-permute-start(bf16[68,64,128]{2,1,0:T(8,128)(2,1)S(1)} %shard_map.84), channel_id=1, source_target_pairs={{0,1},{1,0},{2,3},{3,2},{4,5},{5,4},{6,7},{7,6},{8,9},{9,8},{10,11... | collective-permute-start | bytes 3342344 | tf_op jit(solution)/shard_map/ppermute | solution.py:318
  22.3 4.5 %collective-permute-start.6 = (bf16[32,8,128]{2,1,0:T(8,128)(2,1)S(1)}, bf16[32,8,128]{2,1,0:T(8,128)(2,1)S(1)}, u32[]{:S(2)}, u32[]{:S(2)}) collective-permute-start(bf16[32,8,128]{2,1,0:T(8,128)(2,1)S(1)} %shard_map.81.rest_0_.state), channel_id=1, source_target_pairs={{0,2},{1,3},{2,0},{3,1},{4,6},{5,7},{6,4},{7,5},{8,10},{9,11},{10,... | collective-permute-start | bytes 196616 | tf_op jit(solution)/shard_map/ppermute | solution.py:318
  29.6 4.9 %collective-permute-start.10 = (bf16[2,2,4,8,128]{4,3,2,1,0:T(8,128)(2,1)S(1)}, bf16[2,2,4,8,128]{4,3,2,1,0:T(8,128)(2,1)S(1)}, u32[]{:S(2)}, u32[]{:S(2)}) collective-permute-start(bf16[2,2,4,8,128]{4,3,2,1,0:T(8,128)(2,1)S(1)} %get-tuple-element.64), channel_id=1, source_target_pairs={{0,6},{1,14},{2,4},{3,12},{4,2},{5,10},{6,0},{7,8},{8,7},{9,15},{1... | collective-permute-start | bytes 98312 | tf_op jit(solution)/shard_map/ppermute | solution.py:318
  32.4 2.1 %collective-permute-start.7 = (bf16[2,2,4,8,128]{4,3,2,1,0:T(8,128)(2,1)S(1)}, bf16[2,2,4,8,128]{4,3,2,1,0:T(8,128)(2,1)S(1)}, u32[]{:S(2)}, u32[]{:S(2)}) collective-permute-start(bf16[2,2,4,8,128]{4,3,2,1,0:T(8,128)(2,1)S(1)} %get-tuple-element.61), channel_id=1, source_target_pairs={{0,0},{1,8},{2,2},{3,10},{4,4},{5,12},{6,6},{7,14},{8,1},{9,9},{10... | collective-permute-start | bytes 98312 | tf_op jit(solution)/shard_map/ppermute | solution.py:318
  33.1 4.2 %collective-permute-start.8 = (bf16[2,2,4,8,128]{4,3,2,1,0:T(8,128)(2,1)S(1)}, bf16[2,2,4,8,128]{4,3,2,1,0:T(8,128)(2,1)S(1)}, u32[]{:S(2)}, u32[]{:S(2)}) collective-permute-start(bf16[2,2,4,8,128]{4,3,2,1,0:T(8,128)(2,1)S(1)} %get-tuple-element.62), channel_id=1, source_target_pairs={{0,2},{1,10},{2,0},{3,8},{4,6},{5,14},{6,4},{7,12},{8,3},{9,11},{1... | collective-permute-start | bytes 98312 | tf_op jit(solution)/shard_map/ppermute | solution.py:318
  33.6 3.9 %collective-permute-start.9 = (bf16[2,2,4,8,128]{4,3,2,1,0:T(8,128)(2,1)S(1)}, bf16[2,2,4,8,128]{4,3,2,1,0:T(8,128)(2,1)S(1)}, u32[]{:S(2)}, u32[]{:S(2)}) collective-permute-start(bf16[2,2,4,8,128]{4,3,2,1,0:T(8,128)(2,1)S(1)} %get-tuple-element.63), channel_id=1, source_target_pairs={{0,4},{1,12},{2,6},{3,14},{4,0},{5,8},{6,2},{7,10},{8,5},{9,13},{1... | collective-permute-start | bytes 98312 | tf_op jit(solution)/shard_map/ppermute | solution.py:318
  39.9 8.8 %collective-permute-start.11 = (bf16[32,8,128]{2,1,0:T(8,128)(2,1)S(1)}, bf16[32,8,128]{2,1,0:T(8,128)(2,1)S(1)}, u32[]{:S(2)}, u32[]{:S(2)}) collective-permute-start(bf16[32,8,128]{2,1,0:T(8,128)(2,1)S(1)} %shard_map.92), channel_id=1, source_target_pairs={{0,1},{1,0},{2,3},{3,2},{4,5},{5,4},{6,7},{7,6},{8,9},{9,8},{10,11... | collective-permute-start | bytes 196616 | tf_op jit(solution)/shard_map/ppermute | solution.py:318
  47.2 4.7 %collective-permute-start.14 = (bf16[32,8,128]{2,1,0:T(8,128)(2,1)S(1)}, bf16[32,8,128]{2,1,0:T(8,128)(2,1)S(1)}, u32[]{:S(2)}, u32[]{:S(2)}) collective-permute-start(bf16[32,8,128]{2,1,0:T(8,128)(2,1)S(1)} %get-tuple-element.66.state), channel_id=1, source_target_pairs={{0,2},{1,3},{2,0},{3,1},{4,6},{5,7},{6,4},{7,5},{8,10},{9,11},{10,... | collective-permute-start | bytes 196616 | tf_op jit(solution)/shard_map/ppermute | solution.py:318
  48.7 4.3 %collective-permute-start.12 = (bf16[32,8,128]{2,1,0:T(8,128)(2,1)S(1)}, bf16[32,8,128]{2,1,0:T(8,128)(2,1)S(1)}, u32[]{:S(2)}, u32[]{:S(2)}) collective-permute-start(bf16[32,8,128]{2,1,0:T(8,128)(2,1)S(1)} %collective-permute-done.11.state), channel_id=1, source_target_pairs={{0,2},{1,3},{2,0},{3,1},{4,6},{5,7},{6,4},{7,5},{8,10},{9,11},{10,... | collective-permute-start | bytes 196616 | tf_op jit(solution)/shard_map/ppermute | solution.py:318
  52.3 4.3 %collective-permute-start.15 = (bf16[32,8,128]{2,1,0:T(8,128)(2,1)S(1)}, bf16[32,8,128]{2,1,0:T(8,128)(2,1)S(1)}, u32[]{:S(2)}, u32[]{:S(2)}) collective-permute-start(bf16[32,8,128]{2,1,0:T(8,128)(2,1)S(1)} %shard_map.98.state), channel_id=1, source_target_pairs={{0,4},{1,5},{2,6},{3,7},{4,0},{5,1},{6,2},{7,3},{8,12},{9,13},{10,... | collective-permute-start | bytes 196616 | tf_op jit(solution)/shard_map/ppermute | solution.py:318
  53.4 5.0 %collective-permute-start.13 = (bf16[32,8,128]{2,1,0:T(8,128)(2,1)S(1)}, bf16[32,8,128]{2,1,0:T(8,128)(2,1)S(1)}, u32[]{:S(2)}, u32[]{:S(2)}) collective-permute-start(bf16[32,8,128]{2,1,0:T(8,128)(2,1)S(1)} %shard_map.94.state.rest_0_), channel_id=1, source_target_pairs={{0,4},{1,5},{2,6},{3,7},{4,0},{5,1},{6,2},{7,3},{8,12},{9,13},{10,... | collective-permute-start | bytes 196616 | tf_op jit(solution)/shard_map/ppermute | solution.py:318
  57.1 6.0 %collective-permute-start.17 = (bf16[32,8,128]{2,1,0:T(8,128)(2,1)S(1)}, bf16[32,8,128]{2,1,0:T(8,128)(2,1)S(1)}, u32[]{:S(2)}, u32[]{:S(2)}) collective-permute-start(bf16[32,8,128]{2,1,0:T(8,128)(2,1)S(1)} %shard_map.100.state), channel_id=1, source_target_pairs={{0,8},{1,9},{2,10},{3,11},{4,12},{5,13},{6,14},{7,15},{8,0},{9,1},... | collective-permute-start | bytes 196616 | tf_op jit(solution)/shard_map/ppermute | solution.py:318
  58.9 6.1 %collective-permute-start.16 = (bf16[32,8,128]{2,1,0:T(8,128)(2,1)S(1)}, bf16[32,8,128]{2,1,0:T(8,128)(2,1)S(1)}, u32[]{:S(2)}, u32[]{:S(2)}) collective-permute-start(bf16[32,8,128]{2,1,0:T(8,128)(2,1)S(1)} %shard_map.96.state.rest_0_), channel_id=1, source_target_pairs={{0,8},{1,9},{2,10},{3,11},{4,12},{5,13},{6,14},{7,15},{8,0},{9,1},... | collective-permute-start | bytes 196616 | tf_op jit(solution)/shard_map/ppermute | solution.py:318
  61.6 1.2 %copy-start.5 = (bf16[64,32,256]{2,1,0:T(8,128)(2,1)S(1)}, bf16[64,32,256]{2,1,0:T(8,128)(2,1)}, u32[]{:S(2)}) copy-start(bf16[64,32,256]{2,1,0:T(8,128)(2,1)} %interp.3) | copy-start | bytes 3145732

commit v5 on v4

--- a/solution.py
+++ b/solution.py
@@ -9,7 +9,8 @@
 
 LANES = 128
 GROUP = 4
-START_LIMIT = 62_700_000
+KERNEL_COST = 1024
+START_COST = 2**22
 
 
 def digits():
@@ -19,6 +20,16 @@
 
 def lanes_of(chunk):
     return pl.ds(pl.multiple_of(chunk * LANES, LANES), LANES)
+
+
+def pick(chunk, read):
+    near, far = read(lanes_of(chunk)).astype(jnp.float32), read(lanes_of(1 - chunk)).astype(jnp.float32)
+    return merge(chunk, near, far)
+
+
+def merge(number, near, far):
+    side = lax.broadcasted_iota(jnp.int32, near.shape, near.ndim - 1) // (LANES // 2)
+    return jnp.where(side == number, near, pltpu.roll(far, LANES // 2, near.ndim - 1))
 
 
 def rows_of(half, rank):
@@ -58,42 +69,34 @@
 
 def level_load(blocks, level, half, chunk):
     rank = blocks.shape[1]
-    return lambda row: blocks[level, pl.ds(row, GROUP), rows_of(half, rank), lanes_of(chunk)]
+    return lambda row: pick(chunk, lambda lanes: blocks[level, pl.ds(row, GROUP), rows_of(half, rank), lanes])
 
 
 def present_of(pattern, level, half, chunk):
-    pair = [pattern[level, place:place + 1, lanes_of(chunk)].astype(jnp.float32) for place in range(2)]
-    return jnp.where(half == 0, pair[0], pair[1])
-
-
-def coeff_kernel(interp, samples, first, second, held_interp, held_samples, wide, total, sems):
-    rank, depth = first.shape[0], held_samples.shape[1]
+    def read(lanes):
+        pair = [pattern[level, place:place + 1, lanes].astype(jnp.float32) for place in range(2)]
+        return jnp.broadcast_to(jnp.where(half == 0, pair[0], pair[1]), (8, LANES))
+
+    return pick(chunk, read)
+
+
+def coeff_kernel(interp, samples, first, second, wide, total):
+    rank, depth = first.shape[0], samples.shape[0] // 2
     core = digits()[3]
-    pairs = []
-    for turn, chunk in enumerate((1 - core, core)):
+    for turn in range(2):
+        lanes = slice(turn * LANES, (turn + 1) * LANES)
         for half in range(2):
-            place, part = turn * 2 + half, pl.ds(half * depth, depth)
-            pairs.append((
-                pltpu.make_async_copy(samples.at[part, :, lanes_of(chunk)], held_samples.at[place], sems.at[2 * place]),
-                pltpu.make_async_copy(interp.at[:, part, lanes_of(chunk)], held_interp.at[place], sems.at[2 * place + 1]),
-            ))
-    for pair in pairs:
-        for copy in pair:
-            copy.start()
-    for place, pair in enumerate(pairs):
-        for copy in pair:
-            copy.wait()
-        spread(wide, lambda row: held_interp[place, pl.ds(row, GROUP)], rank, depth)
-        state = [held_samples[place, index].astype(jnp.float32) for index in range(depth)]
-        out = (first, second)[place // 2]
-
-        def emit(row, value):
-            if place % 2 == 0:
-                total[row] = value
-            else:
-                out[row] = (total[row] + value).astype(jnp.bfloat16)
-
-        multiply(wide, state, rank, emit)
+            part = slice(half * depth, (half + 1) * depth)
+            spread(wide, lambda row: interp[pl.ds(row, GROUP), part, lanes], rank, depth)
+            state = [samples[half * depth + index, :, lanes].astype(jnp.float32) for index in range(depth)]
+
+            def emit(row, value):
+                total[turn, row] = value if half == 0 else total[turn, row] + value
+
+            multiply(wide, state, rank, emit)
+    for row in range(rank):
+        for out, chunk in ((first, 1 - core), (second, core)):
+            out[row] = merge(chunk, total[chunk, row], total[1 - chunk, row]).astype(jnp.bfloat16)
 
 
 def near_kernel(level, bit, flip, blocks, pattern, state, *rest):
@@ -124,14 +127,15 @@
     chunk = 1 - digits()[3]
     for place, (blocks, pattern, level) in enumerate(((top_blocks, top_pattern, top_level), (bottom_blocks, bottom_pattern, 0))):
         for half in range(2):
-            present = present_of(pattern, level, half, chunk)[None]
-
-            def body(row, carry):
-                rows = blocks[level, pl.ds(row, 1), half * rank:(half + 1) * rank, lanes_of(chunk)]
-                out[place * rank + row, half * rank:(half + 1) * rank, :] = (rows.astype(jnp.float32) * present)[0].astype(jnp.bfloat16)
+            present = present_of(pattern, level, half, chunk)[:1][None]
+            load = level_load(blocks, level, half, chunk)
+
+            def body(step, carry):
+                span = pl.ds(place * rank + step * GROUP, GROUP)
+                out[span, half * rank:(half + 1) * rank, :] = (load(step * GROUP) * present).astype(jnp.bfloat16)
                 return carry
 
-            lax.fori_loop(0, rank, body, 0)
+            lax.fori_loop(0, rank // GROUP, body, 0)
 
 
 def shared_load(shared, place, half):
@@ -198,7 +202,7 @@
 def pair_far_kernel(level, slot, pattern, wide, shared, near, *rest):
     outs, (total, packed) = rest[:4], rest[4:]
     rank = near.shape[1]
-    _, mid, low, core = digits()
+    high, _, low, core = digits()
     rows = sent_rows(shared)
     present = present_of(pattern, level, 1 - core, core)
     fold = LANES // slot
@@ -212,7 +216,7 @@
         for place, piece in enumerate(pieces):
             packed[core ^ box, place] = piece.astype(jnp.bfloat16)
     for turn, out in enumerate(outs):
-        first = ((mid ^ (turn // 2)) * 2 + (low ^ (turn % 2))) * 2
+        first = ((high ^ (turn // 2)) * 2 + (low ^ (turn % 2))) * 2
         for box in range(2):
             for last in range(2):
                 out[box, last] = packed[box, first + last]
@@ -244,11 +248,11 @@
 
 def open_kernel(slot, pattern, wide, *rest):
     pieces, (out, states, total, packed) = rest[:4], rest[4:]
-    _, mid, low, core = digits()
+    high, _, low, core = digits()
     fold = LANES // slot
     depth = out.shape[0] // fold
     for turn, piece in enumerate(pieces):
-        first = ((mid ^ (turn // 2)) * 2 + (low ^ (turn % 2))) * 2
+        first = ((high ^ (turn // 2)) * 2 + (low ^ (turn % 2))) * 2
         for box in range(2):
             for last in range(2):
                 packed[last, first + box] = piece[box, last]
@@ -259,44 +263,59 @@
     pair_box(wide, total, states, [present_of(pattern, 0, half, core) for half in range(2)], out)
 
 
-def other_kernel(wide, states, after, out, total):
+def other_kernel(wide, states, out, total):
     pair_box(wide, total, states, (None, None), out)
 
 
-def interp_kernel(interp, after, first_wide, second_wide):
+def interp_kernel(interp, first_wide, second_wide):
     core = digits()[3]
     for wide, chunk in ((first_wide, core), (second_wide, 1 - core)):
-        spread(wide, lambda row: interp[pl.ds(row, GROUP), :, lanes_of(chunk)], interp.shape[0], interp.shape[1])
-
-
-def last_kernel(level, bit, flip, pattern, wide, image_wide, partner, near, *rest):
-    image, held, total, sems = rest[-4:]
+        spread(wide, lambda row: pick(chunk, lambda lanes: interp[pl.ds(row, GROUP), :, lanes]), interp.shape[0], interp.shape[1])
+
+
+def image_rows(level, bit, flip, pattern, wide, partner, near, total):
     places = digits()
     chunk, other = places[3] ^ flip, 1 - places[3 - bit]
-    rank, depth = total.shape[0], held.shape[0]
-
-    def emit_state(row, value):
+
+    def emit(row, value):
         total[row] = (near[row] + value).astype(jnp.bfloat16).astype(jnp.float32)
 
-    multiply(wide, state_rows(partner, present_of(pattern, level, other, chunk)), rank, emit_state)
-    rows = [total[index] for index in range(rank)]
-    parts = 4
-    size = depth // parts
+    multiply(wide, state_rows(partner, present_of(pattern, level, other, chunk)), total.shape[0], emit)
+    return [total[index] for index in range(total.shape[0])]
+
+
+def first_image_kernel(level, bit, pattern, wide, image_wide, partner, near, out, total):
+    rows = image_rows(level, bit, 0, pattern, wide, partner, near, total)
+
+    def emit(row, value):
+        out[row] = value
+
+    multiply(image_wide, rows, out.shape[0], emit)
+
+
+def last_kernel(level, bit, pattern, wide, image_wide, partner, near, ready, image, held, total, sems):
+    core = digits()[3]
+    rows = image_rows(level, bit, 1, pattern, wide, partner, near, total)
+    rank, parts = total.shape[0], sems.shape[0]
+    size = held.shape[0] // parts
     copies = []
     for part in range(parts):
 
         def emit(row, value):
-            held[part * size + row] = value.astype(jnp.bfloat16)
+            place = part * size + row
+            first = ready[place]
+            held[place, :, lanes_of(core)] = merge(core, first, value).astype(jnp.bfloat16)
+            held[place, :, lanes_of(1 - core)] = merge(1 - core, value, first).astype(jnp.bfloat16)
 
         multiply(image_wide.at[pl.ds(part * size * rank, size * rank), :], rows, size, emit)
         span = pl.ds(part * size, size)
-        copies.append(pltpu.make_async_copy(held.at[span], image.at[span, :, lanes_of(chunk)], sems.at[part]))
+        copies.append(pltpu.make_async_copy(held.at[span], image.at[span], sems.at[part]))
         copies[-1].start()
     for copy in copies:
         copy.wait()
 
 
-def run(kernel, outs, operands, scratch=(), products=1, in_specs=None, out_specs=None, aliases=None, limit=16 * 2**20):
+def run(kernel, outs, operands, scratch=(), products=1, in_specs=None, out_specs=None, aliases=None, limit=16 * 2**20, cost=KERNEL_COST):
     whole = pl.BlockSpec(memory_space=pltpu.VMEM)
     single = not isinstance(outs, list)
     shapes = [outs] if single else outs
@@ -308,7 +327,7 @@
         scratch_shapes=list(scratch),
         input_output_aliases=aliases or {},
         compiler_params=pltpu.CompilerParams(vmem_limit_bytes=limit),
-        cost_estimate=pl.CostEstimate(flops=products * 2**21, bytes_accessed=products * 2**19, transcendentals=0),
+        cost_estimate=pl.CostEstimate(flops=products * cost, bytes_accessed=products * cost, transcendentals=0),
     )(*operands)
     return result[0] if single else result
 
@@ -324,7 +343,7 @@
 
 def crossed(source, turn):
     high, mid, low, core = source // 8 % 2, source // 4 % 2, source // 2 % 2, source % 2
-    return ((core * 2 + (mid ^ (turn // 2))) * 2 + (low ^ (turn % 2))) * 2 + high
+    return (((high ^ (turn // 2)) * 2 + core) * 2 + (low ^ (turn % 2))) * 2 + mid
 
 
 def fast_local(samples, interp_in, top_blocks, top_pattern, bottom_blocks, bottom_pattern, interp_out):
@@ -340,13 +359,12 @@
     total = pltpu.VMEM((rank, rhs_count, LANES), jnp.float32)
     wide = pltpu.VMEM((rank * rank, LANES), jnp.float32)
     packed = pltpu.VMEM((2, fold, rank // fold, rhs_count, LANES), jnp.bfloat16)
-    whole, anywhere = pl.BlockSpec(memory_space=pltpu.VMEM), pl.BlockSpec(memory_space=pl.ANY)
-
-    def level_nears(blocks, pattern, level, bit, order):
+
+    def level_nears(blocks, pattern, level, bit, order, extra=()):
         return {
             flip: run(
                 functools.partial(near_kernel, level, bit, flip), [partial, spread_out],
-                (blocks, pattern, current[flip]) + ((current[1 - flip],) if place < len(order) - 1 else ()), (wide,),
+                (blocks, pattern, current[flip]) + ((current[1 - flip], *extra) if place < len(order) - 1 else ()), (wide,),
             )
             for place, flip in enumerate(order)
         }
@@ -362,23 +380,19 @@
     current = {}
     current[1], current[0] = run(
         coeff_kernel, [state, state], (interp_in, samples),
-        (
-            pltpu.VMEM((4, rank, depth // 2, LANES), jnp.bfloat16),
-            pltpu.VMEM((4, depth // 2, rhs_count, LANES), jnp.bfloat16),
-            pltpu.VMEM((rank * depth // 2, LANES), jnp.float32), total, pltpu.SemaphoreType.DMA((8,)),
-        ),
-        4, [anywhere] * 2, limit=START_LIMIT,
-    )
+        (pltpu.VMEM((rank * depth // 2, LANES), jnp.float32), pltpu.VMEM((2, rank, rhs_count, LANES), jnp.float32)),
+        4, cost=START_COST,
+    )
+    share_rows = 2 * rank + rank * rhs_count // (2 * rank)
+    shared_shape = jax.ShapeDtypeStruct((share_rows, 2 * rank, LANES), jnp.bfloat16)
+    shared = run(functools.partial(share_kernel, 3), shared_shape, (top_blocks, top_pattern, bottom_blocks, bottom_pattern))
     for level in range(3):
         bit = 3 - level
         partner = {flip: swapped(current[flip], bit) for flip in (1, 0)}
-        near = level_nears(top_blocks, top_pattern, level, bit, (1, 0))
+        near = level_nears(top_blocks, top_pattern, level, bit, (1, 0), (shared,) if level == 1 else ())
         if level < 2:
             current = level_fars(top_pattern, level, bit, (1, 0))
 
-    share_rows = 2 * rank + rank * rhs_count // (2 * rank)
-    shared_shape = jax.ShapeDtypeStruct((share_rows, 2 * rank, LANES), jnp.bfloat16)
-    shared = run(functools.partial(share_kernel, 3), shared_shape, (top_blocks, top_pattern, bottom_blocks, bottom_pattern))
     shared = run(
         functools.partial(send_kernel, 2, 1, 1), shared_shape, (top_pattern, partner[1], *near[1], shared), aliases={4: 0},
     )
@@ -404,28 +418,28 @@
     current = {0: first}
     partner = {0: swapped(first, 1)}
     near = level_nears(bottom_blocks, bottom_pattern, 1, 1, (0,))
-    current[1] = swapped(run(other_kernel, state, (other_wide, states, near[0][0]), (total,), 2), 0)
+    current[1] = swapped(run(other_kernel, state, (other_wide, states), (total,), 2), 0)
     partner[1] = swapped(current[1], 1)
     near.update(level_nears(bottom_blocks, bottom_pattern, 1, 1, (1,)))
     current = level_fars(bottom_pattern, 1, 1, (0, 1))
+    image_spread = jax.ShapeDtypeStruct((out_depth * rank, LANES), jnp.float32)
+    image_wide = run(interp_kernel, [image_spread] * 2, (interp_out,))
     for level in (2, 3):
         partner = {flip: swapped(current[flip], level) for flip in (0, 1)}
-        near = level_nears(bottom_blocks, bottom_pattern, level, level, (0, 1))
+        near = level_nears(bottom_blocks, bottom_pattern, level, level, (0, 1), image_wide)
         if level == 2:
             current = level_fars(bottom_pattern, level, level, (0, 1))
 
-    image_spread = jax.ShapeDtypeStruct((out_depth * rank, LANES), jnp.float32)
-    image_wide = run(interp_kernel, [image_spread] * 2, (interp_out, near[0][0]))
-    image = jax.ShapeDtypeStruct((out_depth, rhs_count, box_count), jnp.bfloat16)
-    out = ()
-    for flip in (0, 1):
-        operands = (bottom_pattern, near[flip][1], image_wide[flip], partner[flip], near[flip][0])
-        out = (run(
-            functools.partial(last_kernel, 3, 3, flip), image, operands + out,
-            (pltpu.VMEM((out_depth, rhs_count, LANES), jnp.bfloat16), total, pltpu.SemaphoreType.DMA((4,))), 3,
-            [whole] * 5 + [anywhere] * flip, [anywhere], {5: 0} if flip else None,
-        ),)
-    return out[0]
+    ready = run(
+        functools.partial(first_image_kernel, 3, 3), jax.ShapeDtypeStruct((out_depth, rhs_count, LANES), jnp.float32),
+        (bottom_pattern, near[0][1], image_wide[0], partner[0], near[0][0]), (total,), 3,
+    )
+    return run(
+        functools.partial(last_kernel, 3, 3), jax.ShapeDtypeStruct((out_depth, rhs_count, box_count), jnp.bfloat16),
+        (bottom_pattern, near[1][1], image_wide[1], partner[1], near[1][0], ready),
+        (pltpu.VMEM((out_depth, rhs_count, box_count), jnp.bfloat16), total, pltpu.SemaphoreType.DMA((4,))), 3,
+        out_specs=[pl.BlockSpec(memory_space=pl.ANY)],
+    )
 
 
 def contract(weights, state):

time: 67.1 us -> 81.1 us (1.21)
  Pallas kernels: 23.1 us -> 44.1 us
  starting transfers between devices: 29.7 us -> 24.9 us
  waiting for transfers between devices: 9.22 us -> 7.04 us
    pallas_call x32, Pallas kernels: 23.1 us -> 44.1 us  [run(): pl.pallas_call(kernel, out_shape=shapes, in_specs=in_specs or [whole] * l...]
    ppermute x18, starting transfers between devices: 29.7 us -> 24.9 us  [permuted(): return lax.ppermute(value, 'leaf', pairs)]
    ppermute x18, waiting for transfers between devices: 9.22 us -> 7.04 us  [permuted(): return lax.ppermute(value, 'leaf', pairs)]
    unnamed x18 -> x16, local copies, waits for them, and re-layouts: 4.56 us -> 4.4 us
  transfers between devices with their start and end apart: 18 -> 18, of which waited for: 7 -> 5; matrix products, arithmetic and copies ran while one was open for 0% -> 0% of each run, Pallas kernels for 19% -> 41%
where the time goes in v5:
time: 81.1 us; the launch traced here: 80.9 us
  Pallas kernels  44.1 us (54%)
  starting transfers between devices  24.9 us (31%)
  waiting for transfers between devices  7.04 us (9%)
  local copies, waits for them, and re-layouts  4.4 us (5%)
    pallas_call x32, Pallas kernels, run(): pl.pallas_call(kernel, out_shape=shapes, in_specs=in_specs or [whole] * l...  44.1 us
    ppermute x18, starting transfers between devices, permuted(): return lax.ppermute(value, 'leaf', pairs)  24.9 us
    ppermute x18, waiting for transfers between devices, permuted(): return lax.ppermute(value, 'leaf', pairs)  7.04 us
    unnamed x16, local copies, waits for them, and re-layouts  4.4 us
  transfers between devices with their start and end apart: 18, of which 5 were waited for; matrix products, arithmetic and copies ran while one was open for 0% of the time, Pallas kernels for 41%

profile of v5, /device:TPU:0, one launch (start us, length us, event | category | flops | bytes accessed | tf_op | source)
XLA Modules:
  0.0 80.9 jit_solution(1832474712779318660)
XLA Ops:
  0.0 1.2 %copy-done.5 = bf16[32,64,256]{2,1,0:T(8,128)(2,1)S(1)} copy-done((bf16[32,64,256]{2,1,0:T(8,128)(2,1)S(1)}, bf16[32,64,256]{2,1,0:T(8,128)(2,1)}, u32[]{:S(2)}) %copy-start.5) | copy-done | bytes 1048600
  1.2 0.9 %copy-done.7 = bf16[64,8,256]{2,1,0:T(8,128)(2,1)S(1)} copy-done((bf16[64,8,256]{2,1,0:T(8,128)(2,1)S(1)}, bf16[64,8,256]{2,1,0:T(8,128)(2,1)}, u32[]{:S(2)}) %copy-start.7) | copy-done | bytes 262168
  2.2 1.8 %shard_map.73 = (bf16[32,8,128]{2,1,0:T(8,128)(2,1)S(1)}, bf16[32,8,128]{2,1,0:T(8,128)(2,1)S(1)}) custom-call(bf16[32,64,256]{2,1,0:T(8,128)(2,1)S(1)} %copy-done.5, bf16[64,8,256]{2,1,0:T(8,128)(2,1)S(1)} %copy-done.7), custom_call_target="tpu_custom_call" | custom-call | flops 16777216 | bytes 16777216 | tf_op jit(solution)/shard_map/pallas_call | solution.py:322
  4.0 4.1 %collective-permute-start = (bf16[32,8,128]{2,1,0:T(8,128)(2,1)S(1)}, bf16[32,8,128]{2,1,0:T(8,128)(2,1)S(1)}, u32[]{:S(2)}, u32[]{:S(2)}) collective-permute-start(bf16[32,8,128]{2,1,0:T(8,128)(2,1)S(1)} %get-tuple-element.43.state), channel_id=1, source_target_pairs={{0,8},{1,9},{2,10},{3,11},{4,12},{5,13},{6,14},{7,15},{8,0},{9,1},... | collective-permute-start | bytes 196616 | tf_op jit(solution)/shard_map/ppermute | solution.py:337
  8.1 0.1 collective-permute-start.2
  8.2 2.2 %copy-done = bf16[4,32,64,256]{3,2,1,0:T(8,128)(2,1)S(1)} copy-done((bf16[4,32,64,256]{3,2,1,0:T(8,128)(2,1)S(1)}, bf16[4,32,64,256]{3,2,1,0:T(8,128)(2,1)}, u32[]{:S(2)}) %copy-start) | copy-done | bytes 4194328
  10.4 1.7 %shard_map.74 = (f32[32,8,128]{2,1,0:T(8,128)S(1)}, f32[1024,128]{1,0:T(8,128)S(1)}) custom-call(bf16[4,32,64,256]{3,2,1,0:T(8,128)(2,1)S(1)} %copy-done, s32[4,2,256]{2,1,0:T(2,128)S(1)} %copy-done.3, bf16[32,8,128]{2,1,0:T(8,128)(2,1)S(1)} %get-tuple-element.43.state, bf16[32,8,128]{2,1,0:T(8,128)(2,1)S(1)} %get-tuple-element.44.rest_0_.state), custom_call_target="tpu_custom_call" | custom-call | flops 1024 | bytes 1024 | tf_op jit(solution)/shard_map/pallas_call | solution.py:322
  12.1 0.0 collective-permute-done.partner
  12.1 0.5 shard_map.75.state
  12.6 0.0 copy-start.2
  12.6 0.0 copy-start.4
  12.6 1.9 %collective-permute-start.1 = (bf16[32,8,128]{2,1,0:T(8,128)(2,1)S(1)}, bf16[32,8,128]{2,1,0:T(8,128)(2,1)S(1)}, u32[]{:S(2)}, u32[]{:S(2)}) collective-permute-start(bf16[32,8,128]{2,1,0:T(8,128)(2,1)S(1)} %shard_map.75.state), channel_id=1, source_target_pairs={{0,4},{1,5},{2,6},{3,7},{4,0},{5,1},{6,2},{7,3},{8,12},{9,13},{10,... | collective-permute-start | bytes 196616 | tf_op jit(solution)/shard_map/ppermute | solution.py:337
  14.5 1.7 %shard_map.76 = (f32[32,8,128]{2,1,0:T(8,128)S(1)}, f32[1024,128]{1,0:T(8,128)S(1)}) custom-call(bf16[4,32,64,256]{3,2,1,0:T(8,128)(2,1)S(1)} %copy-done.1, s32[4,2,256]{2,1,0:T(2,128)S(1)} %copy-done.3, bf16[32,8,128]{2,1,0:T(8,128)(2,1)S(1)} %get-tuple-element.44.rest_0_.state), custom_call_target="tpu_custom_call" | custom-call | flops 1024 | bytes 1024 | tf_op jit(solution)/shard_map/pallas_call | solution.py:322
  16.3 2.9 %shard_map.78.rest_1_.shared = bf16[68,64,128]{2,1,0:T(8,128)(2,1)S(1)} custom-call(bf16[4,32,64,256]{3,2,1,0:T(8,128)(2,1)S(1)} %copy-done.1, s32[4,2,256]{2,1,0:T(2,128)S(1)} %copy-done.3, bf16[4,32,64,256]{3,2,1,0:T(8,128)(2,1)S(1)} %copy-done.2, s32[4,2,256]{2,1,0:T(2,128)S(1)} %copy-done.4), custom_call_target="tpu_custom_call" | custom-call | flops 1024 | bytes 1024 | tf_op jit(solution)/shard_map/pallas_call | solution.py:322
  19.2 0.5 shard_map.77.rest_0_.state
  19.7 0.4 collective-permute-start.4
  20.1 1.7 %shard_map.79 = (f32[32,8,128]{2,1,0:T(8,128)S(1)}, f32[1024,128]{1,0:T(8,128)S(1)}) custom-call(bf16[4,32,64,256]{3,2,1,0:T(8,128)(2,1)S(1)} %copy-done.1, s32[4,2,256]{2,1,0:T(2,128)S(1)} %copy-done.3, bf16[32,8,128]{2,1,0:T(8,128)(2,1)S(1)} %shard_map.75.state, bf16[32,8,128]{2,1,0:T(8,128)(2,1)S(1)} %shard_map.77.rest_0_.state, ...), custom_call_target="tpu_custom_call" | custom-call | flops 1024 | bytes 1024 | tf_op jit(solution)/shard_map/pallas_call | solution.py:322
  21.9 0.5 shard_map.80.state
  22.4 1.7 %collective-permute-start.3 = (bf16[32,8,128]{2,1,0:T(8,128)(2,1)S(1)}, bf16[32,8,128]{2,1,0:T(8,128)(2,1)S(1)}, u32[]{:S(2)}, u32[]{:S(2)}) collective-permute-start(bf16[32,8,128]{2,1,0:T(8,128)(2,1)S(1)} %shard_map.80.state), channel_id=1, source_target_pairs={{0,2},{1,3},{2,0},{3,1},{4,6},{5,7},{6,4},{7,5},{8,10},{9,11},{10,... | collective-permute-start | bytes 196616 | tf_op jit(solution)/shard_map/ppermute | solution.py:337
  24.1 1.7 %shard_map.81 = (f32[32,8,128]{2,1,0:T(8,128)S(1)}, f32[1024,128]{1,0:T(8,128)S(1)}) custom-call(bf16[4,32,64,256]{3,2,1,0:T(8,128)(2,1)S(1)} %copy-done.1, s32[4,2,256]{2,1,0:T(2,128)S(1)} %copy-done.3, bf16[32,8,128]{2,1,0:T(8,128)(2,1)S(1)} %shard_map.77.rest_0_.state), custom_call_target="tpu_custom_call" | custom-call | flops 1024 | bytes 1024 | tf_op jit(solution)/shard_map/pallas_call | solution.py:322
  25.8 0.0 collective-permute-done.4.partner
  25.8 0.5 shard_map.82.rest_0_.state
  26.3 1.7 %shard_map.83 = (f32[32,8,128]{2,1,0:T(8,128)S(1)}, f32[1024,128]{1,0:T(8,128)S(1)}) custom-call(bf16[4,32,64,256]{3,2,1,0:T(8,128)(2,1)S(1)} %copy-done.1, s32[4,2,256]{2,1,0:T(2,128)S(1)} %copy-done.3, bf16[32,8,128]{2,1,0:T(8,128)(2,1)S(1)} %shard_map.80.state, bf16[32,8,128]{2,1,0:T(8,128)(2,1)S(1)} %shard_map.82.rest_0_.state), custom_call_target="tpu_custom_call" | custom-call | flops 1024 | bytes 1024 | tf_op jit(solution)/shard_map/pallas_call | solution.py:322
  28.1 0.5 shard_map.84
  28.5 0.1 collective-permute-start.5
  28.6 0.5 collective-permute-start.6
  29.1 1.7 %shard_map.86 = (f32[32,8,128]{2,1,0:T(8,128)S(1)}, f32[1024,128]{1,0:T(8,128)S(1)}) custom-call(bf16[4,32,64,256]{3,2,1,0:T(8,128)(2,1)S(1)} %copy-done.1, s32[4,2,256]{2,1,0:T(2,128)S(1)} %copy-done.3, bf16[32,8,128]{2,1,0:T(8,128)(2,1)S(1)} %shard_map.82.rest_0_.state), custom_call_target="tpu_custom_call" | custom-call | flops 1024 | bytes 1024 | tf_op jit(solution)/shard_map/pallas_call | solution.py:322
  30.8 2.3 %collective-permute-done.6.partner = bf16[32,8,128]{2,1,0:T(8,128)(2,1)S(1)} collective-permute-done((bf16[32,8,128]{2,1,0:T(8,128)(2,1)S(1)}, bf16[32,8,128]{2,1,0:T(8,128)(2,1)S(1)}, u32[]{:S(2)}, u32[]{:S(2)}) %collective-permute-start.6) | collective-permute-done | bytes 65568 | tf_op jit(solution)/shard_map/ppermute | solution.py:337
  33.1 0.5 shard_map.87.state
  33.6 0.0 collective-permute-done.5.shared
  33.6 2.2 %shard_map.88 = (f32[2,32,8,128]{3,2,1,0:T(8,128)S(1)}, f32[2,1024,128]{2,1,0:T(8,128)S(1)}) custom-call(bf16[4,32,64,256]{3,2,1,0:T(8,128)(2,1)S(1)} %copy-done.1, s32[4,2,256]{2,1,0:T(2,128)S(1)} %copy-done.3, bf16[68,64,128]{2,1,0:T(8,128)(2,1)S(1)} %collective-permute-done.5.shared, bf16[32,8,128]{2,1,0:T(8,128)(2,1)S(1)} %shard_map.87.state), custom_call_target="tpu_custom_call" | custom-call | flops 2048 | bytes 2048 | tf_op jit(solution)/shard_map/pallas_call | solution.py:322
  35.9 1.4 %shard_map.89 = (bf16[2,2,4,8,128]{4,3,2,1,0:T(8,128)(2,1)S(1)}, bf16[2,2,4,8,128]{4,3,2,1,0:T(8,128)(2,1)S(1)}, bf16[2,2,4,8,128]{4,3,2,1,0:T(8,128)(2,1)S(1)}, bf16[2,2,4,8,128]{4,3,2,1,0:T(8,128)(2,1)S(1)}) custom-call(s32[4,2,256]{2,1,0:T(2,128)S(1)} %copy-done.3, f32[2,1024,128]{2,1,0:T(8,128)S(1)} %get-tuple-element.59.wide, ...), custom_call_target="tpu_custom_call" | custom-call | flops 2048 | bytes 2048 | tf_op jit(solution)/shard_map/pallas_call | solution.py:322
  37.3 3.1 %collective-permute-start.10 = (bf16[2,2,4,8,128]{4,3,2,1,0:T(8,128)(2,1)S(1)}, bf16[2,2,4,8,128]{4,3,2,1,0:T(8,128)(2,1)S(1)}, u32[]{:S(2)}, u32[]{:S(2)}) collective-permute-start(bf16[2,2,4,8,128]{4,3,2,1,0:T(8,128)(2,1)S(1)} %get-tuple-element.64), channel_id=1, source_target_pairs={{0,10},{1,14},{2,8},{3,12},{4,11},{5,15},{6,9},{7,13},{8,2},{9,6},... | collective-permute-start | bytes 98312 | tf_op jit(solution)/shard_map/ppermute | solution.py:337
  40.4 0.7 collective-permute-start.7
  41.1 1.6 %collective-permute-start.8 = (bf16[2,2,4,8,128]{4,3,2,1,0:T(8,128)(2,1)S(1)}, bf16[2,2,4,8,128]{4,3,2,1,0:T(8,128)(2,1)S(1)}, u32[]{:S(2)}, u32[]{:S(2)}) collective-permute-start(bf16[2,2,4,8,128]{4,3,2,1,0:T(8,128)(2,1)S(1)} %get-tuple-element.62), channel_id=1, source_target_pairs={{0,2},{1,6},{2,0},{3,4},{4,3},{5,7},{6,1},{7,5},{8,10},{9,14},{10,... | collective-permute-start | bytes 98312 | tf_op jit(solution)/shard_map/ppermute | solution.py:337
  42.6 0.0 collective-permute-start.9
  42.6 1.4 %shard_map.85 = (f32[2,1024,128]{2,1,0:T(8,128)S(1)}, f32[2,1024,128]{2,1,0:T(8,128)S(1)}) custom-call(bf16[4,32,64,256]{3,2,1,0:T(8,128)(2,1)S(1)} %copy-done.2, bf16[68,64,128]{2,1,0:T(8,128)(2,1)S(1)} %collective-permute-done.5.shared), custom_call_target="tpu_custom_call" | custom-call | flops 1024 | bytes 1024 | tf_op jit(solution)/shard_map/pallas_call | solution.py:322
  44.1 1.0 %collective-permute-done.8.rest_1_ = bf16[2,2,4,8,128]{4,3,2,1,0:T(8,128)(2,1)S(1)} collective-permute-done((bf16[2,2,4,8,128]{4,3,2,1,0:T(8,128)(2,1)S(1)}, bf16[2,2,4,8,128]{4,3,2,1,0:T(8,128)(2,1)S(1)}, u32[]{:S(2)}, u32[]{:S(2)}) %collective-permute-start.8) | collective-permute-done | bytes 32800 | tf_op jit(solution)/shard_map/ppermute | solution.py:337
  45.0 2.4 %collective-permute-done.9.rest_2_ = bf16[2,2,4,8,128]{4,3,2,1,0:T(8,128)(2,1)S(1)} collective-permute-done((bf16[2,2,4,8,128]{4,3,2,1,0:T(8,128)(2,1)S(1)}, bf16[2,2,4,8,128]{4,3,2,1,0:T(8,128)(2,1)S(1)}, u32[]{:S(2)}, u32[]{:S(2)}) %collective-permute-start.9) | collective-permute-done | bytes 32800 | tf_op jit(solution)/shard_map/ppermute | solution.py:337
  47.5 1.0 %shard_map.90 = (bf16[32,8,128]{2,1,0:T(8,128)(2,1)S(1)}, bf16[2,32,8,128]{3,2,1,0:T(8,128)(2,1)S(1)}) custom-call(s32[4,2,256]{2,1,0:T(2,128)S(1)} %copy-done.4, f32[2,1024,128]{2,1,0:T(8,128)S(1)} %get-tuple-element.56.wide, bf16[2,2,4,8,128]{4,3,2,1,0:T(8,128)(2,1)S(1)} %collective-permute-done.7.rest_0_, ...), custom_call_target="tpu_custom_call" | custom-call | flops 2048 | bytes 2048 | tf_op jit(solution)/shard_map/pallas_call | solution.py:322
  48.5 0.8 shard_map.91
  49.3 4.1 %collective-permute-start.11 = (bf16[32,8,128]{2,1,0:T(8,128)(2,1)S(1)}, bf16[32,8,128]{2,1,0:T(8,128)(2,1)S(1)}, u32[]{:S(2)}, u32[]{:S(2)}) collective-permute-start(bf16[32,8,128]{2,1,0:T(8,128)(2,1)S(1)} %shard_map.91), channel_id=1, source_target_pairs={{0,1},{1,0},{2,3},{3,2},{4,5},{5,4},{6,7},{7,6},{8,9},{9,8},{10,11... | collective-permute-start | bytes 196616 | tf_op jit(solution)/shard_map/ppermute | solution.py:337
  53.3 0.5 collective-permute-start.15
  53.8 0.4 collective-permute-done.11.state
  54.2 1.1 %collective-permute-start.12 = (bf16[32,8,128]{2,1,0:T(8,128)(2,1)S(1)}, bf16[32,8,128]{2,1,0:T(8,128)(2,1)S(1)}, u32[]{:S(2)}, u32[]{:S(2)}) collective-permute-start(bf16[32,8,128]{2,1,0:T(8,128)(2,1)S(1)} %collective-permute-done.11.state), channel_id=1, source_target_pairs={{0,2},{1,3},{2,0},{3,1},{4,6},{5,7},{6,4},{7,5},{8,10},{9,11},{10,... | collective-permute-start | bytes 196616 | tf_op jit(solution)/shard_map/ppermute | solution.py:337
  55.4 1.7 %shard_map.98 = (f32[32,8,128]{2,1,0:T(8,128)S(1)}, f32[1024,128]{1,0:T(8,128)S(1)}) custom-call(bf16[4,32,64,256]{3,2,1,0:T(8,128)(2,1)S(1)} %copy-done.2, s32[4,2,256]{2,1,0:T(2,128)S(1)} %copy-done.4, bf16[32,8,128]{2,1,0:T(8,128)(2,1)S(1)} %get-tuple-element.73.state), custom_call_target="tpu_custom_call" | custom-call | flops 1024 | bytes 1024 | tf_op jit(solution)/shard_map/pallas_call | solution.py:322
  57.1 0.9 %collective-permute-done.15.partner = bf16[32,8,128]{2,1,0:T(8,128)(2,1)S(1)} collective-permute-done((bf16[32,8,128]{2,1,0:T(8,128)(2,1)S(1)}, bf16[32,8,128]{2,1,0:T(8,128)(2,1)S(1)}, u32[]{:S(2)}, u32[]{:S(2)}) %collective-permute-start.15) | collective-permute-done | bytes 65568 | tf_op jit(solution)/shard_map/ppermute | solution.py:337
  58.0 0.5 shard_map.99.state
  58.5 0.1 collective-permute-start.16
  58.6 0.0 copy-start.6
  58.6 1.7 %shard_map.92 = (f32[32,8,128]{2,1,0:T(8,128)S(1)}, f32[1024,128]{1,0:T(8,128)S(1)}) custom-call(bf16[4,32,64,256]{3,2,1,0:T(8,128)(2,1)S(1)} %copy-done.2, s32[4,2,256]{2,1,0:T(2,128)S(1)} %copy-done.4, bf16[32,8,128]{2,1,0:T(8,128)(2,1)S(1)} %collective-permute-done.11.state), custom_call_target="tpu_custom_call" | custom-call | flops 1024 | bytes 1024 | tf_op jit(solution)/shard_map/pallas_call | solution.py:322
  60.4 0.5 shard_map.93.state.rest_0_
  60.9 2.0 %collective-permute-start.13 = (bf16[32,8,128]{2,1,0:T(8,128)(2,1)S(1)}, bf16[32,8,128]{2,1,0:T(8,128)(2,1)S(1)}, u32[]{:S(2)}, u32[]{:S(2)}) collective-permute-start(bf16[32,8,128]{2,1,0:T(8,128)(2,1)S(1)} %shard_map.93.state.rest_0_), channel_id=1, source_target_pairs={{0,4},{1,5},{2,6},{3,7},{4,0},{5,1},{6,2},{7,3},{8,12},{9,13},{10,... | collective-permute-start | bytes 196616 | tf_op jit(solution)/shard_map/ppermute | solution.py:337
  62.9 2.6 %shard_map.97 = (f32[2048,128]{1,0:T(8,128)S(1)}, f32[2048,128]{1,0:T(8,128)S(1)}) custom-call(bf16[64,32,256]{2,1,0:T(8,128)(2,1)S(1)} %copy-done.6), custom_call_target="tpu_custom_call" | custom-call | flops 1024 | bytes 1024 | tf_op jit(solution)/shard_map/pallas_call | solution.py:322
  65.5 1.7 %shard_map.94 = (f32[32,8,128]{2,1,0:T(8,128)S(1)}, f32[1024,128]{1,0:T(8,128)S(1)}) custom-call(bf16[4,32,64,256]{3,2,1,0:T(8,128)(2,1)S(1)} %copy-done.2, s32[4,2,256]{2,1,0:T(2,128)S(1)} %copy-done.4, bf16[32,8,128]{2,1,0:T(8,128)(2,1)S(1)} %shard_map.93.state.rest_0_), custom_call_target="tpu_custom_call" | custom-call | flops 1024 | bytes 1024 | tf_op jit(solution)/shard_map/pallas_call | solution.py:322
  67.3 1.8 %shard_map.100 = (f32[32,8,128]{2,1,0:T(8,128)S(1)}, f32[1024,128]{1,0:T(8,128)S(1)}) custom-call(bf16[4,32,64,256]{3,2,1,0:T(8,128)(2,1)S(1)} %copy-done.2, s32[4,2,256]{2,1,0:T(2,128)S(1)} %copy-done.4, bf16[32,8,128]{2,1,0:T(8,128)(2,1)S(1)} %shard_map.99.state, bf16[32,8,128]{2,1,0:T(8,128)(2,1)S(1)} %shard_map.93.state.rest_0_, ...), custom_call_target="tpu_custom_call" | custom-call | flops 1024 | bytes 1024 | tf_op jit(solution)/shard_map/pallas_call | solution.py:322
  69.0 0.5 shard_map.101.state
  69.5 0.1 collective-permute-start.17
  69.6 0.5 shard_map.95.state.rest_0_
  70.1 3.0 %collective-permute-start.14 = (bf16[32,8,128]{2,1,0:T(8,128)(2,1)S(1)}, bf16[32,8,128]{2,1,0:T(8,128)(2,1)S(1)}, u32[]{:S(2)}, u32[]{:S(2)}) collective-permute-start(bf16[32,8,128]{2,1,0:T(8,128)(2,1)S(1)} %shard_map.95.state.rest_0_), channel_id=1, source_target_pairs={{0,8},{1,9},{2,10},{3,11},{4,12},{5,13},{6,14},{7,15},{8,0},{9,1},... | collective-permute-start | bytes 196616 | tf_op jit(solution)/shard_map/ppermute | solution.py:337
  73.1 1.7 %shard_map.102 = (f32[32,8,128]{2,1,0:T(8,128)S(1)}, f32[1024,128]{1,0:T(8,128)S(1)}) custom-call(bf16[4,32,64,256]{3,2,1,0:T(8,128)(2,1)S(1)} %copy-done.2, s32[4,2,256]{2,1,0:T(2,128)S(1)} %copy-done.4, bf16[32,8,128]{2,1,0:T(8,128)(2,1)S(1)} %shard_map.101.state, bf16[32,8,128]{2,1,0:T(8,128)(2,1)S(1)} %shard_map.95.state.rest_0_, ...), custom_call_target="tpu_custom_call" | custom-call | flops 1024 | bytes 1024 | tf_op jit(solution)/shard_map/pallas_call | solution.py:322
  74.8 1.8 %shard_map.96 = (f32[32,8,128]{2,1,0:T(8,128)S(1)}, f32[1024,128]{1,0:T(8,128)S(1)}) custom-call(bf16[4,32,64,256]{3,2,1,0:T(8,128)(2,1)S(1)} %copy-done.2, s32[4,2,256]{2,1,0:T(2,128)S(1)} %copy-done.4, bf16[32,8,128]{2,1,0:T(8,128)(2,1)S(1)} %shard_map.95.state.rest_0_), custom_call_target="tpu_custom_call" | custom-call | flops 1024 | bytes 1024 | tf_op jit(solution)/shard_map/pallas_call | solution.py:322
  76.6 1.2 %shard_map.103.ready = f32[64,8,128]{2,1,0:T(8,128)S(1)} custom-call(s32[4,2,256]{2,1,0:T(2,128)S(1)} %copy-done.4, f32[1024,128]{1,0:T(8,128)S(1)} %get-tuple-element.79.wide, f32[2048,128]{1,0:T(8,128)S(1)} %get-tuple-element.76.rest_1_.image_wide, bf16[32,8,128]{2,1,0:T(8,128)(2,1)S(1)} %collective-permute-done.17.partner, ...), custom_call_target="tpu_custom_call" | custom-call | flops 3072 | bytes 3072 | tf_op jit(solution)/shard_map/pallas_call | solution.py:322
  77.8 3.0 %shard_map.104 = bf16[64,8,256]{2,1,0:T(8,128)(2,1)} custom-call(s32[4,2,256]{2,1,0:T(2,128)S(1)} %copy-done.4, f32[1024,128]{1,0:T(8,128)S(1)} %get-tuple-element.70.wide, f32[2048,128]{1,0:T(8,128)S(1)} %get-tuple-element.71.rest_2_.image_wide, bf16[32,8,128]{2,1,0:T(8,128)(2,1)S(1)} %collective-permute-done.14.partner, ...), custom_call_target="tpu_custom_call" | custom-call | flops 3072 | bytes 3072 | tf_op jit(solution)/shard_map/pallas_call | solution.py:322
  (20 shorter events, 0.0 us)
Async XLA Ops:
  0.0 8.2 %copy-start.3 = (s32[4,2,256]{2,1,0:T(2,128)S(1)}, s32[4,2,256]{2,1,0:T(2,128)}, u32[]{:S(2)}) copy-start(s32[4,2,256]{2,1,0:T(2,128)} %pattern.40) | copy-start | bytes 24580
  0.0 1.2 %copy-start.5 = (bf16[32,64,256]{2,1,0:T(8,128)(2,1)S(1)}, bf16[32,64,256]{2,1,0:T(8,128)(2,1)}, u32[]{:S(2)}) copy-start(bf16[32,64,256]{2,1,0:T(8,128)(2,1)} %interp.2) | copy-start | bytes 3145732
  1.2 0.9 %copy-start.7 = (bf16[64,8,256]{2,1,0:T(8,128)(2,1)S(1)}, bf16[64,8,256]{2,1,0:T(8,128)(2,1)}, u32[]{:S(2)}) copy-start(bf16[64,8,256]{2,1,0:T(8,128)(2,1)} %samples.1) | copy-start | bytes 786436
  4.0 8.1 %collective-permute-start = (bf16[32,8,128]{2,1,0:T(8,128)(2,1)S(1)}, bf16[32,8,128]{2,1,0:T(8,128)(2,1)S(1)}, u32[]{:S(2)}, u32[]{:S(2)}) collective-permute-start(bf16[32,8,128]{2,1,0:T(8,128)(2,1)S(1)} %get-tuple-element.43.state), channel_id=1, source_target_pairs={{0,8},{1,9},{2,10},{3,11},{4,12},{5,13},{6,14},{7,15},{8,0},{9,1},... | collective-permute-start | bytes 196616 | tf_op jit(solution)/shard_map/ppermute | solution.py:337
  8.1 11.1 %collective-permute-start.2 = (bf16[32,8,128]{2,1,0:T(8,128)(2,1)S(1)}, bf16[32,8,128]{2,1,0:T(8,128)(2,1)S(1)}, u32[]{:S(2)}, u32[]{:S(2)}) collective-permute-start(bf16[32,8,128]{2,1,0:T(8,128)(2,1)S(1)} %get-tuple-element.44.rest_0_.state), channel_id=1, source_target_pairs={{0,8},{1,9},{2,10},{3,11},{4,12},{5,13},{6,14},{7,15},{8,0},{9,1},... | collective-permute-start | bytes 196616 | tf_op jit(solution)/shard_map/ppermute | solution.py:337
  8.2 2.2 %copy-start = (bf16[4,32,64,256]{3,2,1,0:T(8,128)(2,1)S(1)}, bf16[4,32,64,256]{3,2,1,0:T(8,128)(2,1)}, u32[]{:S(2)}) copy-start(bf16[4,32,64,256]{3,2,1,0:T(8,128)(2,1)} %blocks.21) | copy-start | bytes 12582916
  10.4 4.2 %copy-start.1 = (bf16[4,32,64,256]{3,2,1,0:T(8,128)(2,1)S(1)}, bf16[4,32,64,256]{3,2,1,0:T(8,128)(2,1)}, u32[]{:S(2)}) copy-start(bf16[4,32,64,256]{3,2,1,0:T(8,128)(2,1)} %blocks.21) | copy-start | bytes 12582916
  12.6 3.7 %copy-start.2 = (bf16[4,32,64,256]{3,2,1,0:T(8,128)(2,1)S(1)}, bf16[4,32,64,256]{3,2,1,0:T(8,128)(2,1)}, u32[]{:S(2)}) copy-start(bf16[4,32,64,256]{3,2,1,0:T(8,128)(2,1)} %blocks.27) | copy-start | bytes 12582916
  12.6 3.7 %copy-start.4 = (s32[4,2,256]{2,1,0:T(2,128)S(1)}, s32[4,2,256]{2,1,0:T(2,128)}, u32[]{:S(2)}) copy-start(s32[4,2,256]{2,1,0:T(2,128)} %pattern.53) | copy-start | bytes 24580
  12.6 9.2 %collective-permute-start.1 = (bf16[32,8,128]{2,1,0:T(8,128)(2,1)S(1)}, bf16[32,8,128]{2,1,0:T(8,128)(2,1)S(1)}, u32[]{:S(2)}, u32[]{:S(2)}) collective-permute-start(bf16[32,8,128]{2,1,0:T(8,128)(2,1)S(1)} %shard_map.75.state), channel_id=1, source_target_pairs={{0,4},{1,5},{2,6},{3,7},{4,0},{5,1},{6,2},{7,3},{8,12},{9,13},{10,... | collective-permute-start | bytes 196616 | tf_op jit(solution)/shard_map/ppermute | solution.py:337
  19.7 6.1 %collective-permute-start.4 = (bf16[32,8,128]{2,1,0:T(8,128)(2,1)S(1)}, bf16[32,8,128]{2,1,0:T(8,128)(2,1)S(1)}, u32[]{:S(2)}, u32[]{:S(2)}) collective-permute-start(bf16[32,8,128]{2,1,0:T(8,128)(2,1)S(1)} %shard_map.77.rest_0_.state), channel_id=1, source_target_pairs={{0,4},{1,5},{2,6},{3,7},{4,0},{5,1},{6,2},{7,3},{8,12},{9,13},{10,... | collective-permute-start | bytes 196616 | tf_op jit(solution)/shard_map/ppermute | solution.py:337
  22.4 5.7 %collective-permute-start.3 = (bf16[32,8,128]{2,1,0:T(8,128)(2,1)S(1)}, bf16[32,8,128]{2,1,0:T(8,128)(2,1)S(1)}, u32[]{:S(2)}, u32[]{:S(2)}) collective-permute-start(bf16[32,8,128]{2,1,0:T(8,128)(2,1)S(1)} %shard_map.80.state), channel_id=1, source_target_pairs={{0,2},{1,3},{2,0},{3,1},{4,6},{5,7},{6,4},{7,5},{8,10},{9,11},{10,... | collective-permute-start | bytes 196616 | tf_op jit(solution)/shard_map/ppermute | solution.py:337
  28.5 5.1 %collective-permute-start.5 = (bf16[68,64,128]{2,1,0:T(8,128)(2,1)S(1)}, bf16[68,64,128]{2,1,0:T(8,128)(2,1)S(1)}, u32[]{:S(2)}, u32[]{:S(2)}) collective-permute-start(bf16[68,64,128]{2,1,0:T(8,128)(2,1)S(1)} %shard_map.84), channel_id=1, source_target_pairs={{0,1},{1,0},{2,3},{3,2},{4,5},{5,4},{6,7},{7,6},{8,9},{9,8},{10,11... | collective-permute-start | bytes 3342344 | tf_op jit(solution)/shard_map/ppermute | solution.py:337
  28.6 4.5 %collective-permute-start.6 = (bf16[32,8,128]{2,1,0:T(8,128)(2,1)S(1)}, bf16[32,8,128]{2,1,0:T(8,128)(2,1)S(1)}, u32[]{:S(2)}, u32[]{:S(2)}) collective-permute-start(bf16[32,8,128]{2,1,0:T(8,128)(2,1)S(1)} %shard_map.82.rest_0_.state), channel_id=1, source_target_pairs={{0,2},{1,3},{2,0},{3,1},{4,6},{5,7},{6,4},{7,5},{8,10},{9,11},{10,... | collective-permute-start | bytes 196616 | tf_op jit(solution)/shard_map/ppermute | solution.py:337
  37.3 6.8 %collective-permute-start.10 = (bf16[2,2,4,8,128]{4,3,2,1,0:T(8,128)(2,1)S(1)}, bf16[2,2,4,8,128]{4,3,2,1,0:T(8,128)(2,1)S(1)}, u32[]{:S(2)}, u32[]{:S(2)}) collective-permute-start(bf16[2,2,4,8,128]{4,3,2,1,0:T(8,128)(2,1)S(1)} %get-tuple-element.64), channel_id=1, source_target_pairs={{0,10},{1,14},{2,8},{3,12},{4,11},{5,15},{6,9},{7,13},{8,2},{9,6},... | collective-permute-start | bytes 98312 | tf_op jit(solution)/shard_map/ppermute | solution.py:337
  40.4 3.7 %collective-permute-start.7 = (bf16[2,2,4,8,128]{4,3,2,1,0:T(8,128)(2,1)S(1)}, bf16[2,2,4,8,128]{4,3,2,1,0:T(8,128)(2,1)S(1)}, u32[]{:S(2)}, u32[]{:S(2)}) collective-permute-start(bf16[2,2,4,8,128]{4,3,2,1,0:T(8,128)(2,1)S(1)} %get-tuple-element.61), channel_id=1, source_target_pairs={{0,0},{1,4},{2,2},{3,6},{4,1},{5,5},{6,3},{7,7},{8,8},{9,12},{10,1... | collective-permute-start | bytes 98312 | tf_op jit(solution)/shard_map/ppermute | solution.py:337
  41.1 4.0 %collective-permute-start.8 = (bf16[2,2,4,8,128]{4,3,2,1,0:T(8,128)(2,1)S(1)}, bf16[2,2,4,8,128]{4,3,2,1,0:T(8,128)(2,1)S(1)}, u32[]{:S(2)}, u32[]{:S(2)}) collective-permute-start(bf16[2,2,4,8,128]{4,3,2,1,0:T(8,128)(2,1)S(1)} %get-tuple-element.62), channel_id=1, source_target_pairs={{0,2},{1,6},{2,0},{3,4},{4,3},{5,7},{6,1},{7,5},{8,10},{9,14},{10,... | collective-permute-start | bytes 98312 | tf_op jit(solution)/shard_map/ppermute | solution.py:337
  42.6 4.8 %collective-permute-start.9 = (bf16[2,2,4,8,128]{4,3,2,1,0:T(8,128)(2,1)S(1)}, bf16[2,2,4,8,128]{4,3,2,1,0:T(8,128)(2,1)S(1)}, u32[]{:S(2)}, u32[]{:S(2)}) collective-permute-start(bf16[2,2,4,8,128]{4,3,2,1,0:T(8,128)(2,1)S(1)} %get-tuple-element.63), channel_id=1, source_target_pairs={{0,8},{1,12},{2,10},{3,14},{4,9},{5,13},{6,11},{7,15},{8,0},{9,4},... | collective-permute-start | bytes 98312 | tf_op jit(solution)/shard_map/ppermute | solution.py:337
  49.3 5.0 %collective-permute-start.11 = (bf16[32,8,128]{2,1,0:T(8,128)(2,1)S(1)}, bf16[32,8,128]{2,1,0:T(8,128)(2,1)S(1)}, u32[]{:S(2)}, u32[]{:S(2)}) collective-permute-start(bf16[32,8,128]{2,1,0:T(8,128)(2,1)S(1)} %shard_map.91), channel_id=1, source_target_pairs={{0,1},{1,0},{2,3},{3,2},{4,5},{5,4},{6,7},{7,6},{8,9},{9,8},{10,11... | collective-permute-start | bytes 196616 | tf_op jit(solution)/shard_map/ppermute | solution.py:337
  53.3 4.7 %collective-permute-start.15 = (bf16[32,8,128]{2,1,0:T(8,128)(2,1)S(1)}, bf16[32,8,128]{2,1,0:T(8,128)(2,1)S(1)}, u32[]{:S(2)}, u32[]{:S(2)}) collective-permute-start(bf16[32,8,128]{2,1,0:T(8,128)(2,1)S(1)} %get-tuple-element.73.state), channel_id=1, source_target_pairs={{0,2},{1,3},{2,0},{3,1},{4,6},{5,7},{6,4},{7,5},{8,10},{9,11},{10,... | collective-permute-start | bytes 196616 | tf_op jit(solution)/shard_map/ppermute | solution.py:337
  54.2 6.1 %collective-permute-start.12 = (bf16[32,8,128]{2,1,0:T(8,128)(2,1)S(1)}, bf16[32,8,128]{2,1,0:T(8,128)(2,1)S(1)}, u32[]{:S(2)}, u32[]{:S(2)}) collective-permute-start(bf16[32,8,128]{2,1,0:T(8,128)(2,1)S(1)} %collective-permute-done.11.state), channel_id=1, source_target_pairs={{0,2},{1,3},{2,0},{3,1},{4,6},{5,7},{6,4},{7,5},{8,10},{9,11},{10,... | collective-permute-start | bytes 196616 | tf_op jit(solution)/shard_map/ppermute | solution.py:337
  58.5 10.5 %collective-permute-start.16 = (bf16[32,8,128]{2,1,0:T(8,128)(2,1)S(1)}, bf16[32,8,128]{2,1,0:T(8,128)(2,1)S(1)}, u32[]{:S(2)}, u32[]{:S(2)}) collective-permute-start(bf16[32,8,128]{2,1,0:T(8,128)(2,1)S(1)} %shard_map.99.state), channel_id=1, source_target_pairs={{0,4},{1,5},{2,6},{3,7},{4,0},{5,1},{6,2},{7,3},{8,12},{9,13},{10,... | collective-permute-start | bytes 196616 | tf_op jit(solution)/shard_map/ppermute | solution.py:337
  58.6 4.3 %copy-start.6 = (bf16[64,32,256]{2,1,0:T(8,128)(2,1)S(1)}, bf16[64,32,256]{2,1,0:T(8,128)(2,1)}, u32[]{:S(2)}) copy-start(bf16[64,32,256]{2,1,0:T(8,128)(2,1)} %interp.3) | copy-start | bytes 3145732
  60.9 8.7 %collective-permute-start.13 = (bf16[32,8,128]{2,1,0:T(8,128)(2,1)S(1)}, bf16[32,8,128]{2,1,0:T(8,128)(2,1)S(1)}, u32[]{:S(2)}, u32[]{:S(2)}) collective-permute-start(bf16[32,8,128]{2,1,0:T(8,128)(2,1)S(1)} %shard_map.93.state.rest_0_), channel_id=1, source_target_pairs={{0,4},{1,5},{2,6},{3,7},{4,0},{5,1},{6,2},{7,3},{8,12},{9,13},{10,... | collective-permute-start | bytes 196616 | tf_op jit(solution)/shard_map/ppermute | solution.py:337
  69.5 7.1 %collective-permute-start.17 = (bf16[32,8,128]{2,1,0:T(8,128)(2,1)S(1)}, bf16[32,8,128]{2,1,0:T(8,128)(2,1)S(1)}, u32[]{:S(2)}, u32[]{:S(2)}) collective-permute-start(bf16[32,8,128]{2,1,0:T(8,128)(2,1)S(1)} %shard_map.101.state), channel_id=1, source_target_pairs={{0,8},{1,9},{2,10},{3,11},{4,12},{5,13},{6,14},{7,15},{8,0},{9,1},... | collective-permute-start | bytes 196616 | tf_op jit(solution)/shard_map/ppermute | solution.py:337
  70.1 7.7 %collective-permute-start.14 = (bf16[32,8,128]{2,1,0:T(8,128)(2,1)S(1)}, bf16[32,8,128]{2,1,0:T(8,128)(2,1)S(1)}, u32[]{:S(2)}, u32[]{:S(2)}) collective-permute-start(bf16[32,8,128]{2,1,0:T(8,128)(2,1)S(1)} %shard_map.95.state.rest_0_), channel_id=1, source_target_pairs={{0,8},{1,9},{2,10},{3,11},{4,12},{5,13},{6,14},{7,15},{8,0},{9,1},... | collective-permute-start | bytes 196616 | tf_op jit(solution)/shard_map/ppermute | solution.py:337

commit v6 on v5

--- a/solution.py
+++ b/solution.py
@@ -10,7 +10,8 @@
 LANES = 128
 GROUP = 4
 KERNEL_COST = 1024
-START_COST = 2**22
+KERNEL_LIMIT = 16 * 2**20
+FETCH_LIMIT = 53_000_000
 
 
 def digits():
@@ -20,16 +21,6 @@
 
 def lanes_of(chunk):
     return pl.ds(pl.multiple_of(chunk * LANES, LANES), LANES)
-
-
-def pick(chunk, read):
-    near, far = read(lanes_of(chunk)).astype(jnp.float32), read(lanes_of(1 - chunk)).astype(jnp.float32)
-    return merge(chunk, near, far)
-
-
-def merge(number, near, far):
-    side = lax.broadcasted_iota(jnp.int32, near.shape, near.ndim - 1) // (LANES // 2)
-    return jnp.where(side == number, near, pltpu.roll(far, LANES // 2, near.ndim - 1))
 
 
 def rows_of(half, rank):
@@ -69,47 +60,59 @@
 
 def level_load(blocks, level, half, chunk):
     rank = blocks.shape[1]
-    return lambda row: pick(chunk, lambda lanes: blocks[level, pl.ds(row, GROUP), rows_of(half, rank), lanes])
+    return lambda row: blocks[level, pl.ds(row, GROUP), rows_of(half, rank), lanes_of(chunk)]
 
 
 def present_of(pattern, level, half, chunk):
-    def read(lanes):
-        pair = [pattern[level, place:place + 1, lanes].astype(jnp.float32) for place in range(2)]
-        return jnp.broadcast_to(jnp.where(half == 0, pair[0], pair[1]), (8, LANES))
-
-    return pick(chunk, read)
-
-
-def coeff_kernel(interp, samples, first, second, wide, total):
-    rank, depth = first.shape[0], samples.shape[0] // 2
-    core = digits()[3]
-    for turn in range(2):
-        lanes = slice(turn * LANES, (turn + 1) * LANES)
-        for half in range(2):
-            part = slice(half * depth, (half + 1) * depth)
-            spread(wide, lambda row: interp[pl.ds(row, GROUP), part, lanes], rank, depth)
-            state = [samples[half * depth + index, :, lanes].astype(jnp.float32) for index in range(depth)]
-
-            def emit(row, value):
-                total[turn, row] = value if half == 0 else total[turn, row] + value
-
-            multiply(wide, state, rank, emit)
-    for row in range(rank):
-        for out, chunk in ((first, 1 - core), (second, core)):
-            out[row] = merge(chunk, total[chunk, row], total[1 - chunk, row]).astype(jnp.bfloat16)
-
-
-def near_kernel(level, bit, flip, blocks, pattern, state, *rest):
-    out, far_wide, wide = rest[-3:]
+    pair = [pattern[level, place:place + 1, lanes_of(chunk)].astype(jnp.float32) for place in range(2)]
+    return jnp.where(half == 0, pair[0], pair[1])
+
+
+def coeff_kernel(flip, interp, samples, out, wide, total):
+    rank, depth = interp.shape[0], interp.shape[1] // 2
+    lanes = lanes_of(digits()[3] ^ flip)
+    for half in range(2):
+        part = slice(half * depth, (half + 1) * depth)
+        spread(wide, lambda row: interp[pl.ds(row, GROUP), part, lanes], rank, depth)
+        state = [samples[half * depth + index, :, lanes].astype(jnp.float32) for index in range(depth)]
+
+        def emit(row, value):
+            if half == 0:
+                total[row] = value
+            else:
+                out[row] = (total[row] + value).astype(jnp.bfloat16)
+
+        multiply(wide, state, rank, emit)
+
+
+def fetch_kernel(level, bit, blocks, after, *rest):
+    held, sem = rest[-2:]
+    copy = pltpu.make_async_copy(blocks.at[pl.ds(level, 1)], held, sem)
+    copy.start()
+    copy.wait()
+    ahead_kernel(0, bit, held, *rest[:-2])
+
+
+def ahead_kernel(level, bit, blocks, *rest):
+    near_wides, far_wides = rest[-4:-2], rest[-2:]
+    rank = blocks.shape[1]
+    places = digits()
+    own = places[3 - bit]
+    for flip in range(2):
+        chunk = places[3] ^ flip
+        spread(near_wides[flip], level_load(blocks, level, own, chunk), rank, rank)
+        spread(far_wides[flip], level_load(blocks, level, 1 - own, chunk), rank, rank)
+
+
+def near_kernel(level, bit, flip, pattern, state, wide, *rest):
+    out = rest[-1]
     places = digits()
     chunk, own = places[3] ^ flip, places[3 - bit]
-    spread(wide, level_load(blocks, level, own, chunk), blocks.shape[1], blocks.shape[1])
-    spread(far_wide, level_load(blocks, level, 1 - own, chunk), blocks.shape[1], blocks.shape[1])
 
     def emit(row, value):
         out[row] = value
 
-    multiply(wide, state_rows(state, present_of(pattern, level, own, chunk)), blocks.shape[1], emit)
+    multiply(wide, state_rows(state, present_of(pattern, level, own, chunk)), out.shape[0], emit)
 
 
 def far_kernel(level, bit, flip, pattern, partner, near, wide, out):
@@ -127,15 +130,14 @@
     chunk = 1 - digits()[3]
     for place, (blocks, pattern, level) in enumerate(((top_blocks, top_pattern, top_level), (bottom_blocks, bottom_pattern, 0))):
         for half in range(2):
-            present = present_of(pattern, level, half, chunk)[:1][None]
-            load = level_load(blocks, level, half, chunk)
-
-            def body(step, carry):
-                span = pl.ds(place * rank + step * GROUP, GROUP)
-                out[span, half * rank:(half + 1) * rank, :] = (load(step * GROUP) * present).astype(jnp.bfloat16)
+            present = present_of(pattern, level, half, chunk)[None]
+
+            def body(row, carry):
+                rows = blocks[level, pl.ds(row, 1), half * rank:(half + 1) * rank, lanes_of(chunk)]
+                out[place * rank + row, half * rank:(half + 1) * rank, :] = (rows.astype(jnp.float32) * present)[0].astype(jnp.bfloat16)
                 return carry
 
-            lax.fori_loop(0, rank // GROUP, body, 0)
+            lax.fori_loop(0, rank, body, 0)
 
 
 def shared_load(shared, place, half):
@@ -202,7 +204,7 @@
 def pair_far_kernel(level, slot, pattern, wide, shared, near, *rest):
     outs, (total, packed) = rest[:4], rest[4:]
     rank = near.shape[1]
-    high, _, low, core = digits()
+    _, mid, low, core = digits()
     rows = sent_rows(shared)
     present = present_of(pattern, level, 1 - core, core)
     fold = LANES // slot
@@ -216,7 +218,7 @@
         for place, piece in enumerate(pieces):
             packed[core ^ box, place] = piece.astype(jnp.bfloat16)
     for turn, out in enumerate(outs):
-        first = ((high ^ (turn // 2)) * 2 + (low ^ (turn % 2))) * 2
+        first = ((mid ^ (turn // 2)) * 2 + (low ^ (turn % 2))) * 2
         for box in range(2):
             for last in range(2):
                 out[box, last] = packed[box, first + last]
@@ -247,12 +249,12 @@
 
 
 def open_kernel(slot, pattern, wide, *rest):
-    pieces, (out, states, total, packed) = rest[:4], rest[4:]
-    high, _, low, core = digits()
+    pieces, (out, states, total, packed) = rest[:4], rest[-4:]
+    _, mid, low, core = digits()
     fold = LANES // slot
     depth = out.shape[0] // fold
     for turn, piece in enumerate(pieces):
-        first = ((high ^ (turn // 2)) * 2 + (low ^ (turn % 2))) * 2
+        first = ((mid ^ (turn // 2)) * 2 + (low ^ (turn % 2))) * 2
         for box in range(2):
             for last in range(2):
                 packed[last, first + box] = piece[box, last]
@@ -270,7 +272,7 @@
 def interp_kernel(interp, first_wide, second_wide):
     core = digits()[3]
     for wide, chunk in ((first_wide, core), (second_wide, 1 - core)):
-        spread(wide, lambda row: pick(chunk, lambda lanes: interp[pl.ds(row, GROUP), :, lanes]), interp.shape[0], interp.shape[1])
+        spread(wide, lambda row: interp[pl.ds(row, GROUP), :, lanes_of(chunk)], interp.shape[0], interp.shape[1])
 
 
 def image_rows(level, bit, flip, pattern, wide, partner, near, total):
@@ -288,34 +290,32 @@
     rows = image_rows(level, bit, 0, pattern, wide, partner, near, total)
 
     def emit(row, value):
-        out[row] = value
+        out[row] = value.astype(jnp.bfloat16)
 
     multiply(image_wide, rows, out.shape[0], emit)
 
 
 def last_kernel(level, bit, pattern, wide, image_wide, partner, near, ready, image, held, total, sems):
     core = digits()[3]
+    copies = [pltpu.make_async_copy(ready, image.at[:, :, lanes_of(core)], sems.at[0])]
+    copies[0].start()
     rows = image_rows(level, bit, 1, pattern, wide, partner, near, total)
-    rank, parts = total.shape[0], sems.shape[0]
+    rank, parts = total.shape[0], sems.shape[0] - 1
     size = held.shape[0] // parts
-    copies = []
     for part in range(parts):
 
         def emit(row, value):
-            place = part * size + row
-            first = ready[place]
-            held[place, :, lanes_of(core)] = merge(core, first, value).astype(jnp.bfloat16)
-            held[place, :, lanes_of(1 - core)] = merge(1 - core, value, first).astype(jnp.bfloat16)
+            held[part * size + row] = value.astype(jnp.bfloat16)
 
         multiply(image_wide.at[pl.ds(part * size * rank, size * rank), :], rows, size, emit)
         span = pl.ds(part * size, size)
-        copies.append(pltpu.make_async_copy(held.at[span], image.at[span], sems.at[part]))
+        copies.append(pltpu.make_async_copy(held.at[span], image.at[span, :, lanes_of(1 - core)], sems.at[part + 1]))
         copies[-1].start()
     for copy in copies:
         copy.wait()
 
 
-def run(kernel, outs, operands, scratch=(), products=1, in_specs=None, out_specs=None, aliases=None, limit=16 * 2**20, cost=KERNEL_COST):
+def run(kernel, outs, operands, scratch=(), products=1, in_specs=None, out_specs=None, aliases=None, limit=KERNEL_LIMIT):
     whole = pl.BlockSpec(memory_space=pltpu.VMEM)
     single = not isinstance(outs, list)
     shapes = [outs] if single else outs
@@ -327,7 +327,7 @@
         scratch_shapes=list(scratch),
         input_output_aliases=aliases or {},
         compiler_params=pltpu.CompilerParams(vmem_limit_bytes=limit),
-        cost_estimate=pl.CostEstimate(flops=products * cost, bytes_accessed=products * cost, transcendentals=0),
+        cost_estimate=pl.CostEstimate(flops=products * KERNEL_COST, bytes_accessed=products * KERNEL_COST, transcendentals=0),
     )(*operands)
     return result[0] if single else result
 
@@ -343,7 +343,7 @@
 
 def crossed(source, turn):
     high, mid, low, core = source // 8 % 2, source // 4 % 2, source // 2 % 2, source % 2
-    return (((high ^ (turn // 2)) * 2 + core) * 2 + (low ^ (turn % 2))) * 2 + mid
+    return ((core * 2 + (mid ^ (turn // 2))) * 2 + (low ^ (turn % 2))) * 2 + high
 
 
 def fast_local(samples, interp_in, top_blocks, top_pattern, bottom_blocks, bottom_pattern, interp_out):
@@ -360,44 +360,64 @@
     wide = pltpu.VMEM((rank * rank, LANES), jnp.float32)
     packed = pltpu.VMEM((2, fold, rank // fold, rhs_count, LANES), jnp.bfloat16)
 
-    def level_nears(blocks, pattern, level, bit, order, extra=()):
+    def level_wides(blocks, level, bit, *after):
+        wides = run(functools.partial(ahead_kernel, level, bit), [spread_out] * 4, (blocks, *after), products=4)
+        return wides[:2], wides[2:]
+
+    def level_nears(pattern, level, bit, order, wides, extra=()):
         return {
             flip: run(
-                functools.partial(near_kernel, level, bit, flip), [partial, spread_out],
-                (blocks, pattern, current[flip]) + ((current[1 - flip], *extra) if place < len(order) - 1 else ()), (wide,),
+                functools.partial(near_kernel, level, bit, flip), partial,
+                (pattern, current[flip], wides[0][flip]) + ((current[1 - flip], *extra) if place < len(order) - 1 else ()),
             )
             for place, flip in enumerate(order)
         }
 
-    def level_fars(pattern, level, bit, order):
+    def level_fars(pattern, level, bit, order, wides):
         return {
             flip: run(
-                functools.partial(far_kernel, level, bit, flip), state, (pattern, partner[flip], *near[flip]),
+                functools.partial(far_kernel, level, bit, flip), state,
+                (pattern, partner[flip], near[flip], wides[1][flip]),
             )
             for flip in order
         }
 
-    current = {}
-    current[1], current[0] = run(
-        coeff_kernel, [state, state], (interp_in, samples),
-        (pltpu.VMEM((rank * depth // 2, LANES), jnp.float32), pltpu.VMEM((2, rank, rhs_count, LANES), jnp.float32)),
-        4, cost=START_COST,
-    )
+    current = {
+        flip: run(
+            functools.partial(coeff_kernel, flip), state, (interp_in, samples),
+            (pltpu.VMEM((rank * depth // 2, LANES), jnp.float32), total), 2,
+        )
+        for flip in (1, 0)
+    }
     share_rows = 2 * rank + rank * rhs_count // (2 * rank)
     shared_shape = jax.ShapeDtypeStruct((share_rows, 2 * rank, LANES), jnp.bfloat16)
-    shared = run(functools.partial(share_kernel, 3), shared_shape, (top_blocks, top_pattern, bottom_blocks, bottom_pattern))
     for level in range(3):
         bit = 3 - level
         partner = {flip: swapped(current[flip], bit) for flip in (1, 0)}
-        near = level_nears(top_blocks, top_pattern, level, bit, (1, 0), (shared,) if level == 1 else ())
+        if level == 0:
+            wides = run(
+                functools.partial(fetch_kernel, 0, 3), [spread_out] * 4, (top_blocks, current[0]),
+                (pltpu.VMEM((1, *top_blocks.shape[1:]), jnp.bfloat16), pltpu.SemaphoreType.DMA), 4,
+                in_specs=[pl.BlockSpec(memory_space=pl.ANY), pl.BlockSpec(memory_space=pltpu.VMEM)], limit=FETCH_LIMIT,
+            )
+            wides = wides[:2], wides[2:]
+        else:
+            wides = later_wides[level]
+        near = level_nears(top_pattern, level, bit, (1, 0), wides)
+        if level == 0:
+            later_wides = {later: level_wides(top_blocks, later, 3 - later, near[0]) for later in (1, 2)}
+            shared = run(
+                functools.partial(share_kernel, 3), shared_shape,
+                (top_blocks, top_pattern, bottom_blocks, bottom_pattern),
+            )
         if level < 2:
-            current = level_fars(top_pattern, level, bit, (1, 0))
+            current = level_fars(top_pattern, level, bit, (1, 0), wides)
 
     shared = run(
-        functools.partial(send_kernel, 2, 1, 1), shared_shape, (top_pattern, partner[1], *near[1], shared), aliases={4: 0},
+        functools.partial(send_kernel, 2, 1, 1), shared_shape, (top_pattern, partner[1], near[1], wides[1][1], shared), aliases={4: 0},
     )
     shared = swapped(shared, 0)
-    current = level_fars(top_pattern, 2, 1, (0,))
+    current = level_fars(top_pattern, 2, 1, (0,), wides)
 
     pair_near = run(
         functools.partial(pair_near_kernel, 3),
@@ -411,33 +431,33 @@
     )
     pieces = [permuted(value, functools.partial(crossed, turn=turn)) for turn, value in enumerate(pieces)]
     own_wide, other_wide = run(wide_kernel, [pair_spread] * 2, (bottom_blocks, shared))
+    wides = {level: level_wides(bottom_blocks, level, level, pair_near[0]) for level in (1, 2, 3)}
+    image_spread = jax.ShapeDtypeStruct((out_depth * rank, LANES), jnp.float32)
+    image_wide = run(interp_kernel, [image_spread] * 2, (interp_out,))
+    spreads = [wide for level in (1, 2, 3) for group in wides[level] for wide in group]
     first, states = run(
         functools.partial(open_kernel, slot), [state, jax.ShapeDtypeStruct((2, rank, rhs_count, LANES), jnp.bfloat16)],
-        (bottom_pattern, own_wide, *pieces), (total, packed), 2,
+        (bottom_pattern, own_wide, *pieces, *spreads, *image_wide), (total, packed), 2,
     )
     current = {0: first}
     partner = {0: swapped(first, 1)}
-    near = level_nears(bottom_blocks, bottom_pattern, 1, 1, (0,))
     current[1] = swapped(run(other_kernel, state, (other_wide, states), (total,), 2), 0)
     partner[1] = swapped(current[1], 1)
-    near.update(level_nears(bottom_blocks, bottom_pattern, 1, 1, (1,)))
-    current = level_fars(bottom_pattern, 1, 1, (0, 1))
-    image_spread = jax.ShapeDtypeStruct((out_depth * rank, LANES), jnp.float32)
-    image_wide = run(interp_kernel, [image_spread] * 2, (interp_out,))
-    for level in (2, 3):
-        partner = {flip: swapped(current[flip], level) for flip in (0, 1)}
-        near = level_nears(bottom_blocks, bottom_pattern, level, level, (0, 1), image_wide)
-        if level == 2:
-            current = level_fars(bottom_pattern, level, level, (0, 1))
+    for level in (1, 2, 3):
+        if level > 1:
+            partner = {flip: swapped(current[flip], level) for flip in (0, 1)}
+        near = level_nears(bottom_pattern, level, level, (0, 1), wides[level])
+        if level < 3:
+            current = level_fars(bottom_pattern, level, level, (0, 1), wides[level])
 
     ready = run(
-        functools.partial(first_image_kernel, 3, 3), jax.ShapeDtypeStruct((out_depth, rhs_count, LANES), jnp.float32),
-        (bottom_pattern, near[0][1], image_wide[0], partner[0], near[0][0]), (total,), 3,
+        functools.partial(first_image_kernel, 3, 3), jax.ShapeDtypeStruct((out_depth, rhs_count, LANES), jnp.bfloat16),
+        (bottom_pattern, wides[3][1][0], image_wide[0], partner[0], near[0]), (total,), 3,
     )
     return run(
         functools.partial(last_kernel, 3, 3), jax.ShapeDtypeStruct((out_depth, rhs_count, box_count), jnp.bfloat16),
-        (bottom_pattern, near[1][1], image_wide[1], partner[1], near[1][0], ready),
-        (pltpu.VMEM((out_depth, rhs_count, box_count), jnp.bfloat16), total, pltpu.SemaphoreType.DMA((4,))), 3,
+        (bottom_pattern, wides[3][1][1], image_wide[1], partner[1], near[1], ready),
+        (pltpu.VMEM((out_depth, rhs_count, LANES), jnp.bfloat16), total, pltpu.SemaphoreType.DMA((5,))), 3,
         out_specs=[pl.BlockSpec(memory_space=pl.ANY)],
     )
 

time: 81.1 us -> 67.1 us (0.83)
  Pallas kernels: 44.1 us -> 22.2 us
  waiting for transfers between devices: 7.04 us -> 13 us
  starting transfers between devices: 24.9 us -> 29.2 us
  local copies, waits for them, and re-layouts: 4.4 us -> 2.2 us
    pallas_call x32 -> x39, Pallas kernels: 44.1 us -> 22.2 us  [run(): pl.pallas_call(kernel, out_shape=shapes, in_specs=in_specs or [whole] * l...]
    ppermute x18, waiting for transfers between devices: 7.04 us -> 13 us  [permuted(): return lax.ppermute(value, 'leaf', pairs)]
    ppermute x18, starting transfers between devices: 24.9 us -> 29.2 us  [permuted(): return lax.ppermute(value, 'leaf', pairs)]
    unnamed x16 -> x14, local copies, waits for them, and re-layouts: 4.4 us -> 2.2 us
  transfers between devices with their start and end apart: 18 -> 18, of which waited for: 5 -> 13; matrix products, arithmetic and copies ran while one was open for 0% -> 0% of each run, Pallas kernels for 41% -> 22%
where the time goes in v6:
time: 67.1 us; the launch traced here: 66.9 us
  starting transfers between devices  29.2 us (44%)
  Pallas kernels  22.2 us (33%)
  waiting for transfers between devices  13 us (19%)
  local copies, waits for them, and re-layouts  2.2 us (3%)
    ppermute x18, starting transfers between devices, permuted(): return lax.ppermute(value, 'leaf', pairs)  29.2 us
    pallas_call x39, Pallas kernels, run(): pl.pallas_call(kernel, out_shape=shapes, in_specs=in_specs or [whole] * l...  22.2 us
    ppermute x18, waiting for transfers between devices, permuted(): return lax.ppermute(value, 'leaf', pairs)  13 us
    unnamed x14, local copies, waits for them, and re-layouts  2.2 us
  transfers between devices with their start and end apart: 18, of which 13 were waited for; matrix products, arithmetic and copies ran while one was open for 0% of the time, Pallas kernels for 22%

profile of v6, /device:TPU:0, one launch (start us, length us, event | category | flops | bytes accessed | tf_op | source)
XLA Modules:
  0.0 66.9 jit_solution(15946876025201390933)
XLA Ops:
  0.0 1.2 %copy-done.2 = bf16[32,64,256]{2,1,0:T(8,128)(2,1)S(1)} copy-done((bf16[32,64,256]{2,1,0:T(8,128)(2,1)S(1)}, bf16[32,64,256]{2,1,0:T(8,128)(2,1)}, u32[]{:S(2)}) %copy-start.2) | copy-done | bytes 1048600
  1.2 0.9 %copy-done.6 = bf16[64,8,256]{2,1,0:T(8,128)(2,1)S(1)} copy-done((bf16[64,8,256]{2,1,0:T(8,128)(2,1)S(1)}, bf16[64,8,256]{2,1,0:T(8,128)(2,1)}, u32[]{:S(2)}) %copy-start.6) | copy-done | bytes 262168
  2.2 0.9 %shard_map.73.state = bf16[32,8,128]{2,1,0:T(8,128)(2,1)S(1)} custom-call(bf16[32,64,256]{2,1,0:T(8,128)(2,1)S(1)} %copy-done.2, bf16[64,8,256]{2,1,0:T(8,128)(2,1)S(1)} %copy-done.6), custom_call_target="tpu_custom_call" | custom-call | flops 2048 | bytes 2048 | tf_op jit(solution)/shard_map/pallas_call | solution.py:322
  3.0 4.1 %collective-permute-start = (bf16[32,8,128]{2,1,0:T(8,128)(2,1)S(1)}, bf16[32,8,128]{2,1,0:T(8,128)(2,1)S(1)}, u32[]{:S(2)}, u32[]{:S(2)}) collective-permute-start(bf16[32,8,128]{2,1,0:T(8,128)(2,1)S(1)} %shard_map.73.state), channel_id=1, source_target_pairs={{0,8},{1,9},{2,10},{3,11},{4,12},{5,13},{6,14},{7,15},{8,0},{9,1},... | collective-permute-start | bytes 196616 | tf_op jit(solution)/shard_map/ppermute | solution.py:337
  7.1 0.9 %shard_map.74.after.rest_0_.state = bf16[32,8,128]{2,1,0:T(8,128)(2,1)S(1)} custom-call(bf16[32,64,256]{2,1,0:T(8,128)(2,1)S(1)} %copy-done.2, bf16[64,8,256]{2,1,0:T(8,128)(2,1)S(1)} %copy-done.6), custom_call_target="tpu_custom_call" | custom-call | flops 2048 | bytes 2048 | tf_op jit(solution)/shard_map/pallas_call | solution.py:322
  8.1 1.7 %shard_map.75 = (f32[1024,128]{1,0:T(8,128)S(1)}, f32[1024,128]{1,0:T(8,128)S(1)}, f32[1024,128]{1,0:T(8,128)S(1)}, f32[1024,128]{1,0:T(8,128)S(1)}) custom-call(bf16[4,32,64,256]{3,2,1,0:T(8,128)(2,1)} %blocks.11, bf16[32,8,128]{2,1,0:T(8,128)(2,1)S(1)} %shard_map.74.after.rest_0_.state), custom_call_target="tpu_custom_call" | custom-call | flops 4096 | bytes 4096 | tf_op jit(solution)/shard_map/pallas_call | solution.py:322
  9.8 0.4 shard_map.76.near
  10.2 0.6 collective-permute-done.partner
  10.8 0.4 shard_map.77.state
  11.2 2.3 %collective-permute-start.1 = (bf16[32,8,128]{2,1,0:T(8,128)(2,1)S(1)}, bf16[32,8,128]{2,1,0:T(8,128)(2,1)S(1)}, u32[]{:S(2)}, u32[]{:S(2)}) collective-permute-start(bf16[32,8,128]{2,1,0:T(8,128)(2,1)S(1)} %shard_map.77.state), channel_id=1, source_target_pairs={{0,4},{1,5},{2,6},{3,7},{4,0},{5,1},{6,2},{7,3},{8,12},{9,13},{10,... | collective-permute-start | bytes 196616 | tf_op jit(solution)/shard_map/ppermute | solution.py:337
  13.5 0.4 shard_map.78.rest_0_.near
  13.9 0.3 shard_map.79
  14.2 0.4 shard_map.80.rest_0_.state
  14.6 0.6 collective-permute-start.4
  15.3 0.4 shard_map.81.near
  15.7 0.3 collective-permute-done.1.partner
  16.0 0.4 shard_map.82.state
  16.4 1.6 %collective-permute-start.3 = (bf16[32,8,128]{2,1,0:T(8,128)(2,1)S(1)}, bf16[32,8,128]{2,1,0:T(8,128)(2,1)S(1)}, u32[]{:S(2)}, u32[]{:S(2)}) collective-permute-start(bf16[32,8,128]{2,1,0:T(8,128)(2,1)S(1)} %shard_map.82.state), channel_id=1, source_target_pairs={{0,2},{1,3},{2,0},{3,1},{4,6},{5,7},{6,4},{7,5},{8,10},{9,11},{10,... | collective-permute-start | bytes 196616 | tf_op jit(solution)/shard_map/ppermute | solution.py:337
  18.0 0.8 %shard_map.87.shared = bf16[68,64,128]{2,1,0:T(8,128)(2,1)S(1)} custom-call(bf16[4,32,64,256]{3,2,1,0:T(8,128)(2,1)S(1)} %copy-done, s32[4,2,256]{2,1,0:T(2,128)S(1)} %copy-done.3, bf16[4,32,64,256]{3,2,1,0:T(8,128)(2,1)S(1)} %copy-done.1, s32[4,2,256]{2,1,0:T(2,128)S(1)} %copy-done.4), custom_call_target="tpu_custom_call" | custom-call | flops 1024 | bytes 1024 | tf_op jit(solution)/shard_map/pallas_call | solution.py:322
  18.8 0.3 shard_map.83
  19.2 0.4 shard_map.84.near
  19.6 0.4 shard_map.85.rest_0_.state
  20.0 0.4 shard_map.86.near
  20.4 0.3 collective-permute-done.3.partner
  20.7 0.4 shard_map.88
  21.2 1.6 %collective-permute-start.6 = (bf16[32,8,128]{2,1,0:T(8,128)(2,1)S(1)}, bf16[32,8,128]{2,1,0:T(8,128)(2,1)S(1)}, u32[]{:S(2)}, u32[]{:S(2)}) collective-permute-start(bf16[32,8,128]{2,1,0:T(8,128)(2,1)S(1)} %shard_map.85.rest_0_.state), channel_id=1, source_target_pairs={{0,2},{1,3},{2,0},{3,1},{4,6},{5,7},{6,4},{7,5},{8,10},{9,11},{10,... | collective-permute-start | bytes 196616 | tf_op jit(solution)/shard_map/ppermute | solution.py:337
  22.8 0.4 shard_map.89.near
  23.1 2.5 %collective-permute-done.6.partner = bf16[32,8,128]{2,1,0:T(8,128)(2,1)S(1)} collective-permute-done((bf16[32,8,128]{2,1,0:T(8,128)(2,1)S(1)}, bf16[32,8,128]{2,1,0:T(8,128)(2,1)S(1)}, u32[]{:S(2)}, u32[]{:S(2)}) %collective-permute-start.6) | collective-permute-done | bytes 65568 | tf_op jit(solution)/shard_map/ppermute | solution.py:337
  25.7 0.4 shard_map.90.state
  26.1 1.1 %shard_map.91 = (f32[2,32,8,128]{3,2,1,0:T(8,128)S(1)}, f32[2,1024,128]{2,1,0:T(8,128)S(1)}) custom-call(bf16[4,32,64,256]{3,2,1,0:T(8,128)(2,1)S(1)} %copy-done, s32[4,2,256]{2,1,0:T(2,128)S(1)} %copy-done.3, bf16[68,64,128]{2,1,0:T(8,128)(2,1)S(1)} %collective-permute-done.5.shared, bf16[32,8,128]{2,1,0:T(8,128)(2,1)S(1)} %shard_map.90.state), custom_call_target="tpu_custom_call" | custom-call | flops 2048 | bytes 2048 | tf_op jit(solution)/shard_map/pallas_call | solution.py:322
  27.1 1.3 %shard_map.95 = (bf16[2,2,4,8,128]{4,3,2,1,0:T(8,128)(2,1)S(1)}, bf16[2,2,4,8,128]{4,3,2,1,0:T(8,128)(2,1)S(1)}, bf16[2,2,4,8,128]{4,3,2,1,0:T(8,128)(2,1)S(1)}, bf16[2,2,4,8,128]{4,3,2,1,0:T(8,128)(2,1)S(1)}) custom-call(s32[4,2,256]{2,1,0:T(2,128)S(1)} %copy-done.3, f32[2,1024,128]{2,1,0:T(8,128)S(1)} %get-tuple-element.58.wide, ...), custom_call_target="tpu_custom_call" | custom-call | flops 2048 | bytes 2048 | tf_op jit(solution)/shard_map/pallas_call | solution.py:322
  28.5 0.7 collective-permute-start.7
  29.2 1.6 %collective-permute-start.8 = (bf16[2,2,4,8,128]{4,3,2,1,0:T(8,128)(2,1)S(1)}, bf16[2,2,4,8,128]{4,3,2,1,0:T(8,128)(2,1)S(1)}, u32[]{:S(2)}, u32[]{:S(2)}) collective-permute-start(bf16[2,2,4,8,128]{4,3,2,1,0:T(8,128)(2,1)S(1)} %get-tuple-element.60), channel_id=1, source_target_pairs={{0,2},{1,10},{2,0},{3,8},{4,6},{5,14},{6,4},{7,12},{8,3},{9,11},{1... | collective-permute-start | bytes 98312 | tf_op jit(solution)/shard_map/ppermute | solution.py:337
  30.8 2.4 %collective-permute-start.9 = (bf16[2,2,4,8,128]{4,3,2,1,0:T(8,128)(2,1)S(1)}, bf16[2,2,4,8,128]{4,3,2,1,0:T(8,128)(2,1)S(1)}, u32[]{:S(2)}, u32[]{:S(2)}) collective-permute-start(bf16[2,2,4,8,128]{4,3,2,1,0:T(8,128)(2,1)S(1)} %get-tuple-element.61), channel_id=1, source_target_pairs={{0,4},{1,12},{2,6},{3,14},{4,0},{5,8},{6,2},{7,10},{8,5},{9,13},{1... | collective-permute-start | bytes 98312 | tf_op jit(solution)/shard_map/ppermute | solution.py:337
  33.2 0.3 shard_map.93
  33.5 0.3 shard_map.94
  33.8 0.3 shard_map.97
  34.1 0.3 shard_map.96
  34.4 0.3 shard_map.92
  34.8 0.3 collective-permute-done.9.rest_2_
  35.1 2.9 %collective-permute-done.10.rest_3_ = bf16[2,2,4,8,128]{4,3,2,1,0:T(8,128)(2,1)S(1)} collective-permute-done((bf16[2,2,4,8,128]{4,3,2,1,0:T(8,128)(2,1)S(1)}, bf16[2,2,4,8,128]{4,3,2,1,0:T(8,128)(2,1)S(1)}, u32[]{:S(2)}, u32[]{:S(2)}) %collective-permute-start.10) | collective-permute-done | bytes 32800 | tf_op jit(solution)/shard_map/ppermute | solution.py:337
  38.0 1.1 %shard_map.98 = (bf16[32,8,128]{2,1,0:T(8,128)(2,1)S(1)}, bf16[2,32,8,128]{3,2,1,0:T(8,128)(2,1)S(1)}) custom-call(s32[4,2,256]{2,1,0:T(2,128)S(1)} %copy-done.4, f32[2,1024,128]{2,1,0:T(8,128)S(1)} %get-tuple-element.57.wide, bf16[2,2,4,8,128]{4,3,2,1,0:T(8,128)(2,1)S(1)} %collective-permute-done.7.rest_0_, ...), custom_call_target="tpu_custom_call" | custom-call | flops 2048 | bytes 2048 | tf_op jit(solution)/shard_map/pallas_call | solution.py:322
  39.1 0.7 %shard_map.99 = bf16[32,8,128]{2,1,0:T(8,128)(2,1)S(1)} custom-call(f32[2,1024,128]{2,1,0:T(8,128)S(1)} %get-tuple-element.56.wide, bf16[2,32,8,128]{3,2,1,0:T(8,128)(2,1)S(1)} %get-tuple-element.75.states), custom_call_target="tpu_custom_call" | custom-call | flops 2048 | bytes 2048 | tf_op jit(solution)/shard_map/pallas_call | solution.py:322
  39.8 7.5 %collective-permute-start.11 = (bf16[32,8,128]{2,1,0:T(8,128)(2,1)S(1)}, bf16[32,8,128]{2,1,0:T(8,128)(2,1)S(1)}, u32[]{:S(2)}, u32[]{:S(2)}) collective-permute-start(bf16[32,8,128]{2,1,0:T(8,128)(2,1)S(1)} %shard_map.99), channel_id=1, source_target_pairs={{0,1},{1,0},{2,3},{3,2},{4,5},{5,4},{6,7},{7,6},{8,9},{9,8},{10,11... | collective-permute-start | bytes 196616 | tf_op jit(solution)/shard_map/ppermute | solution.py:337
  47.4 0.5 collective-permute-start.15
  47.9 0.4 collective-permute-done.11.state.rest_0_
  48.3 1.1 %collective-permute-start.12 = (bf16[32,8,128]{2,1,0:T(8,128)(2,1)S(1)}, bf16[32,8,128]{2,1,0:T(8,128)(2,1)S(1)}, u32[]{:S(2)}, u32[]{:S(2)}) collective-permute-start(bf16[32,8,128]{2,1,0:T(8,128)(2,1)S(1)} %collective-permute-done.11.state.rest_0_), channel_id=1, source_target_pairs={{0,2},{1,3},{2,0},{3,1},{4,6},{5,7},{6,4},{7,5},{8,10},{9,11},{10,... | collective-permute-start | bytes 196616 | tf_op jit(solution)/shard_map/ppermute | solution.py:337
  49.4 0.4 shard_map.105.near
  49.8 2.3 %collective-permute-done.15.partner = bf16[32,8,128]{2,1,0:T(8,128)(2,1)S(1)} collective-permute-done((bf16[32,8,128]{2,1,0:T(8,128)(2,1)S(1)}, bf16[32,8,128]{2,1,0:T(8,128)(2,1)S(1)}, u32[]{:S(2)}, u32[]{:S(2)}) %collective-permute-start.15) | collective-permute-done | bytes 65568 | tf_op jit(solution)/shard_map/ppermute | solution.py:337
  52.1 0.4 shard_map.106.state
  52.5 0.4 shard_map.100.near
  53.1 0.4 shard_map.101.state.rest_0_
  53.5 2.0 %collective-permute-start.13 = (bf16[32,8,128]{2,1,0:T(8,128)(2,1)S(1)}, bf16[32,8,128]{2,1,0:T(8,128)(2,1)S(1)}, u32[]{:S(2)}, u32[]{:S(2)}) collective-permute-start(bf16[32,8,128]{2,1,0:T(8,128)(2,1)S(1)} %shard_map.101.state.rest_0_), channel_id=1, source_target_pairs={{0,4},{1,5},{2,6},{3,7},{4,0},{5,1},{6,2},{7,3},{8,12},{9,13},{10,... | collective-permute-start | bytes 196616 | tf_op jit(solution)/shard_map/ppermute | solution.py:337
  55.4 0.4 shard_map.102.near
  55.8 0.4 shard_map.107.near
  56.2 1.0 %collective-permute-done.16.partner = bf16[32,8,128]{2,1,0:T(8,128)(2,1)S(1)} collective-permute-done((bf16[32,8,128]{2,1,0:T(8,128)(2,1)S(1)}, bf16[32,8,128]{2,1,0:T(8,128)(2,1)S(1)}, u32[]{:S(2)}, u32[]{:S(2)}) %collective-permute-start.16) | collective-permute-done | bytes 65568 | tf_op jit(solution)/shard_map/ppermute | solution.py:337
  57.2 0.4 shard_map.108.state
  57.9 0.4 shard_map.103.state.rest_0_
  58.4 2.8 %collective-permute-start.14 = (bf16[32,8,128]{2,1,0:T(8,128)(2,1)S(1)}, bf16[32,8,128]{2,1,0:T(8,128)(2,1)S(1)}, u32[]{:S(2)}, u32[]{:S(2)}) collective-permute-start(bf16[32,8,128]{2,1,0:T(8,128)(2,1)S(1)} %shard_map.103.state.rest_0_), channel_id=1, source_target_pairs={{0,8},{1,9},{2,10},{3,11},{4,12},{5,13},{6,14},{7,15},{8,0},{9,1},... | collective-permute-start | bytes 196616 | tf_op jit(solution)/shard_map/ppermute | solution.py:337
  61.1 0.4 shard_map.104.near
  61.5 0.4 shard_map.109.near
  61.9 1.8 %collective-permute-done.17.partner = bf16[32,8,128]{2,1,0:T(8,128)(2,1)S(1)} collective-permute-done((bf16[32,8,128]{2,1,0:T(8,128)(2,1)S(1)}, bf16[32,8,128]{2,1,0:T(8,128)(2,1)S(1)}, u32[]{:S(2)}, u32[]{:S(2)}) %collective-permute-start.17) | collective-permute-done | bytes 65568 | tf_op jit(solution)/shard_map/ppermute | solution.py:337
  63.7 1.2 %shard_map.110.ready = bf16[64,8,128]{2,1,0:T(8,128)(2,1)S(1)} custom-call(s32[4,2,256]{2,1,0:T(2,128)S(1)} %copy-done.4, f32[1024,128]{1,0:T(8,128)S(1)} %get-tuple-element.73.rest_14_.wide, f32[2048,128]{1,0:T(8,128)S(1)} %get-tuple-element.74.rest_16_.image_wide, bf16[32,8,128]{2,1,0:T(8,128)(2,1)S(1)} %collective-permute-done.17.partner, ...), custom_call_target="tpu_custom_call" | custom-call | flops 3072 | bytes 3072 | tf_op jit(solution)/shard_map/pallas_call | solution.py:322
  65.1 1.8 %shard_map.111 = bf16[64,8,256]{2,1,0:T(8,128)(2,1)} custom-call(s32[4,2,256]{2,1,0:T(2,128)S(1)} %copy-done.4, f32[1024,128]{1,0:T(8,128)S(1)} %get-tuple-element.54.rest_15_.wide, f32[2048,128]{1,0:T(8,128)S(1)} %get-tuple-element.55.rest_17_.image_wide, bf16[32,8,128]{2,1,0:T(8,128)(2,1)S(1)} %collective-permute-done.14.partner, ...), custom_call_target="tpu_custom_call" | custom-call | flops 3072 | bytes 3072 | tf_op jit(solution)/shard_map/pallas_call | solution.py:322
  (25 shorter events, 0.9 us)
Async XLA Ops:
  0.0 1.2 %copy-start.2 = (bf16[32,64,256]{2,1,0:T(8,128)(2,1)S(1)}, bf16[32,64,256]{2,1,0:T(8,128)(2,1)}, u32[]{:S(2)}) copy-start(bf16[32,64,256]{2,1,0:T(8,128)(2,1)} %interp.4) | copy-start | bytes 3145732
  1.2 0.9 %copy-start.6 = (bf16[64,8,256]{2,1,0:T(8,128)(2,1)S(1)}, bf16[64,8,256]{2,1,0:T(8,128)(2,1)}, u32[]{:S(2)}) copy-start(bf16[64,8,256]{2,1,0:T(8,128)(2,1)} %samples.3) | copy-start | bytes 786436
  3.0 7.8 %collective-permute-start = (bf16[32,8,128]{2,1,0:T(8,128)(2,1)S(1)}, bf16[32,8,128]{2,1,0:T(8,128)(2,1)S(1)}, u32[]{:S(2)}, u32[]{:S(2)}) collective-permute-start(bf16[32,8,128]{2,1,0:T(8,128)(2,1)S(1)} %shard_map.73.state), channel_id=1, source_target_pairs={{0,8},{1,9},{2,10},{3,11},{4,12},{5,13},{6,14},{7,15},{8,0},{9,1},... | collective-permute-start | bytes 196616 | tf_op jit(solution)/shard_map/ppermute | solution.py:337
  8.0 1.8 %copy-start.3 = (s32[4,2,256]{2,1,0:T(2,128)S(1)}, s32[4,2,256]{2,1,0:T(2,128)}, u32[]{:S(2)}) copy-start(s32[4,2,256]{2,1,0:T(2,128)} %pattern.40) | copy-start | bytes 24580
  8.0 6.2 %collective-permute-start.2 = (bf16[32,8,128]{2,1,0:T(8,128)(2,1)S(1)}, bf16[32,8,128]{2,1,0:T(8,128)(2,1)S(1)}, u32[]{:S(2)}, u32[]{:S(2)}) collective-permute-start(bf16[32,8,128]{2,1,0:T(8,128)(2,1)S(1)} %shard_map.74.after.rest_0_.state), channel_id=1, source_target_pairs={{0,8},{1,9},{2,10},{3,11},{4,12},{5,13},{6,14},{7,15},{8,0},{9,1},... | collective-permute-start | bytes 196616 | tf_op jit(solution)/shard_map/ppermute | solution.py:337
  8.1 5.8 %copy-start = (bf16[4,32,64,256]{3,2,1,0:T(8,128)(2,1)S(1)}, bf16[4,32,64,256]{3,2,1,0:T(8,128)(2,1)}, u32[]{:S(2)}) copy-start(bf16[4,32,64,256]{3,2,1,0:T(8,128)(2,1)} %blocks.11) | copy-start | bytes 12582916
  11.2 4.8 %collective-permute-start.1 = (bf16[32,8,128]{2,1,0:T(8,128)(2,1)S(1)}, bf16[32,8,128]{2,1,0:T(8,128)(2,1)S(1)}, u32[]{:S(2)}, u32[]{:S(2)}) collective-permute-start(bf16[32,8,128]{2,1,0:T(8,128)(2,1)S(1)} %shard_map.77.state), channel_id=1, source_target_pairs={{0,4},{1,5},{2,6},{3,7},{4,0},{5,1},{6,2},{7,3},{8,12},{9,13},{10,... | collective-permute-start | bytes 196616 | tf_op jit(solution)/shard_map/ppermute | solution.py:337
  13.9 4.1 %copy-start.1 = (bf16[4,32,64,256]{3,2,1,0:T(8,128)(2,1)S(1)}, bf16[4,32,64,256]{3,2,1,0:T(8,128)(2,1)}, u32[]{:S(2)}) copy-start(bf16[4,32,64,256]{3,2,1,0:T(8,128)(2,1)} %blocks.15) | copy-start | bytes 12582916
  14.2 3.8 %copy-start.4 = (s32[4,2,256]{2,1,0:T(2,128)S(1)}, s32[4,2,256]{2,1,0:T(2,128)}, u32[]{:S(2)}) copy-start(s32[4,2,256]{2,1,0:T(2,128)} %pattern.53) | copy-start | bytes 24580
  14.6 4.9 %collective-permute-start.4 = (bf16[32,8,128]{2,1,0:T(8,128)(2,1)S(1)}, bf16[32,8,128]{2,1,0:T(8,128)(2,1)S(1)}, u32[]{:S(2)}, u32[]{:S(2)}) collective-permute-start(bf16[32,8,128]{2,1,0:T(8,128)(2,1)S(1)} %shard_map.80.rest_0_.state), channel_id=1, source_target_pairs={{0,4},{1,5},{2,6},{3,7},{4,0},{5,1},{6,2},{7,3},{8,12},{9,13},{10,... | collective-permute-start | bytes 196616 | tf_op jit(solution)/shard_map/ppermute | solution.py:337
  16.4 4.3 %collective-permute-start.3 = (bf16[32,8,128]{2,1,0:T(8,128)(2,1)S(1)}, bf16[32,8,128]{2,1,0:T(8,128)(2,1)S(1)}, u32[]{:S(2)}, u32[]{:S(2)}) collective-permute-start(bf16[32,8,128]{2,1,0:T(8,128)(2,1)S(1)} %shard_map.82.state), channel_id=1, source_target_pairs={{0,2},{1,3},{2,0},{3,1},{4,6},{5,7},{6,4},{7,5},{8,10},{9,11},{10,... | collective-permute-start | bytes 196616 | tf_op jit(solution)/shard_map/ppermute | solution.py:337
  21.1 5.0 %collective-permute-start.5 = (bf16[68,64,128]{2,1,0:T(8,128)(2,1)S(1)}, bf16[68,64,128]{2,1,0:T(8,128)(2,1)S(1)}, u32[]{:S(2)}, u32[]{:S(2)}) collective-permute-start(bf16[68,64,128]{2,1,0:T(8,128)(2,1)S(1)} %shard_map.88), channel_id=1, source_target_pairs={{0,1},{1,0},{2,3},{3,2},{4,5},{5,4},{6,7},{7,6},{8,9},{9,8},{10,11... | collective-permute-start | bytes 3342344 | tf_op jit(solution)/shard_map/ppermute | solution.py:337
  21.2 4.5 %collective-permute-start.6 = (bf16[32,8,128]{2,1,0:T(8,128)(2,1)S(1)}, bf16[32,8,128]{2,1,0:T(8,128)(2,1)S(1)}, u32[]{:S(2)}, u32[]{:S(2)}) collective-permute-start(bf16[32,8,128]{2,1,0:T(8,128)(2,1)S(1)} %shard_map.85.rest_0_.state), channel_id=1, source_target_pairs={{0,2},{1,3},{2,0},{3,1},{4,6},{5,7},{6,4},{7,5},{8,10},{9,11},{10,... | collective-permute-start | bytes 196616 | tf_op jit(solution)/shard_map/ppermute | solution.py:337
  27.1 6.1 %copy-start.5 = (bf16[64,32,256]{2,1,0:T(8,128)(2,1)S(1)}, bf16[64,32,256]{2,1,0:T(8,128)(2,1)}, u32[]{:S(2)}) copy-start(bf16[64,32,256]{2,1,0:T(8,128)(2,1)} %interp.5) | copy-start | bytes 3145732
  28.5 6.3 %collective-permute-start.7 = (bf16[2,2,4,8,128]{4,3,2,1,0:T(8,128)(2,1)S(1)}, bf16[2,2,4,8,128]{4,3,2,1,0:T(8,128)(2,1)S(1)}, u32[]{:S(2)}, u32[]{:S(2)}) collective-permute-start(bf16[2,2,4,8,128]{4,3,2,1,0:T(8,128)(2,1)S(1)} %get-tuple-element.59), channel_id=1, source_target_pairs={{0,0},{1,8},{2,2},{3,10},{4,4},{5,12},{6,6},{7,14},{8,1},{9,9},{10... | collective-permute-start | bytes 98312 | tf_op jit(solution)/shard_map/ppermute | solution.py:337
  29.2 5.6 %collective-permute-start.8 = (bf16[2,2,4,8,128]{4,3,2,1,0:T(8,128)(2,1)S(1)}, bf16[2,2,4,8,128]{4,3,2,1,0:T(8,128)(2,1)S(1)}, u32[]{:S(2)}, u32[]{:S(2)}) collective-permute-start(bf16[2,2,4,8,128]{4,3,2,1,0:T(8,128)(2,1)S(1)} %get-tuple-element.60), channel_id=1, source_target_pairs={{0,2},{1,10},{2,0},{3,8},{4,6},{5,14},{6,4},{7,12},{8,3},{9,11},{1... | collective-permute-start | bytes 98312 | tf_op jit(solution)/shard_map/ppermute | solution.py:337
  30.8 4.3 %collective-permute-start.9 = (bf16[2,2,4,8,128]{4,3,2,1,0:T(8,128)(2,1)S(1)}, bf16[2,2,4,8,128]{4,3,2,1,0:T(8,128)(2,1)S(1)}, u32[]{:S(2)}, u32[]{:S(2)}) collective-permute-start(bf16[2,2,4,8,128]{4,3,2,1,0:T(8,128)(2,1)S(1)} %get-tuple-element.61), channel_id=1, source_target_pairs={{0,4},{1,12},{2,6},{3,14},{4,0},{5,8},{6,2},{7,10},{8,5},{9,13},{1... | collective-permute-start | bytes 98312 | tf_op jit(solution)/shard_map/ppermute | solution.py:337
  33.2 4.8 %collective-permute-start.10 = (bf16[2,2,4,8,128]{4,3,2,1,0:T(8,128)(2,1)S(1)}, bf16[2,2,4,8,128]{4,3,2,1,0:T(8,128)(2,1)S(1)}, u32[]{:S(2)}, u32[]{:S(2)}) collective-permute-start(bf16[2,2,4,8,128]{4,3,2,1,0:T(8,128)(2,1)S(1)} %get-tuple-element.62), channel_id=1, source_target_pairs={{0,6},{1,14},{2,4},{3,12},{4,2},{5,10},{6,0},{7,8},{8,7},{9,15},{1... | collective-permute-start | bytes 98312 | tf_op jit(solution)/shard_map/ppermute | solution.py:337
  39.8 8.4 %collective-permute-start.11 = (bf16[32,8,128]{2,1,0:T(8,128)(2,1)S(1)}, bf16[32,8,128]{2,1,0:T(8,128)(2,1)S(1)}, u32[]{:S(2)}, u32[]{:S(2)}) collective-permute-start(bf16[32,8,128]{2,1,0:T(8,128)(2,1)S(1)} %shard_map.99), channel_id=1, source_target_pairs={{0,1},{1,0},{2,3},{3,2},{4,5},{5,4},{6,7},{7,6},{8,9},{9,8},{10,11... | collective-permute-start | bytes 196616 | tf_op jit(solution)/shard_map/ppermute | solution.py:337
  47.4 4.7 %collective-permute-start.15 = (bf16[32,8,128]{2,1,0:T(8,128)(2,1)S(1)}, bf16[32,8,128]{2,1,0:T(8,128)(2,1)S(1)}, u32[]{:S(2)}, u32[]{:S(2)}) collective-permute-start(bf16[32,8,128]{2,1,0:T(8,128)(2,1)S(1)} %get-tuple-element.76.state), channel_id=1, source_target_pairs={{0,2},{1,3},{2,0},{3,1},{4,6},{5,7},{6,4},{7,5},{8,10},{9,11},{10,... | collective-permute-start | bytes 196616 | tf_op jit(solution)/shard_map/ppermute | solution.py:337
  48.3 4.8 %collective-permute-start.12 = (bf16[32,8,128]{2,1,0:T(8,128)(2,1)S(1)}, bf16[32,8,128]{2,1,0:T(8,128)(2,1)S(1)}, u32[]{:S(2)}, u32[]{:S(2)}) collective-permute-start(bf16[32,8,128]{2,1,0:T(8,128)(2,1)S(1)} %collective-permute-done.11.state.rest_0_), channel_id=1, source_target_pairs={{0,2},{1,3},{2,0},{3,1},{4,6},{5,7},{6,4},{7,5},{8,10},{9,11},{10,... | collective-permute-start | bytes 196616 | tf_op jit(solution)/shard_map/ppermute | solution.py:337
  52.5 4.8 %collective-permute-start.16 = (bf16[32,8,128]{2,1,0:T(8,128)(2,1)S(1)}, bf16[32,8,128]{2,1,0:T(8,128)(2,1)S(1)}, u32[]{:S(2)}, u32[]{:S(2)}) collective-permute-start(bf16[32,8,128]{2,1,0:T(8,128)(2,1)S(1)} %shard_map.106.state), channel_id=1, source_target_pairs={{0,4},{1,5},{2,6},{3,7},{4,0},{5,1},{6,2},{7,3},{8,12},{9,13},{10,... | collective-permute-start | bytes 196616 | tf_op jit(solution)/shard_map/ppermute | solution.py:337
  53.5 4.5 %collective-permute-start.13 = (bf16[32,8,128]{2,1,0:T(8,128)(2,1)S(1)}, bf16[32,8,128]{2,1,0:T(8,128)(2,1)S(1)}, u32[]{:S(2)}, u32[]{:S(2)}) collective-permute-start(bf16[32,8,128]{2,1,0:T(8,128)(2,1)S(1)} %shard_map.101.state.rest_0_), channel_id=1, source_target_pairs={{0,4},{1,5},{2,6},{3,7},{4,0},{5,1},{6,2},{7,3},{8,12},{9,13},{10,... | collective-permute-start | bytes 196616 | tf_op jit(solution)/shard_map/ppermute | solution.py:337
  57.6 6.0 %collective-permute-start.17 = (bf16[32,8,128]{2,1,0:T(8,128)(2,1)S(1)}, bf16[32,8,128]{2,1,0:T(8,128)(2,1)S(1)}, u32[]{:S(2)}, u32[]{:S(2)}) collective-permute-start(bf16[32,8,128]{2,1,0:T(8,128)(2,1)S(1)} %shard_map.108.state), channel_id=1, source_target_pairs={{0,8},{1,9},{2,10},{3,11},{4,12},{5,13},{6,14},{7,15},{8,0},{9,1},... | collective-permute-start | bytes 196616 | tf_op jit(solution)/shard_map/ppermute | solution.py:337
  58.4 6.7 %collective-permute-start.14 = (bf16[32,8,128]{2,1,0:T(8,128)(2,1)S(1)}, bf16[32,8,128]{2,1,0:T(8,128)(2,1)S(1)}, u32[]{:S(2)}, u32[]{:S(2)}) collective-permute-start(bf16[32,8,128]{2,1,0:T(8,128)(2,1)S(1)} %shard_map.103.state.rest_0_), channel_id=1, source_target_pairs={{0,8},{1,9},{2,10},{3,11},{4,12},{5,13},{6,14},{7,15},{8,0},{9,1},... | collective-permute-start | bytes 196616 | tf_op jit(solution)/shard_map/ppermute | solution.py:337

commit v7 on v6

v7 whole, which is shorter than its diff:
```python
import functools

import jax
import jax.numpy as jnp
from jax import lax
from jax.experimental import pallas as pl
from jax.experimental.pallas import tpu as pltpu
from jax.sharding import PartitionSpec as P

LANES = 128
GROUP = 4
KERNEL_COST = 1024
KERNEL_LIMIT = 16 * 2**20
FETCH_LIMIT = 53_000_000


def digits():
    place = lax.axis_index("leaf")
    return lax.rem(place // 8, 2), lax.rem(place // 4, 2), lax.rem(place // 2, 2), lax.rem(place, 2)


def lanes_of(chunk):
    return pl.ds(pl.multiple_of(chunk * LANES, LANES), LANES)


def order_matrix(slot, width, start, back=False):
    lie = lax.broadcasted_iota(jnp.int32, (2 * LANES, width), 1 if back else 0)
    new = lax.broadcasted_iota(jnp.int32, (2 * LANES, width), 0 if back else 1) + start
    half, group, place = new // LANES, new % LANES // (slot // 2), new % (slot // 2)
    return (lie == group * slot + half * (slot // 2) + place).astype(jnp.float32).astype(jnp.bfloat16)


def reorder(rows, matrix):
    return jnp.dot(rows, matrix, preferred_element_type=jnp.float32)


def multiply(wide, state, row_count, emit):
    rank = len(state)

    def body(step, carry):
        for inner in range(GROUP):
            sums = [None, None]
            for index in range(rank):
                weight = wide[pl.ds(step * GROUP * rank + inner * rank + index, 8, stride=0), :]
                term = weight * state[index]
                old = sums[index % 2]
                sums[index % 2] = term if old is None else old + term
            emit(step * GROUP + inner, sums[0] + sums[1])
        return carry

    lax.fori_loop(0, row_count // GROUP, body, 0)


def state_rows(ref, present=None):
    rows = [ref[index].astype(jnp.float32) for index in range(ref.shape[0])]
    return rows if present is None else [row * present for row in rows]


def coeff_kernel(flip, slot, interp, samples, out, wide, held, total):
    rank, depth = interp.shape[0], interp.shape[1] // 2
    rhs_count = samples.shape[1]
    chunk = digits()[3] ^ flip
    matrix = order_matrix(slot, LANES, chunk * LANES)
    held[...] = reorder(samples[...].reshape(2 * depth * rhs_count, 2 * LANES), matrix)
    for half in range(2):
        part = slice(half * depth, (half + 1) * depth)

        def body(step, carry):
            rows = interp[pl.ds(step * 8, 8), part, :].reshape(8 * depth, 2 * LANES)
            wide[pl.ds(step * 8 * depth, 8 * depth), :] = reorder(rows, matrix)
            return carry

        lax.fori_loop(0, rank // 8, body, 0)
        state = [held[(half * depth + index) * rhs_count:(half * depth + index + 1) * rhs_count, :] for index in range(depth)]

        def emit(row, value):
            if half == 0:
                total[row] = value
            else:
                out[row] = (total[row] + value).astype(jnp.bfloat16)

        multiply(wide, state, rank, emit)


def spread(wide, rows_at, row_count, matrix):
    def body(step, carry):
        rows = rows_at(step * 8)
        span = pl.ds(pl.multiple_of(step * rows.shape[0], 8), rows.shape[0])
        both = reorder(rows, matrix)
        wide[0, span, :] = both[:, :LANES]
        wide[1, span, :] = both[:, LANES:]
        return carry

    lax.fori_loop(0, row_count // 8, body, 0)


def spread_level(blocks, level, matrix, wide):
    rank = blocks.shape[1]
    for half in range(2):
        columns = slice(half * rank, (half + 1) * rank)
        spread(
            wide.at[half],
            lambda row: blocks[level, pl.ds(row, 8), columns, :].reshape(8 * rank, 2 * LANES),
            rank, matrix,
        )


def fetch_kernel(slot, blocks, top_pattern, bottom_pattern, after, wide, matrix, back, top_present, bottom_present, held, sem):
    copy = pltpu.make_async_copy(blocks.at[pl.ds(0, 1)], held, sem)
    copy.start()
    matrix[...] = order_matrix(slot, 2 * LANES, 0)
    back[...] = order_matrix(slot, 2 * LANES, 0, True)
    for pattern, present in ((top_pattern, top_present), (bottom_pattern, bottom_present)):
        for level in range(pattern.shape[0]):
            for half in range(2):
                row = pattern[level, half:half + 1, :].astype(jnp.float32)
                both = reorder(jnp.broadcast_to(row, (16, 2 * LANES)).astype(jnp.bfloat16), matrix[...])
                present[0, level, half] = both[:8, :LANES]
                present[1, level, half] = both[:8, LANES:]
    copy.wait()
    spread_level(held, 0, matrix[...], wide)


def ahead_kernel(level, blocks, matrix, *rest):
    spread_level(blocks, level, matrix[...], rest[-1])


def near_kernel(level, bit, flip, present, state, wide, *rest):
    out = rest[-1]
    places = digits()
    chunk, own = places[3] ^ flip, places[3 - bit]

    def emit(row, value):
        out[row] = value

    multiply(wide.at[own, chunk], state_rows(state, present[chunk, level, own]), out.shape[0], emit)


def far_kernel(level, bit, flip, present, partner, near, wide, out):
    places = digits()
    chunk, other = places[3] ^ flip, 1 - places[3 - bit]

    def emit(row, value):
        out[row] = (near[row] + value).astype(jnp.bfloat16)

    multiply(wide.at[other, chunk], state_rows(partner, present[chunk, level, other]), out.shape[0], emit)


def share_kernel(top_level, top_wide, top_present, bottom_wide, bottom_present, *rest):
    out = rest[-1]
    rank = out.shape[1] // 2
    chunk = 1 - digits()[3]
    for place, (wide, present, level) in enumerate(((top_wide, top_present, top_level), (bottom_wide, bottom_present, 0))):
        for half in range(2):
            mask = present[chunk, level, half][:1]

            def body(step, carry):
                rows = wide[half, chunk, pl.ds(pl.multiple_of(step * GROUP * rank, 8), GROUP * rank), :] * mask
                span = pl.ds(place * rank + step * GROUP, GROUP)
                out[span, half * rank:(half + 1) * rank, :] = rows.reshape(GROUP, rank, LANES).astype(jnp.bfloat16)
                return carry

            lax.fori_loop(0, rank // GROUP, body, 0)


def widen_shared(shared, place, half, wide):
    rank = shared.shape[1] // 2

    def body(step, carry):
        rows = shared[pl.ds(place * rank + step * GROUP, GROUP), half * rank:(half + 1) * rank, :].astype(jnp.float32)
        wide[pl.ds(pl.multiple_of(step * GROUP * rank, 8), GROUP * rank), :] = rows.reshape(GROUP * rank, LANES)
        return carry

    lax.fori_loop(0, rank // GROUP, body, 0)


def send_kernel(level, bit, flip, present, partner, near, wide, shared, out):
    rank, per = partner.shape[0], shared.shape[1] // partner.shape[1]
    places = digits()
    chunk, other = places[3] ^ flip, 1 - places[3 - bit]

    def emit(row, value):
        place = pl.ds(pl.multiple_of(lax.rem(row, per) * 8, 8), 8)
        out[2 * rank + row // per, place, :] = (near[row] + value).astype(jnp.bfloat16)

    multiply(wide.at[other, chunk], state_rows(partner, present[chunk, level, other]), rank, emit)


def sent_rows(shared):
    rank = shared.shape[1] // 2
    per = shared.shape[1] // 8
    return [
        shared[2 * rank + row // per, row % per * 8:(row % per + 1) * 8, :].astype(jnp.float32) for row in range(rank)
    ]


def swap_groups(tile, size):
    lane_group = lax.broadcasted_iota(jnp.int32, tile[0].shape, 2) // size
    step = 1
    while step < len(tile):
        low = (lane_group // step) % 2 == 0
        fresh = list(tile)
        for place in range(len(tile)):
            if place & step == 0:
                first, second = tile[place], tile[place + step]
                fresh[place] = jnp.where(low, first, pltpu.roll(second, step * size, 2))
                fresh[place + step] = jnp.where(low, pltpu.roll(first, LANES - step * size, 2), second)
        tile = fresh
        step *= 2
    return tile


def pair_near_kernel(level, present, wide, shared, state, out, far_wide):
    rank = state.shape[0]
    core = digits()[3]
    rows = state_rows(state)
    mask = present[core, level, core]

    for half in range(2):
        widen_shared(shared, 0, half, far_wide.at[half])
    for box in range(2):

        def emit(row, value):
            out[box, row] = value

        if box == 0:
            multiply(wide.at[core, core], [row * mask for row in rows], rank, emit)
        else:
            multiply(far_wide.at[core], rows, rank, emit)


def pair_far_kernel(level, size, present, wide, far_wide, shared, near, out, total):
    rank = near.shape[1]
    core = digits()[3]
    rows = sent_rows(shared)
    mask = present[core, level, 1 - core]
    fold = LANES // size
    depth = rank // fold
    for box in range(2):

        def emit(row, value):
            total[row] = near[box, row] + value

        if box == 0:
            multiply(wide.at[1 - core, core], [row * mask for row in rows], rank, emit)
        else:
            multiply(far_wide.at[1 - core], rows, rank, emit)
        pieces = swap_groups([total[place * depth:(place + 1) * depth] for place in range(fold)], size)
        for place, piece in enumerate(pieces):
            out[place // 2, core ^ box, place % 2] = piece.astype(jnp.bfloat16)


def widen_kernel(shared, wide):
    for half in range(2):
        widen_shared(shared, 1, half, wide.at[half])


def pair_box(wides, total, states, presents, out):
    for half in range(2):
        present = presents[half]
        rows = [states[half, index].astype(jnp.float32) for index in range(out.shape[0])]
        if present is not None:
            rows = [row * present for row in rows]

        def emit(row, value):
            if half == 0:
                total[row] = value
            else:
                out[row] = (total[row] + value).astype(jnp.bfloat16)

        multiply(wides[half], rows, out.shape[0], emit)


def open_kernel(size, present, wide, moved, *rest):
    out, states, total = rest[-3:]
    core = digits()[3]
    fold = LANES // size
    depth = out.shape[0] // fold
    for last in range(2):
        tile = swap_groups([moved[place // 2, place % 2, last].astype(jnp.float32) for place in range(fold)], size)
        for place, rows in enumerate(tile):
            states[last, place * depth:(place + 1) * depth] = rows.astype(jnp.bfloat16)
    pair_box(
        [wide.at[half, core] for half in range(2)], total, states, [present[core, 0, half] for half in range(2)], out,
    )


def other_kernel(wide, states, out, total):
    pair_box([wide.at[half] for half in range(2)], total, states, (None, None), out)


def interp_kernel(interp, matrix, wide):
    rank = interp.shape[1]
    spread(wide, lambda row: interp[pl.ds(row, 8)].reshape(8 * rank, 2 * LANES), interp.shape[0], matrix[...])


def image_rows(level, bit, flip, present, wide, partner, near, total):
    places = digits()
    chunk, other = places[3] ^ flip, 1 - places[3 - bit]

    def emit(row, value):
        total[row] = (near[row] + value).astype(jnp.bfloat16).astype(jnp.float32)

    multiply(wide.at[other, chunk], state_rows(partner, present[chunk, level, other]), total.shape[0], emit)
    return [total[index] for index in range(total.shape[0])]


def first_image_kernel(level, bit, present, wide, image_wide, partner, near, out, total):
    rows = image_rows(level, bit, 0, present, wide, partner, near, total)

    def emit(row, value):
        out[row] = value.astype(jnp.bfloat16)

    multiply(image_wide.at[digits()[3]], rows, out.shape[0], emit)


def last_kernel(level, bit, present, wide, image_wide, partner, near, ready, back, image, both, held, total, sems):
    core = digits()[3]
    for row in range(ready.shape[0]):
        both[row, :, lanes_of(core)] = ready[row]
    rows = image_rows(level, bit, 1, present, wide, partner, near, total)
    rank, parts = total.shape[0], sems.shape[0]
    size, rhs_count = held.shape[0] // parts, held.shape[1]
    copies = []
    for part in range(parts):

        def emit(row, value):
            both[part * size + row, :, lanes_of(1 - core)] = value.astype(jnp.bfloat16)

        multiply(image_wide.at[1 - core, pl.ds(part * size * rank, size * rank), :], rows, size, emit)
        span = pl.ds(part * size, size)
        natural = reorder(both[span].reshape(size * rhs_count, 2 * LANES), back[...])
        held[span] = natural.astype(jnp.bfloat16).reshape(size, rhs_count, 2 * LANES)
        copies.append(pltpu.make_async_copy(held.at[span], image.at[span], sems.at[part]))
        copies[-1].start()
    for copy in copies:
        copy.wait()


def run(kernel, outs, operands, scratch=(), products=1, in_specs=None, out_specs=None, aliases=None, limit=KERNEL_LIMIT):
    whole = pl.BlockSpec(memory_space=pltpu.VMEM)
    single = not isinstance(outs, list)
    shapes = [outs] if single else outs
    result = pl.pallas_call(
        kernel,
        out_shape=shapes,
        in_specs=in_specs or [whole] * len(operands),
        out_specs=out_specs or [whole] * len(shapes),
        scratch_shapes=list(scratch),
        input_output_aliases=aliases or {},
        compiler_params=pltpu.CompilerParams(vmem_limit_bytes=limit),
        cost_estimate=pl.CostEstimate(flops=products * KERNEL_COST, bytes_accessed=products * KERNEL_COST, transcendentals=0),
    )(*operands)
    return result[0] if single else result


def permuted(value, target_of):
    pairs = [(source, target_of(source)) for source in range(lax.axis_size("leaf"))]
    return lax.ppermute(value, "leaf", pairs)


def swapped(value, bit):
    return permuted(value, lambda source: source ^ 2**bit)


def fast_local(samples, interp_in, top_blocks, top_pattern, bottom_blocks, bottom_pattern, interp_out):
    rank, depth = interp_in.shape[:2]
    rhs_count, box_count = samples.shape[1:]
    out_depth = interp_out.shape[0]
    leaf_count = lax.axis_size("leaf")
    slot = box_count // leaf_count
    size = slot // 2
    fold = LANES // size
    bf16, f32 = jnp.bfloat16, jnp.float32
    state = jax.ShapeDtypeStruct((rank, rhs_count, LANES), bf16)
    partial = jax.ShapeDtypeStruct((rank, rhs_count, LANES), f32)
    level_wide = jax.ShapeDtypeStruct((2, 2, rank * rank, LANES), f32)
    pair_wide = jax.ShapeDtypeStruct((2, rank * rank, LANES), f32)
    order = jax.ShapeDtypeStruct((box_count, box_count), bf16)
    presence = jax.ShapeDtypeStruct((2, 4, 2, 8, LANES), f32)
    total = pltpu.VMEM((rank, rhs_count, LANES), f32)
    whole, anywhere = pl.BlockSpec(memory_space=pltpu.VMEM), pl.BlockSpec(memory_space=pl.ANY)

    def ahead(blocks, level, *after):
        return run(functools.partial(ahead_kernel, level), level_wide, (blocks, matrix, *after), products=4)

    def level_nears(present, level, bit, order, wide, extra=()):
        return {
            flip: run(
                functools.partial(near_kernel, level, bit, flip), partial,
                (present, current[flip], wide) + ((current[1 - flip], *extra) if place < len(order) - 1 else ()),
            )
            for place, flip in enumerate(order)
        }

    def level_fars(present, level, bit, order, wide):
        return {
            flip: run(functools.partial(far_kernel, level, bit, flip), state, (present, partner[flip], near[flip], wide))
            for flip in order
        }

    current = {
        flip: run(
            functools.partial(coeff_kernel, flip, slot), state, (interp_in, samples),
            (
                pltpu.VMEM((rank * depth // 2, LANES), f32), pltpu.VMEM((depth * rhs_count, LANES), f32), total,
            ), 2,
        )
        for flip in (1, 0)
    }
    wide, matrix, back, top_present, bottom_present = run(
        functools.partial(fetch_kernel, slot), [level_wide, order, order, presence, presence],
        (top_blocks, top_pattern, bottom_pattern, current[0]),
        (pltpu.VMEM((1, *top_blocks.shape[1:]), bf16), pltpu.SemaphoreType.DMA), 4,
        in_specs=[anywhere, whole, whole, whole], limit=FETCH_LIMIT,
    )
    for level in range(3):
        bit = 3 - level
        partner = {flip: swapped(current[flip], bit) for flip in (1, 0)}
        if level > 0:
            wide = later[level]
        near = level_nears(top_present, level, bit, (1, 0), wide)
        if level == 0:
            later = {number: ahead(top_blocks, number, near[0]) for number in (1, 2, 3)}
            first_wide = ahead(bottom_blocks, 0, near[0])
        if level < 2:
            current = level_fars(top_present, level, bit, (1, 0), wide)

    share_rows = 2 * rank + rank * rhs_count // (2 * rank)
    shared_shape = jax.ShapeDtypeStruct((share_rows, 2 * rank, LANES), bf16)
    shared = run(
        functools.partial(share_kernel, 3), shared_shape, (later[3], top_present, first_wide, bottom_present),
    )
    shared = run(
        functools.partial(send_kernel, 2, 1, 1), shared_shape, (top_present, partner[1], near[1], wide, shared), aliases={4: 0},
    )
    shared = swapped(shared, 0)
    current = level_fars(top_present, 2, 1, (0,), wide)

    pair_near, far_wide = run(
        functools.partial(pair_near_kernel, 3),
        [jax.ShapeDtypeStruct((2, rank, rhs_count, LANES), f32), pair_wide],
        (top_present, later[3], shared, current[0]), products=2,
    )
    piece = jax.ShapeDtypeStruct((leaf_count // 2, 2, 2, rank // fold, rhs_count, LANES), bf16)
    pieces = run(
        functools.partial(pair_far_kernel, 3, size), piece,
        (top_present, later[3], far_wide, shared, pair_near), (total,), 2,
    )
    groups = [[place * 2 + core for place in range(leaf_count // 2)] for core in range(2)]
    moved = lax.all_to_all(pieces, "leaf", split_axis=0, concat_axis=0, axis_index_groups=groups, tiled=True)
    other_wide = run(widen_kernel, pair_wide, (shared,))
    wides = {level: ahead(bottom_blocks, level, pieces) for level in (1, 2, 3)}
    image_wide = run(interp_kernel, jax.ShapeDtypeStruct((2, out_depth * rank, LANES), f32), (interp_out, matrix))
    first, states = run(
        functools.partial(open_kernel, size), [state, jax.ShapeDtypeStruct((2, rank, rhs_count, LANES), bf16)],
        (bottom_present, first_wide, moved, *wides.values(), image_wide, other_wide), (total,), 2,
    )
    current = {0: first}
    partner = {0: swapped(first, 1)}
    current[1] = swapped(run(other_kernel, state, (other_wide, states), (total,), 2), 0)
    partner[1] = swapped(current[1], 1)
    for level in (1, 2, 3):
        if level > 1:
            partner = {flip: swapped(current[flip], level) for flip in (0, 1)}
        near = level_nears(bottom_present, level, level, (0, 1), wides[level])
        if level < 3:
            current = level_fars(bottom_present, level, level, (0, 1), wides[level])

    ready = run(
        functools.partial(first_image_kernel, 3, 3), jax.ShapeDtypeStruct((out_depth, rhs_count, LANES), bf16),
        (bottom_present, wides[3], image_wide, partner[0], near[0]), (total,), 3,
    )
    held = pltpu.VMEM((out_depth, rhs_count, box_count), bf16)
    return run(
        functools.partial(last_kernel, 3, 3), jax.ShapeDtypeStruct((out_depth, rhs_count, box_count), bf16),
        (bottom_present, wides[3], image_wide, partner[1], near[1], ready, back),
        (held, held, total, pltpu.SemaphoreType.DMA((4,))), 3, out_specs=[anywhere],
    )


def contract(weights, state):
    product = weights[:, :, None].astype(jnp.float32) * state[None].astype(jnp.float32)
    return jnp.sum(product, axis=1)


def plain_level(current, blocks, pattern, bit):
    rank = blocks.shape[0]
    partner = swapped(current, bit)
    is_lower = lax.axis_index("leaf") // 2**bit % 2 == 0
    lower = jnp.where(is_lower, current, partner)
    upper = jnp.where(is_lower, partner, current)
    weights = blocks * jnp.repeat(pattern, rank, axis=0).astype(jnp.bfloat16)[None]
    return contract(weights, jnp.concatenate([lower, upper], axis=0)).astype(jnp.bfloat16)


def plain_local(samples, interp_in, top_blocks, top_pattern, bottom_blocks, bottom_pattern, interp_out):
    bit_count = lax.axis_size("leaf").bit_length() - 1
    current = contract(interp_in, samples).astype(jnp.bfloat16)
    for level in range(top_blocks.shape[0]):
        current = plain_level(current, top_blocks[level], top_pattern[level], bit_count - 1 - level)
    flat = current.reshape(-1, current.shape[2])
    current = lax.all_to_all(flat, "leaf", split_axis=1, concat_axis=1, tiled=True).reshape(current.shape)
    for level in range(bottom_blocks.shape[0]):
        current = plain_level(current, bottom_blocks[level], bottom_pattern[level], level)
    return contract(interp_out, current).astype(jnp.bfloat16)


def local(samples, interp_in, top_blocks, *rest):
    four_digits = lax.axis_size("leaf") == 16 and top_blocks.shape[0] == 4
    chosen = fast_local if four_digits and samples.shape[1:] == (8, 2 * LANES) else plain_local
    return chosen(samples, interp_in, top_blocks, *rest)


def solution(mesh):
    boxes = ("parts", "leaf")
    return jax.shard_map(
        local,
        mesh=mesh,
        in_specs=(
            P(None, None, boxes),
            P(None, None, boxes),
            P(None, None, None, boxes),
            P(None, None, boxes),
            P(None, None, None, boxes),
            P(None, None, boxes),
            P(None, None, boxes),
        ),
        out_specs=P(None, None, boxes),
        check_vma=False,
    )
```

time: 67.1 us -> 86.2 us (1.28)
  Pallas kernels: 22.2 us -> 39.6 us
  local copies, waits for them, and re-layouts: 2.2 us -> 14.5 us
  waiting for transfers between devices: 13 us -> 6.64 us
  starting transfers between devices: 29.2 us -> 24.5 us
    pallas_call x39 -> x41, Pallas kernels: 22.2 us -> 39.6 us  [run(): pl.pallas_call(kernel, out_shape=shapes, in_specs=in_specs or [whole] * l...]
    unnamed x14 -> x40, local copies, waits for them, and re-layouts: 2.2 us -> 14.5 us
    ppermute x18 -> x14, starting transfers between devices: 29.2 us -> 19.6 us  [permuted(): return lax.ppermute(value, 'leaf', pairs)]
    ppermute x18 -> x14, waiting for transfers between devices: 13 us -> 6.64 us  [permuted(): return lax.ppermute(value, 'leaf', pairs)]
    all_to_all x0 -> x1, starting transfers between devices: none -> 4.9 us  [fast_local(): lax.all_to_all(pieces, 'leaf', split_axis=0, concat_axis=0, axis_index_gr...]
  transfers between devices with their start and end apart: 18 -> 15, of which waited for: 13 -> 4; matrix products, arithmetic and copies ran while one was open for 0% -> 0% of each run, Pallas kernels for 22% -> 35%
where the time goes in v7:
time: 86.2 us; the launch traced here: 85.7 us
  Pallas kernels  39.6 us (46%)
  starting transfers between devices  24.5 us (28%)
  local copies, waits for them, and re-layouts  14.5 us (17%)
  waiting for transfers between devices  6.64 us (8%)
    pallas_call x41, Pallas kernels, run(): pl.pallas_call(kernel, out_shape=shapes, in_specs=in_specs or [whole] * l...  39.6 us
    ppermute x14, starting transfers between devices, permuted(): return lax.ppermute(value, 'leaf', pairs)  19.6 us
    unnamed x40, local copies, waits for them, and re-layouts  14.5 us
    ppermute x14, waiting for transfers between devices, permuted(): return lax.ppermute(value, 'leaf', pairs)  6.64 us
    all_to_all x1, starting transfers between devices, fast_local(): lax.all_to_all(pieces, 'leaf', split_axis=0, concat_axis=0, axis_index_gr...  4.9 us
  transfers between devices with their start and end apart: 15, of which 4 were waited for; matrix products, arithmetic and copies ran while one was open for 0% of the time, Pallas kernels for 35%

profile of v7, /device:TPU:0, one launch (start us, length us, event | category | flops | bytes accessed | tf_op | source)
XLA Modules:
  0.0 85.7 jit_solution(3433405518770692459)
XLA Ops:
  0.0 1.2 %copy-done.13 = bf16[32,64,256]{2,1,0:T(8,128)(2,1)S(1)} copy-done((bf16[32,64,256]{2,1,0:T(8,128)(2,1)S(1)}, bf16[32,64,256]{2,1,0:T(8,128)(2,1)}, u32[]{:S(2)}) %copy-start.13) | copy-done | bytes 1048600
  1.2 0.9 %copy-done.15 = bf16[64,8,256]{2,1,0:T(8,128)(2,1)S(1)} copy-done((bf16[64,8,256]{2,1,0:T(8,128)(2,1)S(1)}, bf16[64,8,256]{2,1,0:T(8,128)(2,1)}, u32[]{:S(2)}) %copy-start.15) | copy-done | bytes 262168
  2.2 2.4 %shard_map.77.state = bf16[32,8,128]{2,1,0:T(8,128)(2,1)S(1)} custom-call(bf16[32,64,256]{2,1,0:T(8,128)(2,1)S(1)} %copy-done.13, bf16[64,8,256]{2,1,0:T(8,128)(2,1)S(1)} %copy-done.15), custom_call_target="tpu_custom_call" | custom-call | flops 2048 | bytes 2048 | tf_op jit(solution)/shard_map/pallas_call | solution.py:344
  4.6 4.1 %collective-permute-start = (bf16[32,8,128]{2,1,0:T(8,128)(2,1)S(1)}, bf16[32,8,128]{2,1,0:T(8,128)(2,1)S(1)}, u32[]{:S(2)}, u32[]{:S(2)}) collective-permute-start(bf16[32,8,128]{2,1,0:T(8,128)(2,1)S(1)} %shard_map.77.state), channel_id=1, source_target_pairs={{0,8},{1,9},{2,10},{3,11},{4,12},{5,13},{6,14},{7,15},{8,0},{9,1},... | collective-permute-start | bytes 196616 | tf_op jit(solution)/shard_map/ppermute | solution.py:359
  8.7 2.4 %shard_map.73.after.state.rest_0_ = bf16[32,8,128]{2,1,0:T(8,128)(2,1)S(1)} custom-call(bf16[32,64,256]{2,1,0:T(8,128)(2,1)S(1)} %copy-done.13, bf16[64,8,256]{2,1,0:T(8,128)(2,1)S(1)} %copy-done.15), custom_call_target="tpu_custom_call" | custom-call | flops 2048 | bytes 2048 | tf_op jit(solution)/shard_map/pallas_call | solution.py:344
  11.2 2.8 %shard_map.74 = (f32[2,2,1024,128]{3,2,1,0:T(8,128)S(1)}, bf16[256,256]{1,0:T(8,128)(2,1)S(1)}, bf16[256,256]{1,0:T(8,128)(2,1)S(1)}, f32[2,4,2,8,128]{4,3,2,1,0:T(8,128)S(1)}, f32[2,4,2,8,128]{4,3,2,1,0:T(8,128)S(1)}) custom-call(bf16[4,32,64,256]{3,2,1,0:T(8,128)(2,1)} %blocks.11, s32[4,2,256]{2,1,0:T(2,128)S(1)} %copy-done.18, ...), custom_call_target="tpu_custom_call" | custom-call | flops 4096 | bytes 4096 | tf_op jit(solution)/shard_map/pallas_call | solution.py:344
  14.0 0.7 copy-done.16
  14.6 0.4 shard_map.78.near
  15.0 0.4 shard_map.79.state
  15.4 1.9 %collective-permute-start.1 = (bf16[32,8,128]{2,1,0:T(8,128)(2,1)S(1)}, bf16[32,8,128]{2,1,0:T(8,128)(2,1)S(1)}, u32[]{:S(2)}, u32[]{:S(2)}) collective-permute-start(bf16[32,8,128]{2,1,0:T(8,128)(2,1)S(1)} %shard_map.79.state), channel_id=1, source_target_pairs={{0,4},{1,5},{2,6},{3,7},{4,0},{5,1},{6,2},{7,3},{8,12},{9,13},{10,... | collective-permute-start | bytes 196616 | tf_op jit(solution)/shard_map/ppermute | solution.py:359
  17.4 0.4 shard_map.75.rest_0_.near
  17.8 0.4 shard_map.81.rest_0_.state
  18.4 1.5 %shard_map.80.wide = f32[2,2,1024,128]{3,2,1,0:T(8,128)S(1)} custom-call(bf16[4,32,64,256]{3,2,1,0:T(8,128)(2,1)S(1)} %copy-done.5, bf16[256,256]{1,0:T(8,128)(2,1)S(1)} %get-tuple-element.15.matrix, f32[32,8,128]{2,1,0:T(8,128)S(1)} %shard_map.75.rest_0_.near), custom_call_target="tpu_custom_call" | custom-call | flops 4096 | bytes 4096 | tf_op jit(solution)/shard_map/pallas_call | solution.py:344
  19.9 0.4 shard_map.82.near
  20.3 0.4 shard_map.83.state
  20.7 1.9 %collective-permute-start.3 = (bf16[32,8,128]{2,1,0:T(8,128)(2,1)S(1)}, bf16[32,8,128]{2,1,0:T(8,128)(2,1)S(1)}, u32[]{:S(2)}, u32[]{:S(2)}) collective-permute-start(bf16[32,8,128]{2,1,0:T(8,128)(2,1)S(1)} %shard_map.83.state), channel_id=1, source_target_pairs={{0,2},{1,3},{2,0},{3,1},{4,6},{5,7},{6,4},{7,5},{8,10},{9,11},{10,... | collective-permute-start | bytes 196616 | tf_op jit(solution)/shard_map/ppermute | solution.py:359
  22.6 1.5 %shard_map.84.wide = f32[2,2,1024,128]{3,2,1,0:T(8,128)S(1)} custom-call(bf16[4,32,64,256]{3,2,1,0:T(8,128)(2,1)S(1)} %copy-done.5, bf16[256,256]{1,0:T(8,128)(2,1)S(1)} %get-tuple-element.15.matrix, f32[32,8,128]{2,1,0:T(8,128)S(1)} %shard_map.75.rest_0_.near), custom_call_target="tpu_custom_call" | custom-call | flops 4096 | bytes 4096 | tf_op jit(solution)/shard_map/pallas_call | solution.py:344
  24.1 1.5 %shard_map.76.top_wide.wide = f32[2,2,1024,128]{3,2,1,0:T(8,128)S(1)} custom-call(bf16[4,32,64,256]{3,2,1,0:T(8,128)(2,1)S(1)} %copy-done.5, bf16[256,256]{1,0:T(8,128)(2,1)S(1)} %get-tuple-element.15.matrix, f32[32,8,128]{2,1,0:T(8,128)S(1)} %shard_map.75.rest_0_.near), custom_call_target="tpu_custom_call" | custom-call | flops 4096 | bytes 4096 | tf_op jit(solution)/shard_map/pallas_call | solution.py:344
  25.6 0.7 copy-done.6
  26.3 1.5 %shard_map.88.bottom_wide.wide = f32[2,2,1024,128]{3,2,1,0:T(8,128)S(1)} custom-call(bf16[4,32,64,256]{3,2,1,0:T(8,128)(2,1)S(1)} %copy-done.6, bf16[256,256]{1,0:T(8,128)(2,1)S(1)} %get-tuple-element.15.matrix, f32[32,8,128]{2,1,0:T(8,128)S(1)} %shard_map.75.rest_0_.near), custom_call_target="tpu_custom_call" | custom-call | flops 4096 | bytes 4096 | tf_op jit(solution)/shard_map/pallas_call | solution.py:344
  27.8 0.4 shard_map.85.near
  28.2 0.4 shard_map.86.rest_0_.state
  28.6 0.5 copy-done.11
  29.4 0.4 shard_map.87.near
  29.8 0.4 shard_map.90
  30.6 0.4 shard_map.91.near
  30.9 3.9 %collective-permute-done.6.partner = bf16[32,8,128]{2,1,0:T(8,128)(2,1)S(1)} collective-permute-done((bf16[32,8,128]{2,1,0:T(8,128)(2,1)S(1)}, bf16[32,8,128]{2,1,0:T(8,128)(2,1)S(1)}, u32[]{:S(2)}, u32[]{:S(2)}) %collective-permute-start.6) | collective-permute-done | bytes 65568 | tf_op jit(solution)/shard_map/ppermute | solution.py:359
  34.8 0.4 shard_map.92.state
  35.2 0.9 %shard_map.93 = (f32[2,32,8,128]{3,2,1,0:T(8,128)S(1)}, f32[2,1024,128]{2,1,0:T(8,128)S(1)}) custom-call(f32[2,4,2,8,128]{4,3,2,1,0:T(8,128)S(1)} %get-tuple-element.16.present.top_present, f32[2,2,1024,128]{3,2,1,0:T(8,128)S(1)} %shard_map.76.top_wide.wide, bf16[68,64,128]{2,1,0:T(8,128)(2,1)S(1)} %collective-permute-done.5.shared, ...), custom_call_target="tpu_custom_call" | custom-call | flops 2048 | bytes 2048 | tf_op jit(solution)/shard_map/pallas_call | solution.py:344
  36.1 2.0 %shard_map.94.rest_0_ = bf16[8,2,2,2,8,128]{5,4,3,2,1,0:T(8,128)(2,1)} custom-call(f32[2,4,2,8,128]{4,3,2,1,0:T(8,128)S(1)} %get-tuple-element.16.present.top_present, f32[2,2,1024,128]{3,2,1,0:T(8,128)S(1)} %shard_map.76.top_wide.wide, f32[2,1024,128]{2,1,0:T(8,128)S(1)} %get-tuple-element.18.far_wide, ...), custom_call_target="tpu_custom_call" | custom-call | flops 2048 | bytes 2048 | tf_op jit(solution)/shard_map/pallas_call | solution.py:344
  38.1 4.9 %all-to-all-start = ((bf16[8,2,2,2,8,128]{5,4,3,2,1,0:T(8,128)(2,1)}), bf16[8,2,2,2,8,128]{5,4,3,2,1,0:T(8,128)(2,1)S(1)}, u32[]{:S(2)}, u32[]{:S(2)}) async-start(bf16[8,2,2,2,8,128]{5,4,3,2,1,0:T(8,128)(2,1)} %shard_map.94.rest_0_), calls=%async_computation | async-start | bytes 262144 | tf_op jit(solution)/shard_map/all_to_all | solution.py:451
  43.0 1.5 %shard_map.96.rest_3_.image_wide = f32[2,2048,128]{2,1,0:T(8,128)S(1)} custom-call(bf16[64,32,256]{2,1,0:T(8,128)(2,1)S(1)} %copy-done.14, bf16[256,256]{1,0:T(8,128)(2,1)S(1)} %get-tuple-element.15.matrix), custom_call_target="tpu_custom_call" | custom-call | flops 1024 | bytes 1024 | tf_op jit(solution)/shard_map/pallas_call | solution.py:344
  44.6 1.4 %copy-done.8 = f32[2,2048,128]{2,1,0:T(8,128)} copy-done((f32[2,2048,128]{2,1,0:T(8,128)}, f32[2,2048,128]{2,1,0:T(8,128)S(1)}, u32[]{:S(2)}) %copy-start.8) | copy-done | bytes 2097176
  46.0 2.4 %shard_map.99.rest_1_.wide = f32[2,2,1024,128]{3,2,1,0:T(8,128)S(1)} custom-call(bf16[4,32,64,256]{3,2,1,0:T(8,128)(2,1)S(1)} %copy-done.7, bf16[256,256]{1,0:T(8,128)(2,1)S(1)} %get-tuple-element.15.matrix, bf16[8,2,2,2,8,128]{5,4,3,2,1,0:T(8,128)(2,1)} %shard_map.94.rest_0_), custom_call_target="tpu_custom_call" | custom-call | flops 4096 | bytes 4096 | tf_op jit(solution)/shard_map/pallas_call | solution.py:344
  48.5 1.4 %copy-done = f32[2,2,1024,128]{3,2,1,0:T(8,128)} copy-done((f32[2,2,1024,128]{3,2,1,0:T(8,128)}, f32[2,2,1024,128]{3,2,1,0:T(8,128)S(1)}, u32[]{:S(2)}) %copy-start) | copy-done | bytes 2097176
  49.9 2.4 %shard_map.98.rest_0_.wide = f32[2,2,1024,128]{3,2,1,0:T(8,128)S(1)} custom-call(bf16[4,32,64,256]{3,2,1,0:T(8,128)(2,1)S(1)} %copy-done.7, bf16[256,256]{1,0:T(8,128)(2,1)S(1)} %get-tuple-element.15.matrix, bf16[8,2,2,2,8,128]{5,4,3,2,1,0:T(8,128)(2,1)} %shard_map.94.rest_0_), custom_call_target="tpu_custom_call" | custom-call | flops 4096 | bytes 4096 | tf_op jit(solution)/shard_map/pallas_call | solution.py:344
  52.3 1.4 %copy-done.3 = f32[2,2,1024,128]{3,2,1,0:T(8,128)} copy-done((f32[2,2,1024,128]{3,2,1,0:T(8,128)}, f32[2,2,1024,128]{3,2,1,0:T(8,128)S(1)}, u32[]{:S(2)}) %copy-start.3) | copy-done | bytes 2097176
  53.7 2.4 %shard_map.95.rest_2_.wide = f32[2,2,1024,128]{3,2,1,0:T(8,128)S(1)} custom-call(bf16[4,32,64,256]{3,2,1,0:T(8,128)(2,1)S(1)} %copy-done.7, bf16[256,256]{1,0:T(8,128)(2,1)S(1)} %get-tuple-element.15.matrix, bf16[8,2,2,2,8,128]{5,4,3,2,1,0:T(8,128)(2,1)} %shard_map.94.rest_0_), custom_call_target="tpu_custom_call" | custom-call | flops 4096 | bytes 4096 | tf_op jit(solution)/shard_map/pallas_call | solution.py:344
  56.1 1.6 %copy-done.1 = f32[2,2,1024,128]{3,2,1,0:T(8,128)S(1)} copy-done((f32[2,2,1024,128]{3,2,1,0:T(8,128)S(1)}, f32[2,2,1024,128]{3,2,1,0:T(8,128)}, u32[]{:S(2)}) %copy-start.1) | copy-done | bytes 2097176
  57.7 1.6 %copy-done.4 = f32[2,2,1024,128]{3,2,1,0:T(8,128)S(1)} copy-done((f32[2,2,1024,128]{3,2,1,0:T(8,128)S(1)}, f32[2,2,1024,128]{3,2,1,0:T(8,128)}, u32[]{:S(2)}) %copy-start.4) | copy-done | bytes 2097176
  59.3 1.6 %copy-done.9 = f32[2,2048,128]{2,1,0:T(8,128)S(1)} copy-done((f32[2,2048,128]{2,1,0:T(8,128)S(1)}, f32[2,2048,128]{2,1,0:T(8,128)}, u32[]{:S(2)}) %copy-start.9) | copy-done | bytes 2097176
  60.9 1.6 %copy-done.12 = f32[2,2,1024,128]{3,2,1,0:T(8,128)S(1)} copy-done((f32[2,2,1024,128]{3,2,1,0:T(8,128)S(1)}, f32[2,2,1024,128]{3,2,1,0:T(8,128)}, u32[]{:S(2)}) %copy-start.12) | copy-done | bytes 2097176
  62.5 1.1 %shard_map.100 = (bf16[32,8,128]{2,1,0:T(8,128)(2,1)S(1)}, bf16[2,32,8,128]{3,2,1,0:T(8,128)(2,1)S(1)}) custom-call(f32[2,4,2,8,128]{4,3,2,1,0:T(8,128)S(1)} %get-tuple-element.14.bottom_present.present, f32[2,2,1024,128]{3,2,1,0:T(8,128)S(1)} %copy-done.12, bf16[8,2,2,2,8,128]{5,4,3,2,1,0:T(8,128)(2,1)S(1)} %all-to-all-done.moved, ...), custom_call_target="tpu_custom_call" | custom-call | flops 2048 | bytes 2048 | tf_op jit(solution)/shard_map/pallas_call | solution.py:344
  63.6 0.7 shard_map.101
  64.4 2.1 %collective-permute-start.11 = (bf16[32,8,128]{2,1,0:T(8,128)(2,1)S(1)}, bf16[32,8,128]{2,1,0:T(8,128)(2,1)S(1)}, u32[]{:S(2)}, u32[]{:S(2)}) collective-permute-start(bf16[32,8,128]{2,1,0:T(8,128)(2,1)S(1)} %get-tuple-element.21.state), channel_id=1, source_target_pairs={{0,2},{1,3},{2,0},{3,1},{4,6},{5,7},{6,4},{7,5},{8,10},{9,11},{10,... | collective-permute-start | bytes 196616 | tf_op jit(solution)/shard_map/ppermute | solution.py:359
  66.5 1.2 %collective-permute-start.8 = (bf16[32,8,128]{2,1,0:T(8,128)(2,1)S(1)}, bf16[32,8,128]{2,1,0:T(8,128)(2,1)S(1)}, u32[]{:S(2)}, u32[]{:S(2)}) collective-permute-start(bf16[32,8,128]{2,1,0:T(8,128)(2,1)S(1)} %collective-permute-done.7.state.rest_0_), channel_id=1, source_target_pairs={{0,2},{1,3},{2,0},{3,1},{4,6},{5,7},{6,4},{7,5},{8,10},{9,11},{10,... | collective-permute-start | bytes 196616 | tf_op jit(solution)/shard_map/ppermute | solution.py:359
  67.6 0.4 shard_map.107.near
  68.0 1.1 %collective-permute-done.11.partner = bf16[32,8,128]{2,1,0:T(8,128)(2,1)S(1)} collective-permute-done((bf16[32,8,128]{2,1,0:T(8,128)(2,1)S(1)}, bf16[32,8,128]{2,1,0:T(8,128)(2,1)S(1)}, u32[]{:S(2)}, u32[]{:S(2)}) %collective-permute-start.11) | collective-permute-done | bytes 65568 | tf_op jit(solution)/shard_map/ppermute | solution.py:359
  69.1 0.4 shard_map.108.state
  69.5 2.1 %collective-permute-start.12 = (bf16[32,8,128]{2,1,0:T(8,128)(2,1)S(1)}, bf16[32,8,128]{2,1,0:T(8,128)(2,1)S(1)}, u32[]{:S(2)}, u32[]{:S(2)}) collective-permute-start(bf16[32,8,128]{2,1,0:T(8,128)(2,1)S(1)} %shard_map.108.state), channel_id=1, source_target_pairs={{0,4},{1,5},{2,6},{3,7},{4,0},{5,1},{6,2},{7,3},{8,12},{9,13},{10,... | collective-permute-start | bytes 196616 | tf_op jit(solution)/shard_map/ppermute | solution.py:359
  71.6 0.4 shard_map.102.near
  72.0 0.4 shard_map.103.state.rest_0_
  72.8 0.4 shard_map.109.near
  73.1 0.4 shard_map.104.near
  73.5 0.4 collective-permute-done.12.partner
  73.9 0.4 shard_map.110.state
  74.3 3.3 %collective-permute-start.13 = (bf16[32,8,128]{2,1,0:T(8,128)(2,1)S(1)}, bf16[32,8,128]{2,1,0:T(8,128)(2,1)S(1)}, u32[]{:S(2)}, u32[]{:S(2)}) collective-permute-start(bf16[32,8,128]{2,1,0:T(8,128)(2,1)S(1)} %shard_map.110.state), channel_id=1, source_target_pairs={{0,8},{1,9},{2,10},{3,11},{4,12},{5,13},{6,14},{7,15},{8,0},{9,1},... | collective-permute-start | bytes 196616 | tf_op jit(solution)/shard_map/ppermute | solution.py:359
  77.5 0.4 shard_map.105.state.rest_0_
  77.9 2.0 %collective-permute-start.10 = (bf16[32,8,128]{2,1,0:T(8,128)(2,1)S(1)}, bf16[32,8,128]{2,1,0:T(8,128)(2,1)S(1)}, u32[]{:S(2)}, u32[]{:S(2)}) collective-permute-start(bf16[32,8,128]{2,1,0:T(8,128)(2,1)S(1)} %shard_map.105.state.rest_0_), channel_id=1, source_target_pairs={{0,8},{1,9},{2,10},{3,11},{4,12},{5,13},{6,14},{7,15},{8,0},{9,1},... | collective-permute-start | bytes 196616 | tf_op jit(solution)/shard_map/ppermute | solution.py:359
  80.0 0.4 shard_map.111.near
  80.3 0.4 shard_map.106.near
  80.8 1.2 %shard_map.112.ready = bf16[64,8,128]{2,1,0:T(8,128)(2,1)S(1)} custom-call(f32[2,4,2,8,128]{4,3,2,1,0:T(8,128)S(1)} %get-tuple-element.14.bottom_present.present, f32[2,2,1024,128]{3,2,1,0:T(8,128)S(1)} %shard_map.95.rest_2_.wide, f32[2,2048,128]{2,1,0:T(8,128)S(1)} %copy-done.10, bf16[32,8,128]{2,1,0:T(8,128)(2,1)S(1)} %collective-permute-done.13.partner, ...), custom_call_target="tpu_custom_call" | custom-call | flops 3072 | bytes 3072 | tf_op jit(solution)/shard_map/pallas_call | solution.py:344
  81.9 1.3 %collective-permute-done.10.partner = bf16[32,8,128]{2,1,0:T(8,128)(2,1)S(1)} collective-permute-done((bf16[32,8,128]{2,1,0:T(8,128)(2,1)S(1)}, bf16[32,8,128]{2,1,0:T(8,128)(2,1)S(1)}, u32[]{:S(2)}, u32[]{:S(2)}) %collective-permute-start.10) | collective-permute-done | bytes 65568 | tf_op jit(solution)/shard_map/ppermute | solution.py:359
  83.2 2.5 %shard_map.113 = bf16[64,8,256]{2,1,0:T(8,128)(2,1)} custom-call(f32[2,4,2,8,128]{4,3,2,1,0:T(8,128)S(1)} %get-tuple-element.14.bottom_present.present, f32[2,2,1024,128]{3,2,1,0:T(8,128)S(1)} %shard_map.95.rest_2_.wide, f32[2,2048,128]{2,1,0:T(8,128)S(1)} %copy-done.10, bf16[32,8,128]{2,1,0:T(8,128)(2,1)S(1)} %collective-permute-done.10.partner, ...), custom_call_target="tpu_custom_call" | custom-call | flops 3072 | bytes 3072 | tf_op jit(solution)/shard_map/pallas_call | solution.py:344
  (47 shorter events, 1.5 us)
Async XLA Ops:
  0.0 1.2 %copy-start.13 = (bf16[32,64,256]{2,1,0:T(8,128)(2,1)S(1)}, bf16[32,64,256]{2,1,0:T(8,128)(2,1)}, u32[]{:S(2)}) copy-start(bf16[32,64,256]{2,1,0:T(8,128)(2,1)} %interp.4) | copy-start | bytes 3145732
  1.2 0.9 %copy-start.15 = (bf16[64,8,256]{2,1,0:T(8,128)(2,1)S(1)}, bf16[64,8,256]{2,1,0:T(8,128)(2,1)}, u32[]{:S(2)}) copy-start(bf16[64,8,256]{2,1,0:T(8,128)(2,1)} %samples.3) | copy-start | bytes 786436
  2.2 9.0 %copy-start.18 = (s32[4,2,256]{2,1,0:T(2,128)S(1)}, s32[4,2,256]{2,1,0:T(2,128)}, u32[]{:S(2)}) copy-start(s32[4,2,256]{2,1,0:T(2,128)} %top_pattern.1) | copy-start | bytes 24580
  2.2 9.0 %copy-start.19 = (s32[4,2,256]{2,1,0:T(2,128)S(1)}, s32[4,2,256]{2,1,0:T(2,128)}, u32[]{:S(2)}) copy-start(s32[4,2,256]{2,1,0:T(2,128)} %bottom_pattern.1) | copy-start | bytes 24580
  4.6 10.4 %collective-permute-start = (bf16[32,8,128]{2,1,0:T(8,128)(2,1)S(1)}, bf16[32,8,128]{2,1,0:T(8,128)(2,1)S(1)}, u32[]{:S(2)}, u32[]{:S(2)}) collective-permute-start(bf16[32,8,128]{2,1,0:T(8,128)(2,1)S(1)} %shard_map.77.state), channel_id=1, source_target_pairs={{0,8},{1,9},{2,10},{3,11},{4,12},{5,13},{6,14},{7,15},{8,0},{9,1},... | collective-permute-start | bytes 196616 | tf_op jit(solution)/shard_map/ppermute | solution.py:359
  11.1 6.6 %collective-permute-start.2 = (bf16[32,8,128]{2,1,0:T(8,128)(2,1)S(1)}, bf16[32,8,128]{2,1,0:T(8,128)(2,1)S(1)}, u32[]{:S(2)}, u32[]{:S(2)}) collective-permute-start(bf16[32,8,128]{2,1,0:T(8,128)(2,1)S(1)} %shard_map.73.after.state.rest_0_), channel_id=1, source_target_pairs={{0,8},{1,9},{2,10},{3,11},{4,12},{5,13},{6,14},{7,15},{8,0},{9,1},... | collective-permute-start | bytes 196616 | tf_op jit(solution)/shard_map/ppermute | solution.py:359
  14.0 0.7 copy-start.16
  15.4 3.0 %copy-start.5 = (bf16[4,32,64,256]{3,2,1,0:T(8,128)(2,1)S(1)}, bf16[4,32,64,256]{3,2,1,0:T(8,128)(2,1)}, u32[]{:S(2)}) copy-start(bf16[4,32,64,256]{3,2,1,0:T(8,128)(2,1)} %blocks.11) | copy-start | bytes 12582916
  15.4 4.9 %collective-permute-start.1 = (bf16[32,8,128]{2,1,0:T(8,128)(2,1)S(1)}, bf16[32,8,128]{2,1,0:T(8,128)(2,1)S(1)}, u32[]{:S(2)}, u32[]{:S(2)}) collective-permute-start(bf16[32,8,128]{2,1,0:T(8,128)(2,1)S(1)} %shard_map.79.state), channel_id=1, source_target_pairs={{0,4},{1,5},{2,6},{3,7},{4,0},{5,1},{6,2},{7,3},{8,12},{9,13},{10,... | collective-permute-start | bytes 196616 | tf_op jit(solution)/shard_map/ppermute | solution.py:359
  18.2 10.1 %collective-permute-start.4 = (bf16[32,8,128]{2,1,0:T(8,128)(2,1)S(1)}, bf16[32,8,128]{2,1,0:T(8,128)(2,1)S(1)}, u32[]{:S(2)}, u32[]{:S(2)}) collective-permute-start(bf16[32,8,128]{2,1,0:T(8,128)(2,1)S(1)} %shard_map.81.rest_0_.state), channel_id=1, source_target_pairs={{0,4},{1,5},{2,6},{3,7},{4,0},{5,1},{6,2},{7,3},{8,12},{9,13},{10,... | collective-permute-start | bytes 196616 | tf_op jit(solution)/shard_map/ppermute | solution.py:359
  20.7 9.1 %collective-permute-start.3 = (bf16[32,8,128]{2,1,0:T(8,128)(2,1)S(1)}, bf16[32,8,128]{2,1,0:T(8,128)(2,1)S(1)}, u32[]{:S(2)}, u32[]{:S(2)}) collective-permute-start(bf16[32,8,128]{2,1,0:T(8,128)(2,1)S(1)} %shard_map.83.state), channel_id=1, source_target_pairs={{0,2},{1,3},{2,0},{3,1},{4,6},{5,7},{6,4},{7,5},{8,10},{9,11},{10,... | collective-permute-start | bytes 196616 | tf_op jit(solution)/shard_map/ppermute | solution.py:359
  24.1 2.2 %copy-start.6 = (bf16[4,32,64,256]{3,2,1,0:T(8,128)(2,1)S(1)}, bf16[4,32,64,256]{3,2,1,0:T(8,128)(2,1)}, u32[]{:S(2)}) copy-start(bf16[4,32,64,256]{3,2,1,0:T(8,128)(2,1)} %blocks.15) | copy-start | bytes 12582916
  27.8 1.3 %copy-start.11 = (f32[2,2,1024,128]{3,2,1,0:T(8,128)}, f32[2,2,1024,128]{3,2,1,0:T(8,128)S(1)}, u32[]{:S(2)}) copy-start(f32[2,2,1024,128]{3,2,1,0:T(8,128)S(1)} %shard_map.88.bottom_wide.wide) | copy-start | bytes 6291460
  30.2 5.0 %collective-permute-start.5 = (bf16[68,64,128]{2,1,0:T(8,128)(2,1)S(1)}, bf16[68,64,128]{2,1,0:T(8,128)(2,1)S(1)}, u32[]{:S(2)}, u32[]{:S(2)}) collective-permute-start(bf16[68,64,128]{2,1,0:T(8,128)(2,1)S(1)} %shard_map.90), channel_id=1, source_target_pairs={{0,1},{1,0},{2,3},{3,2},{4,5},{5,4},{6,7},{7,6},{8,9},{9,8},{10,11... | collective-permute-start | bytes 3342344 | tf_op jit(solution)/shard_map/ppermute | solution.py:359
  30.3 4.5 %collective-permute-start.6 = (bf16[32,8,128]{2,1,0:T(8,128)(2,1)S(1)}, bf16[32,8,128]{2,1,0:T(8,128)(2,1)S(1)}, u32[]{:S(2)}, u32[]{:S(2)}) collective-permute-start(bf16[32,8,128]{2,1,0:T(8,128)(2,1)S(1)} %shard_map.86.rest_0_.state), channel_id=1, source_target_pairs={{0,2},{1,3},{2,0},{3,1},{4,6},{5,7},{6,4},{7,5},{8,10},{9,11},{10,... | collective-permute-start | bytes 196616 | tf_op jit(solution)/shard_map/ppermute | solution.py:359
  36.1 7.0 %copy-start.14 = (bf16[64,32,256]{2,1,0:T(8,128)(2,1)S(1)}, bf16[64,32,256]{2,1,0:T(8,128)(2,1)}, u32[]{:S(2)}) copy-start(bf16[64,32,256]{2,1,0:T(8,128)(2,1)} %interp.5) | copy-start | bytes 3145732
  38.1 18.0 %all-to-all-start = ((bf16[8,2,2,2,8,128]{5,4,3,2,1,0:T(8,128)(2,1)}), bf16[8,2,2,2,8,128]{5,4,3,2,1,0:T(8,128)(2,1)S(1)}, u32[]{:S(2)}, u32[]{:S(2)}) async-start(bf16[8,2,2,2,8,128]{5,4,3,2,1,0:T(8,128)(2,1)} %shard_map.94.rest_0_), calls=%async_computation | async-start | bytes 262144 | tf_op jit(solution)/shard_map/all_to_all | solution.py:451
  43.0 3.0 %copy-start.7 = (bf16[4,32,64,256]{3,2,1,0:T(8,128)(2,1)S(1)}, bf16[4,32,64,256]{3,2,1,0:T(8,128)(2,1)}, u32[]{:S(2)}) copy-start(bf16[4,32,64,256]{3,2,1,0:T(8,128)(2,1)} %blocks.15) | copy-start | bytes 12582916
  44.6 1.4 %copy-start.8 = (f32[2,2048,128]{2,1,0:T(8,128)}, f32[2,2048,128]{2,1,0:T(8,128)S(1)}, u32[]{:S(2)}) copy-start(f32[2,2048,128]{2,1,0:T(8,128)S(1)} %shard_map.96.rest_3_.image_wide) | copy-start | bytes 6291460
  48.5 1.4 %copy-start = (f32[2,2,1024,128]{3,2,1,0:T(8,128)}, f32[2,2,1024,128]{3,2,1,0:T(8,128)S(1)}, u32[]{:S(2)}) copy-start(f32[2,2,1024,128]{3,2,1,0:T(8,128)S(1)} %shard_map.99.rest_1_.wide) | copy-start | bytes 6291460
  52.3 1.4 %copy-start.3 = (f32[2,2,1024,128]{3,2,1,0:T(8,128)}, f32[2,2,1024,128]{3,2,1,0:T(8,128)S(1)}, u32[]{:S(2)}) copy-start(f32[2,2,1024,128]{3,2,1,0:T(8,128)S(1)} %shard_map.98.rest_0_.wide) | copy-start | bytes 6291460
  56.1 1.6 %copy-start.1 = (f32[2,2,1024,128]{3,2,1,0:T(8,128)S(1)}, f32[2,2,1024,128]{3,2,1,0:T(8,128)}, u32[]{:S(2)}) copy-start(f32[2,2,1024,128]{3,2,1,0:T(8,128)} %copy-done) | copy-start | bytes 6291460
  57.7 1.6 %copy-start.4 = (f32[2,2,1024,128]{3,2,1,0:T(8,128)S(1)}, f32[2,2,1024,128]{3,2,1,0:T(8,128)}, u32[]{:S(2)}) copy-start(f32[2,2,1024,128]{3,2,1,0:T(8,128)} %copy-done.3) | copy-start | bytes 6291460
  59.3 1.6 %copy-start.9 = (f32[2,2048,128]{2,1,0:T(8,128)S(1)}, f32[2,2048,128]{2,1,0:T(8,128)}, u32[]{:S(2)}) copy-start(f32[2,2048,128]{2,1,0:T(8,128)} %copy-done.8) | copy-start | bytes 6291460
  60.9 1.6 %copy-start.12 = (f32[2,2,1024,128]{3,2,1,0:T(8,128)S(1)}, f32[2,2,1024,128]{3,2,1,0:T(8,128)}, u32[]{:S(2)}) copy-start(f32[2,2,1024,128]{3,2,1,0:T(8,128)} %copy-done.11) | copy-start | bytes 6291460
  64.3 2.2 %collective-permute-start.7 = (bf16[32,8,128]{2,1,0:T(8,128)(2,1)S(1)}, bf16[32,8,128]{2,1,0:T(8,128)(2,1)S(1)}, u32[]{:S(2)}, u32[]{:S(2)}) collective-permute-start(bf16[32,8,128]{2,1,0:T(8,128)(2,1)S(1)} %shard_map.101), channel_id=1, source_target_pairs={{0,1},{1,0},{2,3},{3,2},{4,5},{5,4},{6,7},{7,6},{8,9},{9,8},{10,11... | collective-permute-start | bytes 196616 | tf_op jit(solution)/shard_map/ppermute | solution.py:359
  64.4 4.8 %collective-permute-start.11 = (bf16[32,8,128]{2,1,0:T(8,128)(2,1)S(1)}, bf16[32,8,128]{2,1,0:T(8,128)(2,1)S(1)}, u32[]{:S(2)}, u32[]{:S(2)}) collective-permute-start(bf16[32,8,128]{2,1,0:T(8,128)(2,1)S(1)} %get-tuple-element.21.state), channel_id=1, source_target_pairs={{0,2},{1,3},{2,0},{3,1},{4,6},{5,7},{6,4},{7,5},{8,10},{9,11},{10,... | collective-permute-start | bytes 196616 | tf_op jit(solution)/shard_map/ppermute | solution.py:359
  66.5 5.6 %collective-permute-start.8 = (bf16[32,8,128]{2,1,0:T(8,128)(2,1)S(1)}, bf16[32,8,128]{2,1,0:T(8,128)(2,1)S(1)}, u32[]{:S(2)}, u32[]{:S(2)}) collective-permute-start(bf16[32,8,128]{2,1,0:T(8,128)(2,1)S(1)} %collective-permute-done.7.state.rest_0_), channel_id=1, source_target_pairs={{0,2},{1,3},{2,0},{3,1},{4,6},{5,7},{6,4},{7,5},{8,10},{9,11},{10,... | collective-permute-start | bytes 196616 | tf_op jit(solution)/shard_map/ppermute | solution.py:359
  69.5 3.2 %copy-start.2 = (f32[2,2,1024,128]{3,2,1,0:T(8,128)S(1)}, f32[2,2,1024,128]{3,2,1,0:T(8,128)}, u32[]{:S(2)}) copy-start(f32[2,2,1024,128]{3,2,1,0:T(8,128)} %copy-done) | copy-start | bytes 6291460
  69.5 4.3 %collective-permute-start.12 = (bf16[32,8,128]{2,1,0:T(8,128)(2,1)S(1)}, bf16[32,8,128]{2,1,0:T(8,128)(2,1)S(1)}, u32[]{:S(2)}, u32[]{:S(2)}) collective-permute-start(bf16[32,8,128]{2,1,0:T(8,128)(2,1)S(1)} %shard_map.108.state), channel_id=1, source_target_pairs={{0,4},{1,5},{2,6},{3,7},{4,0},{5,1},{6,2},{7,3},{8,12},{9,13},{10,... | collective-permute-start | bytes 196616 | tf_op jit(solution)/shard_map/ppermute | solution.py:359
  72.4 5.1 %collective-permute-start.9 = (bf16[32,8,128]{2,1,0:T(8,128)(2,1)S(1)}, bf16[32,8,128]{2,1,0:T(8,128)(2,1)S(1)}, u32[]{:S(2)}, u32[]{:S(2)}) collective-permute-start(bf16[32,8,128]{2,1,0:T(8,128)(2,1)S(1)} %shard_map.103.state.rest_0_), channel_id=1, source_target_pairs={{0,4},{1,5},{2,6},{3,7},{4,0},{5,1},{6,2},{7,3},{8,12},{9,13},{10,... | collective-permute-start | bytes 196616 | tf_op jit(solution)/shard_map/ppermute | solution.py:359
  74.3 6.5 %collective-permute-start.13 = (bf16[32,8,128]{2,1,0:T(8,128)(2,1)S(1)}, bf16[32,8,128]{2,1,0:T(8,128)(2,1)S(1)}, u32[]{:S(2)}, u32[]{:S(2)}) collective-permute-start(bf16[32,8,128]{2,1,0:T(8,128)(2,1)S(1)} %shard_map.110.state), channel_id=1, source_target_pairs={{0,8},{1,9},{2,10},{3,11},{4,12},{5,13},{6,14},{7,15},{8,0},{9,1},... | collective-permute-start | bytes 196616 | tf_op jit(solution)/shard_map/ppermute | solution.py:359
  77.9 2.8 %copy-start.10 = (f32[2,2048,128]{2,1,0:T(8,128)S(1)}, f32[2,2048,128]{2,1,0:T(8,128)}, u32[]{:S(2)}) copy-start(f32[2,2048,128]{2,1,0:T(8,128)} %copy-done.8) | copy-start | bytes 6291460
  77.9 5.2 %collective-permute-start.10 = (bf16[32,8,128]{2,1,0:T(8,128)(2,1)S(1)}, bf16[32,8,128]{2,1,0:T(8,128)(2,1)S(1)}, u32[]{:S(2)}, u32[]{:S(2)}) collective-permute-start(bf16[32,8,128]{2,1,0:T(8,128)(2,1)S(1)} %shard_map.105.state.rest_0_), channel_id=1, source_target_pairs={{0,8},{1,9},{2,10},{3,11},{4,12},{5,13},{6,14},{7,15},{8,0},{9,1},... | collective-permute-start | bytes 196616 | tf_op jit(solution)/shard_map/ppermute | solution.py:359
  80.7 2.5 %copy-start.17 = (bf16[256,256]{1,0:T(8,128)(2,1)S(1)}, bf16[256,256]{1,0:T(8,128)(2,1)}, u32[]{:S(2)}) copy-start(bf16[256,256]{1,0:T(8,128)(2,1)} %copy-done.16) | copy-start | bytes 393220

commit v8 on v6

--- a/solution.py
+++ b/solution.py
@@ -12,6 +12,7 @@
 KERNEL_COST = 1024
 KERNEL_LIMIT = 16 * 2**20
 FETCH_LIMIT = 53_000_000
+START_LIMIT = 56_250_000
 
 
 def digits():
@@ -68,13 +69,22 @@
     return jnp.where(half == 0, pair[0], pair[1])
 
 
-def coeff_kernel(flip, interp, samples, out, wide, total):
+def coeff_kernel(flip, interp, samples, *rest):
+    out, held_interp, held_samples, wide, total, sems = rest[-6:]
     rank, depth = interp.shape[0], interp.shape[1] // 2
     lanes = lanes_of(digits()[3] ^ flip)
+    copies = []
     for half in range(2):
-        part = slice(half * depth, (half + 1) * depth)
-        spread(wide, lambda row: interp[pl.ds(row, GROUP), part, lanes], rank, depth)
-        state = [samples[half * depth + index, :, lanes].astype(jnp.float32) for index in range(depth)]
+        part = pl.ds(half * depth, depth)
+        copies.append(pltpu.make_async_copy(interp.at[:, part, lanes], held_interp.at[half], sems.at[half]))
+        copies.append(pltpu.make_async_copy(samples.at[part, :, lanes], held_samples.at[half], sems.at[half + 2]))
+    for copy in copies:
+        copy.start()
+    for half in range(2):
+        copies[2 * half].wait()
+        copies[2 * half + 1].wait()
+        spread(wide, lambda row: held_interp[half, pl.ds(row, GROUP)], rank, depth)
+        state = [held_samples[half, index].astype(jnp.float32) for index in range(depth)]
 
         def emit(row, value):
             if half == 0:
@@ -115,7 +125,8 @@
     multiply(wide, state_rows(state, present_of(pattern, level, own, chunk)), out.shape[0], emit)
 
 
-def far_kernel(level, bit, flip, pattern, partner, near, wide, out):
+def far_kernel(level, bit, flip, pattern, partner, near, wide, *rest):
+    out = rest[-1]
     places = digits()
     chunk, other = places[3] ^ flip, 1 - places[3 - bit]
 
@@ -132,12 +143,13 @@
         for half in range(2):
             present = present_of(pattern, level, half, chunk)[None]
 
-            def body(row, carry):
-                rows = blocks[level, pl.ds(row, 1), half * rank:(half + 1) * rank, lanes_of(chunk)]
-                out[place * rank + row, half * rank:(half + 1) * rank, :] = (rows.astype(jnp.float32) * present)[0].astype(jnp.bfloat16)
+            def body(step, carry):
+                rows = blocks[level, pl.ds(step * 8, 8), half * rank:(half + 1) * rank, lanes_of(chunk)]
+                span = pl.ds(place * rank + step * 8, 8)
+                out[span, half * rank:(half + 1) * rank, :] = (rows.astype(jnp.float32) * present).astype(jnp.bfloat16)
                 return carry
 
-            lax.fori_loop(0, rank, body, 0)
+            lax.fori_loop(0, rank // 8, body, 0)
 
 
 def shared_load(shared, place, half):
@@ -181,36 +193,32 @@
     return tile
 
 
-def pair_near_kernel(level, blocks, pattern, shared, state, out, far_wide, wide):
+def pair_far_kernel(level, blocks, pattern, shared, out, near_wide, wide):
     rank = blocks.shape[1]
     core = digits()[3]
+    rows = sent_rows(shared)
+    present = present_of(pattern, level, 1 - core, core)
+    for box in range(2):
+        for target, half in ((wide, 1 - core), (near_wide.at[box], core)):
+            spread(target, level_load(blocks, level, half, core) if box == 0 else shared_load(shared, 0, half), rank, rank)
+
+        def emit(row, value):
+            out[box, row] = value
+
+        multiply(wide, [row * present for row in rows] if box == 0 else rows, rank, emit)
+
+
+def pair_near_kernel(level, slot, pattern, wide, state, far, *rest):
+    outs, (total, packed) = rest[:4], rest[4:]
+    rank = state.shape[0]
+    _, mid, low, core = digits()
     rows = state_rows(state)
     present = present_of(pattern, level, core, core)
-    for box in range(2):
-        for target, half in ((wide, core), (far_wide.at[box], 1 - core)):
-            load = (
-                level_load(blocks, level, half, core)
-                if box == 0
-                else shared_load(shared, 0, half)
-            )
-            spread(target, load, rank, rank)
-
-        def emit(row, value):
-            out[box, row] = value
-
-        multiply(wide, [row * present for row in rows] if box == 0 else rows, rank, emit)
-
-
-def pair_far_kernel(level, slot, pattern, wide, shared, near, *rest):
-    outs, (total, packed) = rest[:4], rest[4:]
-    rank = near.shape[1]
-    _, mid, low, core = digits()
-    rows = sent_rows(shared)
-    present = present_of(pattern, level, 1 - core, core)
     fold = LANES // slot
     for box in range(2):
+
         def emit(row, value):
-            total[row] = near[box, row] + value
+            total[row] = far[box, row] + value
 
         multiply(wide.at[box], [row * present for row in rows] if box == 0 else rows, rank, emit)
         depth = rank // fold
@@ -248,25 +256,29 @@
         multiply(wide.at[half], rows, out.shape[0], emit)
 
 
-def open_kernel(slot, pattern, wide, *rest):
+def open_kernel(slot, wide, kept, *rest):
     pieces, (out, states, total, packed) = rest[:4], rest[-4:]
-    _, mid, low, core = digits()
+    high, mid, low, core = digits()
     fold = LANES // slot
     depth = out.shape[0] // fold
     for turn, piece in enumerate(pieces):
         first = ((mid ^ (turn // 2)) * 2 + (low ^ (turn % 2))) * 2
         for box in range(2):
             for last in range(2):
-                packed[last, first + box] = piece[box, last]
+                value = piece[box, last]
+                if turn == 0:
+                    value = jnp.where(high == core, kept[box, last], value)
+                packed[last, first + box] = value
     for last in range(2):
         tile = swap_groups([packed[last, place].astype(jnp.float32) for place in range(fold)], slot)
         for place, rows in enumerate(tile):
             states[last, place * depth:(place + 1) * depth] = rows.astype(jnp.bfloat16)
+    pair_box(wide, total, states, (None, None), out)
+
+
+def own_kernel(pattern, wide, states, out, total):
+    core = digits()[3]
     pair_box(wide, total, states, [present_of(pattern, 0, half, core) for half in range(2)], out)
-
-
-def other_kernel(wide, states, out, total):
-    pair_box(wide, total, states, (None, None), out)
 
 
 def interp_kernel(interp, first_wide, second_wide):
@@ -334,6 +346,7 @@
 
 def permuted(value, target_of):
     pairs = [(source, target_of(source)) for source in range(lax.axis_size("leaf"))]
+    pairs = [pair for pair in pairs if pair[0] != pair[1]]
     return lax.ppermute(value, "leaf", pairs)
 
 
@@ -373,22 +386,25 @@
             for place, flip in enumerate(order)
         }
 
-    def level_fars(pattern, level, bit, order, wides):
+    def level_fars(pattern, level, bit, order, wides, extra=()):
         return {
             flip: run(
                 functools.partial(far_kernel, level, bit, flip), state,
-                (pattern, partner[flip], near[flip], wides[1][flip]),
+                (pattern, partner[flip], near[flip], wides[1][flip], *extra),
             )
             for flip in order
         }
 
-    current = {
-        flip: run(
-            functools.partial(coeff_kernel, flip), state, (interp_in, samples),
-            (pltpu.VMEM((rank * depth // 2, LANES), jnp.float32), total), 2,
+    current = {}
+    for flip in (1, 0):
+        current[flip] = run(
+            functools.partial(coeff_kernel, flip), state, (interp_in, samples, *current.values()),
+            (
+                pltpu.VMEM((2, rank, depth // 2, LANES), jnp.bfloat16),
+                pltpu.VMEM((2, depth // 2, rhs_count, LANES), jnp.bfloat16),
+                pltpu.VMEM((rank * depth // 2, LANES), jnp.float32), total, pltpu.SemaphoreType.DMA((4,)),
+            ), 2, in_specs=[pl.BlockSpec(memory_space=pl.ANY)] * (2 + len(current)), limit=START_LIMIT,
         )
-        for flip in (1, 0)
-    }
     share_rows = 2 * rank + rank * rhs_count // (2 * rank)
     shared_shape = jax.ShapeDtypeStruct((share_rows, 2 * rank, LANES), jnp.bfloat16)
     for level in range(3):
@@ -417,31 +433,31 @@
         functools.partial(send_kernel, 2, 1, 1), shared_shape, (top_pattern, partner[1], near[1], wides[1][1], shared), aliases={4: 0},
     )
     shared = swapped(shared, 0)
-    current = level_fars(top_pattern, 2, 1, (0,), wides)
-
-    pair_near = run(
-        functools.partial(pair_near_kernel, 3),
+    pair_far, near_wide = run(
+        functools.partial(pair_far_kernel, 3),
         [jax.ShapeDtypeStruct((2, rank, rhs_count, LANES), jnp.float32), pair_spread],
-        (top_blocks, top_pattern, shared, current[0]), (wide,), 2,
-    )
+        (top_blocks, top_pattern, shared), (wide,), 2,
+    )
+    current = level_fars(top_pattern, 2, 1, (0,), wides, (pair_far,))
+
     piece = jax.ShapeDtypeStruct((2, 2, rank // fold, rhs_count, LANES), jnp.bfloat16)
     pieces = run(
-        functools.partial(pair_far_kernel, 3, slot), [piece] * 4,
-        (top_pattern, pair_near[1], shared, pair_near[0]), (total, packed), 2,
-    )
+        functools.partial(pair_near_kernel, 3, slot), [piece] * 4,
+        (top_pattern, near_wide, current[0], pair_far), (total, packed), 2,
+    )
+    kept = pieces[0]
     pieces = [permuted(value, functools.partial(crossed, turn=turn)) for turn, value in enumerate(pieces)]
     own_wide, other_wide = run(wide_kernel, [pair_spread] * 2, (bottom_blocks, shared))
-    wides = {level: level_wides(bottom_blocks, level, level, pair_near[0]) for level in (1, 2, 3)}
+    wides = {level: level_wides(bottom_blocks, level, level, kept) for level in (1, 2, 3)}
     image_spread = jax.ShapeDtypeStruct((out_depth * rank, LANES), jnp.float32)
     image_wide = run(interp_kernel, [image_spread] * 2, (interp_out,))
     spreads = [wide for level in (1, 2, 3) for group in wides[level] for wide in group]
-    first, states = run(
+    second, states = run(
         functools.partial(open_kernel, slot), [state, jax.ShapeDtypeStruct((2, rank, rhs_count, LANES), jnp.bfloat16)],
-        (bottom_pattern, own_wide, *pieces, *spreads, *image_wide), (total, packed), 2,
-    )
-    current = {0: first}
-    partner = {0: swapped(first, 1)}
-    current[1] = swapped(run(other_kernel, state, (other_wide, states), (total,), 2), 0)
+        (other_wide, kept, *pieces, *spreads, *image_wide), (total, packed), 2,
+    )
+    current = {1: swapped(second, 0), 0: run(own_kernel, state, (bottom_pattern, own_wide, states), (total,), 2)}
+    partner = {0: swapped(current[0], 1)}
     partner[1] = swapped(current[1], 1)
     for level in (1, 2, 3):
         if level > 1:

time: 67.1 us -> 61.3 us (0.914)
  waiting for transfers between devices: 13 us -> 9.7 us
  local copies, waits for them, and re-layouts: 2.2 us -> 0.02 us
  starting transfers between devices: 29.2 us -> 27.9 us
  Pallas kernels: 22.2 us -> 23.2 us
    ppermute x18, waiting for transfers between devices: 13 us -> 9.7 us  [permuted(): return lax.ppermute(value, 'leaf', pairs)]
    unnamed x14 -> x10, local copies, waits for them, and re-layouts: 2.2 us -> 0.02 us
    ppermute x18, starting transfers between devices: 29.2 us -> 27.9 us  [permuted(): return lax.ppermute(value, 'leaf', pairs)]
    pallas_call x39, Pallas kernels: 22.2 us -> 23.2 us  [run(): pl.pallas_call(kernel, out_shape=shapes, in_specs=in_specs or [whole] * l...]
  transfers between devices with their start and end apart: 18 -> 18, of which waited for: 13 -> 10; matrix products, arithmetic and copies ran while one was open for 0% -> 0% of each run, Pallas kernels for 22% -> 27%
where the time goes in v8:
time: 61.3 us; the launch traced here: 61.2 us
  starting transfers between devices  27.9 us (46%)
  Pallas kernels  23.2 us (38%)
  waiting for transfers between devices  9.7 us (16%)
    ppermute x18, starting transfers between devices, permuted(): return lax.ppermute(value, 'leaf', pairs)  27.9 us
    pallas_call x39, Pallas kernels, run(): pl.pallas_call(kernel, out_shape=shapes, in_specs=in_specs or [whole] * l...  23.2 us
    ppermute x18, waiting for transfers between devices, permuted(): return lax.ppermute(value, 'leaf', pairs)  9.7 us
  transfers between devices with their start and end apart: 18, of which 10 were waited for; matrix products, arithmetic and copies ran while one was open for 0% of the time, Pallas kernels for 27%

profile of v8, /device:TPU:0, one launch (start us, length us, event | category | flops | bytes accessed | tf_op | source)
XLA Modules:
  0.0 61.2 jit_solution(229491468856571323)
XLA Ops:
  0.0 1.8 %shard_map.73.rest_0_.state = bf16[32,8,128]{2,1,0:T(8,128)(2,1)S(1)} custom-call(bf16[32,64,256]{2,1,0:T(8,128)(2,1)} %interp.4, bf16[64,8,256]{2,1,0:T(8,128)(2,1)} %samples.3), custom_call_target="tpu_custom_call" | custom-call | flops 2048 | bytes 2048 | tf_op jit(solution)/shard_map/pallas_call | solution.py:334
  1.8 4.1 %collective-permute-start = (bf16[32,8,128]{2,1,0:T(8,128)(2,1)S(1)}, bf16[32,8,128]{2,1,0:T(8,128)(2,1)S(1)}, u32[]{:S(2)}, u32[]{:S(2)}) collective-permute-start(bf16[32,8,128]{2,1,0:T(8,128)(2,1)S(1)} %shard_map.73.rest_0_.state), channel_id=1, source_target_pairs={{0,8},{1,9},{2,10},{3,11},{4,12},{5,13},{6,14},{7,15},{8,0},{9,1},... | collective-permute-start | bytes 196616 | tf_op jit(solution)/shard_map/ppermute | solution.py:350
  6.0 1.8 %shard_map.74.after.rest_0_.state = bf16[32,8,128]{2,1,0:T(8,128)(2,1)S(1)} custom-call(bf16[32,64,256]{2,1,0:T(8,128)(2,1)} %interp.4, bf16[64,8,256]{2,1,0:T(8,128)(2,1)} %samples.3, bf16[32,8,128]{2,1,0:T(8,128)(2,1)S(1)} %shard_map.73.rest_0_.state), custom_call_target="tpu_custom_call" | custom-call | flops 2048 | bytes 2048 | tf_op jit(solution)/shard_map/pallas_call | solution.py:334
  7.9 1.7 %shard_map.75 = (f32[1024,128]{1,0:T(8,128)S(1)}, f32[1024,128]{1,0:T(8,128)S(1)}, f32[1024,128]{1,0:T(8,128)S(1)}, f32[1024,128]{1,0:T(8,128)S(1)}) custom-call(bf16[4,32,64,256]{3,2,1,0:T(8,128)(2,1)} %blocks.11, bf16[32,8,128]{2,1,0:T(8,128)(2,1)S(1)} %shard_map.74.after.rest_0_.state), custom_call_target="tpu_custom_call" | custom-call | flops 4096 | bytes 4096 | tf_op jit(solution)/shard_map/pallas_call | solution.py:334
  9.6 0.4 shard_map.76.near
  10.0 0.4 shard_map.77.state
  10.4 2.1 %collective-permute-start.1 = (bf16[32,8,128]{2,1,0:T(8,128)(2,1)S(1)}, bf16[32,8,128]{2,1,0:T(8,128)(2,1)S(1)}, u32[]{:S(2)}, u32[]{:S(2)}) collective-permute-start(bf16[32,8,128]{2,1,0:T(8,128)(2,1)S(1)} %shard_map.77.state), channel_id=1, source_target_pairs={{0,4},{1,5},{2,6},{3,7},{4,0},{5,1},{6,2},{7,3},{8,12},{9,13},{10,... | collective-permute-start | bytes 196616 | tf_op jit(solution)/shard_map/ppermute | solution.py:350
  12.5 0.4 shard_map.78.rest_0_.near
  12.9 0.3 shard_map.79
  13.2 0.2 collective-permute-done.2.partner
  13.4 0.4 shard_map.80.rest_0_.state
  13.8 1.2 %collective-permute-start.4 = (bf16[32,8,128]{2,1,0:T(8,128)(2,1)S(1)}, bf16[32,8,128]{2,1,0:T(8,128)(2,1)S(1)}, u32[]{:S(2)}, u32[]{:S(2)}) collective-permute-start(bf16[32,8,128]{2,1,0:T(8,128)(2,1)S(1)} %shard_map.80.rest_0_.state), channel_id=1, source_target_pairs={{0,4},{1,5},{2,6},{3,7},{4,0},{5,1},{6,2},{7,3},{8,12},{9,13},{10,... | collective-permute-start | bytes 196616 | tf_op jit(solution)/shard_map/ppermute | solution.py:350
  15.1 0.4 shard_map.81.near
  15.5 0.4 shard_map.82.state
  15.9 1.6 %collective-permute-start.3 = (bf16[32,8,128]{2,1,0:T(8,128)(2,1)S(1)}, bf16[32,8,128]{2,1,0:T(8,128)(2,1)S(1)}, u32[]{:S(2)}, u32[]{:S(2)}) collective-permute-start(bf16[32,8,128]{2,1,0:T(8,128)(2,1)S(1)} %shard_map.82.state), channel_id=1, source_target_pairs={{0,2},{1,3},{2,0},{3,1},{4,6},{5,7},{6,4},{7,5},{8,10},{9,11},{10,... | collective-permute-start | bytes 196616 | tf_op jit(solution)/shard_map/ppermute | solution.py:350
  17.5 0.2 shard_map.87.shared
  17.7 0.3 shard_map.83
  18.1 0.4 shard_map.84.near
  18.5 0.4 shard_map.85.rest_0_.state
  18.9 0.4 shard_map.86.near
  19.3 0.9 %collective-permute-done.3.partner = bf16[32,8,128]{2,1,0:T(8,128)(2,1)S(1)} collective-permute-done((bf16[32,8,128]{2,1,0:T(8,128)(2,1)S(1)}, bf16[32,8,128]{2,1,0:T(8,128)(2,1)S(1)}, u32[]{:S(2)}, u32[]{:S(2)}) %collective-permute-start.3) | collective-permute-done | bytes 65568 | tf_op jit(solution)/shard_map/ppermute | solution.py:350
  20.2 0.4 shard_map.88
  20.7 1.6 %collective-permute-start.6 = (bf16[32,8,128]{2,1,0:T(8,128)(2,1)S(1)}, bf16[32,8,128]{2,1,0:T(8,128)(2,1)S(1)}, u32[]{:S(2)}, u32[]{:S(2)}) collective-permute-start(bf16[32,8,128]{2,1,0:T(8,128)(2,1)S(1)} %shard_map.85.rest_0_.state), channel_id=1, source_target_pairs={{0,2},{1,3},{2,0},{3,1},{4,6},{5,7},{6,4},{7,5},{8,10},{9,11},{10,... | collective-permute-start | bytes 196616 | tf_op jit(solution)/shard_map/ppermute | solution.py:350
  22.3 0.4 shard_map.90.near
  22.6 0.8 %collective-permute-done.5.shared = bf16[68,64,128]{2,1,0:T(8,128)(2,1)S(1)} collective-permute-done((bf16[68,64,128]{2,1,0:T(8,128)(2,1)S(1)}, bf16[68,64,128]{2,1,0:T(8,128)(2,1)S(1)}, u32[]{:S(2)}, u32[]{:S(2)}) %collective-permute-start.5) | collective-permute-done | bytes 1114144 | tf_op jit(solution)/shard_map/ppermute | solution.py:350
  23.4 1.0 %shard_map.89 = (f32[2,32,8,128]{3,2,1,0:T(8,128)S(1)}, f32[2,1024,128]{2,1,0:T(8,128)S(1)}) custom-call(bf16[4,32,64,256]{3,2,1,0:T(8,128)(2,1)S(1)} %copy-done, s32[4,2,256]{2,1,0:T(2,128)S(1)} %copy-done.2, bf16[68,64,128]{2,1,0:T(8,128)(2,1)S(1)} %collective-permute-done.5.shared), custom_call_target="tpu_custom_call" | custom-call | flops 2048 | bytes 2048 | tf_op jit(solution)/shard_map/pallas_call | solution.py:334
  24.5 0.7 %collective-permute-done.6.partner = bf16[32,8,128]{2,1,0:T(8,128)(2,1)S(1)} collective-permute-done((bf16[32,8,128]{2,1,0:T(8,128)(2,1)S(1)}, bf16[32,8,128]{2,1,0:T(8,128)(2,1)S(1)}, u32[]{:S(2)}, u32[]{:S(2)}) %collective-permute-start.6) | collective-permute-done | bytes 65568 | tf_op jit(solution)/shard_map/ppermute | solution.py:350
  25.2 0.4 shard_map.91.state
  25.6 1.3 %shard_map.92 = (bf16[2,2,4,8,128]{4,3,2,1,0:T(8,128)(2,1)S(1)}, bf16[2,2,4,8,128]{4,3,2,1,0:T(8,128)(2,1)S(1)}, bf16[2,2,4,8,128]{4,3,2,1,0:T(8,128)(2,1)S(1)}, bf16[2,2,4,8,128]{4,3,2,1,0:T(8,128)(2,1)S(1)}) custom-call(s32[4,2,256]{2,1,0:T(2,128)S(1)} %copy-done.2, f32[2,1024,128]{2,1,0:T(8,128)S(1)} %get-tuple-element.51.wide, ...), custom_call_target="tpu_custom_call" | custom-call | flops 2048 | bytes 2048 | tf_op jit(solution)/shard_map/pallas_call | solution.py:334
  26.9 1.6 %collective-permute-start.8 = (bf16[2,2,4,8,128]{4,3,2,1,0:T(8,128)(2,1)S(1)}, bf16[2,2,4,8,128]{4,3,2,1,0:T(8,128)(2,1)S(1)}, u32[]{:S(2)}, u32[]{:S(2)}) collective-permute-start(bf16[2,2,4,8,128]{4,3,2,1,0:T(8,128)(2,1)S(1)} %get-tuple-element.59), channel_id=1, source_target_pairs={{0,2},{1,10},{2,0},{3,8},{4,6},{5,14},{6,4},{7,12},{8,3},{9,11},{1... | collective-permute-start | bytes 98312 | tf_op jit(solution)/shard_map/ppermute | solution.py:350
  28.5 1.6 %collective-permute-start.9 = (bf16[2,2,4,8,128]{4,3,2,1,0:T(8,128)(2,1)S(1)}, bf16[2,2,4,8,128]{4,3,2,1,0:T(8,128)(2,1)S(1)}, u32[]{:S(2)}, u32[]{:S(2)}) collective-permute-start(bf16[2,2,4,8,128]{4,3,2,1,0:T(8,128)(2,1)S(1)} %get-tuple-element.60), channel_id=1, source_target_pairs={{0,4},{1,12},{2,6},{3,14},{4,0},{5,8},{6,2},{7,10},{8,5},{9,13},{1... | collective-permute-start | bytes 98312 | tf_op jit(solution)/shard_map/ppermute | solution.py:350
  30.1 0.3 collective-permute-start.10
  30.4 0.7 %collective-permute-start.7 = (bf16[2,2,4,8,128]{4,3,2,1,0:T(8,128)(2,1)S(1)}, bf16[2,2,4,8,128]{4,3,2,1,0:T(8,128)(2,1)S(1)}, u32[]{:S(2)}, u32[]{:S(2)}) collective-permute-start(bf16[2,2,4,8,128]{4,3,2,1,0:T(8,128)(2,1)S(1)} %get-tuple-element.55.rest_0_.kept), channel_id=1, source_target_pairs={{1,8},{3,10},{5,12},{7,14},{8,1},{10,3},{12,5},{14,7},{17,24},{19,... | collective-permute-start | bytes 98312 | tf_op jit(solution)/shard_map/ppermute | solution.py:350
  31.1 0.3 shard_map.94
  31.4 0.3 shard_map.95
  31.7 0.3 shard_map.97
  32.0 0.3 shard_map.96
  32.3 0.3 shard_map.93
  32.7 2.2 %collective-permute-done.10.rest_3_ = bf16[2,2,4,8,128]{4,3,2,1,0:T(8,128)(2,1)S(1)} collective-permute-done((bf16[2,2,4,8,128]{4,3,2,1,0:T(8,128)(2,1)S(1)}, bf16[2,2,4,8,128]{4,3,2,1,0:T(8,128)(2,1)S(1)}, u32[]{:S(2)}, u32[]{:S(2)}) %collective-permute-start.10) | collective-permute-done | bytes 32800 | tf_op jit(solution)/shard_map/ppermute | solution.py:350
  34.9 1.0 %shard_map.98 = (bf16[32,8,128]{2,1,0:T(8,128)(2,1)S(1)}, bf16[2,32,8,128]{3,2,1,0:T(8,128)(2,1)S(1)}) custom-call(f32[2,1024,128]{2,1,0:T(8,128)S(1)} %get-tuple-element.58.wide, bf16[2,2,4,8,128]{4,3,2,1,0:T(8,128)(2,1)S(1)} %get-tuple-element.55.rest_0_.kept, bf16[2,2,4,8,128]{4,3,2,1,0:T(8,128)(2,1)S(1)} %collective-permute-done.7.rest_0_, ...), custom_call_target="tpu_custom_call" | custom-call | flops 2048 | bytes 2048 | tf_op jit(solution)/shard_map/pallas_call | solution.py:334
  35.9 5.8 %collective-permute-start.11 = (bf16[32,8,128]{2,1,0:T(8,128)(2,1)S(1)}, bf16[32,8,128]{2,1,0:T(8,128)(2,1)S(1)}, u32[]{:S(2)}, u32[]{:S(2)}) collective-permute-start(bf16[32,8,128]{2,1,0:T(8,128)(2,1)S(1)} %get-tuple-element.74), channel_id=1, source_target_pairs={{0,1},{1,0},{2,3},{3,2},{4,5},{5,4},{6,7},{7,6},{8,9},{9,8},{10,11... | collective-permute-start | bytes 196616 | tf_op jit(solution)/shard_map/ppermute | solution.py:350
  41.7 0.8 %shard_map.104.state = bf16[32,8,128]{2,1,0:T(8,128)(2,1)S(1)} custom-call(s32[4,2,256]{2,1,0:T(2,128)S(1)} %copy-done.3, f32[2,1024,128]{2,1,0:T(8,128)S(1)} %get-tuple-element.75.wide, bf16[2,32,8,128]{3,2,1,0:T(8,128)(2,1)S(1)} %get-tuple-element.76.states), custom_call_target="tpu_custom_call" | custom-call | flops 2048 | bytes 2048 | tf_op jit(solution)/shard_map/pallas_call | solution.py:334
  42.4 1.6 %collective-permute-start.15 = (bf16[32,8,128]{2,1,0:T(8,128)(2,1)S(1)}, bf16[32,8,128]{2,1,0:T(8,128)(2,1)S(1)}, u32[]{:S(2)}, u32[]{:S(2)}) collective-permute-start(bf16[32,8,128]{2,1,0:T(8,128)(2,1)S(1)} %shard_map.104.state), channel_id=1, source_target_pairs={{0,2},{1,3},{2,0},{3,1},{4,6},{5,7},{6,4},{7,5},{8,10},{9,11},{10,... | collective-permute-start | bytes 196616 | tf_op jit(solution)/shard_map/ppermute | solution.py:350
  44.0 0.5 collective-permute-start.12
  44.5 0.4 shard_map.105.near
  44.9 2.3 %collective-permute-done.15.partner = bf16[32,8,128]{2,1,0:T(8,128)(2,1)S(1)} collective-permute-done((bf16[32,8,128]{2,1,0:T(8,128)(2,1)S(1)}, bf16[32,8,128]{2,1,0:T(8,128)(2,1)S(1)}, u32[]{:S(2)}, u32[]{:S(2)}) %collective-permute-start.15) | collective-permute-done | bytes 65568 | tf_op jit(solution)/shard_map/ppermute | solution.py:350
  47.2 0.4 shard_map.106.state
  47.6 0.3 collective-permute-start.16
  47.9 0.4 shard_map.99.near
  48.3 0.4 shard_map.100.state.rest_0_
  48.7 1.8 %collective-permute-start.13 = (bf16[32,8,128]{2,1,0:T(8,128)(2,1)S(1)}, bf16[32,8,128]{2,1,0:T(8,128)(2,1)S(1)}, u32[]{:S(2)}, u32[]{:S(2)}) collective-permute-start(bf16[32,8,128]{2,1,0:T(8,128)(2,1)S(1)} %shard_map.100.state.rest_0_), channel_id=1, source_target_pairs={{0,4},{1,5},{2,6},{3,7},{4,0},{5,1},{6,2},{7,3},{8,12},{9,13},{10,... | collective-permute-start | bytes 196616 | tf_op jit(solution)/shard_map/ppermute | solution.py:350
  50.5 0.4 shard_map.101.near
  50.9 0.4 shard_map.107.near
  51.3 0.6 %collective-permute-done.16.partner = bf16[32,8,128]{2,1,0:T(8,128)(2,1)S(1)} collective-permute-done((bf16[32,8,128]{2,1,0:T(8,128)(2,1)S(1)}, bf16[32,8,128]{2,1,0:T(8,128)(2,1)S(1)}, u32[]{:S(2)}, u32[]{:S(2)}) %collective-permute-start.16) | collective-permute-done | bytes 65568 | tf_op jit(solution)/shard_map/ppermute | solution.py:350
  51.9 0.4 shard_map.108.state
  52.3 0.3 collective-permute-start.17
  52.6 0.4 collective-permute-done.13.partner
  53.0 0.4 shard_map.102.state.rest_0_
  53.4 2.7 %collective-permute-start.14 = (bf16[32,8,128]{2,1,0:T(8,128)(2,1)S(1)}, bf16[32,8,128]{2,1,0:T(8,128)(2,1)S(1)}, u32[]{:S(2)}, u32[]{:S(2)}) collective-permute-start(bf16[32,8,128]{2,1,0:T(8,128)(2,1)S(1)} %shard_map.102.state.rest_0_), channel_id=1, source_target_pairs={{0,8},{1,9},{2,10},{3,11},{4,12},{5,13},{6,14},{7,15},{8,0},{9,1},... | collective-permute-start | bytes 196616 | tf_op jit(solution)/shard_map/ppermute | solution.py:350
  56.1 0.4 shard_map.103.near
  56.5 0.4 shard_map.109.near
  56.8 1.4 %collective-permute-done.17.partner = bf16[32,8,128]{2,1,0:T(8,128)(2,1)S(1)} collective-permute-done((bf16[32,8,128]{2,1,0:T(8,128)(2,1)S(1)}, bf16[32,8,128]{2,1,0:T(8,128)(2,1)S(1)}, u32[]{:S(2)}, u32[]{:S(2)}) %collective-permute-start.17) | collective-permute-done | bytes 65568 | tf_op jit(solution)/shard_map/ppermute | solution.py:350
  58.2 1.1 %shard_map.110.ready = bf16[64,8,128]{2,1,0:T(8,128)(2,1)S(1)} custom-call(s32[4,2,256]{2,1,0:T(2,128)S(1)} %copy-done.3, f32[1024,128]{1,0:T(8,128)S(1)} %get-tuple-element.72.rest_14_.wide, f32[2048,128]{1,0:T(8,128)S(1)} %get-tuple-element.73.rest_16_.image_wide, bf16[32,8,128]{2,1,0:T(8,128)(2,1)S(1)} %collective-permute-done.17.partner, ...), custom_call_target="tpu_custom_call" | custom-call | flops 3072 | bytes 3072 | tf_op jit(solution)/shard_map/pallas_call | solution.py:334
  59.4 1.8 %shard_map.111 = bf16[64,8,256]{2,1,0:T(8,128)(2,1)} custom-call(s32[4,2,256]{2,1,0:T(2,128)S(1)} %copy-done.3, f32[1024,128]{1,0:T(8,128)S(1)} %get-tuple-element.56.rest_15_.wide, f32[2048,128]{1,0:T(8,128)S(1)} %get-tuple-element.57.rest_17_.image_wide, bf16[32,8,128]{2,1,0:T(8,128)(2,1)S(1)} %collective-permute-done.14.partner, ...), custom_call_target="tpu_custom_call" | custom-call | flops 3072 | bytes 3072 | tf_op jit(solution)/shard_map/pallas_call | solution.py:334
  (21 shorter events, 0.3 us)
Async XLA Ops:
  1.8 8.1 %collective-permute-start = (bf16[32,8,128]{2,1,0:T(8,128)(2,1)S(1)}, bf16[32,8,128]{2,1,0:T(8,128)(2,1)S(1)}, u32[]{:S(2)}, u32[]{:S(2)}) collective-permute-start(bf16[32,8,128]{2,1,0:T(8,128)(2,1)S(1)} %shard_map.73.rest_0_.state), channel_id=1, source_target_pairs={{0,8},{1,9},{2,10},{3,11},{4,12},{5,13},{6,14},{7,15},{8,0},{9,1},... | collective-permute-start | bytes 196616 | tf_op jit(solution)/shard_map/ppermute | solution.py:350
  7.8 1.8 %copy-start.2 = (s32[4,2,256]{2,1,0:T(2,128)S(1)}, s32[4,2,256]{2,1,0:T(2,128)}, u32[]{:S(2)}) copy-start(s32[4,2,256]{2,1,0:T(2,128)} %pattern.40) | copy-start | bytes 24580
  7.8 5.6 %collective-permute-start.2 = (bf16[32,8,128]{2,1,0:T(8,128)(2,1)S(1)}, bf16[32,8,128]{2,1,0:T(8,128)(2,1)S(1)}, u32[]{:S(2)}, u32[]{:S(2)}) collective-permute-start(bf16[32,8,128]{2,1,0:T(8,128)(2,1)S(1)} %shard_map.74.after.rest_0_.state), channel_id=1, source_target_pairs={{0,8},{1,9},{2,10},{3,11},{4,12},{5,13},{6,14},{7,15},{8,0},{9,1},... | collective-permute-start | bytes 196616 | tf_op jit(solution)/shard_map/ppermute | solution.py:350
  7.9 4.9 %copy-start = (bf16[4,32,64,256]{3,2,1,0:T(8,128)(2,1)S(1)}, bf16[4,32,64,256]{3,2,1,0:T(8,128)(2,1)}, u32[]{:S(2)}) copy-start(bf16[4,32,64,256]{3,2,1,0:T(8,128)(2,1)} %blocks.11) | copy-start | bytes 12582916
  10.4 5.1 %collective-permute-start.1 = (bf16[32,8,128]{2,1,0:T(8,128)(2,1)S(1)}, bf16[32,8,128]{2,1,0:T(8,128)(2,1)S(1)}, u32[]{:S(2)}, u32[]{:S(2)}) collective-permute-start(bf16[32,8,128]{2,1,0:T(8,128)(2,1)S(1)} %shard_map.77.state), channel_id=1, source_target_pairs={{0,4},{1,5},{2,6},{3,7},{4,0},{5,1},{6,2},{7,3},{8,12},{9,13},{10,... | collective-permute-start | bytes 196616 | tf_op jit(solution)/shard_map/ppermute | solution.py:350
  12.9 4.6 %copy-start.1 = (bf16[4,32,64,256]{3,2,1,0:T(8,128)(2,1)S(1)}, bf16[4,32,64,256]{3,2,1,0:T(8,128)(2,1)}, u32[]{:S(2)}) copy-start(bf16[4,32,64,256]{3,2,1,0:T(8,128)(2,1)} %blocks.15) | copy-start | bytes 12582916
  13.4 4.0 %copy-start.3 = (s32[4,2,256]{2,1,0:T(2,128)S(1)}, s32[4,2,256]{2,1,0:T(2,128)}, u32[]{:S(2)}) copy-start(s32[4,2,256]{2,1,0:T(2,128)} %pattern.53) | copy-start | bytes 24580
  13.8 4.6 %collective-permute-start.4 = (bf16[32,8,128]{2,1,0:T(8,128)(2,1)S(1)}, bf16[32,8,128]{2,1,0:T(8,128)(2,1)S(1)}, u32[]{:S(2)}, u32[]{:S(2)}) collective-permute-start(bf16[32,8,128]{2,1,0:T(8,128)(2,1)S(1)} %shard_map.80.rest_0_.state), channel_id=1, source_target_pairs={{0,4},{1,5},{2,6},{3,7},{4,0},{5,1},{6,2},{7,3},{8,12},{9,13},{10,... | collective-permute-start | bytes 196616 | tf_op jit(solution)/shard_map/ppermute | solution.py:350
  15.9 4.3 %collective-permute-start.3 = (bf16[32,8,128]{2,1,0:T(8,128)(2,1)S(1)}, bf16[32,8,128]{2,1,0:T(8,128)(2,1)S(1)}, u32[]{:S(2)}, u32[]{:S(2)}) collective-permute-start(bf16[32,8,128]{2,1,0:T(8,128)(2,1)S(1)} %shard_map.82.state), channel_id=1, source_target_pairs={{0,2},{1,3},{2,0},{3,1},{4,6},{5,7},{6,4},{7,5},{8,10},{9,11},{10,... | collective-permute-start | bytes 196616 | tf_op jit(solution)/shard_map/ppermute | solution.py:350
  20.6 2.8 %collective-permute-start.5 = (bf16[68,64,128]{2,1,0:T(8,128)(2,1)S(1)}, bf16[68,64,128]{2,1,0:T(8,128)(2,1)S(1)}, u32[]{:S(2)}, u32[]{:S(2)}) collective-permute-start(bf16[68,64,128]{2,1,0:T(8,128)(2,1)S(1)} %shard_map.88), channel_id=1, source_target_pairs={{0,1},{1,0},{2,3},{3,2},{4,5},{5,4},{6,7},{7,6},{8,9},{9,8},{10,11... | collective-permute-start | bytes 3342344 | tf_op jit(solution)/shard_map/ppermute | solution.py:350
  20.7 4.5 %collective-permute-start.6 = (bf16[32,8,128]{2,1,0:T(8,128)(2,1)S(1)}, bf16[32,8,128]{2,1,0:T(8,128)(2,1)S(1)}, u32[]{:S(2)}, u32[]{:S(2)}) collective-permute-start(bf16[32,8,128]{2,1,0:T(8,128)(2,1)S(1)} %shard_map.85.rest_0_.state), channel_id=1, source_target_pairs={{0,2},{1,3},{2,0},{3,1},{4,6},{5,7},{6,4},{7,5},{8,10},{9,11},{10,... | collective-permute-start | bytes 196616 | tf_op jit(solution)/shard_map/ppermute | solution.py:350
  25.2 5.9 %copy-start.4 = (bf16[64,32,256]{2,1,0:T(8,128)(2,1)S(1)}, bf16[64,32,256]{2,1,0:T(8,128)(2,1)}, u32[]{:S(2)}) copy-start(bf16[64,32,256]{2,1,0:T(8,128)(2,1)} %interp.5) | copy-start | bytes 3145732
  26.9 5.8 %collective-permute-start.8 = (bf16[2,2,4,8,128]{4,3,2,1,0:T(8,128)(2,1)S(1)}, bf16[2,2,4,8,128]{4,3,2,1,0:T(8,128)(2,1)S(1)}, u32[]{:S(2)}, u32[]{:S(2)}) collective-permute-start(bf16[2,2,4,8,128]{4,3,2,1,0:T(8,128)(2,1)S(1)} %get-tuple-element.59), channel_id=1, source_target_pairs={{0,2},{1,10},{2,0},{3,8},{4,6},{5,14},{6,4},{7,12},{8,3},{9,11},{1... | collective-permute-start | bytes 98312 | tf_op jit(solution)/shard_map/ppermute | solution.py:350
  28.5 4.2 %collective-permute-start.9 = (bf16[2,2,4,8,128]{4,3,2,1,0:T(8,128)(2,1)S(1)}, bf16[2,2,4,8,128]{4,3,2,1,0:T(8,128)(2,1)S(1)}, u32[]{:S(2)}, u32[]{:S(2)}) collective-permute-start(bf16[2,2,4,8,128]{4,3,2,1,0:T(8,128)(2,1)S(1)} %get-tuple-element.60), channel_id=1, source_target_pairs={{0,4},{1,12},{2,6},{3,14},{4,0},{5,8},{6,2},{7,10},{8,5},{9,13},{1... | collective-permute-start | bytes 98312 | tf_op jit(solution)/shard_map/ppermute | solution.py:350
  30.1 4.8 %collective-permute-start.10 = (bf16[2,2,4,8,128]{4,3,2,1,0:T(8,128)(2,1)S(1)}, bf16[2,2,4,8,128]{4,3,2,1,0:T(8,128)(2,1)S(1)}, u32[]{:S(2)}, u32[]{:S(2)}) collective-permute-start(bf16[2,2,4,8,128]{4,3,2,1,0:T(8,128)(2,1)S(1)} %get-tuple-element.61), channel_id=1, source_target_pairs={{0,6},{1,14},{2,4},{3,12},{4,2},{5,10},{6,0},{7,8},{8,7},{9,15},{1... | collective-permute-start | bytes 98312 | tf_op jit(solution)/shard_map/ppermute | solution.py:350
  30.4 4.5 %collective-permute-start.7 = (bf16[2,2,4,8,128]{4,3,2,1,0:T(8,128)(2,1)S(1)}, bf16[2,2,4,8,128]{4,3,2,1,0:T(8,128)(2,1)S(1)}, u32[]{:S(2)}, u32[]{:S(2)}) collective-permute-start(bf16[2,2,4,8,128]{4,3,2,1,0:T(8,128)(2,1)S(1)} %get-tuple-element.55.rest_0_.kept), channel_id=1, source_target_pairs={{1,8},{3,10},{5,12},{7,14},{8,1},{10,3},{12,5},{14,7},{17,24},{19,... | collective-permute-start | bytes 98312 | tf_op jit(solution)/shard_map/ppermute | solution.py:350
  35.9 8.1 %collective-permute-start.11 = (bf16[32,8,128]{2,1,0:T(8,128)(2,1)S(1)}, bf16[32,8,128]{2,1,0:T(8,128)(2,1)S(1)}, u32[]{:S(2)}, u32[]{:S(2)}) collective-permute-start(bf16[32,8,128]{2,1,0:T(8,128)(2,1)S(1)} %get-tuple-element.74), channel_id=1, source_target_pairs={{0,1},{1,0},{2,3},{3,2},{4,5},{5,4},{6,7},{7,6},{8,9},{9,8},{10,11... | collective-permute-start | bytes 196616 | tf_op jit(solution)/shard_map/ppermute | solution.py:350
  42.4 4.7 %collective-permute-start.15 = (bf16[32,8,128]{2,1,0:T(8,128)(2,1)S(1)}, bf16[32,8,128]{2,1,0:T(8,128)(2,1)S(1)}, u32[]{:S(2)}, u32[]{:S(2)}) collective-permute-start(bf16[32,8,128]{2,1,0:T(8,128)(2,1)S(1)} %shard_map.104.state), channel_id=1, source_target_pairs={{0,2},{1,3},{2,0},{3,1},{4,6},{5,7},{6,4},{7,5},{8,10},{9,11},{10,... | collective-permute-start | bytes 196616 | tf_op jit(solution)/shard_map/ppermute | solution.py:350
  44.0 4.3 %collective-permute-start.12 = (bf16[32,8,128]{2,1,0:T(8,128)(2,1)S(1)}, bf16[32,8,128]{2,1,0:T(8,128)(2,1)S(1)}, u32[]{:S(2)}, u32[]{:S(2)}) collective-permute-start(bf16[32,8,128]{2,1,0:T(8,128)(2,1)S(1)} %collective-permute-done.11.state.rest_0_), channel_id=1, source_target_pairs={{0,2},{1,3},{2,0},{3,1},{4,6},{5,7},{6,4},{7,5},{8,10},{9,11},{10,... | collective-permute-start | bytes 196616 | tf_op jit(solution)/shard_map/ppermute | solution.py:350
  47.6 4.3 %collective-permute-start.16 = (bf16[32,8,128]{2,1,0:T(8,128)(2,1)S(1)}, bf16[32,8,128]{2,1,0:T(8,128)(2,1)S(1)}, u32[]{:S(2)}, u32[]{:S(2)}) collective-permute-start(bf16[32,8,128]{2,1,0:T(8,128)(2,1)S(1)} %shard_map.106.state), channel_id=1, source_target_pairs={{0,4},{1,5},{2,6},{3,7},{4,0},{5,1},{6,2},{7,3},{8,12},{9,13},{10,... | collective-permute-start | bytes 196616 | tf_op jit(solution)/shard_map/ppermute | solution.py:350
  48.7 4.3 %collective-permute-start.13 = (bf16[32,8,128]{2,1,0:T(8,128)(2,1)S(1)}, bf16[32,8,128]{2,1,0:T(8,128)(2,1)S(1)}, u32[]{:S(2)}, u32[]{:S(2)}) collective-permute-start(bf16[32,8,128]{2,1,0:T(8,128)(2,1)S(1)} %shard_map.100.state.rest_0_), channel_id=1, source_target_pairs={{0,4},{1,5},{2,6},{3,7},{4,0},{5,1},{6,2},{7,3},{8,12},{9,13},{10,... | collective-permute-start | bytes 196616 | tf_op jit(solution)/shard_map/ppermute | solution.py:350
  52.3 5.9 %collective-permute-start.17 = (bf16[32,8,128]{2,1,0:T(8,128)(2,1)S(1)}, bf16[32,8,128]{2,1,0:T(8,128)(2,1)S(1)}, u32[]{:S(2)}, u32[]{:S(2)}) collective-permute-start(bf16[32,8,128]{2,1,0:T(8,128)(2,1)S(1)} %shard_map.108.state), channel_id=1, source_target_pairs={{0,8},{1,9},{2,10},{3,11},{4,12},{5,13},{6,14},{7,15},{8,0},{9,1},... | collective-permute-start | bytes 196616 | tf_op jit(solution)/shard_map/ppermute | solution.py:350
  53.4 5.9 %collective-permute-start.14 = (bf16[32,8,128]{2,1,0:T(8,128)(2,1)S(1)}, bf16[32,8,128]{2,1,0:T(8,128)(2,1)S(1)}, u32[]{:S(2)}, u32[]{:S(2)}) collective-permute-start(bf16[32,8,128]{2,1,0:T(8,128)(2,1)S(1)} %shard_map.102.state.rest_0_), channel_id=1, source_target_pairs={{0,8},{1,9},{2,10},{3,11},{4,12},{5,13},{6,14},{7,15},{8,0},{9,1},... | collective-permute-start | bytes 196616 | tf_op jit(solution)/shard_map/ppermute | solution.py:350

commit v9 on v8

--- a/solution.py
+++ b/solution.py
@@ -157,7 +157,8 @@
     return lambda row: shared[pl.ds(place * rank + row, GROUP), rows_of(half, rank), :]
 
 
-def send_kernel(level, bit, flip, pattern, partner, near, wide, shared, out):
+def send_kernel(level, bit, flip, pattern, partner, near, wide, shared, *rest):
+    out = rest[-1]
     rank, per = partner.shape[0], shared.shape[1] // partner.shape[1]
     places = digits()
     chunk, other = places[3] ^ flip, 1 - places[3 - bit]
@@ -395,37 +396,42 @@
             for flip in order
         }
 
-    current = {}
-    for flip in (1, 0):
-        current[flip] = run(
-            functools.partial(coeff_kernel, flip), state, (interp_in, samples, *current.values()),
+    def coefficients(flip, *after):
+        return run(
+            functools.partial(coeff_kernel, flip), state, (interp_in, samples, *after),
             (
                 pltpu.VMEM((2, rank, depth // 2, LANES), jnp.bfloat16),
                 pltpu.VMEM((2, depth // 2, rhs_count, LANES), jnp.bfloat16),
                 pltpu.VMEM((rank * depth // 2, LANES), jnp.float32), total, pltpu.SemaphoreType.DMA((4,)),
-            ), 2, in_specs=[pl.BlockSpec(memory_space=pl.ANY)] * (2 + len(current)), limit=START_LIMIT,
+            ), 2, in_specs=[pl.BlockSpec(memory_space=pl.ANY)] * (2 + len(after)), limit=START_LIMIT,
         )
+
     share_rows = 2 * rank + rank * rhs_count // (2 * rank)
     shared_shape = jax.ShapeDtypeStruct((share_rows, 2 * rank, LANES), jnp.bfloat16)
+    current = {1: coefficients(1)}
     for level in range(3):
         bit = 3 - level
-        partner = {flip: swapped(current[flip], bit) for flip in (1, 0)}
         if level == 0:
+            partner = {1: swapped(current[1], bit)}
             wides = run(
-                functools.partial(fetch_kernel, 0, 3), [spread_out] * 4, (top_blocks, current[0]),
+                functools.partial(fetch_kernel, 0, 3), [spread_out] * 4, (top_blocks, current[1]),
                 (pltpu.VMEM((1, *top_blocks.shape[1:]), jnp.bfloat16), pltpu.SemaphoreType.DMA), 4,
                 in_specs=[pl.BlockSpec(memory_space=pl.ANY), pl.BlockSpec(memory_space=pltpu.VMEM)], limit=FETCH_LIMIT,
             )
             wides = wides[:2], wides[2:]
-        else:
-            wides = later_wides[level]
-        near = level_nears(top_pattern, level, bit, (1, 0), wides)
-        if level == 0:
+            near = level_nears(top_pattern, level, bit, (1,), wides)
+            current[0] = coefficients(0, near[1])
+            partner[0] = swapped(current[0], bit)
+            near.update(level_nears(top_pattern, level, bit, (0,), wides))
             later_wides = {later: level_wides(top_blocks, later, 3 - later, near[0]) for later in (1, 2)}
             shared = run(
                 functools.partial(share_kernel, 3), shared_shape,
                 (top_blocks, top_pattern, bottom_blocks, bottom_pattern),
             )
+        else:
+            partner = {flip: swapped(current[flip], bit) for flip in (1, 0)}
+            wides = later_wides[level]
+            near = level_nears(top_pattern, level, bit, (1, 0), wides)
         if level < 2:
             current = level_fars(top_pattern, level, bit, (1, 0), wides)
 

time: 61.3 us -> 61.5 us (level)
  starting transfers between devices: 27.9 us -> 25.4 us
  waiting for transfers between devices: 9.7 us -> 12.2 us
    ppermute x18, waiting for transfers between devices: 9.7 us -> 12.2 us  [permuted(): return lax.ppermute(value, 'leaf', pairs)]
    ppermute x18, starting transfers between devices: 27.9 us -> 25.4 us  [permuted(): return lax.ppermute(value, 'leaf', pairs)]
where the time goes in v9:
time: 61.5 us; the launch traced here: 61.3 us
  starting transfers between devices  25.4 us (41%)
  Pallas kernels  23.3 us (38%)
  waiting for transfers between devices  12.2 us (20%)
    ppermute x18, starting transfers between devices, permuted(): return lax.ppermute(value, 'leaf', pairs)  25.4 us
    pallas_call x39, Pallas kernels, run(): pl.pallas_call(kernel, out_shape=shapes, in_specs=in_specs or [whole] * l...  23.3 us
    ppermute x18, waiting for transfers between devices, permuted(): return lax.ppermute(value, 'leaf', pairs)  12.2 us
  transfers between devices with their start and end apart: 18, of which 10 were waited for; matrix products, arithmetic and copies ran while one was open for 0% of the time, Pallas kernels for 27%

profile of v9, /device:TPU:0, one launch (start us, length us, event | category | flops | bytes accessed | tf_op | source)
XLA Modules:
  0.0 61.3 jit_solution(4640403053306790954)
XLA Ops:
  0.0 1.8 %shard_map.73.after.state = bf16[32,8,128]{2,1,0:T(8,128)(2,1)S(1)} custom-call(bf16[32,64,256]{2,1,0:T(8,128)(2,1)} %interp.4, bf16[64,8,256]{2,1,0:T(8,128)(2,1)} %samples.3), custom_call_target="tpu_custom_call" | custom-call | flops 2048 | bytes 2048 | tf_op jit(solution)/shard_map/pallas_call | solution.py:335
  1.9 4.1 %collective-permute-start = (bf16[32,8,128]{2,1,0:T(8,128)(2,1)S(1)}, bf16[32,8,128]{2,1,0:T(8,128)(2,1)S(1)}, u32[]{:S(2)}, u32[]{:S(2)}) collective-permute-start(bf16[32,8,128]{2,1,0:T(8,128)(2,1)S(1)} %shard_map.73.after.state), channel_id=1, source_target_pairs={{0,8},{1,9},{2,10},{3,11},{4,12},{5,13},{6,14},{7,15},{8,0},{9,1},... | collective-permute-start | bytes 196616 | tf_op jit(solution)/shard_map/ppermute | solution.py:351
  6.0 1.7 %shard_map.74 = (f32[1024,128]{1,0:T(8,128)S(1)}, f32[1024,128]{1,0:T(8,128)S(1)}, f32[1024,128]{1,0:T(8,128)S(1)}, f32[1024,128]{1,0:T(8,128)S(1)}) custom-call(bf16[4,32,64,256]{3,2,1,0:T(8,128)(2,1)} %blocks.11, bf16[32,8,128]{2,1,0:T(8,128)(2,1)S(1)} %shard_map.73.after.state), custom_call_target="tpu_custom_call" | custom-call | flops 4096 | bytes 4096 | tf_op jit(solution)/shard_map/pallas_call | solution.py:335
  7.7 0.4 shard_map.75.near.rest_0_
  8.0 1.9 %shard_map.77.state = bf16[32,8,128]{2,1,0:T(8,128)(2,1)S(1)} custom-call(bf16[32,64,256]{2,1,0:T(8,128)(2,1)} %interp.4, bf16[64,8,256]{2,1,0:T(8,128)(2,1)} %samples.3, f32[32,8,128]{2,1,0:T(8,128)S(1)} %shard_map.75.near.rest_0_), custom_call_target="tpu_custom_call" | custom-call | flops 2048 | bytes 2048 | tf_op jit(solution)/shard_map/pallas_call | solution.py:335
  9.9 0.1 collective-permute-start.2
  10.0 0.4 shard_map.76.state
  10.4 1.9 %collective-permute-start.1 = (bf16[32,8,128]{2,1,0:T(8,128)(2,1)S(1)}, bf16[32,8,128]{2,1,0:T(8,128)(2,1)S(1)}, u32[]{:S(2)}, u32[]{:S(2)}) collective-permute-start(bf16[32,8,128]{2,1,0:T(8,128)(2,1)S(1)} %shard_map.76.state), channel_id=1, source_target_pairs={{0,4},{1,5},{2,6},{3,7},{4,0},{5,1},{6,2},{7,3},{8,12},{9,13},{10,... | collective-permute-start | bytes 196616 | tf_op jit(solution)/shard_map/ppermute | solution.py:351
  12.4 0.4 shard_map.78.rest_0_.near
  12.8 0.3 shard_map.79
  13.1 2.4 %collective-permute-done.2.partner = bf16[32,8,128]{2,1,0:T(8,128)(2,1)S(1)} collective-permute-done((bf16[32,8,128]{2,1,0:T(8,128)(2,1)S(1)}, bf16[32,8,128]{2,1,0:T(8,128)(2,1)S(1)}, u32[]{:S(2)}, u32[]{:S(2)}) %collective-permute-start.2) | collective-permute-done | bytes 65568 | tf_op jit(solution)/shard_map/ppermute | solution.py:351
  15.5 0.4 shard_map.80.rest_0_.state
  15.9 1.3 %collective-permute-start.4 = (bf16[32,8,128]{2,1,0:T(8,128)(2,1)S(1)}, bf16[32,8,128]{2,1,0:T(8,128)(2,1)S(1)}, u32[]{:S(2)}, u32[]{:S(2)}) collective-permute-start(bf16[32,8,128]{2,1,0:T(8,128)(2,1)S(1)} %shard_map.80.rest_0_.state), channel_id=1, source_target_pairs={{0,4},{1,5},{2,6},{3,7},{4,0},{5,1},{6,2},{7,3},{8,12},{9,13},{10,... | collective-permute-start | bytes 196616 | tf_op jit(solution)/shard_map/ppermute | solution.py:351
  17.2 0.4 shard_map.81.near
  17.6 0.4 shard_map.82.state
  18.0 1.6 %collective-permute-start.3 = (bf16[32,8,128]{2,1,0:T(8,128)(2,1)S(1)}, bf16[32,8,128]{2,1,0:T(8,128)(2,1)S(1)}, u32[]{:S(2)}, u32[]{:S(2)}) collective-permute-start(bf16[32,8,128]{2,1,0:T(8,128)(2,1)S(1)} %shard_map.82.state), channel_id=1, source_target_pairs={{0,2},{1,3},{2,0},{3,1},{4,6},{5,7},{6,4},{7,5},{8,10},{9,11},{10,... | collective-permute-start | bytes 196616 | tf_op jit(solution)/shard_map/ppermute | solution.py:351
  19.6 0.2 shard_map.87.shared
  19.8 0.3 shard_map.83
  20.2 0.4 shard_map.84.near
  20.6 0.4 shard_map.85.rest_0_.state
  21.0 0.4 shard_map.86.near
  21.4 0.9 %collective-permute-done.3.partner = bf16[32,8,128]{2,1,0:T(8,128)(2,1)S(1)} collective-permute-done((bf16[32,8,128]{2,1,0:T(8,128)(2,1)S(1)}, bf16[32,8,128]{2,1,0:T(8,128)(2,1)S(1)}, u32[]{:S(2)}, u32[]{:S(2)}) %collective-permute-start.3) | collective-permute-done | bytes 65568 | tf_op jit(solution)/shard_map/ppermute | solution.py:351
  22.3 0.4 shard_map.88
  22.8 1.6 %collective-permute-start.6 = (bf16[32,8,128]{2,1,0:T(8,128)(2,1)S(1)}, bf16[32,8,128]{2,1,0:T(8,128)(2,1)S(1)}, u32[]{:S(2)}, u32[]{:S(2)}) collective-permute-start(bf16[32,8,128]{2,1,0:T(8,128)(2,1)S(1)} %shard_map.85.rest_0_.state), channel_id=1, source_target_pairs={{0,2},{1,3},{2,0},{3,1},{4,6},{5,7},{6,4},{7,5},{8,10},{9,11},{10,... | collective-permute-start | bytes 196616 | tf_op jit(solution)/shard_map/ppermute | solution.py:351
  24.4 0.4 shard_map.90.near
  24.7 0.8 %collective-permute-done.5.shared = bf16[68,64,128]{2,1,0:T(8,128)(2,1)S(1)} collective-permute-done((bf16[68,64,128]{2,1,0:T(8,128)(2,1)S(1)}, bf16[68,64,128]{2,1,0:T(8,128)(2,1)S(1)}, u32[]{:S(2)}, u32[]{:S(2)}) %collective-permute-start.5) | collective-permute-done | bytes 1114144 | tf_op jit(solution)/shard_map/ppermute | solution.py:351
  25.5 1.0 %shard_map.89 = (f32[2,32,8,128]{3,2,1,0:T(8,128)S(1)}, f32[2,1024,128]{2,1,0:T(8,128)S(1)}) custom-call(bf16[4,32,64,256]{3,2,1,0:T(8,128)(2,1)S(1)} %copy-done, s32[4,2,256]{2,1,0:T(2,128)S(1)} %copy-done.2, bf16[68,64,128]{2,1,0:T(8,128)(2,1)S(1)} %collective-permute-done.5.shared), custom_call_target="tpu_custom_call" | custom-call | flops 2048 | bytes 2048 | tf_op jit(solution)/shard_map/pallas_call | solution.py:335
  26.6 0.7 %collective-permute-done.6.partner = bf16[32,8,128]{2,1,0:T(8,128)(2,1)S(1)} collective-permute-done((bf16[32,8,128]{2,1,0:T(8,128)(2,1)S(1)}, bf16[32,8,128]{2,1,0:T(8,128)(2,1)S(1)}, u32[]{:S(2)}, u32[]{:S(2)}) %collective-permute-start.6) | collective-permute-done | bytes 65568 | tf_op jit(solution)/shard_map/ppermute | solution.py:351
  27.3 0.4 shard_map.91.state
  27.7 1.3 %shard_map.92 = (bf16[2,2,4,8,128]{4,3,2,1,0:T(8,128)(2,1)S(1)}, bf16[2,2,4,8,128]{4,3,2,1,0:T(8,128)(2,1)S(1)}, bf16[2,2,4,8,128]{4,3,2,1,0:T(8,128)(2,1)S(1)}, bf16[2,2,4,8,128]{4,3,2,1,0:T(8,128)(2,1)S(1)}) custom-call(s32[4,2,256]{2,1,0:T(2,128)S(1)} %copy-done.2, f32[2,1024,128]{2,1,0:T(8,128)S(1)} %get-tuple-element.51.wide, ...), custom_call_target="tpu_custom_call" | custom-call | flops 2048 | bytes 2048 | tf_op jit(solution)/shard_map/pallas_call | solution.py:335
  29.0 1.6 %collective-permute-start.8 = (bf16[2,2,4,8,128]{4,3,2,1,0:T(8,128)(2,1)S(1)}, bf16[2,2,4,8,128]{4,3,2,1,0:T(8,128)(2,1)S(1)}, u32[]{:S(2)}, u32[]{:S(2)}) collective-permute-start(bf16[2,2,4,8,128]{4,3,2,1,0:T(8,128)(2,1)S(1)} %get-tuple-element.59), channel_id=1, source_target_pairs={{0,2},{1,10},{2,0},{3,8},{4,6},{5,14},{6,4},{7,12},{8,3},{9,11},{1... | collective-permute-start | bytes 98312 | tf_op jit(solution)/shard_map/ppermute | solution.py:351
  30.6 0.9 %collective-permute-start.9 = (bf16[2,2,4,8,128]{4,3,2,1,0:T(8,128)(2,1)S(1)}, bf16[2,2,4,8,128]{4,3,2,1,0:T(8,128)(2,1)S(1)}, u32[]{:S(2)}, u32[]{:S(2)}) collective-permute-start(bf16[2,2,4,8,128]{4,3,2,1,0:T(8,128)(2,1)S(1)} %get-tuple-element.60), channel_id=1, source_target_pairs={{0,4},{1,12},{2,6},{3,14},{4,0},{5,8},{6,2},{7,10},{8,5},{9,13},{1... | collective-permute-start | bytes 98312 | tf_op jit(solution)/shard_map/ppermute | solution.py:351
  31.4 1.1 %collective-permute-start.10 = (bf16[2,2,4,8,128]{4,3,2,1,0:T(8,128)(2,1)S(1)}, bf16[2,2,4,8,128]{4,3,2,1,0:T(8,128)(2,1)S(1)}, u32[]{:S(2)}, u32[]{:S(2)}) collective-permute-start(bf16[2,2,4,8,128]{4,3,2,1,0:T(8,128)(2,1)S(1)} %get-tuple-element.61), channel_id=1, source_target_pairs={{0,6},{1,14},{2,4},{3,12},{4,2},{5,10},{6,0},{7,8},{8,7},{9,15},{1... | collective-permute-start | bytes 98312 | tf_op jit(solution)/shard_map/ppermute | solution.py:351
  32.5 0.7 %collective-permute-start.7 = (bf16[2,2,4,8,128]{4,3,2,1,0:T(8,128)(2,1)S(1)}, bf16[2,2,4,8,128]{4,3,2,1,0:T(8,128)(2,1)S(1)}, u32[]{:S(2)}, u32[]{:S(2)}) collective-permute-start(bf16[2,2,4,8,128]{4,3,2,1,0:T(8,128)(2,1)S(1)} %get-tuple-element.55.rest_0_.kept), channel_id=1, source_target_pairs={{1,8},{3,10},{5,12},{7,14},{8,1},{10,3},{12,5},{14,7},{17,24},{19,... | collective-permute-start | bytes 98312 | tf_op jit(solution)/shard_map/ppermute | solution.py:351
  33.2 0.3 shard_map.94
  33.5 0.3 shard_map.95
  33.8 0.3 shard_map.97
  34.1 0.3 shard_map.96
  34.4 0.3 shard_map.93
  34.8 1.8 %collective-permute-done.10.rest_3_ = bf16[2,2,4,8,128]{4,3,2,1,0:T(8,128)(2,1)S(1)} collective-permute-done((bf16[2,2,4,8,128]{4,3,2,1,0:T(8,128)(2,1)S(1)}, bf16[2,2,4,8,128]{4,3,2,1,0:T(8,128)(2,1)S(1)}, u32[]{:S(2)}, u32[]{:S(2)}) %collective-permute-start.10) | collective-permute-done | bytes 32800 | tf_op jit(solution)/shard_map/ppermute | solution.py:351
  36.6 1.0 %shard_map.98 = (bf16[32,8,128]{2,1,0:T(8,128)(2,1)S(1)}, bf16[2,32,8,128]{3,2,1,0:T(8,128)(2,1)S(1)}) custom-call(f32[2,1024,128]{2,1,0:T(8,128)S(1)} %get-tuple-element.58.wide, bf16[2,2,4,8,128]{4,3,2,1,0:T(8,128)(2,1)S(1)} %get-tuple-element.55.rest_0_.kept, bf16[2,2,4,8,128]{4,3,2,1,0:T(8,128)(2,1)S(1)} %collective-permute-done.7.rest_0_, ...), custom_call_target="tpu_custom_call" | custom-call | flops 2048 | bytes 2048 | tf_op jit(solution)/shard_map/pallas_call | solution.py:335
  37.6 4.2 %collective-permute-start.11 = (bf16[32,8,128]{2,1,0:T(8,128)(2,1)S(1)}, bf16[32,8,128]{2,1,0:T(8,128)(2,1)S(1)}, u32[]{:S(2)}, u32[]{:S(2)}) collective-permute-start(bf16[32,8,128]{2,1,0:T(8,128)(2,1)S(1)} %get-tuple-element.74), channel_id=1, source_target_pairs={{0,1},{1,0},{2,3},{3,2},{4,5},{5,4},{6,7},{7,6},{8,9},{9,8},{10,11... | collective-permute-start | bytes 196616 | tf_op jit(solution)/shard_map/ppermute | solution.py:351
  41.8 0.8 %shard_map.104.state = bf16[32,8,128]{2,1,0:T(8,128)(2,1)S(1)} custom-call(s32[4,2,256]{2,1,0:T(2,128)S(1)} %copy-done.3, f32[2,1024,128]{2,1,0:T(8,128)S(1)} %get-tuple-element.75.wide, bf16[2,32,8,128]{3,2,1,0:T(8,128)(2,1)S(1)} %get-tuple-element.76.states), custom_call_target="tpu_custom_call" | custom-call | flops 2048 | bytes 2048 | tf_op jit(solution)/shard_map/pallas_call | solution.py:335
  42.5 1.6 %collective-permute-start.15 = (bf16[32,8,128]{2,1,0:T(8,128)(2,1)S(1)}, bf16[32,8,128]{2,1,0:T(8,128)(2,1)S(1)}, u32[]{:S(2)}, u32[]{:S(2)}) collective-permute-start(bf16[32,8,128]{2,1,0:T(8,128)(2,1)S(1)} %shard_map.104.state), channel_id=1, source_target_pairs={{0,2},{1,3},{2,0},{3,1},{4,6},{5,7},{6,4},{7,5},{8,10},{9,11},{10,... | collective-permute-start | bytes 196616 | tf_op jit(solution)/shard_map/ppermute | solution.py:351
  44.2 0.4 collective-permute-start.12
  44.6 0.4 shard_map.105.near
  45.0 2.3 %collective-permute-done.15.partner = bf16[32,8,128]{2,1,0:T(8,128)(2,1)S(1)} collective-permute-done((bf16[32,8,128]{2,1,0:T(8,128)(2,1)S(1)}, bf16[32,8,128]{2,1,0:T(8,128)(2,1)S(1)}, u32[]{:S(2)}, u32[]{:S(2)}) %collective-permute-start.15) | collective-permute-done | bytes 65568 | tf_op jit(solution)/shard_map/ppermute | solution.py:351
  47.3 0.4 shard_map.106.state
  47.8 0.4 shard_map.99.near
  48.1 0.3 collective-permute-done.12.partner
  48.4 0.4 shard_map.100.state.rest_0_
  48.8 1.8 %collective-permute-start.13 = (bf16[32,8,128]{2,1,0:T(8,128)(2,1)S(1)}, bf16[32,8,128]{2,1,0:T(8,128)(2,1)S(1)}, u32[]{:S(2)}, u32[]{:S(2)}) collective-permute-start(bf16[32,8,128]{2,1,0:T(8,128)(2,1)S(1)} %shard_map.100.state.rest_0_), channel_id=1, source_target_pairs={{0,4},{1,5},{2,6},{3,7},{4,0},{5,1},{6,2},{7,3},{8,12},{9,13},{10,... | collective-permute-start | bytes 196616 | tf_op jit(solution)/shard_map/ppermute | solution.py:351
  50.6 0.4 shard_map.101.near
  51.0 0.4 shard_map.107.near
  51.4 0.6 %collective-permute-done.16.partner = bf16[32,8,128]{2,1,0:T(8,128)(2,1)S(1)} collective-permute-done((bf16[32,8,128]{2,1,0:T(8,128)(2,1)S(1)}, bf16[32,8,128]{2,1,0:T(8,128)(2,1)S(1)}, u32[]{:S(2)}, u32[]{:S(2)}) %collective-permute-start.16) | collective-permute-done | bytes 65568 | tf_op jit(solution)/shard_map/ppermute | solution.py:351
  52.0 0.4 shard_map.108.state
  52.5 0.7 %collective-permute-done.13.partner = bf16[32,8,128]{2,1,0:T(8,128)(2,1)S(1)} collective-permute-done((bf16[32,8,128]{2,1,0:T(8,128)(2,1)S(1)}, bf16[32,8,128]{2,1,0:T(8,128)(2,1)S(1)}, u32[]{:S(2)}, u32[]{:S(2)}) %collective-permute-start.13) | collective-permute-done | bytes 65568 | tf_op jit(solution)/shard_map/ppermute | solution.py:351
  53.2 0.4 shard_map.102.state.rest_0_
  53.6 2.3 %collective-permute-start.14 = (bf16[32,8,128]{2,1,0:T(8,128)(2,1)S(1)}, bf16[32,8,128]{2,1,0:T(8,128)(2,1)S(1)}, u32[]{:S(2)}, u32[]{:S(2)}) collective-permute-start(bf16[32,8,128]{2,1,0:T(8,128)(2,1)S(1)} %shard_map.102.state.rest_0_), channel_id=1, source_target_pairs={{0,8},{1,9},{2,10},{3,11},{4,12},{5,13},{6,14},{7,15},{8,0},{9,1},... | collective-permute-start | bytes 196616 | tf_op jit(solution)/shard_map/ppermute | solution.py:351
  55.9 0.4 shard_map.103.near
  56.2 0.4 shard_map.109.near
  56.6 1.7 %collective-permute-done.17.partner = bf16[32,8,128]{2,1,0:T(8,128)(2,1)S(1)} collective-permute-done((bf16[32,8,128]{2,1,0:T(8,128)(2,1)S(1)}, bf16[32,8,128]{2,1,0:T(8,128)(2,1)S(1)}, u32[]{:S(2)}, u32[]{:S(2)}) %collective-permute-start.17) | collective-permute-done | bytes 65568 | tf_op jit(solution)/shard_map/ppermute | solution.py:351
  58.3 1.1 %shard_map.110.ready = bf16[64,8,128]{2,1,0:T(8,128)(2,1)S(1)} custom-call(s32[4,2,256]{2,1,0:T(2,128)S(1)} %copy-done.3, f32[1024,128]{1,0:T(8,128)S(1)} %get-tuple-element.72.rest_14_.wide, f32[2048,128]{1,0:T(8,128)S(1)} %get-tuple-element.73.rest_16_.image_wide, bf16[32,8,128]{2,1,0:T(8,128)(2,1)S(1)} %collective-permute-done.17.partner, ...), custom_call_target="tpu_custom_call" | custom-call | flops 3072 | bytes 3072 | tf_op jit(solution)/shard_map/pallas_call | solution.py:335
  59.5 1.8 %shard_map.111 = bf16[64,8,256]{2,1,0:T(8,128)(2,1)} custom-call(s32[4,2,256]{2,1,0:T(2,128)S(1)} %copy-done.3, f32[1024,128]{1,0:T(8,128)S(1)} %get-tuple-element.56.rest_15_.wide, f32[2048,128]{1,0:T(8,128)S(1)} %get-tuple-element.57.rest_17_.image_wide, bf16[32,8,128]{2,1,0:T(8,128)(2,1)S(1)} %collective-permute-done.14.partner, ...), custom_call_target="tpu_custom_call" | custom-call | flops 3072 | bytes 3072 | tf_op jit(solution)/shard_map/pallas_call | solution.py:335
  (21 shorter events, 0.3 us)
Async XLA Ops:
  1.8 5.8 %copy-start.2 = (s32[4,2,256]{2,1,0:T(2,128)S(1)}, s32[4,2,256]{2,1,0:T(2,128)}, u32[]{:S(2)}) copy-start(s32[4,2,256]{2,1,0:T(2,128)} %pattern.40) | copy-start | bytes 24580
  1.9 8.1 %collective-permute-start = (bf16[32,8,128]{2,1,0:T(8,128)(2,1)S(1)}, bf16[32,8,128]{2,1,0:T(8,128)(2,1)S(1)}, u32[]{:S(2)}, u32[]{:S(2)}) collective-permute-start(bf16[32,8,128]{2,1,0:T(8,128)(2,1)S(1)} %shard_map.73.after.state), channel_id=1, source_target_pairs={{0,8},{1,9},{2,10},{3,11},{4,12},{5,13},{6,14},{7,15},{8,0},{9,1},... | collective-permute-start | bytes 196616 | tf_op jit(solution)/shard_map/ppermute | solution.py:351
  6.0 6.8 %copy-start = (bf16[4,32,64,256]{3,2,1,0:T(8,128)(2,1)S(1)}, bf16[4,32,64,256]{3,2,1,0:T(8,128)(2,1)}, u32[]{:S(2)}) copy-start(bf16[4,32,64,256]{3,2,1,0:T(8,128)(2,1)} %blocks.11) | copy-start | bytes 12582916
  9.9 5.6 %collective-permute-start.2 = (bf16[32,8,128]{2,1,0:T(8,128)(2,1)S(1)}, bf16[32,8,128]{2,1,0:T(8,128)(2,1)S(1)}, u32[]{:S(2)}, u32[]{:S(2)}) collective-permute-start(bf16[32,8,128]{2,1,0:T(8,128)(2,1)S(1)} %shard_map.77.state), channel_id=1, source_target_pairs={{0,8},{1,9},{2,10},{3,11},{4,12},{5,13},{6,14},{7,15},{8,0},{9,1},... | collective-permute-start | bytes 196616 | tf_op jit(solution)/shard_map/ppermute | solution.py:351
  10.4 7.1 %collective-permute-start.1 = (bf16[32,8,128]{2,1,0:T(8,128)(2,1)S(1)}, bf16[32,8,128]{2,1,0:T(8,128)(2,1)S(1)}, u32[]{:S(2)}, u32[]{:S(2)}) collective-permute-start(bf16[32,8,128]{2,1,0:T(8,128)(2,1)S(1)} %shard_map.76.state), channel_id=1, source_target_pairs={{0,4},{1,5},{2,6},{3,7},{4,0},{5,1},{6,2},{7,3},{8,12},{9,13},{10,... | collective-permute-start | bytes 196616 | tf_op jit(solution)/shard_map/ppermute | solution.py:351
  12.8 6.8 %copy-start.1 = (bf16[4,32,64,256]{3,2,1,0:T(8,128)(2,1)S(1)}, bf16[4,32,64,256]{3,2,1,0:T(8,128)(2,1)}, u32[]{:S(2)}) copy-start(bf16[4,32,64,256]{3,2,1,0:T(8,128)(2,1)} %blocks.15) | copy-start | bytes 12582916
  15.5 4.1 %copy-start.3 = (s32[4,2,256]{2,1,0:T(2,128)S(1)}, s32[4,2,256]{2,1,0:T(2,128)}, u32[]{:S(2)}) copy-start(s32[4,2,256]{2,1,0:T(2,128)} %pattern.53) | copy-start | bytes 24580
  15.9 4.7 %collective-permute-start.4 = (bf16[32,8,128]{2,1,0:T(8,128)(2,1)S(1)}, bf16[32,8,128]{2,1,0:T(8,128)(2,1)S(1)}, u32[]{:S(2)}, u32[]{:S(2)}) collective-permute-start(bf16[32,8,128]{2,1,0:T(8,128)(2,1)S(1)} %shard_map.80.rest_0_.state), channel_id=1, source_target_pairs={{0,4},{1,5},{2,6},{3,7},{4,0},{5,1},{6,2},{7,3},{8,12},{9,13},{10,... | collective-permute-start | bytes 196616 | tf_op jit(solution)/shard_map/ppermute | solution.py:351
  18.0 4.3 %collective-permute-start.3 = (bf16[32,8,128]{2,1,0:T(8,128)(2,1)S(1)}, bf16[32,8,128]{2,1,0:T(8,128)(2,1)S(1)}, u32[]{:S(2)}, u32[]{:S(2)}) collective-permute-start(bf16[32,8,128]{2,1,0:T(8,128)(2,1)S(1)} %shard_map.82.state), channel_id=1, source_target_pairs={{0,2},{1,3},{2,0},{3,1},{4,6},{5,7},{6,4},{7,5},{8,10},{9,11},{10,... | collective-permute-start | bytes 196616 | tf_op jit(solution)/shard_map/ppermute | solution.py:351
  22.7 2.8 %collective-permute-start.5 = (bf16[68,64,128]{2,1,0:T(8,128)(2,1)S(1)}, bf16[68,64,128]{2,1,0:T(8,128)(2,1)S(1)}, u32[]{:S(2)}, u32[]{:S(2)}) collective-permute-start(bf16[68,64,128]{2,1,0:T(8,128)(2,1)S(1)} %shard_map.88), channel_id=1, source_target_pairs={{0,1},{1,0},{2,3},{3,2},{4,5},{5,4},{6,7},{7,6},{8,9},{9,8},{10,11... | collective-permute-start | bytes 3342344 | tf_op jit(solution)/shard_map/ppermute | solution.py:351
  22.8 4.5 %collective-permute-start.6 = (bf16[32,8,128]{2,1,0:T(8,128)(2,1)S(1)}, bf16[32,8,128]{2,1,0:T(8,128)(2,1)S(1)}, u32[]{:S(2)}, u32[]{:S(2)}) collective-permute-start(bf16[32,8,128]{2,1,0:T(8,128)(2,1)S(1)} %shard_map.85.rest_0_.state), channel_id=1, source_target_pairs={{0,2},{1,3},{2,0},{3,1},{4,6},{5,7},{6,4},{7,5},{8,10},{9,11},{10,... | collective-permute-start | bytes 196616 | tf_op jit(solution)/shard_map/ppermute | solution.py:351
  27.3 5.9 %copy-start.4 = (bf16[64,32,256]{2,1,0:T(8,128)(2,1)S(1)}, bf16[64,32,256]{2,1,0:T(8,128)(2,1)}, u32[]{:S(2)}) copy-start(bf16[64,32,256]{2,1,0:T(8,128)(2,1)} %interp.5) | copy-start | bytes 3145732
  29.0 5.8 %collective-permute-start.8 = (bf16[2,2,4,8,128]{4,3,2,1,0:T(8,128)(2,1)S(1)}, bf16[2,2,4,8,128]{4,3,2,1,0:T(8,128)(2,1)S(1)}, u32[]{:S(2)}, u32[]{:S(2)}) collective-permute-start(bf16[2,2,4,8,128]{4,3,2,1,0:T(8,128)(2,1)S(1)} %get-tuple-element.59), channel_id=1, source_target_pairs={{0,2},{1,10},{2,0},{3,8},{4,6},{5,14},{6,4},{7,12},{8,3},{9,11},{1... | collective-permute-start | bytes 98312 | tf_op jit(solution)/shard_map/ppermute | solution.py:351
  30.6 4.2 %collective-permute-start.9 = (bf16[2,2,4,8,128]{4,3,2,1,0:T(8,128)(2,1)S(1)}, bf16[2,2,4,8,128]{4,3,2,1,0:T(8,128)(2,1)S(1)}, u32[]{:S(2)}, u32[]{:S(2)}) collective-permute-start(bf16[2,2,4,8,128]{4,3,2,1,0:T(8,128)(2,1)S(1)} %get-tuple-element.60), channel_id=1, source_target_pairs={{0,4},{1,12},{2,6},{3,14},{4,0},{5,8},{6,2},{7,10},{8,5},{9,13},{1... | collective-permute-start | bytes 98312 | tf_op jit(solution)/shard_map/ppermute | solution.py:351
  31.4 5.2 %collective-permute-start.10 = (bf16[2,2,4,8,128]{4,3,2,1,0:T(8,128)(2,1)S(1)}, bf16[2,2,4,8,128]{4,3,2,1,0:T(8,128)(2,1)S(1)}, u32[]{:S(2)}, u32[]{:S(2)}) collective-permute-start(bf16[2,2,4,8,128]{4,3,2,1,0:T(8,128)(2,1)S(1)} %get-tuple-element.61), channel_id=1, source_target_pairs={{0,6},{1,14},{2,4},{3,12},{4,2},{5,10},{6,0},{7,8},{8,7},{9,15},{1... | collective-permute-start | bytes 98312 | tf_op jit(solution)/shard_map/ppermute | solution.py:351
  32.5 4.1 %collective-permute-start.7 = (bf16[2,2,4,8,128]{4,3,2,1,0:T(8,128)(2,1)S(1)}, bf16[2,2,4,8,128]{4,3,2,1,0:T(8,128)(2,1)S(1)}, u32[]{:S(2)}, u32[]{:S(2)}) collective-permute-start(bf16[2,2,4,8,128]{4,3,2,1,0:T(8,128)(2,1)S(1)} %get-tuple-element.55.rest_0_.kept), channel_id=1, source_target_pairs={{1,8},{3,10},{5,12},{7,14},{8,1},{10,3},{12,5},{14,7},{17,24},{19,... | collective-permute-start | bytes 98312 | tf_op jit(solution)/shard_map/ppermute | solution.py:351
  37.6 6.6 %collective-permute-start.11 = (bf16[32,8,128]{2,1,0:T(8,128)(2,1)S(1)}, bf16[32,8,128]{2,1,0:T(8,128)(2,1)S(1)}, u32[]{:S(2)}, u32[]{:S(2)}) collective-permute-start(bf16[32,8,128]{2,1,0:T(8,128)(2,1)S(1)} %get-tuple-element.74), channel_id=1, source_target_pairs={{0,1},{1,0},{2,3},{3,2},{4,5},{5,4},{6,7},{7,6},{8,9},{9,8},{10,11... | collective-permute-start | bytes 196616 | tf_op jit(solution)/shard_map/ppermute | solution.py:351
  42.5 4.8 %collective-permute-start.15 = (bf16[32,8,128]{2,1,0:T(8,128)(2,1)S(1)}, bf16[32,8,128]{2,1,0:T(8,128)(2,1)S(1)}, u32[]{:S(2)}, u32[]{:S(2)}) collective-permute-start(bf16[32,8,128]{2,1,0:T(8,128)(2,1)S(1)} %shard_map.104.state), channel_id=1, source_target_pairs={{0,2},{1,3},{2,0},{3,1},{4,6},{5,7},{6,4},{7,5},{8,10},{9,11},{10,... | collective-permute-start | bytes 196616 | tf_op jit(solution)/shard_map/ppermute | solution.py:351
  44.2 4.3 %collective-permute-start.12 = (bf16[32,8,128]{2,1,0:T(8,128)(2,1)S(1)}, bf16[32,8,128]{2,1,0:T(8,128)(2,1)S(1)}, u32[]{:S(2)}, u32[]{:S(2)}) collective-permute-start(bf16[32,8,128]{2,1,0:T(8,128)(2,1)S(1)} %collective-permute-done.11.state.rest_0_), channel_id=1, source_target_pairs={{0,2},{1,3},{2,0},{3,1},{4,6},{5,7},{6,4},{7,5},{8,10},{9,11},{10,... | collective-permute-start | bytes 196616 | tf_op jit(solution)/shard_map/ppermute | solution.py:351
  47.7 4.3 %collective-permute-start.16 = (bf16[32,8,128]{2,1,0:T(8,128)(2,1)S(1)}, bf16[32,8,128]{2,1,0:T(8,128)(2,1)S(1)}, u32[]{:S(2)}, u32[]{:S(2)}) collective-permute-start(bf16[32,8,128]{2,1,0:T(8,128)(2,1)S(1)} %shard_map.106.state), channel_id=1, source_target_pairs={{0,4},{1,5},{2,6},{3,7},{4,0},{5,1},{6,2},{7,3},{8,12},{9,13},{10,... | collective-permute-start | bytes 196616 | tf_op jit(solution)/shard_map/ppermute | solution.py:351
  48.8 4.3 %collective-permute-start.13 = (bf16[32,8,128]{2,1,0:T(8,128)(2,1)S(1)}, bf16[32,8,128]{2,1,0:T(8,128)(2,1)S(1)}, u32[]{:S(2)}, u32[]{:S(2)}) collective-permute-start(bf16[32,8,128]{2,1,0:T(8,128)(2,1)S(1)} %shard_map.100.state.rest_0_), channel_id=1, source_target_pairs={{0,4},{1,5},{2,6},{3,7},{4,0},{5,1},{6,2},{7,3},{8,12},{9,13},{10,... | collective-permute-start | bytes 196616 | tf_op jit(solution)/shard_map/ppermute | solution.py:351
  52.4 5.9 %collective-permute-start.17 = (bf16[32,8,128]{2,1,0:T(8,128)(2,1)S(1)}, bf16[32,8,128]{2,1,0:T(8,128)(2,1)S(1)}, u32[]{:S(2)}, u32[]{:S(2)}) collective-permute-start(bf16[32,8,128]{2,1,0:T(8,128)(2,1)S(1)} %shard_map.108.state), channel_id=1, source_target_pairs={{0,8},{1,9},{2,10},{3,11},{4,12},{5,13},{6,14},{7,15},{8,0},{9,1},... | collective-permute-start | bytes 196616 | tf_op jit(solution)/shard_map/ppermute | solution.py:351
  53.6 5.9 %collective-permute-start.14 = (bf16[32,8,128]{2,1,0:T(8,128)(2,1)S(1)}, bf16[32,8,128]{2,1,0:T(8,128)(2,1)S(1)}, u32[]{:S(2)}, u32[]{:S(2)}) collective-permute-start(bf16[32,8,128]{2,1,0:T(8,128)(2,1)S(1)} %shard_map.102.state.rest_0_), channel_id=1, source_target_pairs={{0,8},{1,9},{2,10},{3,11},{4,12},{5,13},{6,14},{7,15},{8,0},{9,1},... | collective-permute-start | bytes 196616 | tf_op jit(solution)/shard_map/ppermute | solution.py:351

commit v10 on v9

--- a/solution.py
+++ b/solution.py
@@ -11,7 +11,7 @@
 GROUP = 4
 KERNEL_COST = 1024
 KERNEL_LIMIT = 16 * 2**20
-FETCH_LIMIT = 53_000_000
+FETCH_LIMIT = 53_850_000
 START_LIMIT = 56_250_000
 
 
@@ -95,12 +95,13 @@
         multiply(wide, state, rank, emit)
 
 
-def fetch_kernel(level, bit, blocks, after, *rest):
+def second_kernel(level, bit, flip, blocks, interp, samples, after, *rest):
     held, sem = rest[-2:]
     copy = pltpu.make_async_copy(blocks.at[pl.ds(level, 1)], held, sem)
     copy.start()
+    coeff_kernel(flip, interp, samples, rest[0], *rest[5:-2])
     copy.wait()
-    ahead_kernel(0, bit, held, *rest[:-2])
+    ahead_kernel(0, bit, held, *rest[1:5])
 
 
 def ahead_kernel(level, bit, blocks, *rest):
@@ -396,32 +397,30 @@
             for flip in order
         }
 
-    def coefficients(flip, *after):
-        return run(
-            functools.partial(coeff_kernel, flip), state, (interp_in, samples, *after),
-            (
-                pltpu.VMEM((2, rank, depth // 2, LANES), jnp.bfloat16),
-                pltpu.VMEM((2, depth // 2, rhs_count, LANES), jnp.bfloat16),
-                pltpu.VMEM((rank * depth // 2, LANES), jnp.float32), total, pltpu.SemaphoreType.DMA((4,)),
-            ), 2, in_specs=[pl.BlockSpec(memory_space=pl.ANY)] * (2 + len(after)), limit=START_LIMIT,
-        )
-
+    coeff_scratch = (
+        pltpu.VMEM((2, rank, depth // 2, LANES), jnp.bfloat16),
+        pltpu.VMEM((2, depth // 2, rhs_count, LANES), jnp.bfloat16),
+        pltpu.VMEM((rank * depth // 2, LANES), jnp.float32), total, pltpu.SemaphoreType.DMA((4,)),
+    )
     share_rows = 2 * rank + rank * rhs_count // (2 * rank)
     shared_shape = jax.ShapeDtypeStruct((share_rows, 2 * rank, LANES), jnp.bfloat16)
-    current = {1: coefficients(1)}
+    current = {1: run(
+        functools.partial(coeff_kernel, 1), state, (interp_in, samples), coeff_scratch, 2,
+        in_specs=[pl.BlockSpec(memory_space=pl.ANY)] * 2, limit=START_LIMIT,
+    )}
     for level in range(3):
         bit = 3 - level
         if level == 0:
             partner = {1: swapped(current[1], bit)}
-            wides = run(
-                functools.partial(fetch_kernel, 0, 3), [spread_out] * 4, (top_blocks, current[1]),
-                (pltpu.VMEM((1, *top_blocks.shape[1:]), jnp.bfloat16), pltpu.SemaphoreType.DMA), 4,
-                in_specs=[pl.BlockSpec(memory_space=pl.ANY), pl.BlockSpec(memory_space=pltpu.VMEM)], limit=FETCH_LIMIT,
+            current[0], *wides = run(
+                functools.partial(second_kernel, 0, 3, 0), [state] + [spread_out] * 4,
+                (top_blocks, interp_in, samples, current[1]),
+                coeff_scratch + (pltpu.VMEM((1, *top_blocks.shape[1:]), jnp.bfloat16), pltpu.SemaphoreType.DMA), 4,
+                in_specs=[pl.BlockSpec(memory_space=pl.ANY)] * 4, limit=FETCH_LIMIT,
             )
             wides = wides[:2], wides[2:]
+            partner[0] = swapped(current[0], bit)
             near = level_nears(top_pattern, level, bit, (1,), wides)
-            current[0] = coefficients(0, near[1])
-            partner[0] = swapped(current[0], bit)
             near.update(level_nears(top_pattern, level, bit, (0,), wides))
             later_wides = {later: level_wides(top_blocks, later, 3 - later, near[0]) for later in (1, 2)}
             shared = run(

time: 61.5 us -> 60.2 us (0.979)
  Pallas kernels: 23.3 us -> 22.5 us
    pallas_call x39 -> x38, Pallas kernels: 23.3 us -> 22.5 us  [run(): pl.pallas_call(kernel, out_shape=shapes, in_specs=in_specs or [whole] * l...]
  transfers between devices with their start and end apart: 18 -> 18, of which waited for: 10 -> 11; matrix products, arithmetic and copies ran while one was open for 0% -> 0% of each run, Pallas kernels for 27% -> 26%
where the time goes in v10:
time: 60.2 us; the launch traced here: 60.1 us
  starting transfers between devices  25.6 us (43%)
  Pallas kernels  22.5 us (37%)
  waiting for transfers between devices  11.7 us (19%)
    ppermute x18, starting transfers between devices, permuted(): return lax.ppermute(value, 'leaf', pairs)  25.6 us
    pallas_call x38, Pallas kernels, run(): pl.pallas_call(kernel, out_shape=shapes, in_specs=in_specs or [whole] * l...  22.5 us
    ppermute x18, waiting for transfers between devices, permuted(): return lax.ppermute(value, 'leaf', pairs)  11.7 us
  transfers between devices with their start and end apart: 18, of which 11 were waited for; matrix products, arithmetic and copies ran while one was open for 0% of the time, Pallas kernels for 26%

profile of v10, /device:TPU:0, one launch (start us, length us, event | category | flops | bytes accessed | tf_op | source)
XLA Modules:
  0.0 60.1 jit_solution(3507393100689614580)
XLA Ops:
  0.0 1.9 %shard_map.73.after.state = bf16[32,8,128]{2,1,0:T(8,128)(2,1)S(1)} custom-call(bf16[32,64,256]{2,1,0:T(8,128)(2,1)} %interp.4, bf16[64,8,256]{2,1,0:T(8,128)(2,1)} %samples.3), custom_call_target="tpu_custom_call" | custom-call | flops 2048 | bytes 2048 | tf_op jit(solution)/shard_map/pallas_call | solution.py:336
  1.9 4.1 %collective-permute-start = (bf16[32,8,128]{2,1,0:T(8,128)(2,1)S(1)}, bf16[32,8,128]{2,1,0:T(8,128)(2,1)S(1)}, u32[]{:S(2)}, u32[]{:S(2)}) collective-permute-start(bf16[32,8,128]{2,1,0:T(8,128)(2,1)S(1)} %shard_map.73.after.state), channel_id=1, source_target_pairs={{0,8},{1,9},{2,10},{3,11},{4,12},{5,13},{6,14},{7,15},{8,0},{9,1},... | collective-permute-start | bytes 196616 | tf_op jit(solution)/shard_map/ppermute | solution.py:352
  6.0 2.6 %shard_map.74 = (bf16[32,8,128]{2,1,0:T(8,128)(2,1)S(1)}, f32[1024,128]{1,0:T(8,128)S(1)}, f32[1024,128]{1,0:T(8,128)S(1)}, f32[1024,128]{1,0:T(8,128)S(1)}, f32[1024,128]{1,0:T(8,128)S(1)}) custom-call(bf16[4,32,64,256]{3,2,1,0:T(8,128)(2,1)} %blocks.11, bf16[32,64,256]{2,1,0:T(8,128)(2,1)} %interp.4, bf16[64,8,256]{2,1,0:T(8,128)(2,1)S(1)} %copy-done.5, ...), custom_call_target="tpu_custom_call" | custom-call | flops 4096 | bytes 4096 | tf_op jit(solution)/shard_map/pallas_call | solution.py:336
  8.6 0.1 collective-permute-start.2
  8.7 0.4 shard_map.75.near
  9.1 0.5 collective-permute-done.partner
  9.7 0.4 shard_map.76.state
  10.1 1.4 %collective-permute-start.1 = (bf16[32,8,128]{2,1,0:T(8,128)(2,1)S(1)}, bf16[32,8,128]{2,1,0:T(8,128)(2,1)S(1)}, u32[]{:S(2)}, u32[]{:S(2)}) collective-permute-start(bf16[32,8,128]{2,1,0:T(8,128)(2,1)S(1)} %shard_map.76.state), channel_id=1, source_target_pairs={{0,4},{1,5},{2,6},{3,7},{4,0},{5,1},{6,2},{7,3},{8,12},{9,13},{10,... | collective-permute-start | bytes 196616 | tf_op jit(solution)/shard_map/ppermute | solution.py:352
  11.5 0.4 shard_map.77.rest_0_.near
  11.9 0.3 shard_map.78
  12.2 2.0 %collective-permute-done.2.partner = bf16[32,8,128]{2,1,0:T(8,128)(2,1)S(1)} collective-permute-done((bf16[32,8,128]{2,1,0:T(8,128)(2,1)S(1)}, bf16[32,8,128]{2,1,0:T(8,128)(2,1)S(1)}, u32[]{:S(2)}, u32[]{:S(2)}) %collective-permute-start.2) | collective-permute-done | bytes 65568 | tf_op jit(solution)/shard_map/ppermute | solution.py:352
  14.2 0.4 shard_map.79.rest_0_.state
  14.6 1.9 %collective-permute-start.4 = (bf16[32,8,128]{2,1,0:T(8,128)(2,1)S(1)}, bf16[32,8,128]{2,1,0:T(8,128)(2,1)S(1)}, u32[]{:S(2)}, u32[]{:S(2)}) collective-permute-start(bf16[32,8,128]{2,1,0:T(8,128)(2,1)S(1)} %shard_map.79.rest_0_.state), channel_id=1, source_target_pairs={{0,4},{1,5},{2,6},{3,7},{4,0},{5,1},{6,2},{7,3},{8,12},{9,13},{10,... | collective-permute-start | bytes 196616 | tf_op jit(solution)/shard_map/ppermute | solution.py:352
  16.5 0.4 shard_map.80.near
  16.9 0.4 shard_map.81.state
  17.3 1.6 %collective-permute-start.3 = (bf16[32,8,128]{2,1,0:T(8,128)(2,1)S(1)}, bf16[32,8,128]{2,1,0:T(8,128)(2,1)S(1)}, u32[]{:S(2)}, u32[]{:S(2)}) collective-permute-start(bf16[32,8,128]{2,1,0:T(8,128)(2,1)S(1)} %shard_map.81.state), channel_id=1, source_target_pairs={{0,2},{1,3},{2,0},{3,1},{4,6},{5,7},{6,4},{7,5},{8,10},{9,11},{10,... | collective-permute-start | bytes 196616 | tf_op jit(solution)/shard_map/ppermute | solution.py:352
  18.9 0.2 shard_map.86.shared
  19.2 0.3 shard_map.82
  19.5 0.4 shard_map.83.near
  19.9 0.4 shard_map.84.rest_0_.state
  20.3 0.4 shard_map.85.near
  20.7 0.9 %collective-permute-done.3.partner = bf16[32,8,128]{2,1,0:T(8,128)(2,1)S(1)} collective-permute-done((bf16[32,8,128]{2,1,0:T(8,128)(2,1)S(1)}, bf16[32,8,128]{2,1,0:T(8,128)(2,1)S(1)}, u32[]{:S(2)}, u32[]{:S(2)}) %collective-permute-start.3) | collective-permute-done | bytes 65568 | tf_op jit(solution)/shard_map/ppermute | solution.py:352
  21.7 0.4 shard_map.87
  22.1 1.6 %collective-permute-start.6 = (bf16[32,8,128]{2,1,0:T(8,128)(2,1)S(1)}, bf16[32,8,128]{2,1,0:T(8,128)(2,1)S(1)}, u32[]{:S(2)}, u32[]{:S(2)}) collective-permute-start(bf16[32,8,128]{2,1,0:T(8,128)(2,1)S(1)} %shard_map.84.rest_0_.state), channel_id=1, source_target_pairs={{0,2},{1,3},{2,0},{3,1},{4,6},{5,7},{6,4},{7,5},{8,10},{9,11},{10,... | collective-permute-start | bytes 196616 | tf_op jit(solution)/shard_map/ppermute | solution.py:352
  23.7 0.4 shard_map.89.near
  24.1 0.8 %collective-permute-done.5.shared = bf16[68,64,128]{2,1,0:T(8,128)(2,1)S(1)} collective-permute-done((bf16[68,64,128]{2,1,0:T(8,128)(2,1)S(1)}, bf16[68,64,128]{2,1,0:T(8,128)(2,1)S(1)}, u32[]{:S(2)}, u32[]{:S(2)}) %collective-permute-start.5) | collective-permute-done | bytes 1114144 | tf_op jit(solution)/shard_map/ppermute | solution.py:352
  24.9 1.0 %shard_map.88 = (f32[2,32,8,128]{3,2,1,0:T(8,128)S(1)}, f32[2,1024,128]{2,1,0:T(8,128)S(1)}) custom-call(bf16[4,32,64,256]{3,2,1,0:T(8,128)(2,1)S(1)} %copy-done, s32[4,2,256]{2,1,0:T(2,128)S(1)} %copy-done.2, bf16[68,64,128]{2,1,0:T(8,128)(2,1)S(1)} %collective-permute-done.5.shared), custom_call_target="tpu_custom_call" | custom-call | flops 2048 | bytes 2048 | tf_op jit(solution)/shard_map/pallas_call | solution.py:336
  25.9 0.7 %collective-permute-done.6.partner = bf16[32,8,128]{2,1,0:T(8,128)(2,1)S(1)} collective-permute-done((bf16[32,8,128]{2,1,0:T(8,128)(2,1)S(1)}, bf16[32,8,128]{2,1,0:T(8,128)(2,1)S(1)}, u32[]{:S(2)}, u32[]{:S(2)}) %collective-permute-start.6) | collective-permute-done | bytes 65568 | tf_op jit(solution)/shard_map/ppermute | solution.py:352
  26.6 0.4 shard_map.90.state
  27.0 1.3 %shard_map.91 = (bf16[2,2,4,8,128]{4,3,2,1,0:T(8,128)(2,1)S(1)}, bf16[2,2,4,8,128]{4,3,2,1,0:T(8,128)(2,1)S(1)}, bf16[2,2,4,8,128]{4,3,2,1,0:T(8,128)(2,1)S(1)}, bf16[2,2,4,8,128]{4,3,2,1,0:T(8,128)(2,1)S(1)}) custom-call(s32[4,2,256]{2,1,0:T(2,128)S(1)} %copy-done.2, f32[2,1024,128]{2,1,0:T(8,128)S(1)} %get-tuple-element.53.wide, ...), custom_call_target="tpu_custom_call" | custom-call | flops 2048 | bytes 2048 | tf_op jit(solution)/shard_map/pallas_call | solution.py:336
  28.3 1.6 %collective-permute-start.8 = (bf16[2,2,4,8,128]{4,3,2,1,0:T(8,128)(2,1)S(1)}, bf16[2,2,4,8,128]{4,3,2,1,0:T(8,128)(2,1)S(1)}, u32[]{:S(2)}, u32[]{:S(2)}) collective-permute-start(bf16[2,2,4,8,128]{4,3,2,1,0:T(8,128)(2,1)S(1)} %get-tuple-element.61), channel_id=1, source_target_pairs={{0,2},{1,10},{2,0},{3,8},{4,6},{5,14},{6,4},{7,12},{8,3},{9,11},{1... | collective-permute-start | bytes 98312 | tf_op jit(solution)/shard_map/ppermute | solution.py:352
  29.9 0.2 collective-permute-start.9
  30.1 1.8 %collective-permute-start.10 = (bf16[2,2,4,8,128]{4,3,2,1,0:T(8,128)(2,1)S(1)}, bf16[2,2,4,8,128]{4,3,2,1,0:T(8,128)(2,1)S(1)}, u32[]{:S(2)}, u32[]{:S(2)}) collective-permute-start(bf16[2,2,4,8,128]{4,3,2,1,0:T(8,128)(2,1)S(1)} %get-tuple-element.63), channel_id=1, source_target_pairs={{0,6},{1,14},{2,4},{3,12},{4,2},{5,10},{6,0},{7,8},{8,7},{9,15},{1... | collective-permute-start | bytes 98312 | tf_op jit(solution)/shard_map/ppermute | solution.py:352
  31.9 0.7 %collective-permute-start.7 = (bf16[2,2,4,8,128]{4,3,2,1,0:T(8,128)(2,1)S(1)}, bf16[2,2,4,8,128]{4,3,2,1,0:T(8,128)(2,1)S(1)}, u32[]{:S(2)}, u32[]{:S(2)}) collective-permute-start(bf16[2,2,4,8,128]{4,3,2,1,0:T(8,128)(2,1)S(1)} %get-tuple-element.57.rest_0_.kept), channel_id=1, source_target_pairs={{1,8},{3,10},{5,12},{7,14},{8,1},{10,3},{12,5},{14,7},{17,24},{19,... | collective-permute-start | bytes 98312 | tf_op jit(solution)/shard_map/ppermute | solution.py:352
  32.5 0.3 shard_map.93
  32.8 0.3 shard_map.94
  33.1 0.3 shard_map.96
  33.4 0.3 shard_map.95
  33.8 0.3 shard_map.92
  34.1 1.2 %collective-permute-done.10.rest_3_ = bf16[2,2,4,8,128]{4,3,2,1,0:T(8,128)(2,1)S(1)} collective-permute-done((bf16[2,2,4,8,128]{4,3,2,1,0:T(8,128)(2,1)S(1)}, bf16[2,2,4,8,128]{4,3,2,1,0:T(8,128)(2,1)S(1)}, u32[]{:S(2)}, u32[]{:S(2)}) %collective-permute-start.10) | collective-permute-done | bytes 32800 | tf_op jit(solution)/shard_map/ppermute | solution.py:352
  35.3 1.0 %shard_map.97 = (bf16[32,8,128]{2,1,0:T(8,128)(2,1)S(1)}, bf16[2,32,8,128]{3,2,1,0:T(8,128)(2,1)S(1)}) custom-call(f32[2,1024,128]{2,1,0:T(8,128)S(1)} %get-tuple-element.60.wide, bf16[2,2,4,8,128]{4,3,2,1,0:T(8,128)(2,1)S(1)} %get-tuple-element.57.rest_0_.kept, bf16[2,2,4,8,128]{4,3,2,1,0:T(8,128)(2,1)S(1)} %collective-permute-done.7.rest_0_, ...), custom_call_target="tpu_custom_call" | custom-call | flops 2048 | bytes 2048 | tf_op jit(solution)/shard_map/pallas_call | solution.py:336
  36.3 4.3 %collective-permute-start.11 = (bf16[32,8,128]{2,1,0:T(8,128)(2,1)S(1)}, bf16[32,8,128]{2,1,0:T(8,128)(2,1)S(1)}, u32[]{:S(2)}, u32[]{:S(2)}) collective-permute-start(bf16[32,8,128]{2,1,0:T(8,128)(2,1)S(1)} %get-tuple-element.76), channel_id=1, source_target_pairs={{0,1},{1,0},{2,3},{3,2},{4,5},{5,4},{6,7},{7,6},{8,9},{9,8},{10,11... | collective-permute-start | bytes 196616 | tf_op jit(solution)/shard_map/ppermute | solution.py:352
  40.6 0.8 %shard_map.103.state = bf16[32,8,128]{2,1,0:T(8,128)(2,1)S(1)} custom-call(s32[4,2,256]{2,1,0:T(2,128)S(1)} %copy-done.3, f32[2,1024,128]{2,1,0:T(8,128)S(1)} %get-tuple-element.77.wide, bf16[2,32,8,128]{3,2,1,0:T(8,128)(2,1)S(1)} %get-tuple-element.78.states), custom_call_target="tpu_custom_call" | custom-call | flops 2048 | bytes 2048 | tf_op jit(solution)/shard_map/pallas_call | solution.py:336
  41.3 1.6 %collective-permute-start.15 = (bf16[32,8,128]{2,1,0:T(8,128)(2,1)S(1)}, bf16[32,8,128]{2,1,0:T(8,128)(2,1)S(1)}, u32[]{:S(2)}, u32[]{:S(2)}) collective-permute-start(bf16[32,8,128]{2,1,0:T(8,128)(2,1)S(1)} %shard_map.103.state), channel_id=1, source_target_pairs={{0,2},{1,3},{2,0},{3,1},{4,6},{5,7},{6,4},{7,5},{8,10},{9,11},{10,... | collective-permute-start | bytes 196616 | tf_op jit(solution)/shard_map/ppermute | solution.py:352
  42.9 0.5 collective-permute-start.12
  43.4 0.4 shard_map.104.near
  43.8 2.3 %collective-permute-done.15.partner = bf16[32,8,128]{2,1,0:T(8,128)(2,1)S(1)} collective-permute-done((bf16[32,8,128]{2,1,0:T(8,128)(2,1)S(1)}, bf16[32,8,128]{2,1,0:T(8,128)(2,1)S(1)}, u32[]{:S(2)}, u32[]{:S(2)}) %collective-permute-start.15) | collective-permute-done | bytes 65568 | tf_op jit(solution)/shard_map/ppermute | solution.py:352
  46.0 0.4 shard_map.105.state
  46.5 0.4 shard_map.98.near
  46.9 0.3 collective-permute-done.12.partner
  47.2 0.4 shard_map.99.state.rest_0_
  47.6 1.8 %collective-permute-start.13 = (bf16[32,8,128]{2,1,0:T(8,128)(2,1)S(1)}, bf16[32,8,128]{2,1,0:T(8,128)(2,1)S(1)}, u32[]{:S(2)}, u32[]{:S(2)}) collective-permute-start(bf16[32,8,128]{2,1,0:T(8,128)(2,1)S(1)} %shard_map.99.state.rest_0_), channel_id=1, source_target_pairs={{0,4},{1,5},{2,6},{3,7},{4,0},{5,1},{6,2},{7,3},{8,12},{9,13},{10,... | collective-permute-start | bytes 196616 | tf_op jit(solution)/shard_map/ppermute | solution.py:352
  49.4 0.4 shard_map.100.near
  49.8 0.4 shard_map.106.near
  50.1 0.6 %collective-permute-done.16.partner = bf16[32,8,128]{2,1,0:T(8,128)(2,1)S(1)} collective-permute-done((bf16[32,8,128]{2,1,0:T(8,128)(2,1)S(1)}, bf16[32,8,128]{2,1,0:T(8,128)(2,1)S(1)}, u32[]{:S(2)}, u32[]{:S(2)}) %collective-permute-start.16) | collective-permute-done | bytes 65568 | tf_op jit(solution)/shard_map/ppermute | solution.py:352
  50.8 0.4 shard_map.107.state
  51.2 0.7 %collective-permute-done.13.partner = bf16[32,8,128]{2,1,0:T(8,128)(2,1)S(1)} collective-permute-done((bf16[32,8,128]{2,1,0:T(8,128)(2,1)S(1)}, bf16[32,8,128]{2,1,0:T(8,128)(2,1)S(1)}, u32[]{:S(2)}, u32[]{:S(2)}) %collective-permute-start.13) | collective-permute-done | bytes 65568 | tf_op jit(solution)/shard_map/ppermute | solution.py:352
  51.9 0.4 shard_map.101.state.rest_0_
  52.3 2.3 %collective-permute-start.14 = (bf16[32,8,128]{2,1,0:T(8,128)(2,1)S(1)}, bf16[32,8,128]{2,1,0:T(8,128)(2,1)S(1)}, u32[]{:S(2)}, u32[]{:S(2)}) collective-permute-start(bf16[32,8,128]{2,1,0:T(8,128)(2,1)S(1)} %shard_map.101.state.rest_0_), channel_id=1, source_target_pairs={{0,8},{1,9},{2,10},{3,11},{4,12},{5,13},{6,14},{7,15},{8,0},{9,1},... | collective-permute-start | bytes 196616 | tf_op jit(solution)/shard_map/ppermute | solution.py:352
  54.6 0.4 shard_map.102.near
  55.0 0.4 shard_map.108.near
  55.4 1.7 %collective-permute-done.17.partner = bf16[32,8,128]{2,1,0:T(8,128)(2,1)S(1)} collective-permute-done((bf16[32,8,128]{2,1,0:T(8,128)(2,1)S(1)}, bf16[32,8,128]{2,1,0:T(8,128)(2,1)S(1)}, u32[]{:S(2)}, u32[]{:S(2)}) %collective-permute-start.17) | collective-permute-done | bytes 65568 | tf_op jit(solution)/shard_map/ppermute | solution.py:352
  57.1 1.1 %shard_map.109.ready = bf16[64,8,128]{2,1,0:T(8,128)(2,1)S(1)} custom-call(s32[4,2,256]{2,1,0:T(2,128)S(1)} %copy-done.3, f32[1024,128]{1,0:T(8,128)S(1)} %get-tuple-element.74.rest_14_.wide, f32[2048,128]{1,0:T(8,128)S(1)} %get-tuple-element.75.rest_16_.image_wide, bf16[32,8,128]{2,1,0:T(8,128)(2,1)S(1)} %collective-permute-done.17.partner, ...), custom_call_target="tpu_custom_call" | custom-call | flops 3072 | bytes 3072 | tf_op jit(solution)/shard_map/pallas_call | solution.py:336
  58.2 1.8 %shard_map.110 = bf16[64,8,256]{2,1,0:T(8,128)(2,1)} custom-call(s32[4,2,256]{2,1,0:T(2,128)S(1)} %copy-done.3, f32[1024,128]{1,0:T(8,128)S(1)} %get-tuple-element.58.rest_15_.wide, f32[2048,128]{1,0:T(8,128)S(1)} %get-tuple-element.59.rest_17_.image_wide, bf16[32,8,128]{2,1,0:T(8,128)(2,1)S(1)} %collective-permute-done.14.partner, ...), custom_call_target="tpu_custom_call" | custom-call | flops 3072 | bytes 3072 | tf_op jit(solution)/shard_map/pallas_call | solution.py:336
  (22 shorter events, 0.3 us)
Async XLA Ops:
  0.0 6.0 %copy-start.5 = (bf16[64,8,256]{2,1,0:T(8,128)(2,1)S(1)}, bf16[64,8,256]{2,1,0:T(8,128)(2,1)}, u32[]{:S(2)}) copy-start(bf16[64,8,256]{2,1,0:T(8,128)(2,1)} %samples.3) | copy-start | bytes 786436
  1.9 6.8 %copy-start.2 = (s32[4,2,256]{2,1,0:T(2,128)S(1)}, s32[4,2,256]{2,1,0:T(2,128)}, u32[]{:S(2)}) copy-start(s32[4,2,256]{2,1,0:T(2,128)} %pattern.40) | copy-start | bytes 24580
  1.9 7.8 %collective-permute-start = (bf16[32,8,128]{2,1,0:T(8,128)(2,1)S(1)}, bf16[32,8,128]{2,1,0:T(8,128)(2,1)S(1)}, u32[]{:S(2)}, u32[]{:S(2)}) collective-permute-start(bf16[32,8,128]{2,1,0:T(8,128)(2,1)S(1)} %shard_map.73.after.state), channel_id=1, source_target_pairs={{0,8},{1,9},{2,10},{3,11},{4,12},{5,13},{6,14},{7,15},{8,0},{9,1},... | collective-permute-start | bytes 196616 | tf_op jit(solution)/shard_map/ppermute | solution.py:352
  6.0 5.9 %copy-start = (bf16[4,32,64,256]{3,2,1,0:T(8,128)(2,1)S(1)}, bf16[4,32,64,256]{3,2,1,0:T(8,128)(2,1)}, u32[]{:S(2)}) copy-start(bf16[4,32,64,256]{3,2,1,0:T(8,128)(2,1)} %blocks.11) | copy-start | bytes 12582916
  8.6 5.6 %collective-permute-start.2 = (bf16[32,8,128]{2,1,0:T(8,128)(2,1)S(1)}, bf16[32,8,128]{2,1,0:T(8,128)(2,1)S(1)}, u32[]{:S(2)}, u32[]{:S(2)}) collective-permute-start(bf16[32,8,128]{2,1,0:T(8,128)(2,1)S(1)} %get-tuple-element.44.state), channel_id=1, source_target_pairs={{0,8},{1,9},{2,10},{3,11},{4,12},{5,13},{6,14},{7,15},{8,0},{9,1},... | collective-permute-start | bytes 196616 | tf_op jit(solution)/shard_map/ppermute | solution.py:352
  10.1 6.8 %collective-permute-start.1 = (bf16[32,8,128]{2,1,0:T(8,128)(2,1)S(1)}, bf16[32,8,128]{2,1,0:T(8,128)(2,1)S(1)}, u32[]{:S(2)}, u32[]{:S(2)}) collective-permute-start(bf16[32,8,128]{2,1,0:T(8,128)(2,1)S(1)} %shard_map.76.state), channel_id=1, source_target_pairs={{0,4},{1,5},{2,6},{3,7},{4,0},{5,1},{6,2},{7,3},{8,12},{9,13},{10,... | collective-permute-start | bytes 196616 | tf_op jit(solution)/shard_map/ppermute | solution.py:352
  11.9 7.0 %copy-start.1 = (bf16[4,32,64,256]{3,2,1,0:T(8,128)(2,1)S(1)}, bf16[4,32,64,256]{3,2,1,0:T(8,128)(2,1)}, u32[]{:S(2)}) copy-start(bf16[4,32,64,256]{3,2,1,0:T(8,128)(2,1)} %blocks.15) | copy-start | bytes 12582916
  14.2 4.7 %copy-start.3 = (s32[4,2,256]{2,1,0:T(2,128)S(1)}, s32[4,2,256]{2,1,0:T(2,128)}, u32[]{:S(2)}) copy-start(s32[4,2,256]{2,1,0:T(2,128)} %pattern.53) | copy-start | bytes 24580
  14.6 5.3 %collective-permute-start.4 = (bf16[32,8,128]{2,1,0:T(8,128)(2,1)S(1)}, bf16[32,8,128]{2,1,0:T(8,128)(2,1)S(1)}, u32[]{:S(2)}, u32[]{:S(2)}) collective-permute-start(bf16[32,8,128]{2,1,0:T(8,128)(2,1)S(1)} %shard_map.79.rest_0_.state), channel_id=1, source_target_pairs={{0,4},{1,5},{2,6},{3,7},{4,0},{5,1},{6,2},{7,3},{8,12},{9,13},{10,... | collective-permute-start | bytes 196616 | tf_op jit(solution)/shard_map/ppermute | solution.py:352
  17.3 4.3 %collective-permute-start.3 = (bf16[32,8,128]{2,1,0:T(8,128)(2,1)S(1)}, bf16[32,8,128]{2,1,0:T(8,128)(2,1)S(1)}, u32[]{:S(2)}, u32[]{:S(2)}) collective-permute-start(bf16[32,8,128]{2,1,0:T(8,128)(2,1)S(1)} %shard_map.81.state), channel_id=1, source_target_pairs={{0,2},{1,3},{2,0},{3,1},{4,6},{5,7},{6,4},{7,5},{8,10},{9,11},{10,... | collective-permute-start | bytes 196616 | tf_op jit(solution)/shard_map/ppermute | solution.py:352
  22.1 2.8 %collective-permute-start.5 = (bf16[68,64,128]{2,1,0:T(8,128)(2,1)S(1)}, bf16[68,64,128]{2,1,0:T(8,128)(2,1)S(1)}, u32[]{:S(2)}, u32[]{:S(2)}) collective-permute-start(bf16[68,64,128]{2,1,0:T(8,128)(2,1)S(1)} %shard_map.87), channel_id=1, source_target_pairs={{0,1},{1,0},{2,3},{3,2},{4,5},{5,4},{6,7},{7,6},{8,9},{9,8},{10,11... | collective-permute-start | bytes 3342344 | tf_op jit(solution)/shard_map/ppermute | solution.py:352
  22.1 4.5 %collective-permute-start.6 = (bf16[32,8,128]{2,1,0:T(8,128)(2,1)S(1)}, bf16[32,8,128]{2,1,0:T(8,128)(2,1)S(1)}, u32[]{:S(2)}, u32[]{:S(2)}) collective-permute-start(bf16[32,8,128]{2,1,0:T(8,128)(2,1)S(1)} %shard_map.84.rest_0_.state), channel_id=1, source_target_pairs={{0,2},{1,3},{2,0},{3,1},{4,6},{5,7},{6,4},{7,5},{8,10},{9,11},{10,... | collective-permute-start | bytes 196616 | tf_op jit(solution)/shard_map/ppermute | solution.py:352
  26.6 5.9 %copy-start.4 = (bf16[64,32,256]{2,1,0:T(8,128)(2,1)S(1)}, bf16[64,32,256]{2,1,0:T(8,128)(2,1)}, u32[]{:S(2)}) copy-start(bf16[64,32,256]{2,1,0:T(8,128)(2,1)} %interp.5) | copy-start | bytes 3145732
  28.3 5.8 %collective-permute-start.8 = (bf16[2,2,4,8,128]{4,3,2,1,0:T(8,128)(2,1)S(1)}, bf16[2,2,4,8,128]{4,3,2,1,0:T(8,128)(2,1)S(1)}, u32[]{:S(2)}, u32[]{:S(2)}) collective-permute-start(bf16[2,2,4,8,128]{4,3,2,1,0:T(8,128)(2,1)S(1)} %get-tuple-element.61), channel_id=1, source_target_pairs={{0,2},{1,10},{2,0},{3,8},{4,6},{5,14},{6,4},{7,12},{8,3},{9,11},{1... | collective-permute-start | bytes 98312 | tf_op jit(solution)/shard_map/ppermute | solution.py:352
  29.9 4.2 %collective-permute-start.9 = (bf16[2,2,4,8,128]{4,3,2,1,0:T(8,128)(2,1)S(1)}, bf16[2,2,4,8,128]{4,3,2,1,0:T(8,128)(2,1)S(1)}, u32[]{:S(2)}, u32[]{:S(2)}) collective-permute-start(bf16[2,2,4,8,128]{4,3,2,1,0:T(8,128)(2,1)S(1)} %get-tuple-element.62), channel_id=1, source_target_pairs={{0,4},{1,12},{2,6},{3,14},{4,0},{5,8},{6,2},{7,10},{8,5},{9,13},{1... | collective-permute-start | bytes 98312 | tf_op jit(solution)/shard_map/ppermute | solution.py:352
  30.1 5.2 %collective-permute-start.10 = (bf16[2,2,4,8,128]{4,3,2,1,0:T(8,128)(2,1)S(1)}, bf16[2,2,4,8,128]{4,3,2,1,0:T(8,128)(2,1)S(1)}, u32[]{:S(2)}, u32[]{:S(2)}) collective-permute-start(bf16[2,2,4,8,128]{4,3,2,1,0:T(8,128)(2,1)S(1)} %get-tuple-element.63), channel_id=1, source_target_pairs={{0,6},{1,14},{2,4},{3,12},{4,2},{5,10},{6,0},{7,8},{8,7},{9,15},{1... | collective-permute-start | bytes 98312 | tf_op jit(solution)/shard_map/ppermute | solution.py:352
  31.9 3.4 %collective-permute-start.7 = (bf16[2,2,4,8,128]{4,3,2,1,0:T(8,128)(2,1)S(1)}, bf16[2,2,4,8,128]{4,3,2,1,0:T(8,128)(2,1)S(1)}, u32[]{:S(2)}, u32[]{:S(2)}) collective-permute-start(bf16[2,2,4,8,128]{4,3,2,1,0:T(8,128)(2,1)S(1)} %get-tuple-element.57.rest_0_.kept), channel_id=1, source_target_pairs={{1,8},{3,10},{5,12},{7,14},{8,1},{10,3},{12,5},{14,7},{17,24},{19,... | collective-permute-start | bytes 98312 | tf_op jit(solution)/shard_map/ppermute | solution.py:352
  36.3 6.6 %collective-permute-start.11 = (bf16[32,8,128]{2,1,0:T(8,128)(2,1)S(1)}, bf16[32,8,128]{2,1,0:T(8,128)(2,1)S(1)}, u32[]{:S(2)}, u32[]{:S(2)}) collective-permute-start(bf16[32,8,128]{2,1,0:T(8,128)(2,1)S(1)} %get-tuple-element.76), channel_id=1, source_target_pairs={{0,1},{1,0},{2,3},{3,2},{4,5},{5,4},{6,7},{7,6},{8,9},{9,8},{10,11... | collective-permute-start | bytes 196616 | tf_op jit(solution)/shard_map/ppermute | solution.py:352
  41.3 4.7 %collective-permute-start.15 = (bf16[32,8,128]{2,1,0:T(8,128)(2,1)S(1)}, bf16[32,8,128]{2,1,0:T(8,128)(2,1)S(1)}, u32[]{:S(2)}, u32[]{:S(2)}) collective-permute-start(bf16[32,8,128]{2,1,0:T(8,128)(2,1)S(1)} %shard_map.103.state), channel_id=1, source_target_pairs={{0,2},{1,3},{2,0},{3,1},{4,6},{5,7},{6,4},{7,5},{8,10},{9,11},{10,... | collective-permute-start | bytes 196616 | tf_op jit(solution)/shard_map/ppermute | solution.py:352
  42.9 4.3 %collective-permute-start.12 = (bf16[32,8,128]{2,1,0:T(8,128)(2,1)S(1)}, bf16[32,8,128]{2,1,0:T(8,128)(2,1)S(1)}, u32[]{:S(2)}, u32[]{:S(2)}) collective-permute-start(bf16[32,8,128]{2,1,0:T(8,128)(2,1)S(1)} %collective-permute-done.11.state.rest_0_), channel_id=1, source_target_pairs={{0,2},{1,3},{2,0},{3,1},{4,6},{5,7},{6,4},{7,5},{8,10},{9,11},{10,... | collective-permute-start | bytes 196616 | tf_op jit(solution)/shard_map/ppermute | solution.py:352
  46.4 4.3 %collective-permute-start.16 = (bf16[32,8,128]{2,1,0:T(8,128)(2,1)S(1)}, bf16[32,8,128]{2,1,0:T(8,128)(2,1)S(1)}, u32[]{:S(2)}, u32[]{:S(2)}) collective-permute-start(bf16[32,8,128]{2,1,0:T(8,128)(2,1)S(1)} %shard_map.105.state), channel_id=1, source_target_pairs={{0,4},{1,5},{2,6},{3,7},{4,0},{5,1},{6,2},{7,3},{8,12},{9,13},{10,... | collective-permute-start | bytes 196616 | tf_op jit(solution)/shard_map/ppermute | solution.py:352
  47.6 4.3 %collective-permute-start.13 = (bf16[32,8,128]{2,1,0:T(8,128)(2,1)S(1)}, bf16[32,8,128]{2,1,0:T(8,128)(2,1)S(1)}, u32[]{:S(2)}, u32[]{:S(2)}) collective-permute-start(bf16[32,8,128]{2,1,0:T(8,128)(2,1)S(1)} %shard_map.99.state.rest_0_), channel_id=1, source_target_pairs={{0,4},{1,5},{2,6},{3,7},{4,0},{5,1},{6,2},{7,3},{8,12},{9,13},{10,... | collective-permute-start | bytes 196616 | tf_op jit(solution)/shard_map/ppermute | solution.py:352
  51.2 5.9 %collective-permute-start.17 = (bf16[32,8,128]{2,1,0:T(8,128)(2,1)S(1)}, bf16[32,8,128]{2,1,0:T(8,128)(2,1)S(1)}, u32[]{:S(2)}, u32[]{:S(2)}) collective-permute-start(bf16[32,8,128]{2,1,0:T(8,128)(2,1)S(1)} %shard_map.107.state), channel_id=1, source_target_pairs={{0,8},{1,9},{2,10},{3,11},{4,12},{5,13},{6,14},{7,15},{8,0},{9,1},... | collective-permute-start | bytes 196616 | tf_op jit(solution)/shard_map/ppermute | solution.py:352
  52.3 5.9 %collective-permute-start.14 = (bf16[32,8,128]{2,1,0:T(8,128)(2,1)S(1)}, bf16[32,8,128]{2,1,0:T(8,128)(2,1)S(1)}, u32[]{:S(2)}, u32[]{:S(2)}) collective-permute-start(bf16[32,8,128]{2,1,0:T(8,128)(2,1)S(1)} %shard_map.101.state.rest_0_), channel_id=1, source_target_pairs={{0,8},{1,9},{2,10},{3,11},{4,12},{5,13},{6,14},{7,15},{8,0},{9,1},... | collective-permute-start | bytes 196616 | tf_op jit(solution)/shard_map/ppermute | solution.py:352

commit v11 on v10

--- a/solution.py
+++ b/solution.py
@@ -9,6 +9,7 @@
 
 LANES = 128
 GROUP = 4
+ROWS = 8
 KERNEL_COST = 1024
 KERNEL_LIMIT = 16 * 2**20
 FETCH_LIMIT = 53_850_000
@@ -41,17 +42,17 @@
     rank = len(state)
 
     def body(step, carry):
-        for inner in range(GROUP):
+        for inner in range(ROWS):
             sums = [None, None]
             for index in range(rank):
-                weight = wide[pl.ds(step * GROUP * rank + inner * rank + index, 8, stride=0), :]
+                weight = wide[pl.ds(step * ROWS * rank + inner * rank + index, 8, stride=0), :]
                 term = weight * state[index]
                 old = sums[index % 2]
                 sums[index % 2] = term if old is None else old + term
-            emit(step * GROUP + inner, sums[0] + sums[1])
+            emit(step * ROWS + inner, sums[0] + sums[1])
         return carry
 
-    lax.fori_loop(0, row_count // GROUP, body, 0)
+    lax.fori_loop(0, row_count // ROWS, body, 0)
 
 
 def state_rows(ref, present=None):
@@ -224,9 +225,9 @@
 
         multiply(wide.at[box], [row * present for row in rows] if box == 0 else rows, rank, emit)
         depth = rank // fold
-        pieces = swap_groups([total[place * depth:(place + 1) * depth] for place in range(fold)], slot)
+        pieces = swap_groups([total[place * depth:(place + 1) * depth].astype(jnp.bfloat16) for place in range(fold)], slot)
         for place, piece in enumerate(pieces):
-            packed[core ^ box, place] = piece.astype(jnp.bfloat16)
+            packed[core ^ box, place] = piece
     for turn, out in enumerate(outs):
         first = ((mid ^ (turn // 2)) * 2 + (low ^ (turn % 2))) * 2
         for box in range(2):
@@ -272,9 +273,9 @@
                     value = jnp.where(high == core, kept[box, last], value)
                 packed[last, first + box] = value
     for last in range(2):
-        tile = swap_groups([packed[last, place].astype(jnp.float32) for place in range(fold)], slot)
+        tile = swap_groups([packed[last, place] for place in range(fold)], slot)
         for place, rows in enumerate(tile):
-            states[last, place * depth:(place + 1) * depth] = rows.astype(jnp.bfloat16)
+            states[last, place * depth:(place + 1) * depth] = rows
     pair_box(wide, total, states, (None, None), out)
 
 
@@ -392,9 +393,9 @@
         return {
             flip: run(
                 functools.partial(far_kernel, level, bit, flip), state,
-                (pattern, partner[flip], near[flip], wides[1][flip], *extra),
+                (pattern, partner[flip], near[flip], wides[1][flip]) + (tuple(extra) if place == len(order) - 1 else ()),
             )
-            for flip in order
+            for place, flip in enumerate(order)
         }
 
     coeff_scratch = (
@@ -432,7 +433,7 @@
             wides = later_wides[level]
             near = level_nears(top_pattern, level, bit, (1, 0), wides)
         if level < 2:
-            current = level_fars(top_pattern, level, bit, (1, 0), wides)
+            current = level_fars(top_pattern, level, bit, (1, 0), wides, later_wides[2][0] if level == 0 else ())
 
     shared = run(
         functools.partial(send_kernel, 2, 1, 1), shared_shape, (top_pattern, partner[1], near[1], wides[1][1], shared), aliases={4: 0},

time: 60.2 us -> 59.7 us (level)
  Pallas kernels: 22.5 us -> 20.8 us
    pallas_call x38, Pallas kernels: 22.5 us -> 20.8 us  [run(): pl.pallas_call(kernel, out_shape=shapes, in_specs=in_specs or [whole] * l...]
    ppermute x18, starting transfers between devices: 25.6 us -> 26.2 us  [permuted(): return lax.ppermute(value, 'leaf', pairs)]
  transfers between devices with their start and end apart: 18 -> 18, of which waited for: 11 -> 11; matrix products, arithmetic and copies ran while one was open for 0% -> 0% of each run, Pallas kernels for 26% -> 24%
where the time goes in v11:
time: 59.7 us; the launch traced here: 59.5 us
  starting transfers between devices  26.2 us (44%)
  Pallas kernels  20.8 us (35%)
  waiting for transfers between devices  12.2 us (20%)
    ppermute x18, starting transfers between devices, permuted(): return lax.ppermute(value, 'leaf', pairs)  26.2 us
    pallas_call x38, Pallas kernels, run(): pl.pallas_call(kernel, out_shape=shapes, in_specs=in_specs or [whole] * l...  20.8 us
    ppermute x18, waiting for transfers between devices, permuted(): return lax.ppermute(value, 'leaf', pairs)  12.2 us
  transfers between devices with their start and end apart: 18, of which 11 were waited for; matrix products, arithmetic and copies ran while one was open for 0% of the time, Pallas kernels for 24%

profile of v11, /device:TPU:0, one launch (start us, length us, event | category | flops | bytes accessed | tf_op | source)
XLA Modules:
  0.0 59.5 jit_solution(5925286538164646439)
XLA Ops:
  0.0 1.8 %shard_map.73.after.state = bf16[32,8,128]{2,1,0:T(8,128)(2,1)S(1)} custom-call(bf16[32,64,256]{2,1,0:T(8,128)(2,1)} %interp.4, bf16[64,8,256]{2,1,0:T(8,128)(2,1)} %samples.3), custom_call_target="tpu_custom_call" | custom-call | flops 2048 | bytes 2048 | tf_op jit(solution)/shard_map/pallas_call | solution.py:337
  1.8 4.1 %collective-permute-start = (bf16[32,8,128]{2,1,0:T(8,128)(2,1)S(1)}, bf16[32,8,128]{2,1,0:T(8,128)(2,1)S(1)}, u32[]{:S(2)}, u32[]{:S(2)}) collective-permute-start(bf16[32,8,128]{2,1,0:T(8,128)(2,1)S(1)} %shard_map.73.after.state), channel_id=1, source_target_pairs={{0,8},{1,9},{2,10},{3,11},{4,12},{5,13},{6,14},{7,15},{8,0},{9,1},... | collective-permute-start | bytes 196616 | tf_op jit(solution)/shard_map/ppermute | solution.py:353
  5.9 2.5 %shard_map.74 = (bf16[32,8,128]{2,1,0:T(8,128)(2,1)S(1)}, f32[1024,128]{1,0:T(8,128)S(1)}, f32[1024,128]{1,0:T(8,128)S(1)}, f32[1024,128]{1,0:T(8,128)S(1)}, f32[1024,128]{1,0:T(8,128)S(1)}) custom-call(bf16[4,32,64,256]{3,2,1,0:T(8,128)(2,1)} %blocks.11, bf16[32,64,256]{2,1,0:T(8,128)(2,1)} %interp.4, bf16[64,8,256]{2,1,0:T(8,128)(2,1)S(1)} %copy-done.5, ...), custom_call_target="tpu_custom_call" | custom-call | flops 4096 | bytes 4096 | tf_op jit(solution)/shard_map/pallas_call | solution.py:337
  8.6 0.3 shard_map.75.near
  8.9 0.7 %collective-permute-done.partner = bf16[32,8,128]{2,1,0:T(8,128)(2,1)S(1)} collective-permute-done((bf16[32,8,128]{2,1,0:T(8,128)(2,1)S(1)}, bf16[32,8,128]{2,1,0:T(8,128)(2,1)S(1)}, u32[]{:S(2)}, u32[]{:S(2)}) %collective-permute-start) | collective-permute-done | bytes 65568 | tf_op jit(solution)/shard_map/ppermute | solution.py:353
  9.6 0.4 shard_map.76.state
  9.9 1.3 %collective-permute-start.1 = (bf16[32,8,128]{2,1,0:T(8,128)(2,1)S(1)}, bf16[32,8,128]{2,1,0:T(8,128)(2,1)S(1)}, u32[]{:S(2)}, u32[]{:S(2)}) collective-permute-start(bf16[32,8,128]{2,1,0:T(8,128)(2,1)S(1)} %shard_map.76.state), channel_id=1, source_target_pairs={{0,4},{1,5},{2,6},{3,7},{4,0},{5,1},{6,2},{7,3},{8,12},{9,13},{10,... | collective-permute-start | bytes 196616 | tf_op jit(solution)/shard_map/ppermute | solution.py:353
  11.2 0.3 shard_map.77.rest_0_.near
  11.6 0.3 shard_map.79
  11.9 2.1 %collective-permute-done.2.partner = bf16[32,8,128]{2,1,0:T(8,128)(2,1)S(1)} collective-permute-done((bf16[32,8,128]{2,1,0:T(8,128)(2,1)S(1)}, bf16[32,8,128]{2,1,0:T(8,128)(2,1)S(1)}, u32[]{:S(2)}, u32[]{:S(2)}) %collective-permute-start.2) | collective-permute-done | bytes 65568 | tf_op jit(solution)/shard_map/ppermute | solution.py:353
  14.0 0.4 shard_map.80.rest_0_.state
  14.4 1.9 %collective-permute-start.4 = (bf16[32,8,128]{2,1,0:T(8,128)(2,1)S(1)}, bf16[32,8,128]{2,1,0:T(8,128)(2,1)S(1)}, u32[]{:S(2)}, u32[]{:S(2)}) collective-permute-start(bf16[32,8,128]{2,1,0:T(8,128)(2,1)S(1)} %shard_map.80.rest_0_.state), channel_id=1, source_target_pairs={{0,4},{1,5},{2,6},{3,7},{4,0},{5,1},{6,2},{7,3},{8,12},{9,13},{10,... | collective-permute-start | bytes 196616 | tf_op jit(solution)/shard_map/ppermute | solution.py:353
  16.3 0.3 shard_map.78
  16.6 0.3 shard_map.81.near
  17.0 0.4 shard_map.82.state
  17.3 1.6 %collective-permute-start.3 = (bf16[32,8,128]{2,1,0:T(8,128)(2,1)S(1)}, bf16[32,8,128]{2,1,0:T(8,128)(2,1)S(1)}, u32[]{:S(2)}, u32[]{:S(2)}) collective-permute-start(bf16[32,8,128]{2,1,0:T(8,128)(2,1)S(1)} %shard_map.82.state), channel_id=1, source_target_pairs={{0,2},{1,3},{2,0},{3,1},{4,6},{5,7},{6,4},{7,5},{8,10},{9,11},{10,... | collective-permute-start | bytes 196616 | tf_op jit(solution)/shard_map/ppermute | solution.py:353
  18.9 0.3 shard_map.83.near
  19.3 0.4 shard_map.84.rest_0_.state
  19.7 0.3 shard_map.86.shared
  19.9 0.4 shard_map.85.near
  20.3 1.4 %collective-permute-done.3.partner = bf16[32,8,128]{2,1,0:T(8,128)(2,1)S(1)} collective-permute-done((bf16[32,8,128]{2,1,0:T(8,128)(2,1)S(1)}, bf16[32,8,128]{2,1,0:T(8,128)(2,1)S(1)}, u32[]{:S(2)}, u32[]{:S(2)}) %collective-permute-start.3) | collective-permute-done | bytes 65568 | tf_op jit(solution)/shard_map/ppermute | solution.py:353
  21.7 0.3 shard_map.87
  22.1 1.6 %collective-permute-start.6 = (bf16[32,8,128]{2,1,0:T(8,128)(2,1)S(1)}, bf16[32,8,128]{2,1,0:T(8,128)(2,1)S(1)}, u32[]{:S(2)}, u32[]{:S(2)}) collective-permute-start(bf16[32,8,128]{2,1,0:T(8,128)(2,1)S(1)} %shard_map.84.rest_0_.state), channel_id=1, source_target_pairs={{0,2},{1,3},{2,0},{3,1},{4,6},{5,7},{6,4},{7,5},{8,10},{9,11},{10,... | collective-permute-start | bytes 196616 | tf_op jit(solution)/shard_map/ppermute | solution.py:353
  23.7 0.3 shard_map.89.near
  24.0 0.8 %collective-permute-done.5.shared = bf16[68,64,128]{2,1,0:T(8,128)(2,1)S(1)} collective-permute-done((bf16[68,64,128]{2,1,0:T(8,128)(2,1)S(1)}, bf16[68,64,128]{2,1,0:T(8,128)(2,1)S(1)}, u32[]{:S(2)}, u32[]{:S(2)}) %collective-permute-start.5) | collective-permute-done | bytes 1114144 | tf_op jit(solution)/shard_map/ppermute | solution.py:353
  24.8 0.9 %shard_map.88 = (f32[2,32,8,128]{3,2,1,0:T(8,128)S(1)}, f32[2,1024,128]{2,1,0:T(8,128)S(1)}) custom-call(bf16[4,32,64,256]{3,2,1,0:T(8,128)(2,1)S(1)} %copy-done, s32[4,2,256]{2,1,0:T(2,128)S(1)} %copy-done.2, bf16[68,64,128]{2,1,0:T(8,128)(2,1)S(1)} %collective-permute-done.5.shared), custom_call_target="tpu_custom_call" | custom-call | flops 2048 | bytes 2048 | tf_op jit(solution)/shard_map/pallas_call | solution.py:337
  25.8 0.8 %collective-permute-done.6.partner = bf16[32,8,128]{2,1,0:T(8,128)(2,1)S(1)} collective-permute-done((bf16[32,8,128]{2,1,0:T(8,128)(2,1)S(1)}, bf16[32,8,128]{2,1,0:T(8,128)(2,1)S(1)}, u32[]{:S(2)}, u32[]{:S(2)}) %collective-permute-start.6) | collective-permute-done | bytes 65568 | tf_op jit(solution)/shard_map/ppermute | solution.py:353
  26.6 0.4 shard_map.90.state
  27.0 1.2 %shard_map.91 = (bf16[2,2,4,8,128]{4,3,2,1,0:T(8,128)(2,1)S(1)}, bf16[2,2,4,8,128]{4,3,2,1,0:T(8,128)(2,1)S(1)}, bf16[2,2,4,8,128]{4,3,2,1,0:T(8,128)(2,1)S(1)}, bf16[2,2,4,8,128]{4,3,2,1,0:T(8,128)(2,1)S(1)}) custom-call(s32[4,2,256]{2,1,0:T(2,128)S(1)} %copy-done.2, f32[2,1024,128]{2,1,0:T(8,128)S(1)} %get-tuple-element.54.wide, ...), custom_call_target="tpu_custom_call" | custom-call | flops 2048 | bytes 2048 | tf_op jit(solution)/shard_map/pallas_call | solution.py:337
  28.2 1.6 %collective-permute-start.8 = (bf16[2,2,4,8,128]{4,3,2,1,0:T(8,128)(2,1)S(1)}, bf16[2,2,4,8,128]{4,3,2,1,0:T(8,128)(2,1)S(1)}, u32[]{:S(2)}, u32[]{:S(2)}) collective-permute-start(bf16[2,2,4,8,128]{4,3,2,1,0:T(8,128)(2,1)S(1)} %get-tuple-element.61), channel_id=1, source_target_pairs={{0,2},{1,10},{2,0},{3,8},{4,6},{5,14},{6,4},{7,12},{8,3},{9,11},{1... | collective-permute-start | bytes 98312 | tf_op jit(solution)/shard_map/ppermute | solution.py:353
  29.8 0.1 collective-permute-start.9
  29.9 1.8 %collective-permute-start.10 = (bf16[2,2,4,8,128]{4,3,2,1,0:T(8,128)(2,1)S(1)}, bf16[2,2,4,8,128]{4,3,2,1,0:T(8,128)(2,1)S(1)}, u32[]{:S(2)}, u32[]{:S(2)}) collective-permute-start(bf16[2,2,4,8,128]{4,3,2,1,0:T(8,128)(2,1)S(1)} %get-tuple-element.63), channel_id=1, source_target_pairs={{0,6},{1,14},{2,4},{3,12},{4,2},{5,10},{6,0},{7,8},{8,7},{9,15},{1... | collective-permute-start | bytes 98312 | tf_op jit(solution)/shard_map/ppermute | solution.py:353
  31.8 0.7 %collective-permute-start.7 = (bf16[2,2,4,8,128]{4,3,2,1,0:T(8,128)(2,1)S(1)}, bf16[2,2,4,8,128]{4,3,2,1,0:T(8,128)(2,1)S(1)}, u32[]{:S(2)}, u32[]{:S(2)}) collective-permute-start(bf16[2,2,4,8,128]{4,3,2,1,0:T(8,128)(2,1)S(1)} %get-tuple-element.57.rest_0_.kept), channel_id=1, source_target_pairs={{1,8},{3,10},{5,12},{7,14},{8,1},{10,3},{12,5},{14,7},{17,24},{19,... | collective-permute-start | bytes 98312 | tf_op jit(solution)/shard_map/ppermute | solution.py:353
  32.4 0.3 shard_map.93
  32.7 0.3 shard_map.94
  33.0 0.3 shard_map.96
  33.3 0.3 shard_map.95
  33.7 0.3 shard_map.92
  34.0 0.8 %collective-permute-done.10.rest_3_ = bf16[2,2,4,8,128]{4,3,2,1,0:T(8,128)(2,1)S(1)} collective-permute-done((bf16[2,2,4,8,128]{4,3,2,1,0:T(8,128)(2,1)S(1)}, bf16[2,2,4,8,128]{4,3,2,1,0:T(8,128)(2,1)S(1)}, u32[]{:S(2)}, u32[]{:S(2)}) %collective-permute-start.10) | collective-permute-done | bytes 32800 | tf_op jit(solution)/shard_map/ppermute | solution.py:353
  34.8 1.0 %shard_map.97 = (bf16[32,8,128]{2,1,0:T(8,128)(2,1)S(1)}, bf16[2,32,8,128]{3,2,1,0:T(8,128)(2,1)S(1)}) custom-call(f32[2,1024,128]{2,1,0:T(8,128)S(1)} %get-tuple-element.60.wide, bf16[2,2,4,8,128]{4,3,2,1,0:T(8,128)(2,1)S(1)} %get-tuple-element.57.rest_0_.kept, bf16[2,2,4,8,128]{4,3,2,1,0:T(8,128)(2,1)S(1)} %collective-permute-done.7.rest_0_, ...), custom_call_target="tpu_custom_call" | custom-call | flops 2048 | bytes 2048 | tf_op jit(solution)/shard_map/pallas_call | solution.py:337
  35.8 4.7 %collective-permute-start.11 = (bf16[32,8,128]{2,1,0:T(8,128)(2,1)S(1)}, bf16[32,8,128]{2,1,0:T(8,128)(2,1)S(1)}, u32[]{:S(2)}, u32[]{:S(2)}) collective-permute-start(bf16[32,8,128]{2,1,0:T(8,128)(2,1)S(1)} %get-tuple-element.76), channel_id=1, source_target_pairs={{0,1},{1,0},{2,3},{3,2},{4,5},{5,4},{6,7},{7,6},{8,9},{9,8},{10,11... | collective-permute-start | bytes 196616 | tf_op jit(solution)/shard_map/ppermute | solution.py:353
  40.5 0.7 %shard_map.103.state = bf16[32,8,128]{2,1,0:T(8,128)(2,1)S(1)} custom-call(s32[4,2,256]{2,1,0:T(2,128)S(1)} %copy-done.3, f32[2,1024,128]{2,1,0:T(8,128)S(1)} %get-tuple-element.77.wide, bf16[2,32,8,128]{3,2,1,0:T(8,128)(2,1)S(1)} %get-tuple-element.78.states), custom_call_target="tpu_custom_call" | custom-call | flops 2048 | bytes 2048 | tf_op jit(solution)/shard_map/pallas_call | solution.py:337
  41.2 1.6 %collective-permute-start.15 = (bf16[32,8,128]{2,1,0:T(8,128)(2,1)S(1)}, bf16[32,8,128]{2,1,0:T(8,128)(2,1)S(1)}, u32[]{:S(2)}, u32[]{:S(2)}) collective-permute-start(bf16[32,8,128]{2,1,0:T(8,128)(2,1)S(1)} %shard_map.103.state), channel_id=1, source_target_pairs={{0,2},{1,3},{2,0},{3,1},{4,6},{5,7},{6,4},{7,5},{8,10},{9,11},{10,... | collective-permute-start | bytes 196616 | tf_op jit(solution)/shard_map/ppermute | solution.py:353
  42.8 0.5 collective-permute-start.12
  43.3 0.3 shard_map.104.near
  43.6 2.3 %collective-permute-done.15.partner = bf16[32,8,128]{2,1,0:T(8,128)(2,1)S(1)} collective-permute-done((bf16[32,8,128]{2,1,0:T(8,128)(2,1)S(1)}, bf16[32,8,128]{2,1,0:T(8,128)(2,1)S(1)}, u32[]{:S(2)}, u32[]{:S(2)}) %collective-permute-start.15) | collective-permute-done | bytes 65568 | tf_op jit(solution)/shard_map/ppermute | solution.py:353
  45.9 0.3 shard_map.105.state
  46.3 0.3 shard_map.98.near
  46.7 0.4 collective-permute-done.12.partner
  47.0 0.3 shard_map.99.state.rest_0_
  47.4 1.7 %collective-permute-start.13 = (bf16[32,8,128]{2,1,0:T(8,128)(2,1)S(1)}, bf16[32,8,128]{2,1,0:T(8,128)(2,1)S(1)}, u32[]{:S(2)}, u32[]{:S(2)}) collective-permute-start(bf16[32,8,128]{2,1,0:T(8,128)(2,1)S(1)} %shard_map.99.state.rest_0_), channel_id=1, source_target_pairs={{0,4},{1,5},{2,6},{3,7},{4,0},{5,1},{6,2},{7,3},{8,12},{9,13},{10,... | collective-permute-start | bytes 196616 | tf_op jit(solution)/shard_map/ppermute | solution.py:353
  49.1 0.3 shard_map.100.near
  49.4 0.3 shard_map.106.near
  49.8 0.8 %collective-permute-done.16.partner = bf16[32,8,128]{2,1,0:T(8,128)(2,1)S(1)} collective-permute-done((bf16[32,8,128]{2,1,0:T(8,128)(2,1)S(1)}, bf16[32,8,128]{2,1,0:T(8,128)(2,1)S(1)}, u32[]{:S(2)}, u32[]{:S(2)}) %collective-permute-start.16) | collective-permute-done | bytes 65568 | tf_op jit(solution)/shard_map/ppermute | solution.py:353
  50.6 0.3 shard_map.107.state
  50.9 0.2 collective-permute-start.17
  51.1 0.6 collective-permute-done.13.partner
  51.7 0.3 shard_map.101.state.rest_0_
  52.0 2.5 %collective-permute-start.14 = (bf16[32,8,128]{2,1,0:T(8,128)(2,1)S(1)}, bf16[32,8,128]{2,1,0:T(8,128)(2,1)S(1)}, u32[]{:S(2)}, u32[]{:S(2)}) collective-permute-start(bf16[32,8,128]{2,1,0:T(8,128)(2,1)S(1)} %shard_map.101.state.rest_0_), channel_id=1, source_target_pairs={{0,8},{1,9},{2,10},{3,11},{4,12},{5,13},{6,14},{7,15},{8,0},{9,1},... | collective-permute-start | bytes 196616 | tf_op jit(solution)/shard_map/ppermute | solution.py:353
  54.6 0.3 shard_map.102.near
  54.9 0.3 shard_map.108.near
  55.2 1.6 %collective-permute-done.17.partner = bf16[32,8,128]{2,1,0:T(8,128)(2,1)S(1)} collective-permute-done((bf16[32,8,128]{2,1,0:T(8,128)(2,1)S(1)}, bf16[32,8,128]{2,1,0:T(8,128)(2,1)S(1)}, u32[]{:S(2)}, u32[]{:S(2)}) %collective-permute-start.17) | collective-permute-done | bytes 65568 | tf_op jit(solution)/shard_map/ppermute | solution.py:353
  56.9 1.0 %shard_map.109.ready = bf16[64,8,128]{2,1,0:T(8,128)(2,1)S(1)} custom-call(s32[4,2,256]{2,1,0:T(2,128)S(1)} %copy-done.3, f32[1024,128]{1,0:T(8,128)S(1)} %get-tuple-element.74.rest_14_.wide, f32[2048,128]{1,0:T(8,128)S(1)} %get-tuple-element.75.rest_16_.image_wide, bf16[32,8,128]{2,1,0:T(8,128)(2,1)S(1)} %collective-permute-done.17.partner, ...), custom_call_target="tpu_custom_call" | custom-call | flops 3072 | bytes 3072 | tf_op jit(solution)/shard_map/pallas_call | solution.py:337
  57.9 1.7 %shard_map.110 = bf16[64,8,256]{2,1,0:T(8,128)(2,1)} custom-call(s32[4,2,256]{2,1,0:T(2,128)S(1)} %copy-done.3, f32[1024,128]{1,0:T(8,128)S(1)} %get-tuple-element.58.rest_15_.wide, f32[2048,128]{1,0:T(8,128)S(1)} %get-tuple-element.59.rest_17_.image_wide, bf16[32,8,128]{2,1,0:T(8,128)(2,1)S(1)} %collective-permute-done.14.partner, ...), custom_call_target="tpu_custom_call" | custom-call | flops 3072 | bytes 3072 | tf_op jit(solution)/shard_map/pallas_call | solution.py:337
  (22 shorter events, 0.3 us)
Async XLA Ops:
  0.0 5.9 %copy-start.5 = (bf16[64,8,256]{2,1,0:T(8,128)(2,1)S(1)}, bf16[64,8,256]{2,1,0:T(8,128)(2,1)}, u32[]{:S(2)}) copy-start(bf16[64,8,256]{2,1,0:T(8,128)(2,1)} %samples.3) | copy-start | bytes 786436
  1.8 6.8 %copy-start.2 = (s32[4,2,256]{2,1,0:T(2,128)S(1)}, s32[4,2,256]{2,1,0:T(2,128)}, u32[]{:S(2)}) copy-start(s32[4,2,256]{2,1,0:T(2,128)} %pattern.40) | copy-start | bytes 24580
  1.8 7.8 %collective-permute-start = (bf16[32,8,128]{2,1,0:T(8,128)(2,1)S(1)}, bf16[32,8,128]{2,1,0:T(8,128)(2,1)S(1)}, u32[]{:S(2)}, u32[]{:S(2)}) collective-permute-start(bf16[32,8,128]{2,1,0:T(8,128)(2,1)S(1)} %shard_map.73.after.state), channel_id=1, source_target_pairs={{0,8},{1,9},{2,10},{3,11},{4,12},{5,13},{6,14},{7,15},{8,0},{9,1},... | collective-permute-start | bytes 196616 | tf_op jit(solution)/shard_map/ppermute | solution.py:353
  5.9 5.7 %copy-start = (bf16[4,32,64,256]{3,2,1,0:T(8,128)(2,1)S(1)}, bf16[4,32,64,256]{3,2,1,0:T(8,128)(2,1)}, u32[]{:S(2)}) copy-start(bf16[4,32,64,256]{3,2,1,0:T(8,128)(2,1)} %blocks.11) | copy-start | bytes 12582916
  8.5 5.6 %collective-permute-start.2 = (bf16[32,8,128]{2,1,0:T(8,128)(2,1)S(1)}, bf16[32,8,128]{2,1,0:T(8,128)(2,1)S(1)}, u32[]{:S(2)}, u32[]{:S(2)}) collective-permute-start(bf16[32,8,128]{2,1,0:T(8,128)(2,1)S(1)} %get-tuple-element.44.state), channel_id=1, source_target_pairs={{0,8},{1,9},{2,10},{3,11},{4,12},{5,13},{6,14},{7,15},{8,0},{9,1},... | collective-permute-start | bytes 196616 | tf_op jit(solution)/shard_map/ppermute | solution.py:353
  9.9 7.0 %collective-permute-start.1 = (bf16[32,8,128]{2,1,0:T(8,128)(2,1)S(1)}, bf16[32,8,128]{2,1,0:T(8,128)(2,1)S(1)}, u32[]{:S(2)}, u32[]{:S(2)}) collective-permute-start(bf16[32,8,128]{2,1,0:T(8,128)(2,1)S(1)} %shard_map.76.state), channel_id=1, source_target_pairs={{0,4},{1,5},{2,6},{3,7},{4,0},{5,1},{6,2},{7,3},{8,12},{9,13},{10,... | collective-permute-start | bytes 196616 | tf_op jit(solution)/shard_map/ppermute | solution.py:353
  14.4 4.9 %collective-permute-start.4 = (bf16[32,8,128]{2,1,0:T(8,128)(2,1)S(1)}, bf16[32,8,128]{2,1,0:T(8,128)(2,1)S(1)}, u32[]{:S(2)}, u32[]{:S(2)}) collective-permute-start(bf16[32,8,128]{2,1,0:T(8,128)(2,1)S(1)} %shard_map.80.rest_0_.state), channel_id=1, source_target_pairs={{0,4},{1,5},{2,6},{3,7},{4,0},{5,1},{6,2},{7,3},{8,12},{9,13},{10,... | collective-permute-start | bytes 196616 | tf_op jit(solution)/shard_map/ppermute | solution.py:353
  16.3 3.3 %copy-start.1 = (bf16[4,32,64,256]{3,2,1,0:T(8,128)(2,1)S(1)}, bf16[4,32,64,256]{3,2,1,0:T(8,128)(2,1)}, u32[]{:S(2)}) copy-start(bf16[4,32,64,256]{3,2,1,0:T(8,128)(2,1)} %blocks.15) | copy-start | bytes 12582916
  17.0 2.7 %copy-start.3 = (s32[4,2,256]{2,1,0:T(2,128)S(1)}, s32[4,2,256]{2,1,0:T(2,128)}, u32[]{:S(2)}) copy-start(s32[4,2,256]{2,1,0:T(2,128)} %pattern.53) | copy-start | bytes 24580
  17.3 4.3 %collective-permute-start.3 = (bf16[32,8,128]{2,1,0:T(8,128)(2,1)S(1)}, bf16[32,8,128]{2,1,0:T(8,128)(2,1)S(1)}, u32[]{:S(2)}, u32[]{:S(2)}) collective-permute-start(bf16[32,8,128]{2,1,0:T(8,128)(2,1)S(1)} %shard_map.82.state), channel_id=1, source_target_pairs={{0,2},{1,3},{2,0},{3,1},{4,6},{5,7},{6,4},{7,5},{8,10},{9,11},{10,... | collective-permute-start | bytes 196616 | tf_op jit(solution)/shard_map/ppermute | solution.py:353
  22.0 2.8 %collective-permute-start.5 = (bf16[68,64,128]{2,1,0:T(8,128)(2,1)S(1)}, bf16[68,64,128]{2,1,0:T(8,128)(2,1)S(1)}, u32[]{:S(2)}, u32[]{:S(2)}) collective-permute-start(bf16[68,64,128]{2,1,0:T(8,128)(2,1)S(1)} %shard_map.87), channel_id=1, source_target_pairs={{0,1},{1,0},{2,3},{3,2},{4,5},{5,4},{6,7},{7,6},{8,9},{9,8},{10,11... | collective-permute-start | bytes 3342344 | tf_op jit(solution)/shard_map/ppermute | solution.py:353
  22.1 4.5 %collective-permute-start.6 = (bf16[32,8,128]{2,1,0:T(8,128)(2,1)S(1)}, bf16[32,8,128]{2,1,0:T(8,128)(2,1)S(1)}, u32[]{:S(2)}, u32[]{:S(2)}) collective-permute-start(bf16[32,8,128]{2,1,0:T(8,128)(2,1)S(1)} %shard_map.84.rest_0_.state), channel_id=1, source_target_pairs={{0,2},{1,3},{2,0},{3,1},{4,6},{5,7},{6,4},{7,5},{8,10},{9,11},{10,... | collective-permute-start | bytes 196616 | tf_op jit(solution)/shard_map/ppermute | solution.py:353
  26.6 5.8 %copy-start.4 = (bf16[64,32,256]{2,1,0:T(8,128)(2,1)S(1)}, bf16[64,32,256]{2,1,0:T(8,128)(2,1)}, u32[]{:S(2)}) copy-start(bf16[64,32,256]{2,1,0:T(8,128)(2,1)} %interp.5) | copy-start | bytes 3145732
  28.2 5.8 %collective-permute-start.8 = (bf16[2,2,4,8,128]{4,3,2,1,0:T(8,128)(2,1)S(1)}, bf16[2,2,4,8,128]{4,3,2,1,0:T(8,128)(2,1)S(1)}, u32[]{:S(2)}, u32[]{:S(2)}) collective-permute-start(bf16[2,2,4,8,128]{4,3,2,1,0:T(8,128)(2,1)S(1)} %get-tuple-element.61), channel_id=1, source_target_pairs={{0,2},{1,10},{2,0},{3,8},{4,6},{5,14},{6,4},{7,12},{8,3},{9,11},{1... | collective-permute-start | bytes 98312 | tf_op jit(solution)/shard_map/ppermute | solution.py:353
  29.8 4.2 %collective-permute-start.9 = (bf16[2,2,4,8,128]{4,3,2,1,0:T(8,128)(2,1)S(1)}, bf16[2,2,4,8,128]{4,3,2,1,0:T(8,128)(2,1)S(1)}, u32[]{:S(2)}, u32[]{:S(2)}) collective-permute-start(bf16[2,2,4,8,128]{4,3,2,1,0:T(8,128)(2,1)S(1)} %get-tuple-element.62), channel_id=1, source_target_pairs={{0,4},{1,12},{2,6},{3,14},{4,0},{5,8},{6,2},{7,10},{8,5},{9,13},{1... | collective-permute-start | bytes 98312 | tf_op jit(solution)/shard_map/ppermute | solution.py:353
  29.9 4.8 %collective-permute-start.10 = (bf16[2,2,4,8,128]{4,3,2,1,0:T(8,128)(2,1)S(1)}, bf16[2,2,4,8,128]{4,3,2,1,0:T(8,128)(2,1)S(1)}, u32[]{:S(2)}, u32[]{:S(2)}) collective-permute-start(bf16[2,2,4,8,128]{4,3,2,1,0:T(8,128)(2,1)S(1)} %get-tuple-element.63), channel_id=1, source_target_pairs={{0,6},{1,14},{2,4},{3,12},{4,2},{5,10},{6,0},{7,8},{8,7},{9,15},{1... | collective-permute-start | bytes 98312 | tf_op jit(solution)/shard_map/ppermute | solution.py:353
  31.8 3.0 %collective-permute-start.7 = (bf16[2,2,4,8,128]{4,3,2,1,0:T(8,128)(2,1)S(1)}, bf16[2,2,4,8,128]{4,3,2,1,0:T(8,128)(2,1)S(1)}, u32[]{:S(2)}, u32[]{:S(2)}) collective-permute-start(bf16[2,2,4,8,128]{4,3,2,1,0:T(8,128)(2,1)S(1)} %get-tuple-element.57.rest_0_.kept), channel_id=1, source_target_pairs={{1,8},{3,10},{5,12},{7,14},{8,1},{10,3},{12,5},{14,7},{17,24},{19,... | collective-permute-start | bytes 98312 | tf_op jit(solution)/shard_map/ppermute | solution.py:353
  35.8 6.9 %collective-permute-start.11 = (bf16[32,8,128]{2,1,0:T(8,128)(2,1)S(1)}, bf16[32,8,128]{2,1,0:T(8,128)(2,1)S(1)}, u32[]{:S(2)}, u32[]{:S(2)}) collective-permute-start(bf16[32,8,128]{2,1,0:T(8,128)(2,1)S(1)} %get-tuple-element.76), channel_id=1, source_target_pairs={{0,1},{1,0},{2,3},{3,2},{4,5},{5,4},{6,7},{7,6},{8,9},{9,8},{10,11... | collective-permute-start | bytes 196616 | tf_op jit(solution)/shard_map/ppermute | solution.py:353
  41.2 4.7 %collective-permute-start.15 = (bf16[32,8,128]{2,1,0:T(8,128)(2,1)S(1)}, bf16[32,8,128]{2,1,0:T(8,128)(2,1)S(1)}, u32[]{:S(2)}, u32[]{:S(2)}) collective-permute-start(bf16[32,8,128]{2,1,0:T(8,128)(2,1)S(1)} %shard_map.103.state), channel_id=1, source_target_pairs={{0,2},{1,3},{2,0},{3,1},{4,6},{5,7},{6,4},{7,5},{8,10},{9,11},{10,... | collective-permute-start | bytes 196616 | tf_op jit(solution)/shard_map/ppermute | solution.py:353
  42.8 4.3 %collective-permute-start.12 = (bf16[32,8,128]{2,1,0:T(8,128)(2,1)S(1)}, bf16[32,8,128]{2,1,0:T(8,128)(2,1)S(1)}, u32[]{:S(2)}, u32[]{:S(2)}) collective-permute-start(bf16[32,8,128]{2,1,0:T(8,128)(2,1)S(1)} %collective-permute-done.11.state.rest_0_), channel_id=1, source_target_pairs={{0,2},{1,3},{2,0},{3,1},{4,6},{5,7},{6,4},{7,5},{8,10},{9,11},{10,... | collective-permute-start | bytes 196616 | tf_op jit(solution)/shard_map/ppermute | solution.py:353
  46.2 4.3 %collective-permute-start.16 = (bf16[32,8,128]{2,1,0:T(8,128)(2,1)S(1)}, bf16[32,8,128]{2,1,0:T(8,128)(2,1)S(1)}, u32[]{:S(2)}, u32[]{:S(2)}) collective-permute-start(bf16[32,8,128]{2,1,0:T(8,128)(2,1)S(1)} %shard_map.105.state), channel_id=1, source_target_pairs={{0,4},{1,5},{2,6},{3,7},{4,0},{5,1},{6,2},{7,3},{8,12},{9,13},{10,... | collective-permute-start | bytes 196616 | tf_op jit(solution)/shard_map/ppermute | solution.py:353
  47.4 4.3 %collective-permute-start.13 = (bf16[32,8,128]{2,1,0:T(8,128)(2,1)S(1)}, bf16[32,8,128]{2,1,0:T(8,128)(2,1)S(1)}, u32[]{:S(2)}, u32[]{:S(2)}) collective-permute-start(bf16[32,8,128]{2,1,0:T(8,128)(2,1)S(1)} %shard_map.99.state.rest_0_), channel_id=1, source_target_pairs={{0,4},{1,5},{2,6},{3,7},{4,0},{5,1},{6,2},{7,3},{8,12},{9,13},{10,... | collective-permute-start | bytes 196616 | tf_op jit(solution)/shard_map/ppermute | solution.py:353
  50.9 5.9 %collective-permute-start.17 = (bf16[32,8,128]{2,1,0:T(8,128)(2,1)S(1)}, bf16[32,8,128]{2,1,0:T(8,128)(2,1)S(1)}, u32[]{:S(2)}, u32[]{:S(2)}) collective-permute-start(bf16[32,8,128]{2,1,0:T(8,128)(2,1)S(1)} %shard_map.107.state), channel_id=1, source_target_pairs={{0,8},{1,9},{2,10},{3,11},{4,12},{5,13},{6,14},{7,15},{8,0},{9,1},... | collective-permute-start | bytes 196616 | tf_op jit(solution)/shard_map/ppermute | solution.py:353
  52.0 5.8 %collective-permute-start.14 = (bf16[32,8,128]{2,1,0:T(8,128)(2,1)S(1)}, bf16[32,8,128]{2,1,0:T(8,128)(2,1)S(1)}, u32[]{:S(2)}, u32[]{:S(2)}) collective-permute-start(bf16[32,8,128]{2,1,0:T(8,128)(2,1)S(1)} %shard_map.101.state.rest_0_), channel_id=1, source_target_pairs={{0,8},{1,9},{2,10},{3,11},{4,12},{5,13},{6,14},{7,15},{8,0},{9,1},... | collective-permute-start | bytes 196616 | tf_op jit(solution)/shard_map/ppermute | solution.py:353

commit v12 on v11

--- a/solution.py
+++ b/solution.py
@@ -10,7 +10,7 @@
 LANES = 128
 GROUP = 4
 ROWS = 8
-KERNEL_COST = 1024
+KERNEL_COST = 2**19
 KERNEL_LIMIT = 16 * 2**20
 FETCH_LIMIT = 53_850_000
 START_LIMIT = 56_250_000
@@ -96,13 +96,12 @@
         multiply(wide, state, rank, emit)
 
 
-def second_kernel(level, bit, flip, blocks, interp, samples, after, *rest):
-    held, sem = rest[-2:]
-    copy = pltpu.make_async_copy(blocks.at[pl.ds(level, 1)], held, sem)
+def second_kernel(flip, blocks, interp, samples, after, out, held, *rest):
+    sem = rest[-1]
+    copy = pltpu.make_async_copy(blocks.at[pl.ds(0, 1)], held, sem)
     copy.start()
-    coeff_kernel(flip, interp, samples, rest[0], *rest[5:-2])
+    coeff_kernel(flip, interp, samples, out, *rest[:-1])
     copy.wait()
-    ahead_kernel(0, bit, held, *rest[1:5])
 
 
 def ahead_kernel(level, bit, blocks, *rest):
@@ -181,7 +180,8 @@
 
 
 def swap_groups(tile, slot):
-    lane_group = lax.broadcasted_iota(jnp.int32, tile[0].shape, 2) // slot
+    axis = tile[0].ndim - 1
+    lane_group = lax.broadcasted_iota(jnp.int32, tile[0].shape, axis) // slot
     step = 1
     while step < len(tile):
         low = (lane_group // step) % 2 == 0
@@ -189,8 +189,8 @@
         for place in range(len(tile)):
             if place & step == 0:
                 first, second = tile[place], tile[place + step]
-                fresh[place] = jnp.where(low, first, pltpu.roll(second, step * slot, 2))
-                fresh[place + step] = jnp.where(low, pltpu.roll(first, LANES - step * slot, 2), second)
+                fresh[place] = jnp.where(low, first, pltpu.roll(second, step * slot, axis))
+                fresh[place + step] = jnp.where(low, pltpu.roll(first, LANES - step * slot, axis), second)
         tile = fresh
         step *= 2
     return tile
@@ -225,7 +225,9 @@
 
         multiply(wide.at[box], [row * present for row in rows] if box == 0 else rows, rank, emit)
         depth = rank // fold
-        pieces = swap_groups([total[place * depth:(place + 1) * depth].astype(jnp.bfloat16) for place in range(fold)], slot)
+        rows_of_piece = depth * total.shape[1]
+        flat = total[...].reshape(fold, rows_of_piece, LANES).astype(jnp.bfloat16)
+        pieces = swap_groups([flat[place] for place in range(fold)], slot)
         for place, piece in enumerate(pieces):
             packed[core ^ box, place] = piece
     for turn, out in enumerate(outs):
@@ -275,7 +277,8 @@
     for last in range(2):
         tile = swap_groups([packed[last, place] for place in range(fold)], slot)
         for place, rows in enumerate(tile):
-            states[last, place * depth:(place + 1) * depth] = rows
+            rows = rows.astype(jnp.float32).reshape(depth, states.shape[2], LANES)
+            states[last, place * depth:(place + 1) * depth] = rows.astype(jnp.bfloat16)
     pair_box(wide, total, states, (None, None), out)
 
 
@@ -374,7 +377,7 @@
     pair_spread = jax.ShapeDtypeStruct((2, rank * rank, LANES), jnp.float32)
     total = pltpu.VMEM((rank, rhs_count, LANES), jnp.float32)
     wide = pltpu.VMEM((rank * rank, LANES), jnp.float32)
-    packed = pltpu.VMEM((2, fold, rank // fold, rhs_count, LANES), jnp.bfloat16)
+    packed = pltpu.VMEM((2, fold, rank // fold * rhs_count, LANES), jnp.bfloat16)
 
     def level_wides(blocks, level, bit, *after):
         wides = run(functools.partial(ahead_kernel, level, bit), [spread_out] * 4, (blocks, *after), products=4)
@@ -413,13 +416,13 @@
         bit = 3 - level
         if level == 0:
             partner = {1: swapped(current[1], bit)}
-            current[0], *wides = run(
-                functools.partial(second_kernel, 0, 3, 0), [state] + [spread_out] * 4,
-                (top_blocks, interp_in, samples, current[1]),
-                coeff_scratch + (pltpu.VMEM((1, *top_blocks.shape[1:]), jnp.bfloat16), pltpu.SemaphoreType.DMA), 4,
+            current[0], first_blocks = run(
+                functools.partial(second_kernel, 0),
+                [state, jax.ShapeDtypeStruct((1, *top_blocks.shape[1:]), jnp.bfloat16)],
+                (top_blocks, interp_in, samples, current[1]), coeff_scratch + (pltpu.SemaphoreType.DMA,), 4,
                 in_specs=[pl.BlockSpec(memory_space=pl.ANY)] * 4, limit=FETCH_LIMIT,
             )
-            wides = wides[:2], wides[2:]
+            wides = level_wides(first_blocks, 0, bit)
             partner[0] = swapped(current[0], bit)
             near = level_nears(top_pattern, level, bit, (1,), wides)
             near.update(level_nears(top_pattern, level, bit, (0,), wides))
@@ -446,7 +449,7 @@
     )
     current = level_fars(top_pattern, 2, 1, (0,), wides, (pair_far,))
 
-    piece = jax.ShapeDtypeStruct((2, 2, rank // fold, rhs_count, LANES), jnp.bfloat16)
+    piece = jax.ShapeDtypeStruct((2, 2, rank // fold * rhs_count, LANES), jnp.bfloat16)
     pieces = run(
         functools.partial(pair_near_kernel, 3, slot), [piece] * 4,
         (top_pattern, near_wide, current[0], pair_far), (total, packed), 2,

time: 59.7 us -> 60.7 us (1.017)
  starting transfers between devices: 26.2 us -> 28 us
  Pallas kernels: 20.8 us -> 19.8 us
    ppermute x18, starting transfers between devices: 26.2 us -> 28 us  [permuted(): return lax.ppermute(value, 'leaf', pairs)]
    pallas_call x38 -> x39, Pallas kernels: 20.8 us -> 19.8 us  [run(): pl.pallas_call(kernel, out_shape=shapes, in_specs=in_specs or [whole] * l...]
  transfers between devices with their start and end apart: 18 -> 18, of which waited for: 11 -> 10; matrix products, arithmetic and copies ran while one was open for 0% -> 0% of each run, Pallas kernels for 24% -> 22%
where the time goes in v12:
time: 60.7 us; the launch traced here: 60.5 us
  starting transfers between devices  28 us (46%)
  Pallas kernels  19.8 us (33%)
  waiting for transfers between devices  12.4 us (20%)
    ppermute x18, starting transfers between devices, permuted(): return lax.ppermute(value, 'leaf', pairs)  28 us
    pallas_call x39, Pallas kernels, run(): pl.pallas_call(kernel, out_shape=shapes, in_specs=in_specs or [whole] * l...  19.8 us
    ppermute x18, waiting for transfers between devices, permuted(): return lax.ppermute(value, 'leaf', pairs)  12.4 us
  transfers between devices with their start and end apart: 18, of which 10 were waited for; matrix products, arithmetic and copies ran while one was open for 0% of the time, Pallas kernels for 22%

profile of v12, /device:TPU:0, one launch (start us, length us, event | category | flops | bytes accessed | tf_op | source)
XLA Modules:
  0.0 60.5 jit_solution(17094870015831531216)
XLA Ops:
  0.0 1.8 %shard_map.73.after.state = bf16[32,8,128]{2,1,0:T(8,128)(2,1)S(1)} custom-call(bf16[32,64,256]{2,1,0:T(8,128)(2,1)} %interp.4, bf16[64,8,256]{2,1,0:T(8,128)(2,1)} %samples.3), custom_call_target="tpu_custom_call" | custom-call | flops 1048576 | bytes 1048576 | tf_op jit(solution)/shard_map/pallas_call | solution.py:340
  1.9 4.1 %collective-permute-start = (bf16[32,8,128]{2,1,0:T(8,128)(2,1)S(1)}, bf16[32,8,128]{2,1,0:T(8,128)(2,1)S(1)}, u32[]{:S(2)}, u32[]{:S(2)}) collective-permute-start(bf16[32,8,128]{2,1,0:T(8,128)(2,1)S(1)} %shard_map.73.after.state), channel_id=1, source_target_pairs={{0,8},{1,9},{2,10},{3,11},{4,12},{5,13},{6,14},{7,15},{8,0},{9,1},... | collective-permute-start | bytes 196616 | tf_op jit(solution)/shard_map/ppermute | solution.py:356
  6.0 1.4 %shard_map.74 = (bf16[32,8,128]{2,1,0:T(8,128)(2,1)S(1)}, bf16[1,32,64,256]{3,2,1,0:T(8,128)(2,1)S(1)}) custom-call(bf16[4,32,64,256]{3,2,1,0:T(8,128)(2,1)} %blocks.11, bf16[32,64,256]{2,1,0:T(8,128)(2,1)S(1)} %copy-done.2, bf16[64,8,256]{2,1,0:T(8,128)(2,1)S(1)} %copy-done.6, bf16[32,8,128]{2,1,0:T(8,128)(2,1)S(1)} %shard_map.73.after.state), custom_call_target="tpu_custom_call" | custom-call | flops 2097152 | bytes 2097152 | tf_op jit(solution)/shard_map/pallas_call | solution.py:340
  7.4 0.1 collective-permute-start.2
  7.5 0.3 shard_map.75
  7.8 0.3 shard_map.76.near
  8.2 1.5 %collective-permute-done.partner = bf16[32,8,128]{2,1,0:T(8,128)(2,1)S(1)} collective-permute-done((bf16[32,8,128]{2,1,0:T(8,128)(2,1)S(1)}, bf16[32,8,128]{2,1,0:T(8,128)(2,1)S(1)}, u32[]{:S(2)}, u32[]{:S(2)}) %collective-permute-start) | collective-permute-done | bytes 65568 | tf_op jit(solution)/shard_map/ppermute | solution.py:356
  9.6 0.4 shard_map.77.state
  10.0 2.5 %collective-permute-start.1 = (bf16[32,8,128]{2,1,0:T(8,128)(2,1)S(1)}, bf16[32,8,128]{2,1,0:T(8,128)(2,1)S(1)}, u32[]{:S(2)}, u32[]{:S(2)}) collective-permute-start(bf16[32,8,128]{2,1,0:T(8,128)(2,1)S(1)} %shard_map.77.state), channel_id=1, source_target_pairs={{0,4},{1,5},{2,6},{3,7},{4,0},{5,1},{6,2},{7,3},{8,12},{9,13},{10,... | collective-permute-start | bytes 196616 | tf_op jit(solution)/shard_map/ppermute | solution.py:356
  12.5 0.3 shard_map.78.rest_0_.near
  12.8 0.3 shard_map.80
  13.2 0.3 shard_map.79
  13.5 0.4 shard_map.81.rest_0_.state
  13.9 0.8 %collective-permute-start.4 = (bf16[32,8,128]{2,1,0:T(8,128)(2,1)S(1)}, bf16[32,8,128]{2,1,0:T(8,128)(2,1)S(1)}, u32[]{:S(2)}, u32[]{:S(2)}) collective-permute-start(bf16[32,8,128]{2,1,0:T(8,128)(2,1)S(1)} %shard_map.81.rest_0_.state), channel_id=1, source_target_pairs={{0,4},{1,5},{2,6},{3,7},{4,0},{5,1},{6,2},{7,3},{8,12},{9,13},{10,... | collective-permute-start | bytes 196616 | tf_op jit(solution)/shard_map/ppermute | solution.py:356
  14.6 0.3 shard_map.82.near
  15.0 0.4 shard_map.83.state
  15.3 1.6 %collective-permute-start.3 = (bf16[32,8,128]{2,1,0:T(8,128)(2,1)S(1)}, bf16[32,8,128]{2,1,0:T(8,128)(2,1)S(1)}, u32[]{:S(2)}, u32[]{:S(2)}) collective-permute-start(bf16[32,8,128]{2,1,0:T(8,128)(2,1)S(1)} %shard_map.83.state), channel_id=1, source_target_pairs={{0,2},{1,3},{2,0},{3,1},{4,6},{5,7},{6,4},{7,5},{8,10},{9,11},{10,... | collective-permute-start | bytes 196616 | tf_op jit(solution)/shard_map/ppermute | solution.py:356
  16.9 0.2 shard_map.87.shared
  17.2 0.4 shard_map.84.near
  17.5 0.7 %collective-permute-done.4.partner = bf16[32,8,128]{2,1,0:T(8,128)(2,1)S(1)} collective-permute-done((bf16[32,8,128]{2,1,0:T(8,128)(2,1)S(1)}, bf16[32,8,128]{2,1,0:T(8,128)(2,1)S(1)}, u32[]{:S(2)}, u32[]{:S(2)}) %collective-permute-start.4) | collective-permute-done | bytes 65568 | tf_op jit(solution)/shard_map/ppermute | solution.py:356
  18.2 0.3 shard_map.85.rest_0_.state
  18.6 0.4 shard_map.86.near
  18.9 0.7 %collective-permute-done.3.partner = bf16[32,8,128]{2,1,0:T(8,128)(2,1)S(1)} collective-permute-done((bf16[32,8,128]{2,1,0:T(8,128)(2,1)S(1)}, bf16[32,8,128]{2,1,0:T(8,128)(2,1)S(1)}, u32[]{:S(2)}, u32[]{:S(2)}) %collective-permute-start.3) | collective-permute-done | bytes 65568 | tf_op jit(solution)/shard_map/ppermute | solution.py:356
  19.7 0.3 shard_map.88
  20.1 1.6 %collective-permute-start.6 = (bf16[32,8,128]{2,1,0:T(8,128)(2,1)S(1)}, bf16[32,8,128]{2,1,0:T(8,128)(2,1)S(1)}, u32[]{:S(2)}, u32[]{:S(2)}) collective-permute-start(bf16[32,8,128]{2,1,0:T(8,128)(2,1)S(1)} %shard_map.85.rest_0_.state), channel_id=1, source_target_pairs={{0,2},{1,3},{2,0},{3,1},{4,6},{5,7},{6,4},{7,5},{8,10},{9,11},{10,... | collective-permute-start | bytes 196616 | tf_op jit(solution)/shard_map/ppermute | solution.py:356
  21.7 0.3 shard_map.90.near
  22.0 0.8 %collective-permute-done.5.shared = bf16[68,64,128]{2,1,0:T(8,128)(2,1)S(1)} collective-permute-done((bf16[68,64,128]{2,1,0:T(8,128)(2,1)S(1)}, bf16[68,64,128]{2,1,0:T(8,128)(2,1)S(1)}, u32[]{:S(2)}, u32[]{:S(2)}) %collective-permute-start.5) | collective-permute-done | bytes 1114144 | tf_op jit(solution)/shard_map/ppermute | solution.py:356
  22.8 0.9 %shard_map.89 = (f32[2,32,8,128]{3,2,1,0:T(8,128)S(1)}, f32[2,1024,128]{2,1,0:T(8,128)S(1)}) custom-call(bf16[4,32,64,256]{3,2,1,0:T(8,128)(2,1)S(1)} %copy-done, s32[4,2,256]{2,1,0:T(2,128)S(1)} %copy-done.3, bf16[68,64,128]{2,1,0:T(8,128)(2,1)S(1)} %collective-permute-done.5.shared), custom_call_target="tpu_custom_call" | custom-call | flops 1048576 | bytes 1048576 | tf_op jit(solution)/shard_map/pallas_call | solution.py:340
  23.8 0.8 %collective-permute-done.6.partner = bf16[32,8,128]{2,1,0:T(8,128)(2,1)S(1)} collective-permute-done((bf16[32,8,128]{2,1,0:T(8,128)(2,1)S(1)}, bf16[32,8,128]{2,1,0:T(8,128)(2,1)S(1)}, u32[]{:S(2)}, u32[]{:S(2)}) %collective-permute-start.6) | collective-permute-done | bytes 65568 | tf_op jit(solution)/shard_map/ppermute | solution.py:356
  24.6 0.3 shard_map.91.state
  24.9 1.2 %shard_map.92 = (bf16[2,2,32,128]{3,2,1,0:T(8,128)(2,1)S(1)}, bf16[2,2,32,128]{3,2,1,0:T(8,128)(2,1)S(1)}, bf16[2,2,32,128]{3,2,1,0:T(8,128)(2,1)S(1)}, bf16[2,2,32,128]{3,2,1,0:T(8,128)(2,1)S(1)}) custom-call(s32[4,2,256]{2,1,0:T(2,128)S(1)} %copy-done.3, f32[2,1024,128]{2,1,0:T(8,128)S(1)} %get-tuple-element.56.wide, ...), custom_call_target="tpu_custom_call" | custom-call | flops 1048576 | bytes 1048576 | tf_op jit(solution)/shard_map/pallas_call | solution.py:340
  26.1 1.6 %collective-permute-start.8 = (bf16[2,2,32,128]{3,2,1,0:T(8,128)(2,1)S(1)}, bf16[2,2,32,128]{3,2,1,0:T(8,128)(2,1)S(1)}, u32[]{:S(2)}, u32[]{:S(2)}) collective-permute-start(bf16[2,2,32,128]{3,2,1,0:T(8,128)(2,1)S(1)} %get-tuple-element.63), channel_id=1, source_target_pairs={{0,2},{1,10},{2,0},{3,8},{4,6},{5,14},{6,4},{7,12},{8,3},{9,11},{1... | collective-permute-start | bytes 98312 | tf_op jit(solution)/shard_map/ppermute | solution.py:356
  27.7 2.1 %collective-permute-start.9 = (bf16[2,2,32,128]{3,2,1,0:T(8,128)(2,1)S(1)}, bf16[2,2,32,128]{3,2,1,0:T(8,128)(2,1)S(1)}, u32[]{:S(2)}, u32[]{:S(2)}) collective-permute-start(bf16[2,2,32,128]{3,2,1,0:T(8,128)(2,1)S(1)} %get-tuple-element.64), channel_id=1, source_target_pairs={{0,4},{1,12},{2,6},{3,14},{4,0},{5,8},{6,2},{7,10},{8,5},{9,13},{1... | collective-permute-start | bytes 98312 | tf_op jit(solution)/shard_map/ppermute | solution.py:356
  29.8 0.7 %collective-permute-start.7 = (bf16[2,2,32,128]{3,2,1,0:T(8,128)(2,1)S(1)}, bf16[2,2,32,128]{3,2,1,0:T(8,128)(2,1)S(1)}, u32[]{:S(2)}, u32[]{:S(2)}) collective-permute-start(bf16[2,2,32,128]{3,2,1,0:T(8,128)(2,1)S(1)} %get-tuple-element.59.rest_0_.kept), channel_id=1, source_target_pairs={{1,8},{3,10},{5,12},{7,14},{8,1},{10,3},{12,5},{14,7},{17,24},{19,... | collective-permute-start | bytes 98312 | tf_op jit(solution)/shard_map/ppermute | solution.py:356
  30.5 0.3 shard_map.94
  30.8 0.3 shard_map.95
  31.0 0.3 shard_map.97
  31.4 0.3 shard_map.96
  31.7 0.3 shard_map.93
  32.0 2.6 %collective-permute-done.10.rest_3_ = bf16[2,2,32,128]{3,2,1,0:T(8,128)(2,1)S(1)} collective-permute-done((bf16[2,2,32,128]{3,2,1,0:T(8,128)(2,1)S(1)}, bf16[2,2,32,128]{3,2,1,0:T(8,128)(2,1)S(1)}, u32[]{:S(2)}, u32[]{:S(2)}) %collective-permute-start.10) | collective-permute-done | bytes 32800 | tf_op jit(solution)/shard_map/ppermute | solution.py:356
  34.6 0.9 %shard_map.98 = (bf16[32,8,128]{2,1,0:T(8,128)(2,1)S(1)}, bf16[2,32,8,128]{3,2,1,0:T(8,128)(2,1)S(1)}) custom-call(f32[2,1024,128]{2,1,0:T(8,128)S(1)} %get-tuple-element.62.wide, bf16[2,2,32,128]{3,2,1,0:T(8,128)(2,1)S(1)} %get-tuple-element.59.rest_0_.kept, bf16[2,2,32,128]{3,2,1,0:T(8,128)(2,1)S(1)} %collective-permute-done.7.rest_0_, ...), custom_call_target="tpu_custom_call" | custom-call | flops 1048576 | bytes 1048576 | tf_op jit(solution)/shard_map/pallas_call | solution.py:340
  35.6 5.8 %collective-permute-start.11 = (bf16[32,8,128]{2,1,0:T(8,128)(2,1)S(1)}, bf16[32,8,128]{2,1,0:T(8,128)(2,1)S(1)}, u32[]{:S(2)}, u32[]{:S(2)}) collective-permute-start(bf16[32,8,128]{2,1,0:T(8,128)(2,1)S(1)} %get-tuple-element.78), channel_id=1, source_target_pairs={{0,1},{1,0},{2,3},{3,2},{4,5},{5,4},{6,7},{7,6},{8,9},{9,8},{10,11... | collective-permute-start | bytes 196616 | tf_op jit(solution)/shard_map/ppermute | solution.py:356
  41.4 0.7 %shard_map.104.state = bf16[32,8,128]{2,1,0:T(8,128)(2,1)S(1)} custom-call(s32[4,2,256]{2,1,0:T(2,128)S(1)} %copy-done.4, f32[2,1024,128]{2,1,0:T(8,128)S(1)} %get-tuple-element.79.wide, bf16[2,32,8,128]{3,2,1,0:T(8,128)(2,1)S(1)} %get-tuple-element.80.states), custom_call_target="tpu_custom_call" | custom-call | flops 1048576 | bytes 1048576 | tf_op jit(solution)/shard_map/pallas_call | solution.py:340
  42.0 1.6 %collective-permute-start.15 = (bf16[32,8,128]{2,1,0:T(8,128)(2,1)S(1)}, bf16[32,8,128]{2,1,0:T(8,128)(2,1)S(1)}, u32[]{:S(2)}, u32[]{:S(2)}) collective-permute-start(bf16[32,8,128]{2,1,0:T(8,128)(2,1)S(1)} %shard_map.104.state), channel_id=1, source_target_pairs={{0,2},{1,3},{2,0},{3,1},{4,6},{5,7},{6,4},{7,5},{8,10},{9,11},{10,... | collective-permute-start | bytes 196616 | tf_op jit(solution)/shard_map/ppermute | solution.py:356
  43.6 0.5 collective-permute-start.12
  44.1 0.3 shard_map.105.near
  44.4 2.3 %collective-permute-done.15.partner = bf16[32,8,128]{2,1,0:T(8,128)(2,1)S(1)} collective-permute-done((bf16[32,8,128]{2,1,0:T(8,128)(2,1)S(1)}, bf16[32,8,128]{2,1,0:T(8,128)(2,1)S(1)}, u32[]{:S(2)}, u32[]{:S(2)}) %collective-permute-start.15) | collective-permute-done | bytes 65568 | tf_op jit(solution)/shard_map/ppermute | solution.py:356
  46.7 0.3 shard_map.106.state
  47.1 0.5 collective-permute-start.16
  47.6 0.3 shard_map.99.near
  47.9 0.4 shard_map.100.state.rest_0_
  48.3 1.7 %collective-permute-start.13 = (bf16[32,8,128]{2,1,0:T(8,128)(2,1)S(1)}, bf16[32,8,128]{2,1,0:T(8,128)(2,1)S(1)}, u32[]{:S(2)}, u32[]{:S(2)}) collective-permute-start(bf16[32,8,128]{2,1,0:T(8,128)(2,1)S(1)} %shard_map.100.state.rest_0_), channel_id=1, source_target_pairs={{0,4},{1,5},{2,6},{3,7},{4,0},{5,1},{6,2},{7,3},{8,12},{9,13},{10,... | collective-permute-start | bytes 196616 | tf_op jit(solution)/shard_map/ppermute | solution.py:356
  49.9 0.3 shard_map.107.near
  50.3 1.2 %collective-permute-done.16.partner = bf16[32,8,128]{2,1,0:T(8,128)(2,1)S(1)} collective-permute-done((bf16[32,8,128]{2,1,0:T(8,128)(2,1)S(1)}, bf16[32,8,128]{2,1,0:T(8,128)(2,1)S(1)}, u32[]{:S(2)}, u32[]{:S(2)}) %collective-permute-start.16) | collective-permute-done | bytes 65568 | tf_op jit(solution)/shard_map/ppermute | solution.py:356
  51.4 0.3 shard_map.108.state
  51.8 0.4 collective-permute-start.17
  52.2 0.3 shard_map.101.near
  52.6 0.3 shard_map.102.state.rest_0_
  52.9 2.6 %collective-permute-start.14 = (bf16[32,8,128]{2,1,0:T(8,128)(2,1)S(1)}, bf16[32,8,128]{2,1,0:T(8,128)(2,1)S(1)}, u32[]{:S(2)}, u32[]{:S(2)}) collective-permute-start(bf16[32,8,128]{2,1,0:T(8,128)(2,1)S(1)} %shard_map.102.state.rest_0_), channel_id=1, source_target_pairs={{0,8},{1,9},{2,10},{3,11},{4,12},{5,13},{6,14},{7,15},{8,0},{9,1},... | collective-permute-start | bytes 196616 | tf_op jit(solution)/shard_map/ppermute | solution.py:356
  55.5 0.3 shard_map.103.near
  55.8 0.3 shard_map.109.near
  56.2 1.7 %collective-permute-done.17.partner = bf16[32,8,128]{2,1,0:T(8,128)(2,1)S(1)} collective-permute-done((bf16[32,8,128]{2,1,0:T(8,128)(2,1)S(1)}, bf16[32,8,128]{2,1,0:T(8,128)(2,1)S(1)}, u32[]{:S(2)}, u32[]{:S(2)}) %collective-permute-start.17) | collective-permute-done | bytes 65568 | tf_op jit(solution)/shard_map/ppermute | solution.py:356
  57.9 1.0 %shard_map.110.ready = bf16[64,8,128]{2,1,0:T(8,128)(2,1)S(1)} custom-call(s32[4,2,256]{2,1,0:T(2,128)S(1)} %copy-done.4, f32[1024,128]{1,0:T(8,128)S(1)} %get-tuple-element.76.rest_14_.wide, f32[2048,128]{1,0:T(8,128)S(1)} %get-tuple-element.77.rest_16_.image_wide, bf16[32,8,128]{2,1,0:T(8,128)(2,1)S(1)} %collective-permute-done.17.partner, ...), custom_call_target="tpu_custom_call" | custom-call | flops 1572864 | bytes 1572864 | tf_op jit(solution)/shard_map/pallas_call | solution.py:340
  58.9 1.7 %shard_map.111 = bf16[64,8,256]{2,1,0:T(8,128)(2,1)} custom-call(s32[4,2,256]{2,1,0:T(2,128)S(1)} %copy-done.4, f32[1024,128]{1,0:T(8,128)S(1)} %get-tuple-element.60.rest_15_.wide, f32[2048,128]{1,0:T(8,128)S(1)} %get-tuple-element.61.rest_17_.image_wide, bf16[32,8,128]{2,1,0:T(8,128)(2,1)S(1)} %collective-permute-done.14.partner, ...), custom_call_target="tpu_custom_call" | custom-call | flops 1572864 | bytes 1572864 | tf_op jit(solution)/shard_map/pallas_call | solution.py:340
  (25 shorter events, 0.2 us)
Async XLA Ops:
  0.0 6.0 %copy-start.2 = (bf16[32,64,256]{2,1,0:T(8,128)(2,1)S(1)}, bf16[32,64,256]{2,1,0:T(8,128)(2,1)}, u32[]{:S(2)}) copy-start(bf16[32,64,256]{2,1,0:T(8,128)(2,1)} %interp.4) | copy-start | bytes 3145732
  0.0 6.0 %copy-start.6 = (bf16[64,8,256]{2,1,0:T(8,128)(2,1)S(1)}, bf16[64,8,256]{2,1,0:T(8,128)(2,1)}, u32[]{:S(2)}) copy-start(bf16[64,8,256]{2,1,0:T(8,128)(2,1)} %samples.3) | copy-start | bytes 786436
  1.9 6.0 %copy-start.3 = (s32[4,2,256]{2,1,0:T(2,128)S(1)}, s32[4,2,256]{2,1,0:T(2,128)}, u32[]{:S(2)}) copy-start(s32[4,2,256]{2,1,0:T(2,128)} %pattern.40) | copy-start | bytes 24580
  1.9 7.8 %collective-permute-start = (bf16[32,8,128]{2,1,0:T(8,128)(2,1)S(1)}, bf16[32,8,128]{2,1,0:T(8,128)(2,1)S(1)}, u32[]{:S(2)}, u32[]{:S(2)}) collective-permute-start(bf16[32,8,128]{2,1,0:T(8,128)(2,1)S(1)} %shard_map.73.after.state), channel_id=1, source_target_pairs={{0,8},{1,9},{2,10},{3,11},{4,12},{5,13},{6,14},{7,15},{8,0},{9,1},... | collective-permute-start | bytes 196616 | tf_op jit(solution)/shard_map/ppermute | solution.py:356
  6.0 6.9 %copy-start = (bf16[4,32,64,256]{3,2,1,0:T(8,128)(2,1)S(1)}, bf16[4,32,64,256]{3,2,1,0:T(8,128)(2,1)}, u32[]{:S(2)}) copy-start(bf16[4,32,64,256]{3,2,1,0:T(8,128)(2,1)} %blocks.11) | copy-start | bytes 12582916
  7.4 6.1 %collective-permute-start.2 = (bf16[32,8,128]{2,1,0:T(8,128)(2,1)S(1)}, bf16[32,8,128]{2,1,0:T(8,128)(2,1)S(1)}, u32[]{:S(2)}, u32[]{:S(2)}) collective-permute-start(bf16[32,8,128]{2,1,0:T(8,128)(2,1)S(1)} %get-tuple-element.46.state), channel_id=1, source_target_pairs={{0,8},{1,9},{2,10},{3,11},{4,12},{5,13},{6,14},{7,15},{8,0},{9,1},... | collective-permute-start | bytes 196616 | tf_op jit(solution)/shard_map/ppermute | solution.py:356
  10.0 5.0 %collective-permute-start.1 = (bf16[32,8,128]{2,1,0:T(8,128)(2,1)S(1)}, bf16[32,8,128]{2,1,0:T(8,128)(2,1)S(1)}, u32[]{:S(2)}, u32[]{:S(2)}) collective-permute-start(bf16[32,8,128]{2,1,0:T(8,128)(2,1)S(1)} %shard_map.77.state), channel_id=1, source_target_pairs={{0,4},{1,5},{2,6},{3,7},{4,0},{5,1},{6,2},{7,3},{8,12},{9,13},{10,... | collective-permute-start | bytes 196616 | tf_op jit(solution)/shard_map/ppermute | solution.py:356
  13.2 3.8 %copy-start.1 = (bf16[4,32,64,256]{3,2,1,0:T(8,128)(2,1)S(1)}, bf16[4,32,64,256]{3,2,1,0:T(8,128)(2,1)}, u32[]{:S(2)}) copy-start(bf16[4,32,64,256]{3,2,1,0:T(8,128)(2,1)} %blocks.15) | copy-start | bytes 12582916
  13.9 3.0 %copy-start.4 = (s32[4,2,256]{2,1,0:T(2,128)S(1)}, s32[4,2,256]{2,1,0:T(2,128)}, u32[]{:S(2)}) copy-start(s32[4,2,256]{2,1,0:T(2,128)} %pattern.53) | copy-start | bytes 24580
  13.9 4.3 %collective-permute-start.4 = (bf16[32,8,128]{2,1,0:T(8,128)(2,1)S(1)}, bf16[32,8,128]{2,1,0:T(8,128)(2,1)S(1)}, u32[]{:S(2)}, u32[]{:S(2)}) collective-permute-start(bf16[32,8,128]{2,1,0:T(8,128)(2,1)S(1)} %shard_map.81.rest_0_.state), channel_id=1, source_target_pairs={{0,4},{1,5},{2,6},{3,7},{4,0},{5,1},{6,2},{7,3},{8,12},{9,13},{10,... | collective-permute-start | bytes 196616 | tf_op jit(solution)/shard_map/ppermute | solution.py:356
  15.3 4.3 %collective-permute-start.3 = (bf16[32,8,128]{2,1,0:T(8,128)(2,1)S(1)}, bf16[32,8,128]{2,1,0:T(8,128)(2,1)S(1)}, u32[]{:S(2)}, u32[]{:S(2)}) collective-permute-start(bf16[32,8,128]{2,1,0:T(8,128)(2,1)S(1)} %shard_map.83.state), channel_id=1, source_target_pairs={{0,2},{1,3},{2,0},{3,1},{4,6},{5,7},{6,4},{7,5},{8,10},{9,11},{10,... | collective-permute-start | bytes 196616 | tf_op jit(solution)/shard_map/ppermute | solution.py:356
  20.0 2.8 %collective-permute-start.5 = (bf16[68,64,128]{2,1,0:T(8,128)(2,1)S(1)}, bf16[68,64,128]{2,1,0:T(8,128)(2,1)S(1)}, u32[]{:S(2)}, u32[]{:S(2)}) collective-permute-start(bf16[68,64,128]{2,1,0:T(8,128)(2,1)S(1)} %shard_map.88), channel_id=1, source_target_pairs={{0,1},{1,0},{2,3},{3,2},{4,5},{5,4},{6,7},{7,6},{8,9},{9,8},{10,11... | collective-permute-start | bytes 3342344 | tf_op jit(solution)/shard_map/ppermute | solution.py:356
  20.1 4.5 %collective-permute-start.6 = (bf16[32,8,128]{2,1,0:T(8,128)(2,1)S(1)}, bf16[32,8,128]{2,1,0:T(8,128)(2,1)S(1)}, u32[]{:S(2)}, u32[]{:S(2)}) collective-permute-start(bf16[32,8,128]{2,1,0:T(8,128)(2,1)S(1)} %shard_map.85.rest_0_.state), channel_id=1, source_target_pairs={{0,2},{1,3},{2,0},{3,1},{4,6},{5,7},{6,4},{7,5},{8,10},{9,11},{10,... | collective-permute-start | bytes 196616 | tf_op jit(solution)/shard_map/ppermute | solution.py:356
  24.6 5.9 %copy-start.5 = (bf16[64,32,256]{2,1,0:T(8,128)(2,1)S(1)}, bf16[64,32,256]{2,1,0:T(8,128)(2,1)}, u32[]{:S(2)}) copy-start(bf16[64,32,256]{2,1,0:T(8,128)(2,1)} %interp.5) | copy-start | bytes 3145732
  26.1 5.9 %collective-permute-start.8 = (bf16[2,2,32,128]{3,2,1,0:T(8,128)(2,1)S(1)}, bf16[2,2,32,128]{3,2,1,0:T(8,128)(2,1)S(1)}, u32[]{:S(2)}, u32[]{:S(2)}) collective-permute-start(bf16[2,2,32,128]{3,2,1,0:T(8,128)(2,1)S(1)} %get-tuple-element.63), channel_id=1, source_target_pairs={{0,2},{1,10},{2,0},{3,8},{4,6},{5,14},{6,4},{7,12},{8,3},{9,11},{1... | collective-permute-start | bytes 98312 | tf_op jit(solution)/shard_map/ppermute | solution.py:356
  27.7 4.3 %collective-permute-start.9 = (bf16[2,2,32,128]{3,2,1,0:T(8,128)(2,1)S(1)}, bf16[2,2,32,128]{3,2,1,0:T(8,128)(2,1)S(1)}, u32[]{:S(2)}, u32[]{:S(2)}) collective-permute-start(bf16[2,2,32,128]{3,2,1,0:T(8,128)(2,1)S(1)} %get-tuple-element.64), channel_id=1, source_target_pairs={{0,4},{1,12},{2,6},{3,14},{4,0},{5,8},{6,2},{7,10},{8,5},{9,13},{1... | collective-permute-start | bytes 98312 | tf_op jit(solution)/shard_map/ppermute | solution.py:356
  29.8 4.8 %collective-permute-start.10 = (bf16[2,2,32,128]{3,2,1,0:T(8,128)(2,1)S(1)}, bf16[2,2,32,128]{3,2,1,0:T(8,128)(2,1)S(1)}, u32[]{:S(2)}, u32[]{:S(2)}) collective-permute-start(bf16[2,2,32,128]{3,2,1,0:T(8,128)(2,1)S(1)} %get-tuple-element.65), channel_id=1, source_target_pairs={{0,6},{1,14},{2,4},{3,12},{4,2},{5,10},{6,0},{7,8},{8,7},{9,15},{1... | collective-permute-start | bytes 98312 | tf_op jit(solution)/shard_map/ppermute | solution.py:356
  29.8 4.8 %collective-permute-start.7 = (bf16[2,2,32,128]{3,2,1,0:T(8,128)(2,1)S(1)}, bf16[2,2,32,128]{3,2,1,0:T(8,128)(2,1)S(1)}, u32[]{:S(2)}, u32[]{:S(2)}) collective-permute-start(bf16[2,2,32,128]{3,2,1,0:T(8,128)(2,1)S(1)} %get-tuple-element.59.rest_0_.kept), channel_id=1, source_target_pairs={{1,8},{3,10},{5,12},{7,14},{8,1},{10,3},{12,5},{14,7},{17,24},{19,... | collective-permute-start | bytes 98312 | tf_op jit(solution)/shard_map/ppermute | solution.py:356
  35.6 8.0 %collective-permute-start.11 = (bf16[32,8,128]{2,1,0:T(8,128)(2,1)S(1)}, bf16[32,8,128]{2,1,0:T(8,128)(2,1)S(1)}, u32[]{:S(2)}, u32[]{:S(2)}) collective-permute-start(bf16[32,8,128]{2,1,0:T(8,128)(2,1)S(1)} %get-tuple-element.78), channel_id=1, source_target_pairs={{0,1},{1,0},{2,3},{3,2},{4,5},{5,4},{6,7},{7,6},{8,9},{9,8},{10,11... | collective-permute-start | bytes 196616 | tf_op jit(solution)/shard_map/ppermute | solution.py:356
  42.0 4.7 %collective-permute-start.15 = (bf16[32,8,128]{2,1,0:T(8,128)(2,1)S(1)}, bf16[32,8,128]{2,1,0:T(8,128)(2,1)S(1)}, u32[]{:S(2)}, u32[]{:S(2)}) collective-permute-start(bf16[32,8,128]{2,1,0:T(8,128)(2,1)S(1)} %shard_map.104.state), channel_id=1, source_target_pairs={{0,2},{1,3},{2,0},{3,1},{4,6},{5,7},{6,4},{7,5},{8,10},{9,11},{10,... | collective-permute-start | bytes 196616 | tf_op jit(solution)/shard_map/ppermute | solution.py:356
  43.6 4.3 %collective-permute-start.12 = (bf16[32,8,128]{2,1,0:T(8,128)(2,1)S(1)}, bf16[32,8,128]{2,1,0:T(8,128)(2,1)S(1)}, u32[]{:S(2)}, u32[]{:S(2)}) collective-permute-start(bf16[32,8,128]{2,1,0:T(8,128)(2,1)S(1)} %collective-permute-done.11.state.rest_0_), channel_id=1, source_target_pairs={{0,2},{1,3},{2,0},{3,1},{4,6},{5,7},{6,4},{7,5},{8,10},{9,11},{10,... | collective-permute-start | bytes 196616 | tf_op jit(solution)/shard_map/ppermute | solution.py:356
  47.1 4.3 %collective-permute-start.16 = (bf16[32,8,128]{2,1,0:T(8,128)(2,1)S(1)}, bf16[32,8,128]{2,1,0:T(8,128)(2,1)S(1)}, u32[]{:S(2)}, u32[]{:S(2)}) collective-permute-start(bf16[32,8,128]{2,1,0:T(8,128)(2,1)S(1)} %shard_map.106.state), channel_id=1, source_target_pairs={{0,4},{1,5},{2,6},{3,7},{4,0},{5,1},{6,2},{7,3},{8,12},{9,13},{10,... | collective-permute-start | bytes 196616 | tf_op jit(solution)/shard_map/ppermute | solution.py:356
  48.3 4.3 %collective-permute-start.13 = (bf16[32,8,128]{2,1,0:T(8,128)(2,1)S(1)}, bf16[32,8,128]{2,1,0:T(8,128)(2,1)S(1)}, u32[]{:S(2)}, u32[]{:S(2)}) collective-permute-start(bf16[32,8,128]{2,1,0:T(8,128)(2,1)S(1)} %shard_map.100.state.rest_0_), channel_id=1, source_target_pairs={{0,4},{1,5},{2,6},{3,7},{4,0},{5,1},{6,2},{7,3},{8,12},{9,13},{10,... | collective-permute-start | bytes 196616 | tf_op jit(solution)/shard_map/ppermute | solution.py:356
  51.8 6.1 %collective-permute-start.17 = (bf16[32,8,128]{2,1,0:T(8,128)(2,1)S(1)}, bf16[32,8,128]{2,1,0:T(8,128)(2,1)S(1)}, u32[]{:S(2)}, u32[]{:S(2)}) collective-permute-start(bf16[32,8,128]{2,1,0:T(8,128)(2,1)S(1)} %shard_map.108.state), channel_id=1, source_target_pairs={{0,8},{1,9},{2,10},{3,11},{4,12},{5,13},{6,14},{7,15},{8,0},{9,1},... | collective-permute-start | bytes 196616 | tf_op jit(solution)/shard_map/ppermute | solution.py:356
  52.9 5.9 %collective-permute-start.14 = (bf16[32,8,128]{2,1,0:T(8,128)(2,1)S(1)}, bf16[32,8,128]{2,1,0:T(8,128)(2,1)S(1)}, u32[]{:S(2)}, u32[]{:S(2)}) collective-permute-start(bf16[32,8,128]{2,1,0:T(8,128)(2,1)S(1)} %shard_map.102.state.rest_0_), channel_id=1, source_target_pairs={{0,8},{1,9},{2,10},{3,11},{4,12},{5,13},{6,14},{7,15},{8,0},{9,1},... | collective-permute-start | bytes 196616 | tf_op jit(solution)/shard_map/ppermute | solution.py:356

commit v13 on v12

--- a/solution.py
+++ b/solution.py
@@ -96,12 +96,13 @@
         multiply(wide, state, rank, emit)
 
 
-def second_kernel(flip, blocks, interp, samples, after, out, held, *rest):
-    sem = rest[-1]
-    copy = pltpu.make_async_copy(blocks.at[pl.ds(0, 1)], held, sem)
+def second_kernel(level, bit, flip, blocks, interp, samples, after, *rest):
+    held, sem = rest[-2:]
+    copy = pltpu.make_async_copy(blocks.at[pl.ds(level, 1)], held, sem)
     copy.start()
-    coeff_kernel(flip, interp, samples, out, *rest[:-1])
+    coeff_kernel(flip, interp, samples, rest[0], *rest[5:-2])
     copy.wait()
+    ahead_kernel(0, bit, held, *rest[1:5])
 
 
 def ahead_kernel(level, bit, blocks, *rest):
@@ -416,13 +417,13 @@
         bit = 3 - level
         if level == 0:
             partner = {1: swapped(current[1], bit)}
-            current[0], first_blocks = run(
-                functools.partial(second_kernel, 0),
-                [state, jax.ShapeDtypeStruct((1, *top_blocks.shape[1:]), jnp.bfloat16)],
-                (top_blocks, interp_in, samples, current[1]), coeff_scratch + (pltpu.SemaphoreType.DMA,), 4,
+            current[0], *wides = run(
+                functools.partial(second_kernel, 0, 3, 0), [state] + [spread_out] * 4,
+                (top_blocks, interp_in, samples, current[1]),
+                coeff_scratch + (pltpu.VMEM((1, *top_blocks.shape[1:]), jnp.bfloat16), pltpu.SemaphoreType.DMA), 4,
                 in_specs=[pl.BlockSpec(memory_space=pl.ANY)] * 4, limit=FETCH_LIMIT,
             )
-            wides = level_wides(first_blocks, 0, bit)
+            wides = wides[:2], wides[2:]
             partner[0] = swapped(current[0], bit)
             near = level_nears(top_pattern, level, bit, (1,), wides)
             near.update(level_nears(top_pattern, level, bit, (0,), wides))

time: 60.7 us -> 59.5 us (0.980)
  starting transfers between devices: 28 us -> 25.9 us
  Pallas kernels: 19.8 us -> 20.6 us
    ppermute x18, starting transfers between devices: 28 us -> 25.9 us  [permuted(): return lax.ppermute(value, 'leaf', pairs)]
    pallas_call x39 -> x38, Pallas kernels: 19.8 us -> 20.6 us  [run(): pl.pallas_call(kernel, out_shape=shapes, in_specs=in_specs or [whole] * l...]
  transfers between devices with their start and end apart: 18 -> 18, of which waited for: 10 -> 11; matrix products, arithmetic and copies ran while one was open for 0% -> 0% of each run, Pallas kernels for 22% -> 24%
where the time goes in v13:
time: 59.5 us; the launch traced here: 59.4 us
  starting transfers between devices  25.9 us (44%)
  Pallas kernels  20.6 us (35%)
  waiting for transfers between devices  12.5 us (21%)
    ppermute x18, starting transfers between devices, permuted(): return lax.ppermute(value, 'leaf', pairs)  25.9 us
    pallas_call x38, Pallas kernels, run(): pl.pallas_call(kernel, out_shape=shapes, in_specs=in_specs or [whole] * l...  20.6 us
    ppermute x18, waiting for transfers between devices, permuted(): return lax.ppermute(value, 'leaf', pairs)  12.5 us
  transfers between devices with their start and end apart: 18, of which 11 were waited for; matrix products, arithmetic and copies ran while one was open for 0% of the time, Pallas kernels for 24%

profile of v13, /device:TPU:0, one launch (start us, length us, event | category | flops | bytes accessed | tf_op | source)
XLA Modules:
  0.0 59.4 jit_solution(5097259649285743120)
XLA Ops:
  0.0 1.8 %shard_map.73.after.state = bf16[32,8,128]{2,1,0:T(8,128)(2,1)S(1)} custom-call(bf16[32,64,256]{2,1,0:T(8,128)(2,1)} %interp.4, bf16[64,8,256]{2,1,0:T(8,128)(2,1)} %samples.3), custom_call_target="tpu_custom_call" | custom-call | flops 1048576 | bytes 1048576 | tf_op jit(solution)/shard_map/pallas_call | solution.py:341
  1.8 4.1 %collective-permute-start = (bf16[32,8,128]{2,1,0:T(8,128)(2,1)S(1)}, bf16[32,8,128]{2,1,0:T(8,128)(2,1)S(1)}, u32[]{:S(2)}, u32[]{:S(2)}) collective-permute-start(bf16[32,8,128]{2,1,0:T(8,128)(2,1)S(1)} %shard_map.73.after.state), channel_id=1, source_target_pairs={{0,8},{1,9},{2,10},{3,11},{4,12},{5,13},{6,14},{7,15},{8,0},{9,1},... | collective-permute-start | bytes 196616 | tf_op jit(solution)/shard_map/ppermute | solution.py:357
  5.9 2.5 %shard_map.74 = (bf16[32,8,128]{2,1,0:T(8,128)(2,1)S(1)}, f32[1024,128]{1,0:T(8,128)S(1)}, f32[1024,128]{1,0:T(8,128)S(1)}, f32[1024,128]{1,0:T(8,128)S(1)}, f32[1024,128]{1,0:T(8,128)S(1)}) custom-call(bf16[4,32,64,256]{3,2,1,0:T(8,128)(2,1)} %blocks.11, bf16[32,64,256]{2,1,0:T(8,128)(2,1)} %interp.4, bf16[64,8,256]{2,1,0:T(8,128)(2,1)S(1)} %copy-done.5, ...), custom_call_target="tpu_custom_call" | custom-call | flops 2097152 | bytes 2097152 | tf_op jit(solution)/shard_map/pallas_call | solution.py:341
  8.6 0.3 shard_map.75.near
  8.9 0.7 %collective-permute-done.partner = bf16[32,8,128]{2,1,0:T(8,128)(2,1)S(1)} collective-permute-done((bf16[32,8,128]{2,1,0:T(8,128)(2,1)S(1)}, bf16[32,8,128]{2,1,0:T(8,128)(2,1)S(1)}, u32[]{:S(2)}, u32[]{:S(2)}) %collective-permute-start) | collective-permute-done | bytes 65568 | tf_op jit(solution)/shard_map/ppermute | solution.py:357
  9.6 0.4 shard_map.76.state
  9.9 1.3 %collective-permute-start.1 = (bf16[32,8,128]{2,1,0:T(8,128)(2,1)S(1)}, bf16[32,8,128]{2,1,0:T(8,128)(2,1)S(1)}, u32[]{:S(2)}, u32[]{:S(2)}) collective-permute-start(bf16[32,8,128]{2,1,0:T(8,128)(2,1)S(1)} %shard_map.76.state), channel_id=1, source_target_pairs={{0,4},{1,5},{2,6},{3,7},{4,0},{5,1},{6,2},{7,3},{8,12},{9,13},{10,... | collective-permute-start | bytes 196616 | tf_op jit(solution)/shard_map/ppermute | solution.py:357
  11.2 0.3 shard_map.77.rest_0_.near
  11.6 0.3 shard_map.79
  11.9 0.3 shard_map.78
  12.3 1.8 %collective-permute-done.2.partner = bf16[32,8,128]{2,1,0:T(8,128)(2,1)S(1)} collective-permute-done((bf16[32,8,128]{2,1,0:T(8,128)(2,1)S(1)}, bf16[32,8,128]{2,1,0:T(8,128)(2,1)S(1)}, u32[]{:S(2)}, u32[]{:S(2)}) %collective-permute-start.2) | collective-permute-done | bytes 65568 | tf_op jit(solution)/shard_map/ppermute | solution.py:357
  14.0 0.4 shard_map.80.rest_0_.state
  14.4 1.9 %collective-permute-start.4 = (bf16[32,8,128]{2,1,0:T(8,128)(2,1)S(1)}, bf16[32,8,128]{2,1,0:T(8,128)(2,1)S(1)}, u32[]{:S(2)}, u32[]{:S(2)}) collective-permute-start(bf16[32,8,128]{2,1,0:T(8,128)(2,1)S(1)} %shard_map.80.rest_0_.state), channel_id=1, source_target_pairs={{0,4},{1,5},{2,6},{3,7},{4,0},{5,1},{6,2},{7,3},{8,12},{9,13},{10,... | collective-permute-start | bytes 196616 | tf_op jit(solution)/shard_map/ppermute | solution.py:357
  16.3 0.3 shard_map.81.near
  16.7 0.4 shard_map.82.state
  17.0 1.6 %collective-permute-start.3 = (bf16[32,8,128]{2,1,0:T(8,128)(2,1)S(1)}, bf16[32,8,128]{2,1,0:T(8,128)(2,1)S(1)}, u32[]{:S(2)}, u32[]{:S(2)}) collective-permute-start(bf16[32,8,128]{2,1,0:T(8,128)(2,1)S(1)} %shard_map.82.state), channel_id=1, source_target_pairs={{0,2},{1,3},{2,0},{3,1},{4,6},{5,7},{6,4},{7,5},{8,10},{9,11},{10,... | collective-permute-start | bytes 196616 | tf_op jit(solution)/shard_map/ppermute | solution.py:357
  18.6 0.2 shard_map.86.shared
  18.9 0.4 shard_map.83.near
  19.2 0.4 shard_map.84.rest_0_.state
  19.6 0.4 shard_map.85.near
  20.0 1.4 %collective-permute-done.3.partner = bf16[32,8,128]{2,1,0:T(8,128)(2,1)S(1)} collective-permute-done((bf16[32,8,128]{2,1,0:T(8,128)(2,1)S(1)}, bf16[32,8,128]{2,1,0:T(8,128)(2,1)S(1)}, u32[]{:S(2)}, u32[]{:S(2)}) %collective-permute-start.3) | collective-permute-done | bytes 65568 | tf_op jit(solution)/shard_map/ppermute | solution.py:357
  21.4 0.3 shard_map.87
  21.8 1.6 %collective-permute-start.6 = (bf16[32,8,128]{2,1,0:T(8,128)(2,1)S(1)}, bf16[32,8,128]{2,1,0:T(8,128)(2,1)S(1)}, u32[]{:S(2)}, u32[]{:S(2)}) collective-permute-start(bf16[32,8,128]{2,1,0:T(8,128)(2,1)S(1)} %shard_map.84.rest_0_.state), channel_id=1, source_target_pairs={{0,2},{1,3},{2,0},{3,1},{4,6},{5,7},{6,4},{7,5},{8,10},{9,11},{10,... | collective-permute-start | bytes 196616 | tf_op jit(solution)/shard_map/ppermute | solution.py:357
  23.4 0.3 shard_map.89.near
  23.7 0.8 %collective-permute-done.5.shared = bf16[68,64,128]{2,1,0:T(8,128)(2,1)S(1)} collective-permute-done((bf16[68,64,128]{2,1,0:T(8,128)(2,1)S(1)}, bf16[68,64,128]{2,1,0:T(8,128)(2,1)S(1)}, u32[]{:S(2)}, u32[]{:S(2)}) %collective-permute-start.5) | collective-permute-done | bytes 1114144 | tf_op jit(solution)/shard_map/ppermute | solution.py:357
  24.5 0.9 %shard_map.88 = (f32[2,32,8,128]{3,2,1,0:T(8,128)S(1)}, f32[2,1024,128]{2,1,0:T(8,128)S(1)}) custom-call(bf16[4,32,64,256]{3,2,1,0:T(8,128)(2,1)S(1)} %copy-done, s32[4,2,256]{2,1,0:T(2,128)S(1)} %copy-done.2, bf16[68,64,128]{2,1,0:T(8,128)(2,1)S(1)} %collective-permute-done.5.shared), custom_call_target="tpu_custom_call" | custom-call | flops 1048576 | bytes 1048576 | tf_op jit(solution)/shard_map/pallas_call | solution.py:341
  25.5 0.8 %collective-permute-done.6.partner = bf16[32,8,128]{2,1,0:T(8,128)(2,1)S(1)} collective-permute-done((bf16[32,8,128]{2,1,0:T(8,128)(2,1)S(1)}, bf16[32,8,128]{2,1,0:T(8,128)(2,1)S(1)}, u32[]{:S(2)}, u32[]{:S(2)}) %collective-permute-start.6) | collective-permute-done | bytes 65568 | tf_op jit(solution)/shard_map/ppermute | solution.py:357
  26.3 0.4 shard_map.90.state
  26.7 1.2 %shard_map.91 = (bf16[2,2,32,128]{3,2,1,0:T(8,128)(2,1)S(1)}, bf16[2,2,32,128]{3,2,1,0:T(8,128)(2,1)S(1)}, bf16[2,2,32,128]{3,2,1,0:T(8,128)(2,1)S(1)}, bf16[2,2,32,128]{3,2,1,0:T(8,128)(2,1)S(1)}) custom-call(s32[4,2,256]{2,1,0:T(2,128)S(1)} %copy-done.2, f32[2,1024,128]{2,1,0:T(8,128)S(1)} %get-tuple-element.54.wide, ...), custom_call_target="tpu_custom_call" | custom-call | flops 1048576 | bytes 1048576 | tf_op jit(solution)/shard_map/pallas_call | solution.py:341
  27.8 1.6 %collective-permute-start.8 = (bf16[2,2,32,128]{3,2,1,0:T(8,128)(2,1)S(1)}, bf16[2,2,32,128]{3,2,1,0:T(8,128)(2,1)S(1)}, u32[]{:S(2)}, u32[]{:S(2)}) collective-permute-start(bf16[2,2,32,128]{3,2,1,0:T(8,128)(2,1)S(1)} %get-tuple-element.61), channel_id=1, source_target_pairs={{0,2},{1,10},{2,0},{3,8},{4,6},{5,14},{6,4},{7,12},{8,3},{9,11},{1... | collective-permute-start | bytes 98312 | tf_op jit(solution)/shard_map/ppermute | solution.py:357
  29.6 1.8 %collective-permute-start.10 = (bf16[2,2,32,128]{3,2,1,0:T(8,128)(2,1)S(1)}, bf16[2,2,32,128]{3,2,1,0:T(8,128)(2,1)S(1)}, u32[]{:S(2)}, u32[]{:S(2)}) collective-permute-start(bf16[2,2,32,128]{3,2,1,0:T(8,128)(2,1)S(1)} %get-tuple-element.63), channel_id=1, source_target_pairs={{0,6},{1,14},{2,4},{3,12},{4,2},{5,10},{6,0},{7,8},{8,7},{9,15},{1... | collective-permute-start | bytes 98312 | tf_op jit(solution)/shard_map/ppermute | solution.py:357
  31.4 0.7 %collective-permute-start.7 = (bf16[2,2,32,128]{3,2,1,0:T(8,128)(2,1)S(1)}, bf16[2,2,32,128]{3,2,1,0:T(8,128)(2,1)S(1)}, u32[]{:S(2)}, u32[]{:S(2)}) collective-permute-start(bf16[2,2,32,128]{3,2,1,0:T(8,128)(2,1)S(1)} %get-tuple-element.57.rest_0_.kept), channel_id=1, source_target_pairs={{1,8},{3,10},{5,12},{7,14},{8,1},{10,3},{12,5},{14,7},{17,24},{19,... | collective-permute-start | bytes 98312 | tf_op jit(solution)/shard_map/ppermute | solution.py:357
  32.1 0.3 shard_map.93
  32.4 0.3 shard_map.94
  32.6 0.3 shard_map.96
  33.0 0.3 shard_map.95
  33.3 0.3 shard_map.92
  33.6 0.8 %collective-permute-done.10.rest_3_ = bf16[2,2,32,128]{3,2,1,0:T(8,128)(2,1)S(1)} collective-permute-done((bf16[2,2,32,128]{3,2,1,0:T(8,128)(2,1)S(1)}, bf16[2,2,32,128]{3,2,1,0:T(8,128)(2,1)S(1)}, u32[]{:S(2)}, u32[]{:S(2)}) %collective-permute-start.10) | collective-permute-done | bytes 32800 | tf_op jit(solution)/shard_map/ppermute | solution.py:357
  34.4 0.9 %shard_map.97 = (bf16[32,8,128]{2,1,0:T(8,128)(2,1)S(1)}, bf16[2,32,8,128]{3,2,1,0:T(8,128)(2,1)S(1)}) custom-call(f32[2,1024,128]{2,1,0:T(8,128)S(1)} %get-tuple-element.60.wide, bf16[2,2,32,128]{3,2,1,0:T(8,128)(2,1)S(1)} %get-tuple-element.57.rest_0_.kept, bf16[2,2,32,128]{3,2,1,0:T(8,128)(2,1)S(1)} %collective-permute-done.7.rest_0_, ...), custom_call_target="tpu_custom_call" | custom-call | flops 1048576 | bytes 1048576 | tf_op jit(solution)/shard_map/pallas_call | solution.py:341
  35.4 4.7 %collective-permute-start.11 = (bf16[32,8,128]{2,1,0:T(8,128)(2,1)S(1)}, bf16[32,8,128]{2,1,0:T(8,128)(2,1)S(1)}, u32[]{:S(2)}, u32[]{:S(2)}) collective-permute-start(bf16[32,8,128]{2,1,0:T(8,128)(2,1)S(1)} %get-tuple-element.76), channel_id=1, source_target_pairs={{0,1},{1,0},{2,3},{3,2},{4,5},{5,4},{6,7},{7,6},{8,9},{9,8},{10,11... | collective-permute-start | bytes 196616 | tf_op jit(solution)/shard_map/ppermute | solution.py:357
  40.1 0.7 %shard_map.103.state = bf16[32,8,128]{2,1,0:T(8,128)(2,1)S(1)} custom-call(s32[4,2,256]{2,1,0:T(2,128)S(1)} %copy-done.3, f32[2,1024,128]{2,1,0:T(8,128)S(1)} %get-tuple-element.77.wide, bf16[2,32,8,128]{3,2,1,0:T(8,128)(2,1)S(1)} %get-tuple-element.78.states), custom_call_target="tpu_custom_call" | custom-call | flops 1048576 | bytes 1048576 | tf_op jit(solution)/shard_map/pallas_call | solution.py:341
  40.7 1.8 %collective-permute-start.15 = (bf16[32,8,128]{2,1,0:T(8,128)(2,1)S(1)}, bf16[32,8,128]{2,1,0:T(8,128)(2,1)S(1)}, u32[]{:S(2)}, u32[]{:S(2)}) collective-permute-start(bf16[32,8,128]{2,1,0:T(8,128)(2,1)S(1)} %shard_map.103.state), channel_id=1, source_target_pairs={{0,2},{1,3},{2,0},{3,1},{4,6},{5,7},{6,4},{7,5},{8,10},{9,11},{10,... | collective-permute-start | bytes 196616 | tf_op jit(solution)/shard_map/ppermute | solution.py:357
  42.5 0.3 collective-permute-start.12
  42.8 0.3 shard_map.104.near
  43.1 2.2 %collective-permute-done.15.partner = bf16[32,8,128]{2,1,0:T(8,128)(2,1)S(1)} collective-permute-done((bf16[32,8,128]{2,1,0:T(8,128)(2,1)S(1)}, bf16[32,8,128]{2,1,0:T(8,128)(2,1)S(1)}, u32[]{:S(2)}, u32[]{:S(2)}) %collective-permute-start.15) | collective-permute-done | bytes 65568 | tf_op jit(solution)/shard_map/ppermute | solution.py:357
  45.3 0.3 shard_map.105.state
  45.7 0.2 collective-permute-start.16
  45.9 0.3 shard_map.98.near
  46.2 0.6 %collective-permute-done.12.partner = bf16[32,8,128]{2,1,0:T(8,128)(2,1)S(1)} collective-permute-done((bf16[32,8,128]{2,1,0:T(8,128)(2,1)S(1)}, bf16[32,8,128]{2,1,0:T(8,128)(2,1)S(1)}, u32[]{:S(2)}, u32[]{:S(2)}) %collective-permute-start.12) | collective-permute-done | bytes 65568 | tf_op jit(solution)/shard_map/ppermute | solution.py:357
  46.8 0.3 shard_map.99.state.rest_0_
  47.1 1.4 %collective-permute-start.13 = (bf16[32,8,128]{2,1,0:T(8,128)(2,1)S(1)}, bf16[32,8,128]{2,1,0:T(8,128)(2,1)S(1)}, u32[]{:S(2)}, u32[]{:S(2)}) collective-permute-start(bf16[32,8,128]{2,1,0:T(8,128)(2,1)S(1)} %shard_map.99.state.rest_0_), channel_id=1, source_target_pairs={{0,4},{1,5},{2,6},{3,7},{4,0},{5,1},{6,2},{7,3},{8,12},{9,13},{10,... | collective-permute-start | bytes 196616 | tf_op jit(solution)/shard_map/ppermute | solution.py:357
  48.5 0.3 shard_map.106.near
  48.8 1.2 %collective-permute-done.16.partner = bf16[32,8,128]{2,1,0:T(8,128)(2,1)S(1)} collective-permute-done((bf16[32,8,128]{2,1,0:T(8,128)(2,1)S(1)}, bf16[32,8,128]{2,1,0:T(8,128)(2,1)S(1)}, u32[]{:S(2)}, u32[]{:S(2)}) %collective-permute-start.16) | collective-permute-done | bytes 65568 | tf_op jit(solution)/shard_map/ppermute | solution.py:357
  50.0 0.3 shard_map.107.state
  50.3 0.7 %collective-permute-start.17 = (bf16[32,8,128]{2,1,0:T(8,128)(2,1)S(1)}, bf16[32,8,128]{2,1,0:T(8,128)(2,1)S(1)}, u32[]{:S(2)}, u32[]{:S(2)}) collective-permute-start(bf16[32,8,128]{2,1,0:T(8,128)(2,1)S(1)} %shard_map.107.state), channel_id=1, source_target_pairs={{0,8},{1,9},{2,10},{3,11},{4,12},{5,13},{6,14},{7,15},{8,0},{9,1},... | collective-permute-start | bytes 196616 | tf_op jit(solution)/shard_map/ppermute | solution.py:357
  51.0 0.3 shard_map.100.near
  51.3 0.3 collective-permute-done.13.partner
  51.7 0.3 shard_map.101.state.rest_0_
  52.0 2.1 %collective-permute-start.14 = (bf16[32,8,128]{2,1,0:T(8,128)(2,1)S(1)}, bf16[32,8,128]{2,1,0:T(8,128)(2,1)S(1)}, u32[]{:S(2)}, u32[]{:S(2)}) collective-permute-start(bf16[32,8,128]{2,1,0:T(8,128)(2,1)S(1)} %shard_map.101.state.rest_0_), channel_id=1, source_target_pairs={{0,8},{1,9},{2,10},{3,11},{4,12},{5,13},{6,14},{7,15},{8,0},{9,1},... | collective-permute-start | bytes 196616 | tf_op jit(solution)/shard_map/ppermute | solution.py:357
  54.1 0.3 shard_map.102.near
  54.4 0.3 shard_map.108.near
  54.7 1.9 %collective-permute-done.17.partner = bf16[32,8,128]{2,1,0:T(8,128)(2,1)S(1)} collective-permute-done((bf16[32,8,128]{2,1,0:T(8,128)(2,1)S(1)}, bf16[32,8,128]{2,1,0:T(8,128)(2,1)S(1)}, u32[]{:S(2)}, u32[]{:S(2)}) %collective-permute-start.17) | collective-permute-done | bytes 65568 | tf_op jit(solution)/shard_map/ppermute | solution.py:357
  56.7 1.0 %shard_map.109.ready = bf16[64,8,128]{2,1,0:T(8,128)(2,1)S(1)} custom-call(s32[4,2,256]{2,1,0:T(2,128)S(1)} %copy-done.3, f32[1024,128]{1,0:T(8,128)S(1)} %get-tuple-element.74.rest_14_.wide, f32[2048,128]{1,0:T(8,128)S(1)} %get-tuple-element.75.rest_16_.image_wide, bf16[32,8,128]{2,1,0:T(8,128)(2,1)S(1)} %collective-permute-done.17.partner, ...), custom_call_target="tpu_custom_call" | custom-call | flops 1572864 | bytes 1572864 | tf_op jit(solution)/shard_map/pallas_call | solution.py:341
  57.7 1.7 %shard_map.110 = bf16[64,8,256]{2,1,0:T(8,128)(2,1)} custom-call(s32[4,2,256]{2,1,0:T(2,128)S(1)} %copy-done.3, f32[1024,128]{1,0:T(8,128)S(1)} %get-tuple-element.58.rest_15_.wide, f32[2048,128]{1,0:T(8,128)S(1)} %get-tuple-element.59.rest_17_.image_wide, bf16[32,8,128]{2,1,0:T(8,128)(2,1)S(1)} %collective-permute-done.14.partner, ...), custom_call_target="tpu_custom_call" | custom-call | flops 1572864 | bytes 1572864 | tf_op jit(solution)/shard_map/pallas_call | solution.py:341
  (22 shorter events, 0.4 us)
Async XLA Ops:
  0.0 5.9 %copy-start.5 = (bf16[64,8,256]{2,1,0:T(8,128)(2,1)S(1)}, bf16[64,8,256]{2,1,0:T(8,128)(2,1)}, u32[]{:S(2)}) copy-start(bf16[64,8,256]{2,1,0:T(8,128)(2,1)} %samples.3) | copy-start | bytes 786436
  1.8 6.8 %copy-start.2 = (s32[4,2,256]{2,1,0:T(2,128)S(1)}, s32[4,2,256]{2,1,0:T(2,128)}, u32[]{:S(2)}) copy-start(s32[4,2,256]{2,1,0:T(2,128)} %pattern.40) | copy-start | bytes 24580
  1.8 7.8 %collective-permute-start = (bf16[32,8,128]{2,1,0:T(8,128)(2,1)S(1)}, bf16[32,8,128]{2,1,0:T(8,128)(2,1)S(1)}, u32[]{:S(2)}, u32[]{:S(2)}) collective-permute-start(bf16[32,8,128]{2,1,0:T(8,128)(2,1)S(1)} %shard_map.73.after.state), channel_id=1, source_target_pairs={{0,8},{1,9},{2,10},{3,11},{4,12},{5,13},{6,14},{7,15},{8,0},{9,1},... | collective-permute-start | bytes 196616 | tf_op jit(solution)/shard_map/ppermute | solution.py:357
  5.9 5.7 %copy-start = (bf16[4,32,64,256]{3,2,1,0:T(8,128)(2,1)S(1)}, bf16[4,32,64,256]{3,2,1,0:T(8,128)(2,1)}, u32[]{:S(2)}) copy-start(bf16[4,32,64,256]{3,2,1,0:T(8,128)(2,1)} %blocks.11) | copy-start | bytes 12582916
  8.5 5.6 %collective-permute-start.2 = (bf16[32,8,128]{2,1,0:T(8,128)(2,1)S(1)}, bf16[32,8,128]{2,1,0:T(8,128)(2,1)S(1)}, u32[]{:S(2)}, u32[]{:S(2)}) collective-permute-start(bf16[32,8,128]{2,1,0:T(8,128)(2,1)S(1)} %get-tuple-element.44.state), channel_id=1, source_target_pairs={{0,8},{1,9},{2,10},{3,11},{4,12},{5,13},{6,14},{7,15},{8,0},{9,1},... | collective-permute-start | bytes 196616 | tf_op jit(solution)/shard_map/ppermute | solution.py:357
  9.9 6.7 %collective-permute-start.1 = (bf16[32,8,128]{2,1,0:T(8,128)(2,1)S(1)}, bf16[32,8,128]{2,1,0:T(8,128)(2,1)S(1)}, u32[]{:S(2)}, u32[]{:S(2)}) collective-permute-start(bf16[32,8,128]{2,1,0:T(8,128)(2,1)S(1)} %shard_map.76.state), channel_id=1, source_target_pairs={{0,4},{1,5},{2,6},{3,7},{4,0},{5,1},{6,2},{7,3},{8,12},{9,13},{10,... | collective-permute-start | bytes 196616 | tf_op jit(solution)/shard_map/ppermute | solution.py:357
  11.9 6.7 %copy-start.1 = (bf16[4,32,64,256]{3,2,1,0:T(8,128)(2,1)S(1)}, bf16[4,32,64,256]{3,2,1,0:T(8,128)(2,1)}, u32[]{:S(2)}) copy-start(bf16[4,32,64,256]{3,2,1,0:T(8,128)(2,1)} %blocks.15) | copy-start | bytes 12582916
  14.4 4.2 %copy-start.3 = (s32[4,2,256]{2,1,0:T(2,128)S(1)}, s32[4,2,256]{2,1,0:T(2,128)}, u32[]{:S(2)}) copy-start(s32[4,2,256]{2,1,0:T(2,128)} %pattern.53) | copy-start | bytes 24580
  14.4 4.8 %collective-permute-start.4 = (bf16[32,8,128]{2,1,0:T(8,128)(2,1)S(1)}, bf16[32,8,128]{2,1,0:T(8,128)(2,1)S(1)}, u32[]{:S(2)}, u32[]{:S(2)}) collective-permute-start(bf16[32,8,128]{2,1,0:T(8,128)(2,1)S(1)} %shard_map.80.rest_0_.state), channel_id=1, source_target_pairs={{0,4},{1,5},{2,6},{3,7},{4,0},{5,1},{6,2},{7,3},{8,12},{9,13},{10,... | collective-permute-start | bytes 196616 | tf_op jit(solution)/shard_map/ppermute | solution.py:357
  17.0 4.3 %collective-permute-start.3 = (bf16[32,8,128]{2,1,0:T(8,128)(2,1)S(1)}, bf16[32,8,128]{2,1,0:T(8,128)(2,1)S(1)}, u32[]{:S(2)}, u32[]{:S(2)}) collective-permute-start(bf16[32,8,128]{2,1,0:T(8,128)(2,1)S(1)} %shard_map.82.state), channel_id=1, source_target_pairs={{0,2},{1,3},{2,0},{3,1},{4,6},{5,7},{6,4},{7,5},{8,10},{9,11},{10,... | collective-permute-start | bytes 196616 | tf_op jit(solution)/shard_map/ppermute | solution.py:357
  21.7 2.8 %collective-permute-start.5 = (bf16[68,64,128]{2,1,0:T(8,128)(2,1)S(1)}, bf16[68,64,128]{2,1,0:T(8,128)(2,1)S(1)}, u32[]{:S(2)}, u32[]{:S(2)}) collective-permute-start(bf16[68,64,128]{2,1,0:T(8,128)(2,1)S(1)} %shard_map.87), channel_id=1, source_target_pairs={{0,1},{1,0},{2,3},{3,2},{4,5},{5,4},{6,7},{7,6},{8,9},{9,8},{10,11... | collective-permute-start | bytes 3342344 | tf_op jit(solution)/shard_map/ppermute | solution.py:357
  21.8 4.5 %collective-permute-start.6 = (bf16[32,8,128]{2,1,0:T(8,128)(2,1)S(1)}, bf16[32,8,128]{2,1,0:T(8,128)(2,1)S(1)}, u32[]{:S(2)}, u32[]{:S(2)}) collective-permute-start(bf16[32,8,128]{2,1,0:T(8,128)(2,1)S(1)} %shard_map.84.rest_0_.state), channel_id=1, source_target_pairs={{0,2},{1,3},{2,0},{3,1},{4,6},{5,7},{6,4},{7,5},{8,10},{9,11},{10,... | collective-permute-start | bytes 196616 | tf_op jit(solution)/shard_map/ppermute | solution.py:357
  26.3 5.8 %copy-start.4 = (bf16[64,32,256]{2,1,0:T(8,128)(2,1)S(1)}, bf16[64,32,256]{2,1,0:T(8,128)(2,1)}, u32[]{:S(2)}) copy-start(bf16[64,32,256]{2,1,0:T(8,128)(2,1)} %interp.5) | copy-start | bytes 3145732
  27.8 5.8 %collective-permute-start.8 = (bf16[2,2,32,128]{3,2,1,0:T(8,128)(2,1)S(1)}, bf16[2,2,32,128]{3,2,1,0:T(8,128)(2,1)S(1)}, u32[]{:S(2)}, u32[]{:S(2)}) collective-permute-start(bf16[2,2,32,128]{3,2,1,0:T(8,128)(2,1)S(1)} %get-tuple-element.61), channel_id=1, source_target_pairs={{0,2},{1,10},{2,0},{3,8},{4,6},{5,14},{6,4},{7,12},{8,3},{9,11},{1... | collective-permute-start | bytes 98312 | tf_op jit(solution)/shard_map/ppermute | solution.py:357
  29.4 4.2 %collective-permute-start.9 = (bf16[2,2,32,128]{3,2,1,0:T(8,128)(2,1)S(1)}, bf16[2,2,32,128]{3,2,1,0:T(8,128)(2,1)S(1)}, u32[]{:S(2)}, u32[]{:S(2)}) collective-permute-start(bf16[2,2,32,128]{3,2,1,0:T(8,128)(2,1)S(1)} %get-tuple-element.62), channel_id=1, source_target_pairs={{0,4},{1,12},{2,6},{3,14},{4,0},{5,8},{6,2},{7,10},{8,5},{9,13},{1... | collective-permute-start | bytes 98312 | tf_op jit(solution)/shard_map/ppermute | solution.py:357
  29.6 4.9 %collective-permute-start.10 = (bf16[2,2,32,128]{3,2,1,0:T(8,128)(2,1)S(1)}, bf16[2,2,32,128]{3,2,1,0:T(8,128)(2,1)S(1)}, u32[]{:S(2)}, u32[]{:S(2)}) collective-permute-start(bf16[2,2,32,128]{3,2,1,0:T(8,128)(2,1)S(1)} %get-tuple-element.63), channel_id=1, source_target_pairs={{0,6},{1,14},{2,4},{3,12},{4,2},{5,10},{6,0},{7,8},{8,7},{9,15},{1... | collective-permute-start | bytes 98312 | tf_op jit(solution)/shard_map/ppermute | solution.py:357
  31.4 3.0 %collective-permute-start.7 = (bf16[2,2,32,128]{3,2,1,0:T(8,128)(2,1)S(1)}, bf16[2,2,32,128]{3,2,1,0:T(8,128)(2,1)S(1)}, u32[]{:S(2)}, u32[]{:S(2)}) collective-permute-start(bf16[2,2,32,128]{3,2,1,0:T(8,128)(2,1)S(1)} %get-tuple-element.57.rest_0_.kept), channel_id=1, source_target_pairs={{1,8},{3,10},{5,12},{7,14},{8,1},{10,3},{12,5},{14,7},{17,24},{19,... | collective-permute-start | bytes 98312 | tf_op jit(solution)/shard_map/ppermute | solution.py:357
  35.4 7.1 %collective-permute-start.11 = (bf16[32,8,128]{2,1,0:T(8,128)(2,1)S(1)}, bf16[32,8,128]{2,1,0:T(8,128)(2,1)S(1)}, u32[]{:S(2)}, u32[]{:S(2)}) collective-permute-start(bf16[32,8,128]{2,1,0:T(8,128)(2,1)S(1)} %get-tuple-element.76), channel_id=1, source_target_pairs={{0,1},{1,0},{2,3},{3,2},{4,5},{5,4},{6,7},{7,6},{8,9},{9,8},{10,11... | collective-permute-start | bytes 196616 | tf_op jit(solution)/shard_map/ppermute | solution.py:357
  40.7 4.6 %collective-permute-start.15 = (bf16[32,8,128]{2,1,0:T(8,128)(2,1)S(1)}, bf16[32,8,128]{2,1,0:T(8,128)(2,1)S(1)}, u32[]{:S(2)}, u32[]{:S(2)}) collective-permute-start(bf16[32,8,128]{2,1,0:T(8,128)(2,1)S(1)} %shard_map.103.state), channel_id=1, source_target_pairs={{0,2},{1,3},{2,0},{3,1},{4,6},{5,7},{6,4},{7,5},{8,10},{9,11},{10,... | collective-permute-start | bytes 196616 | tf_op jit(solution)/shard_map/ppermute | solution.py:357
  42.5 4.3 %collective-permute-start.12 = (bf16[32,8,128]{2,1,0:T(8,128)(2,1)S(1)}, bf16[32,8,128]{2,1,0:T(8,128)(2,1)S(1)}, u32[]{:S(2)}, u32[]{:S(2)}) collective-permute-start(bf16[32,8,128]{2,1,0:T(8,128)(2,1)S(1)} %collective-permute-done.11.state.rest_0_), channel_id=1, source_target_pairs={{0,2},{1,3},{2,0},{3,1},{4,6},{5,7},{6,4},{7,5},{8,10},{9,11},{10,... | collective-permute-start | bytes 196616 | tf_op jit(solution)/shard_map/ppermute | solution.py:357
  45.7 4.3 %collective-permute-start.16 = (bf16[32,8,128]{2,1,0:T(8,128)(2,1)S(1)}, bf16[32,8,128]{2,1,0:T(8,128)(2,1)S(1)}, u32[]{:S(2)}, u32[]{:S(2)}) collective-permute-start(bf16[32,8,128]{2,1,0:T(8,128)(2,1)S(1)} %shard_map.105.state), channel_id=1, source_target_pairs={{0,4},{1,5},{2,6},{3,7},{4,0},{5,1},{6,2},{7,3},{8,12},{9,13},{10,... | collective-permute-start | bytes 196616 | tf_op jit(solution)/shard_map/ppermute | solution.py:357
  47.1 4.5 %collective-permute-start.13 = (bf16[32,8,128]{2,1,0:T(8,128)(2,1)S(1)}, bf16[32,8,128]{2,1,0:T(8,128)(2,1)S(1)}, u32[]{:S(2)}, u32[]{:S(2)}) collective-permute-start(bf16[32,8,128]{2,1,0:T(8,128)(2,1)S(1)} %shard_map.99.state.rest_0_), channel_id=1, source_target_pairs={{0,4},{1,5},{2,6},{3,7},{4,0},{5,1},{6,2},{7,3},{8,12},{9,13},{10,... | collective-permute-start | bytes 196616 | tf_op jit(solution)/shard_map/ppermute | solution.py:357
  50.3 6.3 %collective-permute-start.17 = (bf16[32,8,128]{2,1,0:T(8,128)(2,1)S(1)}, bf16[32,8,128]{2,1,0:T(8,128)(2,1)S(1)}, u32[]{:S(2)}, u32[]{:S(2)}) collective-permute-start(bf16[32,8,128]{2,1,0:T(8,128)(2,1)S(1)} %shard_map.107.state), channel_id=1, source_target_pairs={{0,8},{1,9},{2,10},{3,11},{4,12},{5,13},{6,14},{7,15},{8,0},{9,1},... | collective-permute-start | bytes 196616 | tf_op jit(solution)/shard_map/ppermute | solution.py:357
  52.0 5.7 %collective-permute-start.14 = (bf16[32,8,128]{2,1,0:T(8,128)(2,1)S(1)}, bf16[32,8,128]{2,1,0:T(8,128)(2,1)S(1)}, u32[]{:S(2)}, u32[]{:S(2)}) collective-permute-start(bf16[32,8,128]{2,1,0:T(8,128)(2,1)S(1)} %shard_map.101.state.rest_0_), channel_id=1, source_target_pairs={{0,8},{1,9},{2,10},{3,11},{4,12},{5,13},{6,14},{7,15},{8,0},{9,1},... | collective-permute-start | bytes 196616 | tf_op jit(solution)/shard_map/ppermute | solution.py:357

commit v14 on v13

--- a/solution.py
+++ b/solution.py
@@ -9,6 +9,7 @@
 
 LANES = 128
 GROUP = 4
+TURNS = (1, 3, 2, 0)
 ROWS = 8
 KERNEL_COST = 2**19
 KERNEL_LIMIT = 16 * 2**20
@@ -232,7 +233,7 @@
         for place, piece in enumerate(pieces):
             packed[core ^ box, place] = piece
     for turn, out in enumerate(outs):
-        first = ((mid ^ (turn // 2)) * 2 + (low ^ (turn % 2))) * 2
+        first = ((mid ^ (TURNS[turn] // 2)) * 2 + (low ^ (TURNS[turn] % 2))) * 2
         for box in range(2):
             for last in range(2):
                 out[box, last] = packed[box, first + last]
@@ -268,11 +269,11 @@
     fold = LANES // slot
     depth = out.shape[0] // fold
     for turn, piece in enumerate(pieces):
-        first = ((mid ^ (turn // 2)) * 2 + (low ^ (turn % 2))) * 2
+        first = ((mid ^ (TURNS[turn] // 2)) * 2 + (low ^ (TURNS[turn] % 2))) * 2
         for box in range(2):
             for last in range(2):
                 value = piece[box, last]
-                if turn == 0:
+                if TURNS[turn] == 0:
                     value = jnp.where(high == core, kept[box, last], value)
                 packed[last, first + box] = value
     for last in range(2):
@@ -363,7 +364,7 @@
 
 def crossed(source, turn):
     high, mid, low, core = source // 8 % 2, source // 4 % 2, source // 2 % 2, source % 2
-    return ((core * 2 + (mid ^ (turn // 2))) * 2 + (low ^ (turn % 2))) * 2 + high
+    return ((core * 2 + (mid ^ (TURNS[turn] // 2))) * 2 + (low ^ (TURNS[turn] % 2))) * 2 + high
 
 
 def fast_local(samples, interp_in, top_blocks, top_pattern, bottom_blocks, bottom_pattern, interp_out):
@@ -455,7 +456,7 @@
         functools.partial(pair_near_kernel, 3, slot), [piece] * 4,
         (top_pattern, near_wide, current[0], pair_far), (total, packed), 2,
     )
-    kept = pieces[0]
+    kept = pieces[TURNS.index(0)]
     pieces = [permuted(value, functools.partial(crossed, turn=turn)) for turn, value in enumerate(pieces)]
     own_wide, other_wide = run(wide_kernel, [pair_spread] * 2, (bottom_blocks, shared))
     wides = {level: level_wides(bottom_blocks, level, level, kept) for level in (1, 2, 3)}

time: 59.5 us -> 59.5 us (level)
  no operation moved by 1% of the time
where the time goes in v14:
time: 59.5 us; the launch traced here: 59.4 us
  starting transfers between devices  26.1 us (44%)
  Pallas kernels  20.6 us (35%)
  waiting for transfers between devices  12.3 us (21%)
    ppermute x18, starting transfers between devices, permuted(): return lax.ppermute(value, 'leaf', pairs)  26.1 us
    pallas_call x38, Pallas kernels, run(): pl.pallas_call(kernel, out_shape=shapes, in_specs=in_specs or [whole] * l...  20.6 us
    ppermute x18, waiting for transfers between devices, permuted(): return lax.ppermute(value, 'leaf', pairs)  12.3 us
  transfers between devices with their start and end apart: 18, of which 11 were waited for; matrix products, arithmetic and copies ran while one was open for 0% of the time, Pallas kernels for 24%

profile of v14, /device:TPU:0, one launch (start us, length us, event | category | flops | bytes accessed | tf_op | source)
XLA Modules:
  0.0 59.4 jit_solution(10555099668024402008)
XLA Ops:
  0.0 1.8 %shard_map.73.after.state = bf16[32,8,128]{2,1,0:T(8,128)(2,1)S(1)} custom-call(bf16[32,64,256]{2,1,0:T(8,128)(2,1)} %interp.4, bf16[64,8,256]{2,1,0:T(8,128)(2,1)} %samples.3), custom_call_target="tpu_custom_call" | custom-call | flops 1048576 | bytes 1048576 | tf_op jit(solution)/shard_map/pallas_call | solution.py:342
  1.8 4.1 %collective-permute-start = (bf16[32,8,128]{2,1,0:T(8,128)(2,1)S(1)}, bf16[32,8,128]{2,1,0:T(8,128)(2,1)S(1)}, u32[]{:S(2)}, u32[]{:S(2)}) collective-permute-start(bf16[32,8,128]{2,1,0:T(8,128)(2,1)S(1)} %shard_map.73.after.state), channel_id=1, source_target_pairs={{0,8},{1,9},{2,10},{3,11},{4,12},{5,13},{6,14},{7,15},{8,0},{9,1},... | collective-permute-start | bytes 196616 | tf_op jit(solution)/shard_map/ppermute | solution.py:358
  5.9 2.5 %shard_map.74 = (bf16[32,8,128]{2,1,0:T(8,128)(2,1)S(1)}, f32[1024,128]{1,0:T(8,128)S(1)}, f32[1024,128]{1,0:T(8,128)S(1)}, f32[1024,128]{1,0:T(8,128)S(1)}, f32[1024,128]{1,0:T(8,128)S(1)}) custom-call(bf16[4,32,64,256]{3,2,1,0:T(8,128)(2,1)} %blocks.11, bf16[32,64,256]{2,1,0:T(8,128)(2,1)} %interp.4, bf16[64,8,256]{2,1,0:T(8,128)(2,1)S(1)} %copy-done.5, ...), custom_call_target="tpu_custom_call" | custom-call | flops 2097152 | bytes 2097152 | tf_op jit(solution)/shard_map/pallas_call | solution.py:342
  8.6 0.3 shard_map.75.near
  8.9 0.7 %collective-permute-done.partner = bf16[32,8,128]{2,1,0:T(8,128)(2,1)S(1)} collective-permute-done((bf16[32,8,128]{2,1,0:T(8,128)(2,1)S(1)}, bf16[32,8,128]{2,1,0:T(8,128)(2,1)S(1)}, u32[]{:S(2)}, u32[]{:S(2)}) %collective-permute-start) | collective-permute-done | bytes 65568 | tf_op jit(solution)/shard_map/ppermute | solution.py:358
  9.6 0.4 shard_map.76.state
  9.9 1.3 %collective-permute-start.1 = (bf16[32,8,128]{2,1,0:T(8,128)(2,1)S(1)}, bf16[32,8,128]{2,1,0:T(8,128)(2,1)S(1)}, u32[]{:S(2)}, u32[]{:S(2)}) collective-permute-start(bf16[32,8,128]{2,1,0:T(8,128)(2,1)S(1)} %shard_map.76.state), channel_id=1, source_target_pairs={{0,4},{1,5},{2,6},{3,7},{4,0},{5,1},{6,2},{7,3},{8,12},{9,13},{10,... | collective-permute-start | bytes 196616 | tf_op jit(solution)/shard_map/ppermute | solution.py:358
  11.2 0.3 shard_map.77.rest_0_.near
  11.6 0.3 shard_map.79
  11.9 0.3 shard_map.78
  12.3 1.8 %collective-permute-done.2.partner = bf16[32,8,128]{2,1,0:T(8,128)(2,1)S(1)} collective-permute-done((bf16[32,8,128]{2,1,0:T(8,128)(2,1)S(1)}, bf16[32,8,128]{2,1,0:T(8,128)(2,1)S(1)}, u32[]{:S(2)}, u32[]{:S(2)}) %collective-permute-start.2) | collective-permute-done | bytes 65568 | tf_op jit(solution)/shard_map/ppermute | solution.py:358
  14.0 0.4 shard_map.80.rest_0_.state
  14.4 1.9 %collective-permute-start.4 = (bf16[32,8,128]{2,1,0:T(8,128)(2,1)S(1)}, bf16[32,8,128]{2,1,0:T(8,128)(2,1)S(1)}, u32[]{:S(2)}, u32[]{:S(2)}) collective-permute-start(bf16[32,8,128]{2,1,0:T(8,128)(2,1)S(1)} %shard_map.80.rest_0_.state), channel_id=1, source_target_pairs={{0,4},{1,5},{2,6},{3,7},{4,0},{5,1},{6,2},{7,3},{8,12},{9,13},{10,... | collective-permute-start | bytes 196616 | tf_op jit(solution)/shard_map/ppermute | solution.py:358
  16.3 0.3 shard_map.81.near
  16.7 0.4 shard_map.82.state
  17.0 1.6 %collective-permute-start.3 = (bf16[32,8,128]{2,1,0:T(8,128)(2,1)S(1)}, bf16[32,8,128]{2,1,0:T(8,128)(2,1)S(1)}, u32[]{:S(2)}, u32[]{:S(2)}) collective-permute-start(bf16[32,8,128]{2,1,0:T(8,128)(2,1)S(1)} %shard_map.82.state), channel_id=1, source_target_pairs={{0,2},{1,3},{2,0},{3,1},{4,6},{5,7},{6,4},{7,5},{8,10},{9,11},{10,... | collective-permute-start | bytes 196616 | tf_op jit(solution)/shard_map/ppermute | solution.py:358
  18.6 0.2 shard_map.86.shared
  18.9 0.4 shard_map.83.near
  19.2 0.4 shard_map.84.rest_0_.state
  19.6 0.4 shard_map.85.near
  20.0 1.4 %collective-permute-done.3.partner = bf16[32,8,128]{2,1,0:T(8,128)(2,1)S(1)} collective-permute-done((bf16[32,8,128]{2,1,0:T(8,128)(2,1)S(1)}, bf16[32,8,128]{2,1,0:T(8,128)(2,1)S(1)}, u32[]{:S(2)}, u32[]{:S(2)}) %collective-permute-start.3) | collective-permute-done | bytes 65568 | tf_op jit(solution)/shard_map/ppermute | solution.py:358
  21.4 0.3 shard_map.87
  21.8 1.6 %collective-permute-start.6 = (bf16[32,8,128]{2,1,0:T(8,128)(2,1)S(1)}, bf16[32,8,128]{2,1,0:T(8,128)(2,1)S(1)}, u32[]{:S(2)}, u32[]{:S(2)}) collective-permute-start(bf16[32,8,128]{2,1,0:T(8,128)(2,1)S(1)} %shard_map.84.rest_0_.state), channel_id=1, source_target_pairs={{0,2},{1,3},{2,0},{3,1},{4,6},{5,7},{6,4},{7,5},{8,10},{9,11},{10,... | collective-permute-start | bytes 196616 | tf_op jit(solution)/shard_map/ppermute | solution.py:358
  23.4 0.3 shard_map.89.near
  23.7 0.8 %collective-permute-done.5.shared = bf16[68,64,128]{2,1,0:T(8,128)(2,1)S(1)} collective-permute-done((bf16[68,64,128]{2,1,0:T(8,128)(2,1)S(1)}, bf16[68,64,128]{2,1,0:T(8,128)(2,1)S(1)}, u32[]{:S(2)}, u32[]{:S(2)}) %collective-permute-start.5) | collective-permute-done | bytes 1114144 | tf_op jit(solution)/shard_map/ppermute | solution.py:358
  24.5 0.9 %shard_map.88 = (f32[2,32,8,128]{3,2,1,0:T(8,128)S(1)}, f32[2,1024,128]{2,1,0:T(8,128)S(1)}) custom-call(bf16[4,32,64,256]{3,2,1,0:T(8,128)(2,1)S(1)} %copy-done, s32[4,2,256]{2,1,0:T(2,128)S(1)} %copy-done.2, bf16[68,64,128]{2,1,0:T(8,128)(2,1)S(1)} %collective-permute-done.5.shared), custom_call_target="tpu_custom_call" | custom-call | flops 1048576 | bytes 1048576 | tf_op jit(solution)/shard_map/pallas_call | solution.py:342
  25.5 0.8 %collective-permute-done.6.partner = bf16[32,8,128]{2,1,0:T(8,128)(2,1)S(1)} collective-permute-done((bf16[32,8,128]{2,1,0:T(8,128)(2,1)S(1)}, bf16[32,8,128]{2,1,0:T(8,128)(2,1)S(1)}, u32[]{:S(2)}, u32[]{:S(2)}) %collective-permute-start.6) | collective-permute-done | bytes 65568 | tf_op jit(solution)/shard_map/ppermute | solution.py:358
  26.3 0.4 shard_map.90.state
  26.7 1.2 %shard_map.91 = (bf16[2,2,32,128]{3,2,1,0:T(8,128)(2,1)S(1)}, bf16[2,2,32,128]{3,2,1,0:T(8,128)(2,1)S(1)}, bf16[2,2,32,128]{3,2,1,0:T(8,128)(2,1)S(1)}, bf16[2,2,32,128]{3,2,1,0:T(8,128)(2,1)S(1)}) custom-call(s32[4,2,256]{2,1,0:T(2,128)S(1)} %copy-done.2, f32[2,1024,128]{2,1,0:T(8,128)S(1)} %get-tuple-element.54.wide, ...), custom_call_target="tpu_custom_call" | custom-call | flops 1048576 | bytes 1048576 | tf_op jit(solution)/shard_map/pallas_call | solution.py:342
  27.8 1.6 %collective-permute-start.7 = (bf16[2,2,32,128]{3,2,1,0:T(8,128)(2,1)S(1)}, bf16[2,2,32,128]{3,2,1,0:T(8,128)(2,1)S(1)}, u32[]{:S(2)}, u32[]{:S(2)}) collective-permute-start(bf16[2,2,32,128]{3,2,1,0:T(8,128)(2,1)S(1)} %get-tuple-element.61), channel_id=1, source_target_pairs={{0,2},{1,10},{2,0},{3,8},{4,6},{5,14},{6,4},{7,12},{8,3},{9,11},{1... | collective-permute-start | bytes 98312 | tf_op jit(solution)/shard_map/ppermute | solution.py:358
  29.5 1.9 %collective-permute-start.9 = (bf16[2,2,32,128]{3,2,1,0:T(8,128)(2,1)S(1)}, bf16[2,2,32,128]{3,2,1,0:T(8,128)(2,1)S(1)}, u32[]{:S(2)}, u32[]{:S(2)}) collective-permute-start(bf16[2,2,32,128]{3,2,1,0:T(8,128)(2,1)S(1)} %get-tuple-element.63), channel_id=1, source_target_pairs={{0,4},{1,12},{2,6},{3,14},{4,0},{5,8},{6,2},{7,10},{8,5},{9,13},{1... | collective-permute-start | bytes 98312 | tf_op jit(solution)/shard_map/ppermute | solution.py:358
  31.4 0.7 %collective-permute-start.10 = (bf16[2,2,32,128]{3,2,1,0:T(8,128)(2,1)S(1)}, bf16[2,2,32,128]{3,2,1,0:T(8,128)(2,1)S(1)}, u32[]{:S(2)}, u32[]{:S(2)}) collective-permute-start(bf16[2,2,32,128]{3,2,1,0:T(8,128)(2,1)S(1)} %get-tuple-element.57.rest_0_.kept), channel_id=1, source_target_pairs={{1,8},{3,10},{5,12},{7,14},{8,1},{10,3},{12,5},{14,7},{17,24},{19,... | collective-permute-start | bytes 98312 | tf_op jit(solution)/shard_map/ppermute | solution.py:358
  32.1 0.3 shard_map.93
  32.4 0.3 shard_map.94
  32.6 0.3 shard_map.96
  33.0 0.3 shard_map.95
  33.3 0.3 shard_map.92
  33.6 0.6 %collective-permute-done.8.rest_1_ = bf16[2,2,32,128]{3,2,1,0:T(8,128)(2,1)S(1)} collective-permute-done((bf16[2,2,32,128]{3,2,1,0:T(8,128)(2,1)S(1)}, bf16[2,2,32,128]{3,2,1,0:T(8,128)(2,1)S(1)}, u32[]{:S(2)}, u32[]{:S(2)}) %collective-permute-start.8) | collective-permute-done | bytes 32800 | tf_op jit(solution)/shard_map/ppermute | solution.py:358
  34.2 0.9 %shard_map.97 = (bf16[32,8,128]{2,1,0:T(8,128)(2,1)S(1)}, bf16[2,32,8,128]{3,2,1,0:T(8,128)(2,1)S(1)}) custom-call(f32[2,1024,128]{2,1,0:T(8,128)S(1)} %get-tuple-element.60.wide, bf16[2,2,32,128]{3,2,1,0:T(8,128)(2,1)S(1)} %get-tuple-element.57.rest_0_.kept, bf16[2,2,32,128]{3,2,1,0:T(8,128)(2,1)S(1)} %collective-permute-done.7.rest_0_, ...), custom_call_target="tpu_custom_call" | custom-call | flops 1048576 | bytes 1048576 | tf_op jit(solution)/shard_map/pallas_call | solution.py:342
  35.2 4.9 %collective-permute-start.11 = (bf16[32,8,128]{2,1,0:T(8,128)(2,1)S(1)}, bf16[32,8,128]{2,1,0:T(8,128)(2,1)S(1)}, u32[]{:S(2)}, u32[]{:S(2)}) collective-permute-start(bf16[32,8,128]{2,1,0:T(8,128)(2,1)S(1)} %get-tuple-element.76), channel_id=1, source_target_pairs={{0,1},{1,0},{2,3},{3,2},{4,5},{5,4},{6,7},{7,6},{8,9},{9,8},{10,11... | collective-permute-start | bytes 196616 | tf_op jit(solution)/shard_map/ppermute | solution.py:358
  40.1 0.7 %shard_map.103.state = bf16[32,8,128]{2,1,0:T(8,128)(2,1)S(1)} custom-call(s32[4,2,256]{2,1,0:T(2,128)S(1)} %copy-done.3, f32[2,1024,128]{2,1,0:T(8,128)S(1)} %get-tuple-element.77.wide, bf16[2,32,8,128]{3,2,1,0:T(8,128)(2,1)S(1)} %get-tuple-element.78.states), custom_call_target="tpu_custom_call" | custom-call | flops 1048576 | bytes 1048576 | tf_op jit(solution)/shard_map/pallas_call | solution.py:342
  40.7 1.8 %collective-permute-start.15 = (bf16[32,8,128]{2,1,0:T(8,128)(2,1)S(1)}, bf16[32,8,128]{2,1,0:T(8,128)(2,1)S(1)}, u32[]{:S(2)}, u32[]{:S(2)}) collective-permute-start(bf16[32,8,128]{2,1,0:T(8,128)(2,1)S(1)} %shard_map.103.state), channel_id=1, source_target_pairs={{0,2},{1,3},{2,0},{3,1},{4,6},{5,7},{6,4},{7,5},{8,10},{9,11},{10,... | collective-permute-start | bytes 196616 | tf_op jit(solution)/shard_map/ppermute | solution.py:358
  42.5 0.3 collective-permute-start.12
  42.8 0.3 shard_map.104.near
  43.1 2.2 %collective-permute-done.15.partner = bf16[32,8,128]{2,1,0:T(8,128)(2,1)S(1)} collective-permute-done((bf16[32,8,128]{2,1,0:T(8,128)(2,1)S(1)}, bf16[32,8,128]{2,1,0:T(8,128)(2,1)S(1)}, u32[]{:S(2)}, u32[]{:S(2)}) %collective-permute-start.15) | collective-permute-done | bytes 65568 | tf_op jit(solution)/shard_map/ppermute | solution.py:358
  45.3 0.3 shard_map.105.state
  45.7 0.2 collective-permute-start.16
  45.8 0.3 shard_map.98.near
  46.2 0.6 %collective-permute-done.12.partner = bf16[32,8,128]{2,1,0:T(8,128)(2,1)S(1)} collective-permute-done((bf16[32,8,128]{2,1,0:T(8,128)(2,1)S(1)}, bf16[32,8,128]{2,1,0:T(8,128)(2,1)S(1)}, u32[]{:S(2)}, u32[]{:S(2)}) %collective-permute-start.12) | collective-permute-done | bytes 65568 | tf_op jit(solution)/shard_map/ppermute | solution.py:358
  46.8 0.3 shard_map.99.state.rest_0_
  47.1 1.4 %collective-permute-start.13 = (bf16[32,8,128]{2,1,0:T(8,128)(2,1)S(1)}, bf16[32,8,128]{2,1,0:T(8,128)(2,1)S(1)}, u32[]{:S(2)}, u32[]{:S(2)}) collective-permute-start(bf16[32,8,128]{2,1,0:T(8,128)(2,1)S(1)} %shard_map.99.state.rest_0_), channel_id=1, source_target_pairs={{0,4},{1,5},{2,6},{3,7},{4,0},{5,1},{6,2},{7,3},{8,12},{9,13},{10,... | collective-permute-start | bytes 196616 | tf_op jit(solution)/shard_map/ppermute | solution.py:358
  48.5 0.3 shard_map.106.near
  48.8 1.2 %collective-permute-done.16.partner = bf16[32,8,128]{2,1,0:T(8,128)(2,1)S(1)} collective-permute-done((bf16[32,8,128]{2,1,0:T(8,128)(2,1)S(1)}, bf16[32,8,128]{2,1,0:T(8,128)(2,1)S(1)}, u32[]{:S(2)}, u32[]{:S(2)}) %collective-permute-start.16) | collective-permute-done | bytes 65568 | tf_op jit(solution)/shard_map/ppermute | solution.py:358
  50.0 0.3 shard_map.107.state
  50.3 0.7 %collective-permute-start.17 = (bf16[32,8,128]{2,1,0:T(8,128)(2,1)S(1)}, bf16[32,8,128]{2,1,0:T(8,128)(2,1)S(1)}, u32[]{:S(2)}, u32[]{:S(2)}) collective-permute-start(bf16[32,8,128]{2,1,0:T(8,128)(2,1)S(1)} %shard_map.107.state), channel_id=1, source_target_pairs={{0,8},{1,9},{2,10},{3,11},{4,12},{5,13},{6,14},{7,15},{8,0},{9,1},... | collective-permute-start | bytes 196616 | tf_op jit(solution)/shard_map/ppermute | solution.py:358
  51.0 0.3 shard_map.100.near
  51.3 0.3 collective-permute-done.13.partner
  51.7 0.3 shard_map.101.state.rest_0_
  52.0 2.1 %collective-permute-start.14 = (bf16[32,8,128]{2,1,0:T(8,128)(2,1)S(1)}, bf16[32,8,128]{2,1,0:T(8,128)(2,1)S(1)}, u32[]{:S(2)}, u32[]{:S(2)}) collective-permute-start(bf16[32,8,128]{2,1,0:T(8,128)(2,1)S(1)} %shard_map.101.state.rest_0_), channel_id=1, source_target_pairs={{0,8},{1,9},{2,10},{3,11},{4,12},{5,13},{6,14},{7,15},{8,0},{9,1},... | collective-permute-start | bytes 196616 | tf_op jit(solution)/shard_map/ppermute | solution.py:358
  54.1 0.3 shard_map.102.near
  54.4 0.3 shard_map.108.near
  54.7 1.9 %collective-permute-done.17.partner = bf16[32,8,128]{2,1,0:T(8,128)(2,1)S(1)} collective-permute-done((bf16[32,8,128]{2,1,0:T(8,128)(2,1)S(1)}, bf16[32,8,128]{2,1,0:T(8,128)(2,1)S(1)}, u32[]{:S(2)}, u32[]{:S(2)}) %collective-permute-start.17) | collective-permute-done | bytes 65568 | tf_op jit(solution)/shard_map/ppermute | solution.py:358
  56.7 1.0 %shard_map.109.ready = bf16[64,8,128]{2,1,0:T(8,128)(2,1)S(1)} custom-call(s32[4,2,256]{2,1,0:T(2,128)S(1)} %copy-done.3, f32[1024,128]{1,0:T(8,128)S(1)} %get-tuple-element.74.rest_14_.wide, f32[2048,128]{1,0:T(8,128)S(1)} %get-tuple-element.75.rest_16_.image_wide, bf16[32,8,128]{2,1,0:T(8,128)(2,1)S(1)} %collective-permute-done.17.partner, ...), custom_call_target="tpu_custom_call" | custom-call | flops 1572864 | bytes 1572864 | tf_op jit(solution)/shard_map/pallas_call | solution.py:342
  57.7 1.7 %shard_map.110 = bf16[64,8,256]{2,1,0:T(8,128)(2,1)} custom-call(s32[4,2,256]{2,1,0:T(2,128)S(1)} %copy-done.3, f32[1024,128]{1,0:T(8,128)S(1)} %get-tuple-element.58.rest_15_.wide, f32[2048,128]{1,0:T(8,128)S(1)} %get-tuple-element.59.rest_17_.image_wide, bf16[32,8,128]{2,1,0:T(8,128)(2,1)S(1)} %collective-permute-done.14.partner, ...), custom_call_target="tpu_custom_call" | custom-call | flops 1572864 | bytes 1572864 | tf_op jit(solution)/shard_map/pallas_call | solution.py:342
  (22 shorter events, 0.3 us)
Async XLA Ops:
  0.0 5.9 %copy-start.5 = (bf16[64,8,256]{2,1,0:T(8,128)(2,1)S(1)}, bf16[64,8,256]{2,1,0:T(8,128)(2,1)}, u32[]{:S(2)}) copy-start(bf16[64,8,256]{2,1,0:T(8,128)(2,1)} %samples.3) | copy-start | bytes 786436
  1.8 6.8 %copy-start.2 = (s32[4,2,256]{2,1,0:T(2,128)S(1)}, s32[4,2,256]{2,1,0:T(2,128)}, u32[]{:S(2)}) copy-start(s32[4,2,256]{2,1,0:T(2,128)} %pattern.40) | copy-start | bytes 24580
  1.8 7.8 %collective-permute-start = (bf16[32,8,128]{2,1,0:T(8,128)(2,1)S(1)}, bf16[32,8,128]{2,1,0:T(8,128)(2,1)S(1)}, u32[]{:S(2)}, u32[]{:S(2)}) collective-permute-start(bf16[32,8,128]{2,1,0:T(8,128)(2,1)S(1)} %shard_map.73.after.state), channel_id=1, source_target_pairs={{0,8},{1,9},{2,10},{3,11},{4,12},{5,13},{6,14},{7,15},{8,0},{9,1},... | collective-permute-start | bytes 196616 | tf_op jit(solution)/shard_map/ppermute | solution.py:358
  5.9 5.7 %copy-start = (bf16[4,32,64,256]{3,2,1,0:T(8,128)(2,1)S(1)}, bf16[4,32,64,256]{3,2,1,0:T(8,128)(2,1)}, u32[]{:S(2)}) copy-start(bf16[4,32,64,256]{3,2,1,0:T(8,128)(2,1)} %blocks.11) | copy-start | bytes 12582916
  8.5 5.6 %collective-permute-start.2 = (bf16[32,8,128]{2,1,0:T(8,128)(2,1)S(1)}, bf16[32,8,128]{2,1,0:T(8,128)(2,1)S(1)}, u32[]{:S(2)}, u32[]{:S(2)}) collective-permute-start(bf16[32,8,128]{2,1,0:T(8,128)(2,1)S(1)} %get-tuple-element.44.state), channel_id=1, source_target_pairs={{0,8},{1,9},{2,10},{3,11},{4,12},{5,13},{6,14},{7,15},{8,0},{9,1},... | collective-permute-start | bytes 196616 | tf_op jit(solution)/shard_map/ppermute | solution.py:358
  9.9 6.7 %collective-permute-start.1 = (bf16[32,8,128]{2,1,0:T(8,128)(2,1)S(1)}, bf16[32,8,128]{2,1,0:T(8,128)(2,1)S(1)}, u32[]{:S(2)}, u32[]{:S(2)}) collective-permute-start(bf16[32,8,128]{2,1,0:T(8,128)(2,1)S(1)} %shard_map.76.state), channel_id=1, source_target_pairs={{0,4},{1,5},{2,6},{3,7},{4,0},{5,1},{6,2},{7,3},{8,12},{9,13},{10,... | collective-permute-start | bytes 196616 | tf_op jit(solution)/shard_map/ppermute | solution.py:358
  11.9 6.7 %copy-start.1 = (bf16[4,32,64,256]{3,2,1,0:T(8,128)(2,1)S(1)}, bf16[4,32,64,256]{3,2,1,0:T(8,128)(2,1)}, u32[]{:S(2)}) copy-start(bf16[4,32,64,256]{3,2,1,0:T(8,128)(2,1)} %blocks.15) | copy-start | bytes 12582916
  14.4 4.2 %copy-start.3 = (s32[4,2,256]{2,1,0:T(2,128)S(1)}, s32[4,2,256]{2,1,0:T(2,128)}, u32[]{:S(2)}) copy-start(s32[4,2,256]{2,1,0:T(2,128)} %pattern.53) | copy-start | bytes 24580
  14.4 4.8 %collective-permute-start.4 = (bf16[32,8,128]{2,1,0:T(8,128)(2,1)S(1)}, bf16[32,8,128]{2,1,0:T(8,128)(2,1)S(1)}, u32[]{:S(2)}, u32[]{:S(2)}) collective-permute-start(bf16[32,8,128]{2,1,0:T(8,128)(2,1)S(1)} %shard_map.80.rest_0_.state), channel_id=1, source_target_pairs={{0,4},{1,5},{2,6},{3,7},{4,0},{5,1},{6,2},{7,3},{8,12},{9,13},{10,... | collective-permute-start | bytes 196616 | tf_op jit(solution)/shard_map/ppermute | solution.py:358
  17.0 4.3 %collective-permute-start.3 = (bf16[32,8,128]{2,1,0:T(8,128)(2,1)S(1)}, bf16[32,8,128]{2,1,0:T(8,128)(2,1)S(1)}, u32[]{:S(2)}, u32[]{:S(2)}) collective-permute-start(bf16[32,8,128]{2,1,0:T(8,128)(2,1)S(1)} %shard_map.82.state), channel_id=1, source_target_pairs={{0,2},{1,3},{2,0},{3,1},{4,6},{5,7},{6,4},{7,5},{8,10},{9,11},{10,... | collective-permute-start | bytes 196616 | tf_op jit(solution)/shard_map/ppermute | solution.py:358
  21.7 2.8 %collective-permute-start.5 = (bf16[68,64,128]{2,1,0:T(8,128)(2,1)S(1)}, bf16[68,64,128]{2,1,0:T(8,128)(2,1)S(1)}, u32[]{:S(2)}, u32[]{:S(2)}) collective-permute-start(bf16[68,64,128]{2,1,0:T(8,128)(2,1)S(1)} %shard_map.87), channel_id=1, source_target_pairs={{0,1},{1,0},{2,3},{3,2},{4,5},{5,4},{6,7},{7,6},{8,9},{9,8},{10,11... | collective-permute-start | bytes 3342344 | tf_op jit(solution)/shard_map/ppermute | solution.py:358
  21.8 4.5 %collective-permute-start.6 = (bf16[32,8,128]{2,1,0:T(8,128)(2,1)S(1)}, bf16[32,8,128]{2,1,0:T(8,128)(2,1)S(1)}, u32[]{:S(2)}, u32[]{:S(2)}) collective-permute-start(bf16[32,8,128]{2,1,0:T(8,128)(2,1)S(1)} %shard_map.84.rest_0_.state), channel_id=1, source_target_pairs={{0,2},{1,3},{2,0},{3,1},{4,6},{5,7},{6,4},{7,5},{8,10},{9,11},{10,... | collective-permute-start | bytes 196616 | tf_op jit(solution)/shard_map/ppermute | solution.py:358
  26.3 5.8 %copy-start.4 = (bf16[64,32,256]{2,1,0:T(8,128)(2,1)S(1)}, bf16[64,32,256]{2,1,0:T(8,128)(2,1)}, u32[]{:S(2)}) copy-start(bf16[64,32,256]{2,1,0:T(8,128)(2,1)} %interp.5) | copy-start | bytes 3145732
  27.8 5.8 %collective-permute-start.7 = (bf16[2,2,32,128]{3,2,1,0:T(8,128)(2,1)S(1)}, bf16[2,2,32,128]{3,2,1,0:T(8,128)(2,1)S(1)}, u32[]{:S(2)}, u32[]{:S(2)}) collective-permute-start(bf16[2,2,32,128]{3,2,1,0:T(8,128)(2,1)S(1)} %get-tuple-element.61), channel_id=1, source_target_pairs={{0,2},{1,10},{2,0},{3,8},{4,6},{5,14},{6,4},{7,12},{8,3},{9,11},{1... | collective-permute-start | bytes 98312 | tf_op jit(solution)/shard_map/ppermute | solution.py:358
  29.4 4.8 %collective-permute-start.8 = (bf16[2,2,32,128]{3,2,1,0:T(8,128)(2,1)S(1)}, bf16[2,2,32,128]{3,2,1,0:T(8,128)(2,1)S(1)}, u32[]{:S(2)}, u32[]{:S(2)}) collective-permute-start(bf16[2,2,32,128]{3,2,1,0:T(8,128)(2,1)S(1)} %get-tuple-element.62), channel_id=1, source_target_pairs={{0,6},{1,14},{2,4},{3,12},{4,2},{5,10},{6,0},{7,8},{8,7},{9,15},{1... | collective-permute-start | bytes 98312 | tf_op jit(solution)/shard_map/ppermute | solution.py:358
  29.5 4.7 %collective-permute-start.9 = (bf16[2,2,32,128]{3,2,1,0:T(8,128)(2,1)S(1)}, bf16[2,2,32,128]{3,2,1,0:T(8,128)(2,1)S(1)}, u32[]{:S(2)}, u32[]{:S(2)}) collective-permute-start(bf16[2,2,32,128]{3,2,1,0:T(8,128)(2,1)S(1)} %get-tuple-element.63), channel_id=1, source_target_pairs={{0,4},{1,12},{2,6},{3,14},{4,0},{5,8},{6,2},{7,10},{8,5},{9,13},{1... | collective-permute-start | bytes 98312 | tf_op jit(solution)/shard_map/ppermute | solution.py:358
  31.4 2.9 %collective-permute-start.10 = (bf16[2,2,32,128]{3,2,1,0:T(8,128)(2,1)S(1)}, bf16[2,2,32,128]{3,2,1,0:T(8,128)(2,1)S(1)}, u32[]{:S(2)}, u32[]{:S(2)}) collective-permute-start(bf16[2,2,32,128]{3,2,1,0:T(8,128)(2,1)S(1)} %get-tuple-element.57.rest_0_.kept), channel_id=1, source_target_pairs={{1,8},{3,10},{5,12},{7,14},{8,1},{10,3},{12,5},{14,7},{17,24},{19,... | collective-permute-start | bytes 98312 | tf_op jit(solution)/shard_map/ppermute | solution.py:358
  35.2 7.3 %collective-permute-start.11 = (bf16[32,8,128]{2,1,0:T(8,128)(2,1)S(1)}, bf16[32,8,128]{2,1,0:T(8,128)(2,1)S(1)}, u32[]{:S(2)}, u32[]{:S(2)}) collective-permute-start(bf16[32,8,128]{2,1,0:T(8,128)(2,1)S(1)} %get-tuple-element.76), channel_id=1, source_target_pairs={{0,1},{1,0},{2,3},{3,2},{4,5},{5,4},{6,7},{7,6},{8,9},{9,8},{10,11... | collective-permute-start | bytes 196616 | tf_op jit(solution)/shard_map/ppermute | solution.py:358
  40.7 4.6 %collective-permute-start.15 = (bf16[32,8,128]{2,1,0:T(8,128)(2,1)S(1)}, bf16[32,8,128]{2,1,0:T(8,128)(2,1)S(1)}, u32[]{:S(2)}, u32[]{:S(2)}) collective-permute-start(bf16[32,8,128]{2,1,0:T(8,128)(2,1)S(1)} %shard_map.103.state), channel_id=1, source_target_pairs={{0,2},{1,3},{2,0},{3,1},{4,6},{5,7},{6,4},{7,5},{8,10},{9,11},{10,... | collective-permute-start | bytes 196616 | tf_op jit(solution)/shard_map/ppermute | solution.py:358
  42.5 4.3 %collective-permute-start.12 = (bf16[32,8,128]{2,1,0:T(8,128)(2,1)S(1)}, bf16[32,8,128]{2,1,0:T(8,128)(2,1)S(1)}, u32[]{:S(2)}, u32[]{:S(2)}) collective-permute-start(bf16[32,8,128]{2,1,0:T(8,128)(2,1)S(1)} %collective-permute-done.11.state.rest_0_), channel_id=1, source_target_pairs={{0,2},{1,3},{2,0},{3,1},{4,6},{5,7},{6,4},{7,5},{8,10},{9,11},{10,... | collective-permute-start | bytes 196616 | tf_op jit(solution)/shard_map/ppermute | solution.py:358
  45.7 4.3 %collective-permute-start.16 = (bf16[32,8,128]{2,1,0:T(8,128)(2,1)S(1)}, bf16[32,8,128]{2,1,0:T(8,128)(2,1)S(1)}, u32[]{:S(2)}, u32[]{:S(2)}) collective-permute-start(bf16[32,8,128]{2,1,0:T(8,128)(2,1)S(1)} %shard_map.105.state), channel_id=1, source_target_pairs={{0,4},{1,5},{2,6},{3,7},{4,0},{5,1},{6,2},{7,3},{8,12},{9,13},{10,... | collective-permute-start | bytes 196616 | tf_op jit(solution)/shard_map/ppermute | solution.py:358
  47.1 4.5 %collective-permute-start.13 = (bf16[32,8,128]{2,1,0:T(8,128)(2,1)S(1)}, bf16[32,8,128]{2,1,0:T(8,128)(2,1)S(1)}, u32[]{:S(2)}, u32[]{:S(2)}) collective-permute-start(bf16[32,8,128]{2,1,0:T(8,128)(2,1)S(1)} %shard_map.99.state.rest_0_), channel_id=1, source_target_pairs={{0,4},{1,5},{2,6},{3,7},{4,0},{5,1},{6,2},{7,3},{8,12},{9,13},{10,... | collective-permute-start | bytes 196616 | tf_op jit(solution)/shard_map/ppermute | solution.py:358
  50.3 6.3 %collective-permute-start.17 = (bf16[32,8,128]{2,1,0:T(8,128)(2,1)S(1)}, bf16[32,8,128]{2,1,0:T(8,128)(2,1)S(1)}, u32[]{:S(2)}, u32[]{:S(2)}) collective-permute-start(bf16[32,8,128]{2,1,0:T(8,128)(2,1)S(1)} %shard_map.107.state), channel_id=1, source_target_pairs={{0,8},{1,9},{2,10},{3,11},{4,12},{5,13},{6,14},{7,15},{8,0},{9,1},... | collective-permute-start | bytes 196616 | tf_op jit(solution)/shard_map/ppermute | solution.py:358
  52.0 5.7 %collective-permute-start.14 = (bf16[32,8,128]{2,1,0:T(8,128)(2,1)S(1)}, bf16[32,8,128]{2,1,0:T(8,128)(2,1)S(1)}, u32[]{:S(2)}, u32[]{:S(2)}) collective-permute-start(bf16[32,8,128]{2,1,0:T(8,128)(2,1)S(1)} %shard_map.101.state.rest_0_), channel_id=1, source_target_pairs={{0,8},{1,9},{2,10},{3,11},{4,12},{5,13},{6,14},{7,15},{8,0},{9,1},... | collective-permute-start | bytes 196616 | tf_op jit(solution)/shard_map/ppermute | solution.py:358

commit v15 on v13

--- a/solution.py
+++ b/solution.py
@@ -9,7 +9,7 @@
 
 LANES = 128
 GROUP = 4
-ROWS = 8
+ROWS = 16
 KERNEL_COST = 2**19
 KERNEL_LIMIT = 16 * 2**20
 FETCH_LIMIT = 53_850_000

time: 59.5 us -> 58.8 us (0.988)
  Pallas kernels: 20.6 us -> 19.6 us
    pallas_call x38, Pallas kernels: 20.6 us -> 19.6 us  [run(): pl.pallas_call(kernel, out_shape=shapes, in_specs=in_specs or [whole] * l...]
  transfers between devices with their start and end apart: 18 -> 18, of which waited for: 11 -> 11; matrix products, arithmetic and copies ran while one was open for 0% -> 0% of each run, Pallas kernels for 24% -> 23%
where the time goes in v15:
time: 58.8 us; the launch traced here: 58.6 us
  starting transfers between devices  26.3 us (45%)
  Pallas kernels  19.6 us (33%)
  waiting for transfers between devices  12.4 us (21%)
    ppermute x18, starting transfers between devices, permuted(): return lax.ppermute(value, 'leaf', pairs)  26.3 us
    pallas_call x38, Pallas kernels, run(): pl.pallas_call(kernel, out_shape=shapes, in_specs=in_specs or [whole] * l...  19.6 us
    ppermute x18, waiting for transfers between devices, permuted(): return lax.ppermute(value, 'leaf', pairs)  12.4 us
  transfers between devices with their start and end apart: 18, of which 11 were waited for; matrix products, arithmetic and copies ran while one was open for 0% of the time, Pallas kernels for 23%

profile of v15, /device:TPU:0, one launch (start us, length us, event | category | flops | bytes accessed | tf_op | source)
XLA Modules:
  0.0 58.6 jit_solution(11896395363792358707)
XLA Ops:
  0.0 1.7 %shard_map.73.after.state = bf16[32,8,128]{2,1,0:T(8,128)(2,1)S(1)} custom-call(bf16[32,64,256]{2,1,0:T(8,128)(2,1)} %interp.4, bf16[64,8,256]{2,1,0:T(8,128)(2,1)} %samples.3), custom_call_target="tpu_custom_call" | custom-call | flops 1048576 | bytes 1048576 | tf_op jit(solution)/shard_map/pallas_call | solution.py:341
  1.8 4.1 %collective-permute-start = (bf16[32,8,128]{2,1,0:T(8,128)(2,1)S(1)}, bf16[32,8,128]{2,1,0:T(8,128)(2,1)S(1)}, u32[]{:S(2)}, u32[]{:S(2)}) collective-permute-start(bf16[32,8,128]{2,1,0:T(8,128)(2,1)S(1)} %shard_map.73.after.state), channel_id=1, source_target_pairs={{0,8},{1,9},{2,10},{3,11},{4,12},{5,13},{6,14},{7,15},{8,0},{9,1},... | collective-permute-start | bytes 196616 | tf_op jit(solution)/shard_map/ppermute | solution.py:357
  5.9 2.5 %shard_map.74 = (bf16[32,8,128]{2,1,0:T(8,128)(2,1)S(1)}, f32[1024,128]{1,0:T(8,128)S(1)}, f32[1024,128]{1,0:T(8,128)S(1)}, f32[1024,128]{1,0:T(8,128)S(1)}, f32[1024,128]{1,0:T(8,128)S(1)}) custom-call(bf16[4,32,64,256]{3,2,1,0:T(8,128)(2,1)} %blocks.11, bf16[32,64,256]{2,1,0:T(8,128)(2,1)} %interp.4, bf16[64,8,256]{2,1,0:T(8,128)(2,1)S(1)} %copy-done.5, ...), custom_call_target="tpu_custom_call" | custom-call | flops 2097152 | bytes 2097152 | tf_op jit(solution)/shard_map/pallas_call | solution.py:341
  8.5 0.3 shard_map.75.near
  8.8 0.7 %collective-permute-done.partner = bf16[32,8,128]{2,1,0:T(8,128)(2,1)S(1)} collective-permute-done((bf16[32,8,128]{2,1,0:T(8,128)(2,1)S(1)}, bf16[32,8,128]{2,1,0:T(8,128)(2,1)S(1)}, u32[]{:S(2)}, u32[]{:S(2)}) %collective-permute-start) | collective-permute-done | bytes 65568 | tf_op jit(solution)/shard_map/ppermute | solution.py:357
  9.5 0.3 shard_map.76.state
  9.9 1.2 %collective-permute-start.1 = (bf16[32,8,128]{2,1,0:T(8,128)(2,1)S(1)}, bf16[32,8,128]{2,1,0:T(8,128)(2,1)S(1)}, u32[]{:S(2)}, u32[]{:S(2)}) collective-permute-start(bf16[32,8,128]{2,1,0:T(8,128)(2,1)S(1)} %shard_map.76.state), channel_id=1, source_target_pairs={{0,4},{1,5},{2,6},{3,7},{4,0},{5,1},{6,2},{7,3},{8,12},{9,13},{10,... | collective-permute-start | bytes 196616 | tf_op jit(solution)/shard_map/ppermute | solution.py:357
  11.1 0.3 shard_map.77.rest_0_.near
  11.4 0.3 shard_map.79
  11.8 0.3 shard_map.78
  12.1 1.8 %collective-permute-done.2.partner = bf16[32,8,128]{2,1,0:T(8,128)(2,1)S(1)} collective-permute-done((bf16[32,8,128]{2,1,0:T(8,128)(2,1)S(1)}, bf16[32,8,128]{2,1,0:T(8,128)(2,1)S(1)}, u32[]{:S(2)}, u32[]{:S(2)}) %collective-permute-start.2) | collective-permute-done | bytes 65568 | tf_op jit(solution)/shard_map/ppermute | solution.py:357
  13.9 0.3 shard_map.80.rest_0_.state
  14.3 1.9 %collective-permute-start.4 = (bf16[32,8,128]{2,1,0:T(8,128)(2,1)S(1)}, bf16[32,8,128]{2,1,0:T(8,128)(2,1)S(1)}, u32[]{:S(2)}, u32[]{:S(2)}) collective-permute-start(bf16[32,8,128]{2,1,0:T(8,128)(2,1)S(1)} %shard_map.80.rest_0_.state), channel_id=1, source_target_pairs={{0,4},{1,5},{2,6},{3,7},{4,0},{5,1},{6,2},{7,3},{8,12},{9,13},{10,... | collective-permute-start | bytes 196616 | tf_op jit(solution)/shard_map/ppermute | solution.py:357
  16.2 0.3 shard_map.81.near
  16.5 0.3 shard_map.82.state
  16.9 1.6 %collective-permute-start.3 = (bf16[32,8,128]{2,1,0:T(8,128)(2,1)S(1)}, bf16[32,8,128]{2,1,0:T(8,128)(2,1)S(1)}, u32[]{:S(2)}, u32[]{:S(2)}) collective-permute-start(bf16[32,8,128]{2,1,0:T(8,128)(2,1)S(1)} %shard_map.82.state), channel_id=1, source_target_pairs={{0,2},{1,3},{2,0},{3,1},{4,6},{5,7},{6,4},{7,5},{8,10},{9,11},{10,... | collective-permute-start | bytes 196616 | tf_op jit(solution)/shard_map/ppermute | solution.py:357
  18.5 0.2 shard_map.86.shared
  18.7 0.3 shard_map.83.near
  19.1 0.3 shard_map.84.rest_0_.state
  19.4 0.3 shard_map.85.near
  19.8 1.5 %collective-permute-done.3.partner = bf16[32,8,128]{2,1,0:T(8,128)(2,1)S(1)} collective-permute-done((bf16[32,8,128]{2,1,0:T(8,128)(2,1)S(1)}, bf16[32,8,128]{2,1,0:T(8,128)(2,1)S(1)}, u32[]{:S(2)}, u32[]{:S(2)}) %collective-permute-start.3) | collective-permute-done | bytes 65568 | tf_op jit(solution)/shard_map/ppermute | solution.py:357
  21.2 0.3 shard_map.87
  21.6 1.6 %collective-permute-start.6 = (bf16[32,8,128]{2,1,0:T(8,128)(2,1)S(1)}, bf16[32,8,128]{2,1,0:T(8,128)(2,1)S(1)}, u32[]{:S(2)}, u32[]{:S(2)}) collective-permute-start(bf16[32,8,128]{2,1,0:T(8,128)(2,1)S(1)} %shard_map.84.rest_0_.state), channel_id=1, source_target_pairs={{0,2},{1,3},{2,0},{3,1},{4,6},{5,7},{6,4},{7,5},{8,10},{9,11},{10,... | collective-permute-start | bytes 196616 | tf_op jit(solution)/shard_map/ppermute | solution.py:357
  23.2 0.3 shard_map.89.near
  23.5 0.8 %collective-permute-done.5.shared = bf16[68,64,128]{2,1,0:T(8,128)(2,1)S(1)} collective-permute-done((bf16[68,64,128]{2,1,0:T(8,128)(2,1)S(1)}, bf16[68,64,128]{2,1,0:T(8,128)(2,1)S(1)}, u32[]{:S(2)}, u32[]{:S(2)}) %collective-permute-start.5) | collective-permute-done | bytes 1114144 | tf_op jit(solution)/shard_map/ppermute | solution.py:357
  24.4 0.9 %shard_map.88 = (f32[2,32,8,128]{3,2,1,0:T(8,128)S(1)}, f32[2,1024,128]{2,1,0:T(8,128)S(1)}) custom-call(bf16[4,32,64,256]{3,2,1,0:T(8,128)(2,1)S(1)} %copy-done, s32[4,2,256]{2,1,0:T(2,128)S(1)} %copy-done.2, bf16[68,64,128]{2,1,0:T(8,128)(2,1)S(1)} %collective-permute-done.5.shared), custom_call_target="tpu_custom_call" | custom-call | flops 1048576 | bytes 1048576 | tf_op jit(solution)/shard_map/pallas_call | solution.py:341
  25.2 0.9 %collective-permute-done.6.partner = bf16[32,8,128]{2,1,0:T(8,128)(2,1)S(1)} collective-permute-done((bf16[32,8,128]{2,1,0:T(8,128)(2,1)S(1)}, bf16[32,8,128]{2,1,0:T(8,128)(2,1)S(1)}, u32[]{:S(2)}, u32[]{:S(2)}) %collective-permute-start.6) | collective-permute-done | bytes 65568 | tf_op jit(solution)/shard_map/ppermute | solution.py:357
  26.1 0.3 shard_map.90.state
  26.5 1.1 %shard_map.91 = (bf16[2,2,32,128]{3,2,1,0:T(8,128)(2,1)S(1)}, bf16[2,2,32,128]{3,2,1,0:T(8,128)(2,1)S(1)}, bf16[2,2,32,128]{3,2,1,0:T(8,128)(2,1)S(1)}, bf16[2,2,32,128]{3,2,1,0:T(8,128)(2,1)S(1)}) custom-call(s32[4,2,256]{2,1,0:T(2,128)S(1)} %copy-done.2, f32[2,1024,128]{2,1,0:T(8,128)S(1)} %get-tuple-element.54.wide, ...), custom_call_target="tpu_custom_call" | custom-call | flops 1048576 | bytes 1048576 | tf_op jit(solution)/shard_map/pallas_call | solution.py:341
  27.6 1.6 %collective-permute-start.8 = (bf16[2,2,32,128]{3,2,1,0:T(8,128)(2,1)S(1)}, bf16[2,2,32,128]{3,2,1,0:T(8,128)(2,1)S(1)}, u32[]{:S(2)}, u32[]{:S(2)}) collective-permute-start(bf16[2,2,32,128]{3,2,1,0:T(8,128)(2,1)S(1)} %get-tuple-element.61), channel_id=1, source_target_pairs={{0,2},{1,10},{2,0},{3,8},{4,6},{5,14},{6,4},{7,12},{8,3},{9,11},{1... | collective-permute-start | bytes 98312 | tf_op jit(solution)/shard_map/ppermute | solution.py:357
  29.2 0.1 collective-permute-start.9
  29.3 1.8 %collective-permute-start.10 = (bf16[2,2,32,128]{3,2,1,0:T(8,128)(2,1)S(1)}, bf16[2,2,32,128]{3,2,1,0:T(8,128)(2,1)S(1)}, u32[]{:S(2)}, u32[]{:S(2)}) collective-permute-start(bf16[2,2,32,128]{3,2,1,0:T(8,128)(2,1)S(1)} %get-tuple-element.63), channel_id=1, source_target_pairs={{0,6},{1,14},{2,4},{3,12},{4,2},{5,10},{6,0},{7,8},{8,7},{9,15},{1... | collective-permute-start | bytes 98312 | tf_op jit(solution)/shard_map/ppermute | solution.py:357
  31.1 0.7 %collective-permute-start.7 = (bf16[2,2,32,128]{3,2,1,0:T(8,128)(2,1)S(1)}, bf16[2,2,32,128]{3,2,1,0:T(8,128)(2,1)S(1)}, u32[]{:S(2)}, u32[]{:S(2)}) collective-permute-start(bf16[2,2,32,128]{3,2,1,0:T(8,128)(2,1)S(1)} %get-tuple-element.57.rest_0_.kept), channel_id=1, source_target_pairs={{1,8},{3,10},{5,12},{7,14},{8,1},{10,3},{12,5},{14,7},{17,24},{19,... | collective-permute-start | bytes 98312 | tf_op jit(solution)/shard_map/ppermute | solution.py:357
  31.8 0.3 shard_map.93
  32.1 0.3 shard_map.94
  32.4 0.3 shard_map.96
  32.7 0.3 shard_map.95
  33.0 0.3 shard_map.92
  33.4 0.7 %collective-permute-done.10.rest_3_ = bf16[2,2,32,128]{3,2,1,0:T(8,128)(2,1)S(1)} collective-permute-done((bf16[2,2,32,128]{3,2,1,0:T(8,128)(2,1)S(1)}, bf16[2,2,32,128]{3,2,1,0:T(8,128)(2,1)S(1)}, u32[]{:S(2)}, u32[]{:S(2)}) %collective-permute-start.10) | collective-permute-done | bytes 32800 | tf_op jit(solution)/shard_map/ppermute | solution.py:357
  34.1 0.9 %shard_map.97 = (bf16[32,8,128]{2,1,0:T(8,128)(2,1)S(1)}, bf16[2,32,8,128]{3,2,1,0:T(8,128)(2,1)S(1)}) custom-call(f32[2,1024,128]{2,1,0:T(8,128)S(1)} %get-tuple-element.60.wide, bf16[2,2,32,128]{3,2,1,0:T(8,128)(2,1)S(1)} %get-tuple-element.57.rest_0_.kept, bf16[2,2,32,128]{3,2,1,0:T(8,128)(2,1)S(1)} %collective-permute-done.7.rest_0_, ...), custom_call_target="tpu_custom_call" | custom-call | flops 1048576 | bytes 1048576 | tf_op jit(solution)/shard_map/pallas_call | solution.py:341
  35.0 4.8 %collective-permute-start.11 = (bf16[32,8,128]{2,1,0:T(8,128)(2,1)S(1)}, bf16[32,8,128]{2,1,0:T(8,128)(2,1)S(1)}, u32[]{:S(2)}, u32[]{:S(2)}) collective-permute-start(bf16[32,8,128]{2,1,0:T(8,128)(2,1)S(1)} %get-tuple-element.76), channel_id=1, source_target_pairs={{0,1},{1,0},{2,3},{3,2},{4,5},{5,4},{6,7},{7,6},{8,9},{9,8},{10,11... | collective-permute-start | bytes 196616 | tf_op jit(solution)/shard_map/ppermute | solution.py:357
  39.8 0.6 %shard_map.103.state = bf16[32,8,128]{2,1,0:T(8,128)(2,1)S(1)} custom-call(s32[4,2,256]{2,1,0:T(2,128)S(1)} %copy-done.3, f32[2,1024,128]{2,1,0:T(8,128)S(1)} %get-tuple-element.77.wide, bf16[2,32,8,128]{3,2,1,0:T(8,128)(2,1)S(1)} %get-tuple-element.78.states), custom_call_target="tpu_custom_call" | custom-call | flops 1048576 | bytes 1048576 | tf_op jit(solution)/shard_map/pallas_call | solution.py:341
  40.4 1.6 %collective-permute-start.15 = (bf16[32,8,128]{2,1,0:T(8,128)(2,1)S(1)}, bf16[32,8,128]{2,1,0:T(8,128)(2,1)S(1)}, u32[]{:S(2)}, u32[]{:S(2)}) collective-permute-start(bf16[32,8,128]{2,1,0:T(8,128)(2,1)S(1)} %shard_map.103.state), channel_id=1, source_target_pairs={{0,2},{1,3},{2,0},{3,1},{4,6},{5,7},{6,4},{7,5},{8,10},{9,11},{10,... | collective-permute-start | bytes 196616 | tf_op jit(solution)/shard_map/ppermute | solution.py:357
  42.0 0.5 collective-permute-start.12
  42.5 0.3 shard_map.104.near
  42.8 2.3 %collective-permute-done.15.partner = bf16[32,8,128]{2,1,0:T(8,128)(2,1)S(1)} collective-permute-done((bf16[32,8,128]{2,1,0:T(8,128)(2,1)S(1)}, bf16[32,8,128]{2,1,0:T(8,128)(2,1)S(1)}, u32[]{:S(2)}, u32[]{:S(2)}) %collective-permute-start.15) | collective-permute-done | bytes 65568 | tf_op jit(solution)/shard_map/ppermute | solution.py:357
  45.1 0.3 shard_map.105.state
  45.5 0.3 shard_map.98.near
  45.8 0.5 collective-permute-done.12.partner
  46.3 0.3 shard_map.99.state.rest_0_
  46.6 1.6 %collective-permute-start.13 = (bf16[32,8,128]{2,1,0:T(8,128)(2,1)S(1)}, bf16[32,8,128]{2,1,0:T(8,128)(2,1)S(1)}, u32[]{:S(2)}, u32[]{:S(2)}) collective-permute-start(bf16[32,8,128]{2,1,0:T(8,128)(2,1)S(1)} %shard_map.99.state.rest_0_), channel_id=1, source_target_pairs={{0,4},{1,5},{2,6},{3,7},{4,0},{5,1},{6,2},{7,3},{8,12},{9,13},{10,... | collective-permute-start | bytes 196616 | tf_op jit(solution)/shard_map/ppermute | solution.py:357
  48.2 0.3 shard_map.106.near
  48.6 1.2 %collective-permute-done.16.partner = bf16[32,8,128]{2,1,0:T(8,128)(2,1)S(1)} collective-permute-done((bf16[32,8,128]{2,1,0:T(8,128)(2,1)S(1)}, bf16[32,8,128]{2,1,0:T(8,128)(2,1)S(1)}, u32[]{:S(2)}, u32[]{:S(2)}) %collective-permute-start.16) | collective-permute-done | bytes 65568 | tf_op jit(solution)/shard_map/ppermute | solution.py:357
  49.8 0.3 shard_map.107.state
  50.1 0.4 collective-permute-start.17
  50.5 0.3 shard_map.100.near
  50.8 0.2 collective-permute-done.13.partner
  51.0 0.3 shard_map.101.state.rest_0_
  51.3 2.5 %collective-permute-start.14 = (bf16[32,8,128]{2,1,0:T(8,128)(2,1)S(1)}, bf16[32,8,128]{2,1,0:T(8,128)(2,1)S(1)}, u32[]{:S(2)}, u32[]{:S(2)}) collective-permute-start(bf16[32,8,128]{2,1,0:T(8,128)(2,1)S(1)} %shard_map.101.state.rest_0_), channel_id=1, source_target_pairs={{0,8},{1,9},{2,10},{3,11},{4,12},{5,13},{6,14},{7,15},{8,0},{9,1},... | collective-permute-start | bytes 196616 | tf_op jit(solution)/shard_map/ppermute | solution.py:357
  53.8 0.3 shard_map.102.near
  54.1 0.3 shard_map.108.near
  54.4 1.7 %collective-permute-done.17.partner = bf16[32,8,128]{2,1,0:T(8,128)(2,1)S(1)} collective-permute-done((bf16[32,8,128]{2,1,0:T(8,128)(2,1)S(1)}, bf16[32,8,128]{2,1,0:T(8,128)(2,1)S(1)}, u32[]{:S(2)}, u32[]{:S(2)}) %collective-permute-start.17) | collective-permute-done | bytes 65568 | tf_op jit(solution)/shard_map/ppermute | solution.py:357
  56.1 0.9 %shard_map.109.ready = bf16[64,8,128]{2,1,0:T(8,128)(2,1)S(1)} custom-call(s32[4,2,256]{2,1,0:T(2,128)S(1)} %copy-done.3, f32[1024,128]{1,0:T(8,128)S(1)} %get-tuple-element.74.rest_14_.wide, f32[2048,128]{1,0:T(8,128)S(1)} %get-tuple-element.75.rest_16_.image_wide, bf16[32,8,128]{2,1,0:T(8,128)(2,1)S(1)} %collective-permute-done.17.partner, ...), custom_call_target="tpu_custom_call" | custom-call | flops 1572864 | bytes 1572864 | tf_op jit(solution)/shard_map/pallas_call | solution.py:341
  57.1 1.5 %shard_map.110 = bf16[64,8,256]{2,1,0:T(8,128)(2,1)} custom-call(s32[4,2,256]{2,1,0:T(2,128)S(1)} %copy-done.3, f32[1024,128]{1,0:T(8,128)S(1)} %get-tuple-element.58.rest_15_.wide, f32[2048,128]{1,0:T(8,128)S(1)} %get-tuple-element.59.rest_17_.image_wide, bf16[32,8,128]{2,1,0:T(8,128)(2,1)S(1)} %collective-permute-done.14.partner, ...), custom_call_target="tpu_custom_call" | custom-call | flops 1572864 | bytes 1572864 | tf_op jit(solution)/shard_map/pallas_call | solution.py:341
  (22 shorter events, 0.3 us)
Async XLA Ops:
  0.0 5.9 %copy-start.5 = (bf16[64,8,256]{2,1,0:T(8,128)(2,1)S(1)}, bf16[64,8,256]{2,1,0:T(8,128)(2,1)}, u32[]{:S(2)}) copy-start(bf16[64,8,256]{2,1,0:T(8,128)(2,1)} %samples.3) | copy-start | bytes 786436
  1.8 6.7 %copy-start.2 = (s32[4,2,256]{2,1,0:T(2,128)S(1)}, s32[4,2,256]{2,1,0:T(2,128)}, u32[]{:S(2)}) copy-start(s32[4,2,256]{2,1,0:T(2,128)} %pattern.40) | copy-start | bytes 24580
  1.8 7.8 %collective-permute-start = (bf16[32,8,128]{2,1,0:T(8,128)(2,1)S(1)}, bf16[32,8,128]{2,1,0:T(8,128)(2,1)S(1)}, u32[]{:S(2)}, u32[]{:S(2)}) collective-permute-start(bf16[32,8,128]{2,1,0:T(8,128)(2,1)S(1)} %shard_map.73.after.state), channel_id=1, source_target_pairs={{0,8},{1,9},{2,10},{3,11},{4,12},{5,13},{6,14},{7,15},{8,0},{9,1},... | collective-permute-start | bytes 196616 | tf_op jit(solution)/shard_map/ppermute | solution.py:357
  5.9 5.5 %copy-start = (bf16[4,32,64,256]{3,2,1,0:T(8,128)(2,1)S(1)}, bf16[4,32,64,256]{3,2,1,0:T(8,128)(2,1)}, u32[]{:S(2)}) copy-start(bf16[4,32,64,256]{3,2,1,0:T(8,128)(2,1)} %blocks.11) | copy-start | bytes 12582916
  8.4 5.6 %collective-permute-start.2 = (bf16[32,8,128]{2,1,0:T(8,128)(2,1)S(1)}, bf16[32,8,128]{2,1,0:T(8,128)(2,1)S(1)}, u32[]{:S(2)}, u32[]{:S(2)}) collective-permute-start(bf16[32,8,128]{2,1,0:T(8,128)(2,1)S(1)} %get-tuple-element.44.state), channel_id=1, source_target_pairs={{0,8},{1,9},{2,10},{3,11},{4,12},{5,13},{6,14},{7,15},{8,0},{9,1},... | collective-permute-start | bytes 196616 | tf_op jit(solution)/shard_map/ppermute | solution.py:357
  9.9 6.7 %collective-permute-start.1 = (bf16[32,8,128]{2,1,0:T(8,128)(2,1)S(1)}, bf16[32,8,128]{2,1,0:T(8,128)(2,1)S(1)}, u32[]{:S(2)}, u32[]{:S(2)}) collective-permute-start(bf16[32,8,128]{2,1,0:T(8,128)(2,1)S(1)} %shard_map.76.state), channel_id=1, source_target_pairs={{0,4},{1,5},{2,6},{3,7},{4,0},{5,1},{6,2},{7,3},{8,12},{9,13},{10,... | collective-permute-start | bytes 196616 | tf_op jit(solution)/shard_map/ppermute | solution.py:357
  11.7 6.7 %copy-start.1 = (bf16[4,32,64,256]{3,2,1,0:T(8,128)(2,1)S(1)}, bf16[4,32,64,256]{3,2,1,0:T(8,128)(2,1)}, u32[]{:S(2)}) copy-start(bf16[4,32,64,256]{3,2,1,0:T(8,128)(2,1)} %blocks.15) | copy-start | bytes 12582916
  14.3 4.2 %copy-start.3 = (s32[4,2,256]{2,1,0:T(2,128)S(1)}, s32[4,2,256]{2,1,0:T(2,128)}, u32[]{:S(2)}) copy-start(s32[4,2,256]{2,1,0:T(2,128)} %pattern.53) | copy-start | bytes 24580
  14.3 4.8 %collective-permute-start.4 = (bf16[32,8,128]{2,1,0:T(8,128)(2,1)S(1)}, bf16[32,8,128]{2,1,0:T(8,128)(2,1)S(1)}, u32[]{:S(2)}, u32[]{:S(2)}) collective-permute-start(bf16[32,8,128]{2,1,0:T(8,128)(2,1)S(1)} %shard_map.80.rest_0_.state), channel_id=1, source_target_pairs={{0,4},{1,5},{2,6},{3,7},{4,0},{5,1},{6,2},{7,3},{8,12},{9,13},{10,... | collective-permute-start | bytes 196616 | tf_op jit(solution)/shard_map/ppermute | solution.py:357
  16.9 4.3 %collective-permute-start.3 = (bf16[32,8,128]{2,1,0:T(8,128)(2,1)S(1)}, bf16[32,8,128]{2,1,0:T(8,128)(2,1)S(1)}, u32[]{:S(2)}, u32[]{:S(2)}) collective-permute-start(bf16[32,8,128]{2,1,0:T(8,128)(2,1)S(1)} %shard_map.82.state), channel_id=1, source_target_pairs={{0,2},{1,3},{2,0},{3,1},{4,6},{5,7},{6,4},{7,5},{8,10},{9,11},{10,... | collective-permute-start | bytes 196616 | tf_op jit(solution)/shard_map/ppermute | solution.py:357
  21.5 2.8 %collective-permute-start.5 = (bf16[68,64,128]{2,1,0:T(8,128)(2,1)S(1)}, bf16[68,64,128]{2,1,0:T(8,128)(2,1)S(1)}, u32[]{:S(2)}, u32[]{:S(2)}) collective-permute-start(bf16[68,64,128]{2,1,0:T(8,128)(2,1)S(1)} %shard_map.87), channel_id=1, source_target_pairs={{0,1},{1,0},{2,3},{3,2},{4,5},{5,4},{6,7},{7,6},{8,9},{9,8},{10,11... | collective-permute-start | bytes 3342344 | tf_op jit(solution)/shard_map/ppermute | solution.py:357
  21.6 4.5 %collective-permute-start.6 = (bf16[32,8,128]{2,1,0:T(8,128)(2,1)S(1)}, bf16[32,8,128]{2,1,0:T(8,128)(2,1)S(1)}, u32[]{:S(2)}, u32[]{:S(2)}) collective-permute-start(bf16[32,8,128]{2,1,0:T(8,128)(2,1)S(1)} %shard_map.84.rest_0_.state), channel_id=1, source_target_pairs={{0,2},{1,3},{2,0},{3,1},{4,6},{5,7},{6,4},{7,5},{8,10},{9,11},{10,... | collective-permute-start | bytes 196616 | tf_op jit(solution)/shard_map/ppermute | solution.py:357
  26.1 5.7 %copy-start.4 = (bf16[64,32,256]{2,1,0:T(8,128)(2,1)S(1)}, bf16[64,32,256]{2,1,0:T(8,128)(2,1)}, u32[]{:S(2)}) copy-start(bf16[64,32,256]{2,1,0:T(8,128)(2,1)} %interp.5) | copy-start | bytes 3145732
  27.6 5.8 %collective-permute-start.8 = (bf16[2,2,32,128]{3,2,1,0:T(8,128)(2,1)S(1)}, bf16[2,2,32,128]{3,2,1,0:T(8,128)(2,1)S(1)}, u32[]{:S(2)}, u32[]{:S(2)}) collective-permute-start(bf16[2,2,32,128]{3,2,1,0:T(8,128)(2,1)S(1)} %get-tuple-element.61), channel_id=1, source_target_pairs={{0,2},{1,10},{2,0},{3,8},{4,6},{5,14},{6,4},{7,12},{8,3},{9,11},{1... | collective-permute-start | bytes 98312 | tf_op jit(solution)/shard_map/ppermute | solution.py:357
  29.2 4.2 %collective-permute-start.9 = (bf16[2,2,32,128]{3,2,1,0:T(8,128)(2,1)S(1)}, bf16[2,2,32,128]{3,2,1,0:T(8,128)(2,1)S(1)}, u32[]{:S(2)}, u32[]{:S(2)}) collective-permute-start(bf16[2,2,32,128]{3,2,1,0:T(8,128)(2,1)S(1)} %get-tuple-element.62), channel_id=1, source_target_pairs={{0,4},{1,12},{2,6},{3,14},{4,0},{5,8},{6,2},{7,10},{8,5},{9,13},{1... | collective-permute-start | bytes 98312 | tf_op jit(solution)/shard_map/ppermute | solution.py:357
  29.3 4.8 %collective-permute-start.10 = (bf16[2,2,32,128]{3,2,1,0:T(8,128)(2,1)S(1)}, bf16[2,2,32,128]{3,2,1,0:T(8,128)(2,1)S(1)}, u32[]{:S(2)}, u32[]{:S(2)}) collective-permute-start(bf16[2,2,32,128]{3,2,1,0:T(8,128)(2,1)S(1)} %get-tuple-element.63), channel_id=1, source_target_pairs={{0,6},{1,14},{2,4},{3,12},{4,2},{5,10},{6,0},{7,8},{8,7},{9,15},{1... | collective-permute-start | bytes 98312 | tf_op jit(solution)/shard_map/ppermute | solution.py:357
  31.1 3.0 %collective-permute-start.7 = (bf16[2,2,32,128]{3,2,1,0:T(8,128)(2,1)S(1)}, bf16[2,2,32,128]{3,2,1,0:T(8,128)(2,1)S(1)}, u32[]{:S(2)}, u32[]{:S(2)}) collective-permute-start(bf16[2,2,32,128]{3,2,1,0:T(8,128)(2,1)S(1)} %get-tuple-element.57.rest_0_.kept), channel_id=1, source_target_pairs={{1,8},{3,10},{5,12},{7,14},{8,1},{10,3},{12,5},{14,7},{17,24},{19,... | collective-permute-start | bytes 98312 | tf_op jit(solution)/shard_map/ppermute | solution.py:357
  35.0 7.0 %collective-permute-start.11 = (bf16[32,8,128]{2,1,0:T(8,128)(2,1)S(1)}, bf16[32,8,128]{2,1,0:T(8,128)(2,1)S(1)}, u32[]{:S(2)}, u32[]{:S(2)}) collective-permute-start(bf16[32,8,128]{2,1,0:T(8,128)(2,1)S(1)} %get-tuple-element.76), channel_id=1, source_target_pairs={{0,1},{1,0},{2,3},{3,2},{4,5},{5,4},{6,7},{7,6},{8,9},{9,8},{10,11... | collective-permute-start | bytes 196616 | tf_op jit(solution)/shard_map/ppermute | solution.py:357
  40.4 4.7 %collective-permute-start.15 = (bf16[32,8,128]{2,1,0:T(8,128)(2,1)S(1)}, bf16[32,8,128]{2,1,0:T(8,128)(2,1)S(1)}, u32[]{:S(2)}, u32[]{:S(2)}) collective-permute-start(bf16[32,8,128]{2,1,0:T(8,128)(2,1)S(1)} %shard_map.103.state), channel_id=1, source_target_pairs={{0,2},{1,3},{2,0},{3,1},{4,6},{5,7},{6,4},{7,5},{8,10},{9,11},{10,... | collective-permute-start | bytes 196616 | tf_op jit(solution)/shard_map/ppermute | solution.py:357
  42.0 4.3 %collective-permute-start.12 = (bf16[32,8,128]{2,1,0:T(8,128)(2,1)S(1)}, bf16[32,8,128]{2,1,0:T(8,128)(2,1)S(1)}, u32[]{:S(2)}, u32[]{:S(2)}) collective-permute-start(bf16[32,8,128]{2,1,0:T(8,128)(2,1)S(1)} %collective-permute-done.11.state.rest_0_), channel_id=1, source_target_pairs={{0,2},{1,3},{2,0},{3,1},{4,6},{5,7},{6,4},{7,5},{8,10},{9,11},{10,... | collective-permute-start | bytes 196616 | tf_op jit(solution)/shard_map/ppermute | solution.py:357
  45.4 4.3 %collective-permute-start.16 = (bf16[32,8,128]{2,1,0:T(8,128)(2,1)S(1)}, bf16[32,8,128]{2,1,0:T(8,128)(2,1)S(1)}, u32[]{:S(2)}, u32[]{:S(2)}) collective-permute-start(bf16[32,8,128]{2,1,0:T(8,128)(2,1)S(1)} %shard_map.105.state), channel_id=1, source_target_pairs={{0,4},{1,5},{2,6},{3,7},{4,0},{5,1},{6,2},{7,3},{8,12},{9,13},{10,... | collective-permute-start | bytes 196616 | tf_op jit(solution)/shard_map/ppermute | solution.py:357
  46.6 4.3 %collective-permute-start.13 = (bf16[32,8,128]{2,1,0:T(8,128)(2,1)S(1)}, bf16[32,8,128]{2,1,0:T(8,128)(2,1)S(1)}, u32[]{:S(2)}, u32[]{:S(2)}) collective-permute-start(bf16[32,8,128]{2,1,0:T(8,128)(2,1)S(1)} %shard_map.99.state.rest_0_), channel_id=1, source_target_pairs={{0,4},{1,5},{2,6},{3,7},{4,0},{5,1},{6,2},{7,3},{8,12},{9,13},{10,... | collective-permute-start | bytes 196616 | tf_op jit(solution)/shard_map/ppermute | solution.py:357
  50.1 6.0 %collective-permute-start.17 = (bf16[32,8,128]{2,1,0:T(8,128)(2,1)S(1)}, bf16[32,8,128]{2,1,0:T(8,128)(2,1)S(1)}, u32[]{:S(2)}, u32[]{:S(2)}) collective-permute-start(bf16[32,8,128]{2,1,0:T(8,128)(2,1)S(1)} %shard_map.107.state), channel_id=1, source_target_pairs={{0,8},{1,9},{2,10},{3,11},{4,12},{5,13},{6,14},{7,15},{8,0},{9,1},... | collective-permute-start | bytes 196616 | tf_op jit(solution)/shard_map/ppermute | solution.py:357
  51.3 5.8 %collective-permute-start.14 = (bf16[32,8,128]{2,1,0:T(8,128)(2,1)S(1)}, bf16[32,8,128]{2,1,0:T(8,128)(2,1)S(1)}, u32[]{:S(2)}, u32[]{:S(2)}) collective-permute-start(bf16[32,8,128]{2,1,0:T(8,128)(2,1)S(1)} %shard_map.101.state.rest_0_), channel_id=1, source_target_pairs={{0,8},{1,9},{2,10},{3,11},{4,12},{5,13},{6,14},{7,15},{8,0},{9,1},... | collective-permute-start | bytes 196616 | tf_op jit(solution)/shard_map/ppermute | solution.py:357

commit v16 on v15

--- a/solution.py
+++ b/solution.py
@@ -9,7 +9,7 @@
 
 LANES = 128
 GROUP = 4
-ROWS = 16
+ROWS = 32
 KERNEL_COST = 2**19
 KERNEL_LIMIT = 16 * 2**20
 FETCH_LIMIT = 53_850_000
@@ -39,20 +39,20 @@
 
 
 def multiply(wide, state, row_count, emit):
-    rank = len(state)
+    rank, rows = len(state), min(ROWS, row_count)
 
     def body(step, carry):
-        for inner in range(ROWS):
+        for inner in range(rows):
             sums = [None, None]
             for index in range(rank):
-                weight = wide[pl.ds(step * ROWS * rank + inner * rank + index, 8, stride=0), :]
+                weight = wide[pl.ds(step * rows * rank + inner * rank + index, 8, stride=0), :]
                 term = weight * state[index]
                 old = sums[index % 2]
                 sums[index % 2] = term if old is None else old + term
-            emit(step * ROWS + inner, sums[0] + sums[1])
+            emit(step * rows + inner, sums[0] + sums[1])
         return carry
 
-    lax.fori_loop(0, row_count // ROWS, body, 0)
+    lax.fori_loop(0, row_count // rows, body, 0)
 
 
 def state_rows(ref, present=None):

time: 58.8 us -> 58.5 us (level)
  Pallas kernels: 19.6 us -> 18.8 us
    pallas_call x38, Pallas kernels: 19.6 us -> 18.8 us  [run(): pl.pallas_call(kernel, out_shape=shapes, in_specs=in_specs or [whole] * l...]
  transfers between devices with their start and end apart: 18 -> 18, of which waited for: 11 -> 11; matrix products, arithmetic and copies ran while one was open for 0% -> 0% of each run, Pallas kernels for 23% -> 22%
where the time goes in v16:
time: 58.5 us; the launch traced here: 58.4 us
  starting transfers between devices  26.3 us (45%)
  Pallas kernels  18.8 us (32%)
  waiting for transfers between devices  12.8 us (22%)
    ppermute x18, starting transfers between devices, permuted(): return lax.ppermute(value, 'leaf', pairs)  26.3 us
    pallas_call x38, Pallas kernels, run(): pl.pallas_call(kernel, out_shape=shapes, in_specs=in_specs or [whole] * l...  18.8 us
    ppermute x18, waiting for transfers between devices, permuted(): return lax.ppermute(value, 'leaf', pairs)  12.8 us
  transfers between devices with their start and end apart: 18, of which 11 were waited for; matrix products, arithmetic and copies ran while one was open for 0% of the time, Pallas kernels for 22%

profile of v16, /device:TPU:0, one launch (start us, length us, event | category | flops | bytes accessed | tf_op | source)
XLA Modules:
  0.0 58.4 jit_solution(6478196945306876406)
XLA Ops:
  0.0 1.7 %shard_map.73.after.state = bf16[32,8,128]{2,1,0:T(8,128)(2,1)S(1)} custom-call(bf16[32,64,256]{2,1,0:T(8,128)(2,1)} %interp.4, bf16[64,8,256]{2,1,0:T(8,128)(2,1)} %samples.3), custom_call_target="tpu_custom_call" | custom-call | flops 1048576 | bytes 1048576 | tf_op jit(solution)/shard_map/pallas_call | solution.py:341
  1.7 4.1 %collective-permute-start = (bf16[32,8,128]{2,1,0:T(8,128)(2,1)S(1)}, bf16[32,8,128]{2,1,0:T(8,128)(2,1)S(1)}, u32[]{:S(2)}, u32[]{:S(2)}) collective-permute-start(bf16[32,8,128]{2,1,0:T(8,128)(2,1)S(1)} %shard_map.73.after.state), channel_id=1, source_target_pairs={{0,8},{1,9},{2,10},{3,11},{4,12},{5,13},{6,14},{7,15},{8,0},{9,1},... | collective-permute-start | bytes 196616 | tf_op jit(solution)/shard_map/ppermute | solution.py:357
  5.8 2.4 %shard_map.74 = (bf16[32,8,128]{2,1,0:T(8,128)(2,1)S(1)}, f32[1024,128]{1,0:T(8,128)S(1)}, f32[1024,128]{1,0:T(8,128)S(1)}, f32[1024,128]{1,0:T(8,128)S(1)}, f32[1024,128]{1,0:T(8,128)S(1)}) custom-call(bf16[4,32,64,256]{3,2,1,0:T(8,128)(2,1)} %blocks.11, bf16[32,64,256]{2,1,0:T(8,128)(2,1)} %interp.4, bf16[64,8,256]{2,1,0:T(8,128)(2,1)S(1)} %copy-done.5, ...), custom_call_target="tpu_custom_call" | custom-call | flops 2097152 | bytes 2097152 | tf_op jit(solution)/shard_map/pallas_call | solution.py:341
  8.4 0.3 shard_map.75.near
  8.7 0.8 %collective-permute-done.partner = bf16[32,8,128]{2,1,0:T(8,128)(2,1)S(1)} collective-permute-done((bf16[32,8,128]{2,1,0:T(8,128)(2,1)S(1)}, bf16[32,8,128]{2,1,0:T(8,128)(2,1)S(1)}, u32[]{:S(2)}, u32[]{:S(2)}) %collective-permute-start) | collective-permute-done | bytes 65568 | tf_op jit(solution)/shard_map/ppermute | solution.py:357
  9.5 0.3 shard_map.76.state
  9.8 1.2 %collective-permute-start.1 = (bf16[32,8,128]{2,1,0:T(8,128)(2,1)S(1)}, bf16[32,8,128]{2,1,0:T(8,128)(2,1)S(1)}, u32[]{:S(2)}, u32[]{:S(2)}) collective-permute-start(bf16[32,8,128]{2,1,0:T(8,128)(2,1)S(1)} %shard_map.76.state), channel_id=1, source_target_pairs={{0,4},{1,5},{2,6},{3,7},{4,0},{5,1},{6,2},{7,3},{8,12},{9,13},{10,... | collective-permute-start | bytes 196616 | tf_op jit(solution)/shard_map/ppermute | solution.py:357
  10.9 0.3 shard_map.77.rest_0_.near
  11.2 0.3 shard_map.79
  11.6 0.3 shard_map.78
  11.9 1.9 %collective-permute-done.2.partner = bf16[32,8,128]{2,1,0:T(8,128)(2,1)S(1)} collective-permute-done((bf16[32,8,128]{2,1,0:T(8,128)(2,1)S(1)}, bf16[32,8,128]{2,1,0:T(8,128)(2,1)S(1)}, u32[]{:S(2)}, u32[]{:S(2)}) %collective-permute-start.2) | collective-permute-done | bytes 65568 | tf_op jit(solution)/shard_map/ppermute | solution.py:357
  13.8 0.3 shard_map.80.rest_0_.state
  14.2 1.9 %collective-permute-start.4 = (bf16[32,8,128]{2,1,0:T(8,128)(2,1)S(1)}, bf16[32,8,128]{2,1,0:T(8,128)(2,1)S(1)}, u32[]{:S(2)}, u32[]{:S(2)}) collective-permute-start(bf16[32,8,128]{2,1,0:T(8,128)(2,1)S(1)} %shard_map.80.rest_0_.state), channel_id=1, source_target_pairs={{0,4},{1,5},{2,6},{3,7},{4,0},{5,1},{6,2},{7,3},{8,12},{9,13},{10,... | collective-permute-start | bytes 196616 | tf_op jit(solution)/shard_map/ppermute | solution.py:357
  16.1 0.3 shard_map.81.near
  16.4 0.3 shard_map.82.state
  16.7 1.6 %collective-permute-start.3 = (bf16[32,8,128]{2,1,0:T(8,128)(2,1)S(1)}, bf16[32,8,128]{2,1,0:T(8,128)(2,1)S(1)}, u32[]{:S(2)}, u32[]{:S(2)}) collective-permute-start(bf16[32,8,128]{2,1,0:T(8,128)(2,1)S(1)} %shard_map.82.state), channel_id=1, source_target_pairs={{0,2},{1,3},{2,0},{3,1},{4,6},{5,7},{6,4},{7,5},{8,10},{9,11},{10,... | collective-permute-start | bytes 196616 | tf_op jit(solution)/shard_map/ppermute | solution.py:357
  18.3 0.2 shard_map.86.shared
  18.6 0.3 shard_map.83.near
  18.9 0.3 shard_map.84.rest_0_.state
  19.2 0.3 shard_map.85.near
  19.5 1.6 %collective-permute-done.3.partner = bf16[32,8,128]{2,1,0:T(8,128)(2,1)S(1)} collective-permute-done((bf16[32,8,128]{2,1,0:T(8,128)(2,1)S(1)}, bf16[32,8,128]{2,1,0:T(8,128)(2,1)S(1)}, u32[]{:S(2)}, u32[]{:S(2)}) %collective-permute-start.3) | collective-permute-done | bytes 65568 | tf_op jit(solution)/shard_map/ppermute | solution.py:357
  21.0 0.3 shard_map.87
  21.4 1.6 %collective-permute-start.6 = (bf16[32,8,128]{2,1,0:T(8,128)(2,1)S(1)}, bf16[32,8,128]{2,1,0:T(8,128)(2,1)S(1)}, u32[]{:S(2)}, u32[]{:S(2)}) collective-permute-start(bf16[32,8,128]{2,1,0:T(8,128)(2,1)S(1)} %shard_map.84.rest_0_.state), channel_id=1, source_target_pairs={{0,2},{1,3},{2,0},{3,1},{4,6},{5,7},{6,4},{7,5},{8,10},{9,11},{10,... | collective-permute-start | bytes 196616 | tf_op jit(solution)/shard_map/ppermute | solution.py:357
  23.0 0.3 shard_map.89.near
  23.3 0.9 %collective-permute-done.5.shared = bf16[68,64,128]{2,1,0:T(8,128)(2,1)S(1)} collective-permute-done((bf16[68,64,128]{2,1,0:T(8,128)(2,1)S(1)}, bf16[68,64,128]{2,1,0:T(8,128)(2,1)S(1)}, u32[]{:S(2)}, u32[]{:S(2)}) %collective-permute-start.5) | collective-permute-done | bytes 1114144 | tf_op jit(solution)/shard_map/ppermute | solution.py:357
  24.2 0.8 %shard_map.88 = (f32[2,32,8,128]{3,2,1,0:T(8,128)S(1)}, f32[2,1024,128]{2,1,0:T(8,128)S(1)}) custom-call(bf16[4,32,64,256]{3,2,1,0:T(8,128)(2,1)S(1)} %copy-done, s32[4,2,256]{2,1,0:T(2,128)S(1)} %copy-done.2, bf16[68,64,128]{2,1,0:T(8,128)(2,1)S(1)} %collective-permute-done.5.shared), custom_call_target="tpu_custom_call" | custom-call | flops 1048576 | bytes 1048576 | tf_op jit(solution)/shard_map/pallas_call | solution.py:341
  25.0 0.9 %collective-permute-done.6.partner = bf16[32,8,128]{2,1,0:T(8,128)(2,1)S(1)} collective-permute-done((bf16[32,8,128]{2,1,0:T(8,128)(2,1)S(1)}, bf16[32,8,128]{2,1,0:T(8,128)(2,1)S(1)}, u32[]{:S(2)}, u32[]{:S(2)}) %collective-permute-start.6) | collective-permute-done | bytes 65568 | tf_op jit(solution)/shard_map/ppermute | solution.py:357
  25.9 0.3 shard_map.90.state
  26.2 0.8 %shard_map.91 = (bf16[2,2,32,128]{3,2,1,0:T(8,128)(2,1)S(1)}, bf16[2,2,32,128]{3,2,1,0:T(8,128)(2,1)S(1)}, bf16[2,2,32,128]{3,2,1,0:T(8,128)(2,1)S(1)}, bf16[2,2,32,128]{3,2,1,0:T(8,128)(2,1)S(1)}) custom-call(s32[4,2,256]{2,1,0:T(2,128)S(1)} %copy-done.2, f32[2,1024,128]{2,1,0:T(8,128)S(1)} %get-tuple-element.54.wide, ...), custom_call_target="tpu_custom_call" | custom-call | flops 1048576 | bytes 1048576 | tf_op jit(solution)/shard_map/pallas_call | solution.py:341
  27.1 1.6 %collective-permute-start.8 = (bf16[2,2,32,128]{3,2,1,0:T(8,128)(2,1)S(1)}, bf16[2,2,32,128]{3,2,1,0:T(8,128)(2,1)S(1)}, u32[]{:S(2)}, u32[]{:S(2)}) collective-permute-start(bf16[2,2,32,128]{3,2,1,0:T(8,128)(2,1)S(1)} %get-tuple-element.61), channel_id=1, source_target_pairs={{0,2},{1,10},{2,0},{3,8},{4,6},{5,14},{6,4},{7,12},{8,3},{9,11},{1... | collective-permute-start | bytes 98312 | tf_op jit(solution)/shard_map/ppermute | solution.py:357
  28.7 0.1 collective-permute-start.9
  28.8 1.8 %collective-permute-start.10 = (bf16[2,2,32,128]{3,2,1,0:T(8,128)(2,1)S(1)}, bf16[2,2,32,128]{3,2,1,0:T(8,128)(2,1)S(1)}, u32[]{:S(2)}, u32[]{:S(2)}) collective-permute-start(bf16[2,2,32,128]{3,2,1,0:T(8,128)(2,1)S(1)} %get-tuple-element.63), channel_id=1, source_target_pairs={{0,6},{1,14},{2,4},{3,12},{4,2},{5,10},{6,0},{7,8},{8,7},{9,15},{1... | collective-permute-start | bytes 98312 | tf_op jit(solution)/shard_map/ppermute | solution.py:357
  30.6 0.8 %collective-permute-start.7 = (bf16[2,2,32,128]{3,2,1,0:T(8,128)(2,1)S(1)}, bf16[2,2,32,128]{3,2,1,0:T(8,128)(2,1)S(1)}, u32[]{:S(2)}, u32[]{:S(2)}) collective-permute-start(bf16[2,2,32,128]{3,2,1,0:T(8,128)(2,1)S(1)} %get-tuple-element.57.rest_0_.kept), channel_id=1, source_target_pairs={{1,8},{3,10},{5,12},{7,14},{8,1},{10,3},{12,5},{14,7},{17,24},{19,... | collective-permute-start | bytes 98312 | tf_op jit(solution)/shard_map/ppermute | solution.py:357
  31.5 0.3 shard_map.93
  31.8 0.3 shard_map.94
  32.0 0.3 shard_map.96
  32.4 0.3 shard_map.95
  32.7 0.3 shard_map.92
  33.0 0.6 collective-permute-done.10.rest_3_
  33.6 1.1 %shard_map.97 = (bf16[32,8,128]{2,1,0:T(8,128)(2,1)S(1)}, bf16[2,32,8,128]{3,2,1,0:T(8,128)(2,1)S(1)}) custom-call(f32[2,1024,128]{2,1,0:T(8,128)S(1)} %get-tuple-element.60.wide, bf16[2,2,32,128]{3,2,1,0:T(8,128)(2,1)S(1)} %get-tuple-element.57.rest_0_.kept, bf16[2,2,32,128]{3,2,1,0:T(8,128)(2,1)S(1)} %collective-permute-done.7.rest_0_, ...), custom_call_target="tpu_custom_call" | custom-call | flops 1048576 | bytes 1048576 | tf_op jit(solution)/shard_map/pallas_call | solution.py:341
  34.7 4.8 %collective-permute-start.11 = (bf16[32,8,128]{2,1,0:T(8,128)(2,1)S(1)}, bf16[32,8,128]{2,1,0:T(8,128)(2,1)S(1)}, u32[]{:S(2)}, u32[]{:S(2)}) collective-permute-start(bf16[32,8,128]{2,1,0:T(8,128)(2,1)S(1)} %get-tuple-element.76), channel_id=1, source_target_pairs={{0,1},{1,0},{2,3},{3,2},{4,5},{5,4},{6,7},{7,6},{8,9},{9,8},{10,11... | collective-permute-start | bytes 196616 | tf_op jit(solution)/shard_map/ppermute | solution.py:357
  39.5 0.6 %shard_map.103.state = bf16[32,8,128]{2,1,0:T(8,128)(2,1)S(1)} custom-call(s32[4,2,256]{2,1,0:T(2,128)S(1)} %copy-done.3, f32[2,1024,128]{2,1,0:T(8,128)S(1)} %get-tuple-element.77.wide, bf16[2,32,8,128]{3,2,1,0:T(8,128)(2,1)S(1)} %get-tuple-element.78.states), custom_call_target="tpu_custom_call" | custom-call | flops 1048576 | bytes 1048576 | tf_op jit(solution)/shard_map/pallas_call | solution.py:341
  40.2 1.7 %collective-permute-start.15 = (bf16[32,8,128]{2,1,0:T(8,128)(2,1)S(1)}, bf16[32,8,128]{2,1,0:T(8,128)(2,1)S(1)}, u32[]{:S(2)}, u32[]{:S(2)}) collective-permute-start(bf16[32,8,128]{2,1,0:T(8,128)(2,1)S(1)} %shard_map.103.state), channel_id=1, source_target_pairs={{0,2},{1,3},{2,0},{3,1},{4,6},{5,7},{6,4},{7,5},{8,10},{9,11},{10,... | collective-permute-start | bytes 196616 | tf_op jit(solution)/shard_map/ppermute | solution.py:357
  41.8 0.4 collective-permute-start.12
  42.3 0.3 shard_map.104.near
  42.5 2.4 %collective-permute-done.15.partner = bf16[32,8,128]{2,1,0:T(8,128)(2,1)S(1)} collective-permute-done((bf16[32,8,128]{2,1,0:T(8,128)(2,1)S(1)}, bf16[32,8,128]{2,1,0:T(8,128)(2,1)S(1)}, u32[]{:S(2)}, u32[]{:S(2)}) %collective-permute-start.15) | collective-permute-done | bytes 65568 | tf_op jit(solution)/shard_map/ppermute | solution.py:357
  44.9 0.3 shard_map.105.state
  45.3 0.3 shard_map.98.near
  45.6 0.5 collective-permute-done.12.partner
  46.1 0.3 shard_map.99.state.rest_0_
  46.4 1.6 %collective-permute-start.13 = (bf16[32,8,128]{2,1,0:T(8,128)(2,1)S(1)}, bf16[32,8,128]{2,1,0:T(8,128)(2,1)S(1)}, u32[]{:S(2)}, u32[]{:S(2)}) collective-permute-start(bf16[32,8,128]{2,1,0:T(8,128)(2,1)S(1)} %shard_map.99.state.rest_0_), channel_id=1, source_target_pairs={{0,4},{1,5},{2,6},{3,7},{4,0},{5,1},{6,2},{7,3},{8,12},{9,13},{10,... | collective-permute-start | bytes 196616 | tf_op jit(solution)/shard_map/ppermute | solution.py:357
  48.0 0.3 shard_map.106.near
  48.2 1.3 %collective-permute-done.16.partner = bf16[32,8,128]{2,1,0:T(8,128)(2,1)S(1)} collective-permute-done((bf16[32,8,128]{2,1,0:T(8,128)(2,1)S(1)}, bf16[32,8,128]{2,1,0:T(8,128)(2,1)S(1)}, u32[]{:S(2)}, u32[]{:S(2)}) %collective-permute-start.16) | collective-permute-done | bytes 65568 | tf_op jit(solution)/shard_map/ppermute | solution.py:357
  49.5 0.3 shard_map.107.state
  49.8 0.4 collective-permute-start.17
  50.2 0.3 shard_map.100.near
  50.5 0.2 collective-permute-done.13.partner
  50.7 0.3 shard_map.101.state.rest_0_
  51.0 2.5 %collective-permute-start.14 = (bf16[32,8,128]{2,1,0:T(8,128)(2,1)S(1)}, bf16[32,8,128]{2,1,0:T(8,128)(2,1)S(1)}, u32[]{:S(2)}, u32[]{:S(2)}) collective-permute-start(bf16[32,8,128]{2,1,0:T(8,128)(2,1)S(1)} %shard_map.101.state.rest_0_), channel_id=1, source_target_pairs={{0,8},{1,9},{2,10},{3,11},{4,12},{5,13},{6,14},{7,15},{8,0},{9,1},... | collective-permute-start | bytes 196616 | tf_op jit(solution)/shard_map/ppermute | solution.py:357
  53.5 0.3 shard_map.102.near
  53.8 0.3 shard_map.108.near
  54.1 1.7 %collective-permute-done.17.partner = bf16[32,8,128]{2,1,0:T(8,128)(2,1)S(1)} collective-permute-done((bf16[32,8,128]{2,1,0:T(8,128)(2,1)S(1)}, bf16[32,8,128]{2,1,0:T(8,128)(2,1)S(1)}, u32[]{:S(2)}, u32[]{:S(2)}) %collective-permute-start.17) | collective-permute-done | bytes 65568 | tf_op jit(solution)/shard_map/ppermute | solution.py:357
  55.8 0.9 %shard_map.109.ready = bf16[64,8,128]{2,1,0:T(8,128)(2,1)S(1)} custom-call(s32[4,2,256]{2,1,0:T(2,128)S(1)} %copy-done.3, f32[1024,128]{1,0:T(8,128)S(1)} %get-tuple-element.74.rest_14_.wide, f32[2048,128]{1,0:T(8,128)S(1)} %get-tuple-element.75.rest_16_.image_wide, bf16[32,8,128]{2,1,0:T(8,128)(2,1)S(1)} %collective-permute-done.17.partner, ...), custom_call_target="tpu_custom_call" | custom-call | flops 1572864 | bytes 1572864 | tf_op jit(solution)/shard_map/pallas_call | solution.py:341
  56.7 1.5 %shard_map.110 = bf16[64,8,256]{2,1,0:T(8,128)(2,1)} custom-call(s32[4,2,256]{2,1,0:T(2,128)S(1)} %copy-done.3, f32[1024,128]{1,0:T(8,128)S(1)} %get-tuple-element.58.rest_15_.wide, f32[2048,128]{1,0:T(8,128)S(1)} %get-tuple-element.59.rest_17_.image_wide, bf16[32,8,128]{2,1,0:T(8,128)(2,1)S(1)} %collective-permute-done.14.partner, ...), custom_call_target="tpu_custom_call" | custom-call | flops 1572864 | bytes 1572864 | tf_op jit(solution)/shard_map/pallas_call | solution.py:341
  (22 shorter events, 0.3 us)
Async XLA Ops:
  0.0 5.8 %copy-start.5 = (bf16[64,8,256]{2,1,0:T(8,128)(2,1)S(1)}, bf16[64,8,256]{2,1,0:T(8,128)(2,1)}, u32[]{:S(2)}) copy-start(bf16[64,8,256]{2,1,0:T(8,128)(2,1)} %samples.3) | copy-start | bytes 786436
  1.7 6.7 %copy-start.2 = (s32[4,2,256]{2,1,0:T(2,128)S(1)}, s32[4,2,256]{2,1,0:T(2,128)}, u32[]{:S(2)}) copy-start(s32[4,2,256]{2,1,0:T(2,128)} %pattern.40) | copy-start | bytes 24580
  1.7 7.8 %collective-permute-start = (bf16[32,8,128]{2,1,0:T(8,128)(2,1)S(1)}, bf16[32,8,128]{2,1,0:T(8,128)(2,1)S(1)}, u32[]{:S(2)}, u32[]{:S(2)}) collective-permute-start(bf16[32,8,128]{2,1,0:T(8,128)(2,1)S(1)} %shard_map.73.after.state), channel_id=1, source_target_pairs={{0,8},{1,9},{2,10},{3,11},{4,12},{5,13},{6,14},{7,15},{8,0},{9,1},... | collective-permute-start | bytes 196616 | tf_op jit(solution)/shard_map/ppermute | solution.py:357
  5.8 5.4 %copy-start = (bf16[4,32,64,256]{3,2,1,0:T(8,128)(2,1)S(1)}, bf16[4,32,64,256]{3,2,1,0:T(8,128)(2,1)}, u32[]{:S(2)}) copy-start(bf16[4,32,64,256]{3,2,1,0:T(8,128)(2,1)} %blocks.11) | copy-start | bytes 12582916
  8.3 5.6 %collective-permute-start.2 = (bf16[32,8,128]{2,1,0:T(8,128)(2,1)S(1)}, bf16[32,8,128]{2,1,0:T(8,128)(2,1)S(1)}, u32[]{:S(2)}, u32[]{:S(2)}) collective-permute-start(bf16[32,8,128]{2,1,0:T(8,128)(2,1)S(1)} %get-tuple-element.44.state), channel_id=1, source_target_pairs={{0,8},{1,9},{2,10},{3,11},{4,12},{5,13},{6,14},{7,15},{8,0},{9,1},... | collective-permute-start | bytes 196616 | tf_op jit(solution)/shard_map/ppermute | solution.py:357
  9.8 6.6 %collective-permute-start.1 = (bf16[32,8,128]{2,1,0:T(8,128)(2,1)S(1)}, bf16[32,8,128]{2,1,0:T(8,128)(2,1)S(1)}, u32[]{:S(2)}, u32[]{:S(2)}) collective-permute-start(bf16[32,8,128]{2,1,0:T(8,128)(2,1)S(1)} %shard_map.76.state), channel_id=1, source_target_pairs={{0,4},{1,5},{2,6},{3,7},{4,0},{5,1},{6,2},{7,3},{8,12},{9,13},{10,... | collective-permute-start | bytes 196616 | tf_op jit(solution)/shard_map/ppermute | solution.py:357
  11.6 6.7 %copy-start.1 = (bf16[4,32,64,256]{3,2,1,0:T(8,128)(2,1)S(1)}, bf16[4,32,64,256]{3,2,1,0:T(8,128)(2,1)}, u32[]{:S(2)}) copy-start(bf16[4,32,64,256]{3,2,1,0:T(8,128)(2,1)} %blocks.15) | copy-start | bytes 12582916
  14.2 4.1 %copy-start.3 = (s32[4,2,256]{2,1,0:T(2,128)S(1)}, s32[4,2,256]{2,1,0:T(2,128)}, u32[]{:S(2)}) copy-start(s32[4,2,256]{2,1,0:T(2,128)} %pattern.53) | copy-start | bytes 24580
  14.2 4.7 %collective-permute-start.4 = (bf16[32,8,128]{2,1,0:T(8,128)(2,1)S(1)}, bf16[32,8,128]{2,1,0:T(8,128)(2,1)S(1)}, u32[]{:S(2)}, u32[]{:S(2)}) collective-permute-start(bf16[32,8,128]{2,1,0:T(8,128)(2,1)S(1)} %shard_map.80.rest_0_.state), channel_id=1, source_target_pairs={{0,4},{1,5},{2,6},{3,7},{4,0},{5,1},{6,2},{7,3},{8,12},{9,13},{10,... | collective-permute-start | bytes 196616 | tf_op jit(solution)/shard_map/ppermute | solution.py:357
  16.7 4.3 %collective-permute-start.3 = (bf16[32,8,128]{2,1,0:T(8,128)(2,1)S(1)}, bf16[32,8,128]{2,1,0:T(8,128)(2,1)S(1)}, u32[]{:S(2)}, u32[]{:S(2)}) collective-permute-start(bf16[32,8,128]{2,1,0:T(8,128)(2,1)S(1)} %shard_map.82.state), channel_id=1, source_target_pairs={{0,2},{1,3},{2,0},{3,1},{4,6},{5,7},{6,4},{7,5},{8,10},{9,11},{10,... | collective-permute-start | bytes 196616 | tf_op jit(solution)/shard_map/ppermute | solution.py:357
  21.3 2.8 %collective-permute-start.5 = (bf16[68,64,128]{2,1,0:T(8,128)(2,1)S(1)}, bf16[68,64,128]{2,1,0:T(8,128)(2,1)S(1)}, u32[]{:S(2)}, u32[]{:S(2)}) collective-permute-start(bf16[68,64,128]{2,1,0:T(8,128)(2,1)S(1)} %shard_map.87), channel_id=1, source_target_pairs={{0,1},{1,0},{2,3},{3,2},{4,5},{5,4},{6,7},{7,6},{8,9},{9,8},{10,11... | collective-permute-start | bytes 3342344 | tf_op jit(solution)/shard_map/ppermute | solution.py:357
  21.4 4.5 %collective-permute-start.6 = (bf16[32,8,128]{2,1,0:T(8,128)(2,1)S(1)}, bf16[32,8,128]{2,1,0:T(8,128)(2,1)S(1)}, u32[]{:S(2)}, u32[]{:S(2)}) collective-permute-start(bf16[32,8,128]{2,1,0:T(8,128)(2,1)S(1)} %shard_map.84.rest_0_.state), channel_id=1, source_target_pairs={{0,2},{1,3},{2,0},{3,1},{4,6},{5,7},{6,4},{7,5},{8,10},{9,11},{10,... | collective-permute-start | bytes 196616 | tf_op jit(solution)/shard_map/ppermute | solution.py:357
  25.9 5.5 %copy-start.4 = (bf16[64,32,256]{2,1,0:T(8,128)(2,1)S(1)}, bf16[64,32,256]{2,1,0:T(8,128)(2,1)}, u32[]{:S(2)}) copy-start(bf16[64,32,256]{2,1,0:T(8,128)(2,1)} %interp.5) | copy-start | bytes 3145732
  27.1 6.0 %collective-permute-start.8 = (bf16[2,2,32,128]{3,2,1,0:T(8,128)(2,1)S(1)}, bf16[2,2,32,128]{3,2,1,0:T(8,128)(2,1)S(1)}, u32[]{:S(2)}, u32[]{:S(2)}) collective-permute-start(bf16[2,2,32,128]{3,2,1,0:T(8,128)(2,1)S(1)} %get-tuple-element.61), channel_id=1, source_target_pairs={{0,2},{1,10},{2,0},{3,8},{4,6},{5,14},{6,4},{7,12},{8,3},{9,11},{1... | collective-permute-start | bytes 98312 | tf_op jit(solution)/shard_map/ppermute | solution.py:357
  28.7 4.4 %collective-permute-start.9 = (bf16[2,2,32,128]{3,2,1,0:T(8,128)(2,1)S(1)}, bf16[2,2,32,128]{3,2,1,0:T(8,128)(2,1)S(1)}, u32[]{:S(2)}, u32[]{:S(2)}) collective-permute-start(bf16[2,2,32,128]{3,2,1,0:T(8,128)(2,1)S(1)} %get-tuple-element.62), channel_id=1, source_target_pairs={{0,4},{1,12},{2,6},{3,14},{4,0},{5,8},{6,2},{7,10},{8,5},{9,13},{1... | collective-permute-start | bytes 98312 | tf_op jit(solution)/shard_map/ppermute | solution.py:357
  28.8 4.8 %collective-permute-start.10 = (bf16[2,2,32,128]{3,2,1,0:T(8,128)(2,1)S(1)}, bf16[2,2,32,128]{3,2,1,0:T(8,128)(2,1)S(1)}, u32[]{:S(2)}, u32[]{:S(2)}) collective-permute-start(bf16[2,2,32,128]{3,2,1,0:T(8,128)(2,1)S(1)} %get-tuple-element.63), channel_id=1, source_target_pairs={{0,6},{1,14},{2,4},{3,12},{4,2},{5,10},{6,0},{7,8},{8,7},{9,15},{1... | collective-permute-start | bytes 98312 | tf_op jit(solution)/shard_map/ppermute | solution.py:357
  30.6 3.0 %collective-permute-start.7 = (bf16[2,2,32,128]{3,2,1,0:T(8,128)(2,1)S(1)}, bf16[2,2,32,128]{3,2,1,0:T(8,128)(2,1)S(1)}, u32[]{:S(2)}, u32[]{:S(2)}) collective-permute-start(bf16[2,2,32,128]{3,2,1,0:T(8,128)(2,1)S(1)} %get-tuple-element.57.rest_0_.kept), channel_id=1, source_target_pairs={{1,8},{3,10},{5,12},{7,14},{8,1},{10,3},{12,5},{14,7},{17,24},{19,... | collective-permute-start | bytes 98312 | tf_op jit(solution)/shard_map/ppermute | solution.py:357
  34.7 7.1 %collective-permute-start.11 = (bf16[32,8,128]{2,1,0:T(8,128)(2,1)S(1)}, bf16[32,8,128]{2,1,0:T(8,128)(2,1)S(1)}, u32[]{:S(2)}, u32[]{:S(2)}) collective-permute-start(bf16[32,8,128]{2,1,0:T(8,128)(2,1)S(1)} %get-tuple-element.76), channel_id=1, source_target_pairs={{0,1},{1,0},{2,3},{3,2},{4,5},{5,4},{6,7},{7,6},{8,9},{9,8},{10,11... | collective-permute-start | bytes 196616 | tf_op jit(solution)/shard_map/ppermute | solution.py:357
  40.2 4.7 %collective-permute-start.15 = (bf16[32,8,128]{2,1,0:T(8,128)(2,1)S(1)}, bf16[32,8,128]{2,1,0:T(8,128)(2,1)S(1)}, u32[]{:S(2)}, u32[]{:S(2)}) collective-permute-start(bf16[32,8,128]{2,1,0:T(8,128)(2,1)S(1)} %shard_map.103.state), channel_id=1, source_target_pairs={{0,2},{1,3},{2,0},{3,1},{4,6},{5,7},{6,4},{7,5},{8,10},{9,11},{10,... | collective-permute-start | bytes 196616 | tf_op jit(solution)/shard_map/ppermute | solution.py:357
  41.8 4.3 %collective-permute-start.12 = (bf16[32,8,128]{2,1,0:T(8,128)(2,1)S(1)}, bf16[32,8,128]{2,1,0:T(8,128)(2,1)S(1)}, u32[]{:S(2)}, u32[]{:S(2)}) collective-permute-start(bf16[32,8,128]{2,1,0:T(8,128)(2,1)S(1)} %collective-permute-done.11.state.rest_0_), channel_id=1, source_target_pairs={{0,2},{1,3},{2,0},{3,1},{4,6},{5,7},{6,4},{7,5},{8,10},{9,11},{10,... | collective-permute-start | bytes 196616 | tf_op jit(solution)/shard_map/ppermute | solution.py:357
  45.2 4.3 %collective-permute-start.16 = (bf16[32,8,128]{2,1,0:T(8,128)(2,1)S(1)}, bf16[32,8,128]{2,1,0:T(8,128)(2,1)S(1)}, u32[]{:S(2)}, u32[]{:S(2)}) collective-permute-start(bf16[32,8,128]{2,1,0:T(8,128)(2,1)S(1)} %shard_map.105.state), channel_id=1, source_target_pairs={{0,4},{1,5},{2,6},{3,7},{4,0},{5,1},{6,2},{7,3},{8,12},{9,13},{10,... | collective-permute-start | bytes 196616 | tf_op jit(solution)/shard_map/ppermute | solution.py:357
  46.4 4.3 %collective-permute-start.13 = (bf16[32,8,128]{2,1,0:T(8,128)(2,1)S(1)}, bf16[32,8,128]{2,1,0:T(8,128)(2,1)S(1)}, u32[]{:S(2)}, u32[]{:S(2)}) collective-permute-start(bf16[32,8,128]{2,1,0:T(8,128)(2,1)S(1)} %shard_map.99.state.rest_0_), channel_id=1, source_target_pairs={{0,4},{1,5},{2,6},{3,7},{4,0},{5,1},{6,2},{7,3},{8,12},{9,13},{10,... | collective-permute-start | bytes 196616 | tf_op jit(solution)/shard_map/ppermute | solution.py:357
  49.8 6.0 %collective-permute-start.17 = (bf16[32,8,128]{2,1,0:T(8,128)(2,1)S(1)}, bf16[32,8,128]{2,1,0:T(8,128)(2,1)S(1)}, u32[]{:S(2)}, u32[]{:S(2)}) collective-permute-start(bf16[32,8,128]{2,1,0:T(8,128)(2,1)S(1)} %shard_map.107.state), channel_id=1, source_target_pairs={{0,8},{1,9},{2,10},{3,11},{4,12},{5,13},{6,14},{7,15},{8,0},{9,1},... | collective-permute-start | bytes 196616 | tf_op jit(solution)/shard_map/ppermute | solution.py:357
  51.0 5.7 %collective-permute-start.14 = (bf16[32,8,128]{2,1,0:T(8,128)(2,1)S(1)}, bf16[32,8,128]{2,1,0:T(8,128)(2,1)S(1)}, u32[]{:S(2)}, u32[]{:S(2)}) collective-permute-start(bf16[32,8,128]{2,1,0:T(8,128)(2,1)S(1)} %shard_map.101.state.rest_0_), channel_id=1, source_target_pairs={{0,8},{1,9},{2,10},{3,11},{4,12},{5,13},{6,14},{7,15},{8,0},{9,1},... | collective-permute-start | bytes 196616 | tf_op jit(solution)/shard_map/ppermute | solution.py:357
